TPU v7x, 32 devices: a whole 2x2x4 slice. The times are simulated.
32 devices in a mesh: slab: 8 (over z, x), energy: 4 (over y, core).
Axes of the slice: x: 2, y: 2, z: 4, core: 2. Of those that a mesh axis runs over, the one named last changes fastest.
Arguments:
- green_lesser: bfloat16 [2, 8, 32, 256, 256], P(None, 'energy', 'slab'), may hold values from -4 to 4
- screened_lesser: bfloat16 [2, 8, 32, 256, 256], P(None, 'energy', 'slab'), may hold values from -4 to 4
- green_retarded: bfloat16 [2, 8, 32, 256, 256], P(None, 'energy', 'slab'), may hold values from -1 to 1
- coupling: bfloat16 [2, 32, 256, 256], P(None, 'slab'), may hold values from -1 to 1
Outputs:
- connected_lesser: float32 [2, 8, 32, 256, 256], P(None, 'energy', 'slab')
All inputs are finite; a program needn't handle non-finite values.
Results may differ from a plain program's by a relative error of at most 0.004.
Values may be sent and summed in bfloat16 or wider, within the bound.
No kernel may reach another device: no remote copies, remote signals or barrier semaphores. Data moves between devices by JAX's collectives and lax.ppermute only.
A program may use at most 128 MiB of HBM per device.

v0:
```python
import jax
import jax.numpy as jnp
from jax import lax
from jax.sharding import PartitionSpec as P


def from_behind(x, axis, by):
    count = lax.axis_size(axis)
    pairs = [(i, i + by) for i in range(count) if 0 <= i + by < count]
    return lax.ppermute(x, axis, pairs)


def convolve_energy(green, screen):
    points = green.shape[1]
    middle = points // 2
    widths = [(0, 0)] * green.ndim
    widths[1] = (points, points)
    padded = jnp.pad(green.astype(jnp.float32), widths)
    screen_wide = screen.astype(jnp.float32)

    def add_offset(offset, totals):
        start = (points + middle - offset).astype(jnp.int32)
        shifted = lax.dynamic_slice_in_dim(padded, start, points, 1)
        weight = lax.dynamic_slice_in_dim(screen_wide, offset.astype(jnp.int32), 1, 1)
        real_part = totals[0] + shifted[0] * weight[0] - shifted[1] * weight[1]
        imag_part = totals[1] + shifted[0] * weight[1] + shifted[1] * weight[0]
        return (real_part, imag_part)

    blank_sum = jnp.zeros(green.shape[1:], jnp.float32)
    totals = lax.fori_loop(0, points, add_offset, (blank_sum, blank_sum))
    return jnp.stack([-totals[1] / points, totals[0] / points]).astype(jnp.bfloat16)


def precise(first, second):
    return jnp.einsum(
        "eij,ejk->eik",
        first,
        second,
        precision=lax.Precision.HIGHEST,
        preferred_element_type=jnp.float32,
    )


def precise_adjoint(first, second):
    return jnp.einsum(
        "eij,ekj->eik",
        first,
        second,
        precision=lax.Precision.HIGHEST,
        preferred_element_type=jnp.float32,
    )


def product(left, right):
    real_part = precise(left[0], right[0]) - precise(left[1], right[1])
    imag_part = precise(left[0], right[1]) + precise(left[1], right[0])
    return (real_part, imag_part)


def congruence(kernel, state, source):
    inner = product(kernel, state)
    outer_re = precise_adjoint(inner[0], kernel[0]) + precise_adjoint(inner[1], kernel[1])
    outer_im = precise_adjoint(inner[1], kernel[0]) - precise_adjoint(inner[0], kernel[1])
    return (outer_re + source[0], outer_im + source[1])


def lowprod(form, first, second):
    return jnp.einsum(form, first, second, preferred_element_type=jnp.float32)


def select_slab(pair, index):
    return (pair[0][:, index], pair[1][:, index])


def per_device(green_lesser, screened_lesser, green_retarded, coupling):
    sigma_rows = convolve_energy(
        lax.all_to_all(green_lesser, "energy", split_axis=3, concat_axis=1, tiled=True),
        lax.all_to_all(screened_lesser, "energy", split_axis=3, concat_axis=1, tiled=True),
    )
    sigma = lax.all_to_all(sigma_rows, "energy", split_axis=1, concat_axis=3, tiled=True)
    green_re = green_retarded[0]
    green_im = green_retarded[1]
    kernel_re = lowprod("esij,sjk->esik", green_re, coupling[0]) - lowprod(
        "esij,sjk->esik", green_im, coupling[1]
    )
    kernel_im = lowprod("esij,sjk->esik", green_re, coupling[1]) + lowprod(
        "esij,sjk->esik", green_im, coupling[0]
    )
    mixed_re = (
        lowprod("esij,esjk->esik", green_re, sigma[0])
        - lowprod("esij,esjk->esik", green_im, sigma[1])
    ).astype(jnp.bfloat16)
    mixed_im = (
        lowprod("esij,esjk->esik", green_re, sigma[1])
        + lowprod("esij,esjk->esik", green_im, sigma[0])
    ).astype(jnp.bfloat16)
    source_re = lowprod("esij,eskj->esik", mixed_re, green_re) + lowprod(
        "esij,eskj->esik", mixed_im, green_im
    )
    source_im = lowprod("esij,eskj->esik", mixed_im, green_re) - lowprod(
        "esij,eskj->esik", mixed_re, green_im
    )
    kernels = (kernel_re, kernel_im)
    sources = (source_re, source_im)
    slab_count = green_retarded.shape[2]
    block_shape = (green_retarded.shape[1], green_retarded.shape[3], green_retarded.shape[4])
    total_map = select_slab(kernels, 0)
    total_add = select_slab(sources, 0)
    for index in range(1, slab_count):
        total_add = congruence(select_slab(kernels, index), total_add, select_slab(sources, index))
        total_map = product(select_slab(kernels, index), total_map)

    def advance(turn, carried):
        applied = congruence(total_map, (carried[0], carried[1]), total_add)
        return from_behind(jnp.stack(applied), "slab", 1)

    carried = lax.fori_loop(
        0, lax.axis_size("slab") - 1, advance, jnp.zeros((2,) + block_shape, jnp.float32)
    )
    incoming = (carried[0], carried[1])
    state = incoming
    outputs = []
    for index in range(slab_count):
        state = congruence(select_slab(kernels, index), state, select_slab(sources, index))
        outputs.append(jnp.stack(state))
    return jnp.stack(outputs, axis=2)


def solution(mesh):
    placed = (
        P(None, "energy", "slab", None, None),
        P(None, "energy", "slab", None, None),
        P(None, "energy", "slab", None, None),
        P(None, "slab", None, None),
    )
    return jax.shard_map(
        per_device,
        mesh=mesh,
        in_specs=placed,
        out_specs=P(None, "energy", "slab", None, None),
        check_vma=False,
    )
```

profile of v0, /device:TPU:24, one launch (start us, length us, event | category | flops | bytes accessed | tf_op | source)
XLA Modules:
  0.0 489.1 jit_solution(9616827355255558958)
XLA Ops:
  0.0 4.5 copy.324
  4.5 4.5 all-to-all-start
  9.0 4.7 copy.326
  16.3 1.9 fusion.70
  18.7 1.8 add_bitcast_fusion
  20.5 14.3 %all-to-all-done = bf16[2,2,4,256,256]{4,2,1,0,3:T(4,128)(2,1)} async-done(((bf16[2,2,4,256,256]{4,2,1,0,3:T(4,128)(2,1)}), bf16[2,2,4,256,256]{4,2,1,0,3:T(4,128)(2,1)}, u32[]{:S(2)}, u32[]{:S(2)}) %all-to-all-start) | async-done | bytes 2097184 | tf_op jit(solution)/shard_map/all_to_all | solution.py:77
  34.7 4.6 all-to-all-start.1
  39.4 2.9 fusion.71
  42.3 2.4 convolution_add_fusion.19
  47.9 2.5 copy.325
  50.4 6.1 %pad_convert_fusion = f32[2,24,4,64,256]{4,3,2,1,0:T(8,128)} fusion(bf16[2,8,4,64,256]{4,3,2,1,0:T(8,128)(2,1)S(1)} %bitcast.389), kind=kLoop, calls=%fused_computation.27 | loop fusion | flops 3145728 | bytes 14680064 | tf_op jit(solution)/shard_map/jit(_pad)/pad | solution.py:18
  56.5 8.6 %all-to-all-done.1 = bf16[2,2,4,256,256]{4,2,1,0,3:T(4,128)(2,1)} async-done(((bf16[2,2,4,256,256]{4,2,1,0,3:T(4,128)(2,1)}), bf16[2,2,4,256,256]{4,2,1,0,3:T(4,128)(2,1)}, u32[]{:S(2)}, u32[]{:S(2)}) %all-to-all-start.1) | async-done | bytes 2097184 | tf_op jit(solution)/shard_map/all_to_all | solution.py:78
  65.1 2.8 convert_bitcast_fusion
  68.0 4.4 copy.327
  72.4 62.6 %while.29 = (s32[]{:T(128)}, f32[8,4,64,256]{3,2,1,0:T(8,128)}, f32[8,4,64,256]{3,2,1,0:T(8,128)}, f32[2,24,4,64,256]{4,3,2,1,0:T(8,128)}, f32[2,8,4,64,256]{4,3...) while((s32[]{:T(128)}, f32[8,4,64,256]{3,2,1,0:T(8,128)}, ...), condition=%wide.region_1.2_spmd.clone, body=%wide.region_0.1_spmd.clone.sunk | while | flops 5242888 | bytes 14155961 | solution.py:30
  73.5 5.7 %fusion.227 = (f32[8,4,64,256]{3,2,1,0:T(8,128)}, f32[8,4,64,256]{3,2,1,0:T(8,128)}) fusion(f32[8,4,64,256]{3,2,1,0:T(8,128)} %get-tuple-element.311, f32[2,24,4,64,256]{4,3,2,1,0:T(8,128)} %get-tuple-element.322, s32[]{:T(128)S(6)} %select_n.20, s32[]{:T(128)S(6)} %add.325, f32[4,64,256]{2,1,0:T(8,128)S(1)} %get-tuple-element.295, ...), kind=kLoop, calls=%fused_computation.22.clone.1 | loop fusion | flops 5242880 | bytes 13107209 | tf_op jit(solution)/shard_map/while/body/eval_jaxpr/add | solution.py:26
  80.2 6.9 %fusion.227 = (f32[8,4,64,256]{3,2,1,0:T(8,128)}, f32[8,4,64,256]{3,2,1,0:T(8,128)}) fusion(f32[8,4,64,256]{3,2,1,0:T(8,128)} %get-tuple-element.311, f32[2,24,4,64,256]{4,3,2,1,0:T(8,128)} %get-tuple-element.322, s32[]{:T(128)S(6)} %select_n.20, s32[]{:T(128)S(6)} %add.325, f32[4,64,256]{2,1,0:T(8,128)S(1)} %get-tuple-element.295, ...), kind=kLoop, calls=%fused_computation.22.clone.1 | loop fusion | flops 5242880 | bytes 13107209 | tf_op jit(solution)/shard_map/while/body/eval_jaxpr/add | solution.py:26
  88.2 6.9 %fusion.227 = (f32[8,4,64,256]{3,2,1,0:T(8,128)}, f32[8,4,64,256]{3,2,1,0:T(8,128)}) fusion(f32[8,4,64,256]{3,2,1,0:T(8,128)} %get-tuple-element.311, f32[2,24,4,64,256]{4,3,2,1,0:T(8,128)} %get-tuple-element.322, s32[]{:T(128)S(6)} %select_n.20, s32[]{:T(128)S(6)} %add.325, f32[4,64,256]{2,1,0:T(8,128)S(1)} %get-tuple-element.295, ...), kind=kLoop, calls=%fused_computation.22.clone.1 | loop fusion | flops 5242880 | bytes 13107209 | tf_op jit(solution)/shard_map/while/body/eval_jaxpr/add | solution.py:26
  96.2 6.9 %fusion.227 = (f32[8,4,64,256]{3,2,1,0:T(8,128)}, f32[8,4,64,256]{3,2,1,0:T(8,128)}) fusion(f32[8,4,64,256]{3,2,1,0:T(8,128)} %get-tuple-element.311, f32[2,24,4,64,256]{4,3,2,1,0:T(8,128)} %get-tuple-element.322, s32[]{:T(128)S(6)} %select_n.20, s32[]{:T(128)S(6)} %add.325, f32[4,64,256]{2,1,0:T(8,128)S(1)} %get-tuple-element.295, ...), kind=kLoop, calls=%fused_computation.22.clone.1 | loop fusion | flops 5242880 | bytes 13107209 | tf_op jit(solution)/shard_map/while/body/eval_jaxpr/add | solution.py:26
  104.1 6.9 %fusion.227 = (f32[8,4,64,256]{3,2,1,0:T(8,128)}, f32[8,4,64,256]{3,2,1,0:T(8,128)}) fusion(f32[8,4,64,256]{3,2,1,0:T(8,128)} %get-tuple-element.311, f32[2,24,4,64,256]{4,3,2,1,0:T(8,128)} %get-tuple-element.322, s32[]{:T(128)S(6)} %select_n.20, s32[]{:T(128)S(6)} %add.325, f32[4,64,256]{2,1,0:T(8,128)S(1)} %get-tuple-element.295, ...), kind=kLoop, calls=%fused_computation.22.clone.1 | loop fusion | flops 5242880 | bytes 13107209 | tf_op jit(solution)/shard_map/while/body/eval_jaxpr/add | solution.py:26
  112.1 6.9 %fusion.227 = (f32[8,4,64,256]{3,2,1,0:T(8,128)}, f32[8,4,64,256]{3,2,1,0:T(8,128)}) fusion(f32[8,4,64,256]{3,2,1,0:T(8,128)} %get-tuple-element.311, f32[2,24,4,64,256]{4,3,2,1,0:T(8,128)} %get-tuple-element.322, s32[]{:T(128)S(6)} %select_n.20, s32[]{:T(128)S(6)} %add.325, f32[4,64,256]{2,1,0:T(8,128)S(1)} %get-tuple-element.295, ...), kind=kLoop, calls=%fused_computation.22.clone.1 | loop fusion | flops 5242880 | bytes 13107209 | tf_op jit(solution)/shard_map/while/body/eval_jaxpr/add | solution.py:26
  120.1 6.9 %fusion.227 = (f32[8,4,64,256]{3,2,1,0:T(8,128)}, f32[8,4,64,256]{3,2,1,0:T(8,128)}) fusion(f32[8,4,64,256]{3,2,1,0:T(8,128)} %get-tuple-element.311, f32[2,24,4,64,256]{4,3,2,1,0:T(8,128)} %get-tuple-element.322, s32[]{:T(128)S(6)} %select_n.20, s32[]{:T(128)S(6)} %add.325, f32[4,64,256]{2,1,0:T(8,128)S(1)} %get-tuple-element.295, ...), kind=kLoop, calls=%fused_computation.22.clone.1 | loop fusion | flops 5242880 | bytes 13107209 | tf_op jit(solution)/shard_map/while/body/eval_jaxpr/add | solution.py:26
  128.1 6.9 %fusion.227 = (f32[8,4,64,256]{3,2,1,0:T(8,128)}, f32[8,4,64,256]{3,2,1,0:T(8,128)}) fusion(f32[8,4,64,256]{3,2,1,0:T(8,128)} %get-tuple-element.311, f32[2,24,4,64,256]{4,3,2,1,0:T(8,128)} %get-tuple-element.322, s32[]{:T(128)S(6)} %select_n.20, s32[]{:T(128)S(6)} %add.325, f32[4,64,256]{2,1,0:T(8,128)S(1)} %get-tuple-element.295, ...), kind=kLoop, calls=%fused_computation.22.clone.1 | loop fusion | flops 5242880 | bytes 13107209 | tf_op jit(solution)/shard_map/while/body/eval_jaxpr/add | solution.py:26
  135.0 2.8 fusion.32
  139.3 4.7 all-to-all-start.2
  144.0 2.2 fusion.91
  151.6 18.0 %all-to-all-done.2 = bf16[2,8,4,64,256]{4,3,2,0,1:T(8,128)(2,1)} async-done(((bf16[2,8,4,64,256]{4,3,2,0,1:T(8,128)(2,1)}), bf16[2,8,4,64,256]{4,3,2,0,1:T(8,128)(2,1)}, u32[]{:S(2)}, u32[]{:S(2)}) %all-to-all-start.2) | async-done | bytes 2097184 | tf_op jit(solution)/shard_map/all_to_all | solution.py:80
  169.5 1.7 copy.329
  202.9 250.3 %while.28 = (s32[]{:T(128)}, f32[2,2,256,256]{3,2,1,0:T(8,128)}, f32[2,256,256]{2,1,0:T(8,128)S(1)}, f32[2,256,256]{2,1,0:T(8,128)S(1)}, f32[2,256,256]{2,1,0:T(8,128)}, /*index=5*/f32[2,256,256]{2,1,0:T(8,128)}, s32[]{:T(128)}) while((s32[]{:T(128)}, f32[2,2,256,256]{3,2,1,0:T(8,128)}, f32[2,256,256]{2,1,0:T(8,128)S(1)}, ...), condition=%wide.region_3.4_spmd, body=%wide.region_2.3_spmd.sunk | while | flops 3222274048 | bytes 26214572 | solution.py:117
  204.6 1.7 fusion.223
  206.3 1.7 convolution_add_fusion.21
  208.7 1.8 convolution_subtract_fusion.21
  213.5 3.4 collective-permute-start
  216.9 24.4 %collective-permute-done = f32[2,2,256,256]{3,2,1,0:T(8,128)} collective-permute-done((f32[2,2,256,256]{3,2,1,0:T(8,128)}, f32[2,2,256,256]{3,2,1,0:T(8,128)}, u32[]{:S(2)}, u32[]{:S(2)}) %collective-permute-start) | collective-permute-done | bytes 1048608 | tf_op jit(solution)/shard_map/while/body/eval_jaxpr/ppermute | solution.py:10
  244.7 1.7 convolution_add_fusion.21
  247.1 1.8 convolution_subtract_fusion.21
  252.0 2.5 collective-permute-start
  254.5 24.4 %collective-permute-done = f32[2,2,256,256]{3,2,1,0:T(8,128)} collective-permute-done((f32[2,2,256,256]{3,2,1,0:T(8,128)}, f32[2,2,256,256]{3,2,1,0:T(8,128)}, u32[]{:S(2)}, u32[]{:S(2)}) %collective-permute-start) | collective-permute-done | bytes 1048608 | tf_op jit(solution)/shard_map/while/body/eval_jaxpr/ppermute | solution.py:10
  282.3 1.7 convolution_add_fusion.21
  284.7 1.8 convolution_subtract_fusion.21
  289.5 1.9 collective-permute-start
  291.5 24.1 %collective-permute-done = f32[2,2,256,256]{3,2,1,0:T(8,128)} collective-permute-done((f32[2,2,256,256]{3,2,1,0:T(8,128)}, f32[2,2,256,256]{3,2,1,0:T(8,128)}, u32[]{:S(2)}, u32[]{:S(2)}) %collective-permute-start) | collective-permute-done | bytes 1048608 | tf_op jit(solution)/shard_map/while/body/eval_jaxpr/ppermute | solution.py:10
  318.9 1.7 convolution_add_fusion.21
  321.3 1.8 convolution_subtract_fusion.21
  326.2 1.9 collective-permute-start
  328.1 23.1 %collective-permute-done = f32[2,2,256,256]{3,2,1,0:T(8,128)} collective-permute-done((f32[2,2,256,256]{3,2,1,0:T(8,128)}, f32[2,2,256,256]{3,2,1,0:T(8,128)}, u32[]{:S(2)}, u32[]{:S(2)}) %collective-permute-start) | collective-permute-done | bytes 1048608 | tf_op jit(solution)/shard_map/while/body/eval_jaxpr/ppermute | solution.py:10
  354.6 1.7 convolution_add_fusion.21
  357.0 1.8 convolution_subtract_fusion.21
  361.9 1.9 collective-permute-start
  363.8 22.2 %collective-permute-done = f32[2,2,256,256]{3,2,1,0:T(8,128)} collective-permute-done((f32[2,2,256,256]{3,2,1,0:T(8,128)}, f32[2,2,256,256]{3,2,1,0:T(8,128)}, u32[]{:S(2)}, u32[]{:S(2)}) %collective-permute-start) | collective-permute-done | bytes 1048608 | tf_op jit(solution)/shard_map/while/body/eval_jaxpr/ppermute | solution.py:10
  387.7 1.7 fusion.223
  389.4 1.7 convolution_add_fusion.21
  391.8 1.8 convolution_subtract_fusion.21
  396.7 1.9 collective-permute-start
  398.6 21.3 %collective-permute-done = f32[2,2,256,256]{3,2,1,0:T(8,128)} collective-permute-done((f32[2,2,256,256]{3,2,1,0:T(8,128)}, f32[2,2,256,256]{3,2,1,0:T(8,128)}, u32[]{:S(2)}, u32[]{:S(2)}) %collective-permute-start) | collective-permute-done | bytes 1048608 | tf_op jit(solution)/shard_map/while/body/eval_jaxpr/ppermute | solution.py:10
  423.3 1.7 convolution_add_fusion.21
  425.7 1.8 convolution_subtract_fusion.21
  430.5 1.9 collective-permute-start
  432.5 20.4 %collective-permute-done = f32[2,2,256,256]{3,2,1,0:T(8,128)} collective-permute-done((f32[2,2,256,256]{3,2,1,0:T(8,128)}, f32[2,2,256,256]{3,2,1,0:T(8,128)}, u32[]{:S(2)}, u32[]{:S(2)}) %collective-permute-start) | collective-permute-done | bytes 1048608 | tf_op jit(solution)/shard_map/while/body/eval_jaxpr/ppermute | solution.py:10
  453.2 2.2 fusion.56
  455.5 2.1 fusion.52
  457.6 2.1 convolution_subtract_fusion.10
  460.4 2.2 convolution_add_fusion.10
  486.4 2.4 copy.409
  (209 shorter events, 123.4 us)
Async XLA Ops:
  4.5 30.2 %all-to-all-start = ((bf16[2,2,4,256,256]{4,2,1,0,3:T(4,128)(2,1)}), bf16[2,2,4,256,256]{4,2,1,0,3:T(4,128)(2,1)}, u32[]{:S(2)}, u32[]{:S(2)}) async-start(bf16[2,2,4,256,256]{4,2,1,0,3:T(4,128)(2,1)} %copy.324), calls=%async_computation | async-start | bytes 4194304 | tf_op jit(solution)/shard_map/all_to_all | solution.py:77
  9.0 4.7 copy-start.4
  13.7 1.6 copy-start.21
  13.8 4.3 copy-start.12
  13.8 4.8 copy-start.14
  34.7 30.4 %all-to-all-start.1 = ((bf16[2,2,4,256,256]{4,2,1,0,3:T(4,128)(2,1)}), bf16[2,2,4,256,256]{4,2,1,0,3:T(4,128)(2,1)}, u32[]{:S(2)}, u32[]{:S(2)}) async-start(bf16[2,2,4,256,256]{4,2,1,0,3:T(4,128)(2,1)} %copy.326), calls=%async_computation.1 | async-start | bytes 4194304 | tf_op jit(solution)/shard_map/all_to_all | solution.py:78
  42.3 3.5 copy-start.22
  42.3 3.5 copy-start
  44.7 3.2 copy-start.18
  46.8 1.1 copy-start.20
  47.9 98.3 %copy-start.16 = (f32[2,256,256]{2,1,0:T(8,128)}, f32[2,256,256]{2,1,0:T(8,128)S(1)}, u32[]{:S(2)}) copy-start(f32[2,256,256]{2,1,0:T(8,128)S(1)} %convolution_add_fusion.18) | copy-start | bytes 1572868
  139.3 30.2 %all-to-all-start.2 = ((bf16[2,8,4,64,256]{4,3,2,0,1:T(8,128)(2,1)}), bf16[2,8,4,64,256]{4,3,2,0,1:T(8,128)(2,1)}, u32[]{:S(2)}, u32[]{:S(2)}) async-start(bf16[2,8,4,64,256]{4,3,2,0,1:T(8,128)(2,1)} %pad_maximum_fusion.2), calls=%async_computation.2 | async-start | bytes 4194304 | tf_op jit(solution)/shard_map/all_to_all | solution.py:80
  144.0 3.3 copy-start.1
  144.0 3.3 copy-start.19
  148.4 2.1 copy-start.17
  171.4 1.6 copy-start.5
  174.1 1.2 copy-start.13
  176.3 1.2 copy-start.15
  178.1 20.7 %copy-start.6 = (f32[2,4,256,256]{3,2,0,1:T(8,128)}, f32[2,4,256,256]{3,2,0,1:T(8,128)S(1)}, u32[]{:S(2)}) copy-start(f32[2,4,256,256]{3,2,0,1:T(8,128)S(1)} %convolution_subtract_fusion.2) | copy-start | bytes 6291460
  179.1 2.0 copy-start.2
  179.7 20.6 %copy-start.8 = (f32[2,4,256,256]{3,2,1,0:T(8,128)}, f32[2,4,256,256]{3,2,1,0:T(8,128)S(1)}, u32[]{:S(2)}) copy-start(f32[2,4,256,256]{3,2,1,0:T(8,128)S(1)} %convolution_add_fusion.2) | copy-start | bytes 6291460
  208.6 2.5 copy-start.10
  210.4 1.4 copy-start.11
  213.5 27.8 %collective-permute-start = (f32[2,2,256,256]{3,2,1,0:T(8,128)}, f32[2,2,256,256]{3,2,1,0:T(8,128)}, u32[]{:S(2)}, u32[]{:S(2)}) collective-permute-start(f32[2,2,256,256]{3,2,1,0:T(8,128)} %pad_maximum_fusion.4), channel_id=1, source_target_pairs={{0,4},{4,8},{8,12},{12,16},{16,20},{20,24},{24,28},{1,5},{5,9},{9,... | collective-permute-start | bytes 3145736 | tf_op jit(solution)/shard_map/while/body/eval_jaxpr/ppermute | solution.py:10
  247.1 2.5 copy-start.10
  248.9 1.4 copy-start.11
  252.0 26.9 %collective-permute-start = (f32[2,2,256,256]{3,2,1,0:T(8,128)}, f32[2,2,256,256]{3,2,1,0:T(8,128)}, u32[]{:S(2)}, u32[]{:S(2)}) collective-permute-start(f32[2,2,256,256]{3,2,1,0:T(8,128)} %pad_maximum_fusion.4), channel_id=1, source_target_pairs={{0,4},{4,8},{8,12},{12,16},{16,20},{20,24},{24,28},{1,5},{5,9},{9,... | collective-permute-start | bytes 3145736 | tf_op jit(solution)/shard_map/while/body/eval_jaxpr/ppermute | solution.py:10
  284.7 2.5 copy-start.10
  286.4 1.4 copy-start.11
  289.5 26.0 %collective-permute-start = (f32[2,2,256,256]{3,2,1,0:T(8,128)}, f32[2,2,256,256]{3,2,1,0:T(8,128)}, u32[]{:S(2)}, u32[]{:S(2)}) collective-permute-start(f32[2,2,256,256]{3,2,1,0:T(8,128)} %pad_maximum_fusion.4), channel_id=1, source_target_pairs={{0,4},{4,8},{8,12},{12,16},{16,20},{20,24},{24,28},{1,5},{5,9},{9,... | collective-permute-start | bytes 3145736 | tf_op jit(solution)/shard_map/while/body/eval_jaxpr/ppermute | solution.py:10
  321.3 2.5 copy-start.10
  323.1 1.4 copy-start.11
  326.2 25.1 %collective-permute-start = (f32[2,2,256,256]{3,2,1,0:T(8,128)}, f32[2,2,256,256]{3,2,1,0:T(8,128)}, u32[]{:S(2)}, u32[]{:S(2)}) collective-permute-start(f32[2,2,256,256]{3,2,1,0:T(8,128)} %pad_maximum_fusion.4), channel_id=1, source_target_pairs={{0,4},{4,8},{8,12},{12,16},{16,20},{20,24},{24,28},{1,5},{5,9},{9,... | collective-permute-start | bytes 3145736 | tf_op jit(solution)/shard_map/while/body/eval_jaxpr/ppermute | solution.py:10
  357.0 2.5 copy-start.10
  358.8 1.4 copy-start.11
  361.9 24.1 %collective-permute-start = (f32[2,2,256,256]{3,2,1,0:T(8,128)}, f32[2,2,256,256]{3,2,1,0:T(8,128)}, u32[]{:S(2)}, u32[]{:S(2)}) collective-permute-start(f32[2,2,256,256]{3,2,1,0:T(8,128)} %pad_maximum_fusion.4), channel_id=1, source_target_pairs={{0,4},{4,8},{8,12},{12,16},{16,20},{20,24},{24,28},{1,5},{5,9},{9,... | collective-permute-start | bytes 3145736 | tf_op jit(solution)/shard_map/while/body/eval_jaxpr/ppermute | solution.py:10
  391.8 2.5 copy-start.10
  393.6 1.4 copy-start.11
  396.7 23.2 %collective-permute-start = (f32[2,2,256,256]{3,2,1,0:T(8,128)}, f32[2,2,256,256]{3,2,1,0:T(8,128)}, u32[]{:S(2)}, u32[]{:S(2)}) collective-permute-start(f32[2,2,256,256]{3,2,1,0:T(8,128)} %pad_maximum_fusion.4), channel_id=1, source_target_pairs={{0,4},{4,8},{8,12},{12,16},{16,20},{20,24},{24,28},{1,5},{5,9},{9,... | collective-permute-start | bytes 3145736 | tf_op jit(solution)/shard_map/while/body/eval_jaxpr/ppermute | solution.py:10
  425.7 2.5 copy-start.10
  427.4 1.4 copy-start.11
  430.5 22.3 %collective-permute-start = (f32[2,2,256,256]{3,2,1,0:T(8,128)}, f32[2,2,256,256]{3,2,1,0:T(8,128)}, u32[]{:S(2)}, u32[]{:S(2)}) collective-permute-start(f32[2,2,256,256]{3,2,1,0:T(8,128)} %pad_maximum_fusion.4), channel_id=1, source_target_pairs={{0,4},{4,8},{8,12},{12,16},{16,20},{20,24},{24,28},{1,5},{5,9},{9,... | collective-permute-start | bytes 3145736 | tf_op jit(solution)/shard_map/while/body/eval_jaxpr/ppermute | solution.py:10
  453.2 4.4 copy-start.3
  460.3 2.9 copy-start.9
  462.6 1.6 copy-start.7
where the time goes:
time: 498 us; the launch traced here: 489 us
  waiting for transfers between devices  201 us (40%)
  matrix products  146 us (29%)
  other arithmetic  75.4 us (15%)
  local copies, waits for them, and re-layouts  35.1 us (7%)
  starting transfers between devices  29.2 us (6%)
    ppermute x7, waiting for transfers between devices, from_behind(): return lax.ppermute(x, axis, pairs)  160 us
    dot_general x68, matrix products, precise(): jnp.einsum('eij,ejk->eik', first, second, precision=lax.Precision.HIGHEST...  100 us
    add x8, other arithmetic, add_offset(): imag_part = totals[1] + shifted[0] * weight[1] + shifted[1] * weight[0]  54 us
    dot_general x56, matrix products, precise_adjoint(): jnp.einsum('eij,ekj->eik', first, second, precision=lax.Precision.HIGHEST...  39 us
    all_to_all x1, waiting for transfers between devices, per_device(): lax.all_to_all(sigma_rows, 'energy', split_axis=1, concat_axis=3, tiled=T...  18 us
    ppermute x7, starting transfers between devices, from_behind(): return lax.ppermute(x, axis, pairs)  15.4 us
    all_to_all x1, waiting for transfers between devices, per_device(): lax.all_to_all(green_lesser, 'energy', split_axis=3, concat_axis=1, tiled...  14.3 us
    unnamed x44, local copies, waits for them, and re-layouts  13.9 us
  transfers between devices with their start and end apart: 10, of which 10 were waited for; matrix products, arithmetic and copies ran while one was open for 7% of the time, Pallas kernels for 0%

commit v1 on v0

v1 whole, which is shorter than its diff:
```python
import functools

import jax
import jax.numpy as jnp
from jax import lax
from jax.experimental import pallas as pl
from jax.experimental.pallas import tpu as pltpu
from jax.sharding import PartitionSpec as P

BF16 = jnp.bfloat16
F32 = jnp.float32
VMEM_LIMIT = 24 * 1024 * 1024


def params():
    return pltpu.CompilerParams(vmem_limit_bytes=VMEM_LIMIT)


def cost(products, order, nbytes):
    return pl.CostEstimate(
        flops=2 * products * order**3, bytes_accessed=nbytes, transcendentals=0
    )


def split(value):
    high = value.astype(BF16)
    low = (value - high.astype(F32)).astype(BF16)
    return high, low


def panel(re, im):
    return jnp.concatenate(
        [jnp.concatenate([re, im], axis=1), jnp.concatenate([-im, re], axis=1)], axis=0
    )


def dot(left, right):
    return lax.dot_general(left, right, (((1,), (0,)), ((), ())), preferred_element_type=F32)


def dot_nt(left, right):
    return lax.dot_general(left, right, (((1,), (1,)), ((), ())), preferred_element_type=F32)


def times_wide(a_high, a_low, x):
    order = x.shape[0]
    x_high, x_low = split(x)
    xh = panel(x_high[:, :order], x_high[:, order:])
    xl = panel(x_low[:, :order], x_low[:, order:])
    left = jnp.concatenate([a_high, a_high, a_low], axis=1)
    return dot(left, jnp.concatenate([xh, xl, xh], axis=0))


def times_narrow(a_high, a_low, re, im):
    xp = panel(re, im)
    left = jnp.concatenate([a_high, a_low], axis=1)
    return dot(left, jnp.concatenate([xp, xp], axis=0))


def times_adjoint(y, t_high, t_low):
    order = y.shape[0]
    y_high, y_low = split(y)
    th = panel(t_high[:, :order], t_high[:, order:])
    tl = panel(t_low[:, :order], t_low[:, order:])
    left = jnp.concatenate([y_high, y_low, y_high], axis=1)
    return dot_nt(left, jnp.concatenate([th, th, tl], axis=1))


def panels(ref):
    return ref[0], ref[1]


def store_map(ref, value):
    high, low = split(value)
    ref[0] = high
    ref[1] = low


def maps_body(g_ref, c_ref, k_ref, p_ref, carry):
    left = jnp.concatenate([g_ref[0], g_ref[1]], axis=1)
    value = dot(left, panel(c_ref[0], c_ref[1]))
    store_map(k_ref, value)

    @pl.when(pl.program_id(1) == 0)
    def _():
        carry[...] = value

    @pl.when(pl.program_id(1) > 0)
    def _():
        high, low = panels(k_ref)
        carry[...] = times_wide(high, low, carry[...])

    store_map(p_ref, carry[...])


def build_maps(green, coupling):
    _, energies, slabs, order, _ = green.shape
    shape = jax.ShapeDtypeStruct((energies, slabs, 2, order, 2 * order), BF16)
    out_spec = pl.BlockSpec((None, None, 2, order, 2 * order), lambda e, s: (e, s, 0, 0, 0))
    return pl.pallas_call(
        maps_body,
        grid=(energies, slabs),
        in_specs=[
            pl.BlockSpec((2, None, None, order, order), lambda e, s: (0, e, s, 0, 0)),
            pl.BlockSpec((2, None, order, order), lambda e, s: (0, s, 0, 0)),
        ],
        out_specs=[out_spec, out_spec],
        out_shape=[shape, shape],
        scratch_shapes=[pltpu.VMEM((order, 2 * order), F32)],
        compiler_params=params(),
        cost_estimate=cost(16 * energies * slabs, order, 12 * green.size),
        name="maps",
    )(green, coupling)


def map_product_body(a_ref, b_ref, o_ref):
    high, low = panels(a_ref)
    value = times_wide(high, low, b_ref[0].astype(F32) + b_ref[1].astype(F32))
    store_map(o_ref, value)


def map_product(first, second):
    energies, slabs, _, order, _ = first.shape
    spec = pl.BlockSpec((None, None, 2, order, 2 * order), lambda e, s: (e, s, 0, 0, 0))
    return pl.pallas_call(
        map_product_body,
        grid=(energies, slabs),
        in_specs=[spec, pl.BlockSpec((None, 2, order, 2 * order), lambda e, s: (e, 0, 0, 0))],
        out_specs=spec,
        out_shape=jax.ShapeDtypeStruct(first.shape, BF16),
        compiler_params=params(),
        cost_estimate=cost(12 * energies * slabs, order, 4 * first.size),
        name="map_product",
    )(first, second)


def convolve_body(count, energies, *refs):
    ins = refs[:count]
    outs = refs[count : count * (1 + energies)]
    green, screen, total = refs[count * (1 + energies) :]
    me = lax.axis_index("energy")
    points = count * energies
    middle = points // 2
    rows, columns = green.shape[2:]
    for k in range(count):
        base = (me ^ k) * energies
        for e in range(energies):
            green[:, base + e] = ins[k][0, :, e].astype(F32)
            screen[:, base + e] = ins[k][1, :, e].astype(F32)

    def tile(index, _):
        row = pl.multiple_of(index * 8, 8)
        for col in range(0, columns, 128):
            at = (pl.ds(row, 8), pl.ds(col, 128))
            gr = [green[(0, m) + at] for m in range(points)]
            gi = [green[(1, m) + at] for m in range(points)]
            wr = [screen[(0, m) + at] for m in range(points)]
            wi = [screen[(1, m) + at] for m in range(points)]
            for n in range(points):
                re = None
                im = None
                for m in range(points):
                    lag = n - m + middle
                    if 0 <= lag < points:
                        a = gr[m] * wr[lag] - gi[m] * wi[lag]
                        b = gr[m] * wi[lag] + gi[m] * wr[lag]
                        re = a if re is None else re + a
                        im = b if im is None else im + b
                total[(n, 0) + at] = -im / points
                total[(n, 1) + at] = re / points
        return 0

    lax.fori_loop(0, rows // 8, tile, 0)
    for k in range(count):
        base = (me ^ k) * energies
        for e in range(energies):
            outs[k * energies + e][...] = total[base + e].astype(BF16)


def convolve(pieces):
    count = len(pieces)
    _, _, energies, slabs, rows, columns = pieces[0].shape
    in_spec = pl.BlockSpec((2, 2, energies, None, rows, columns), lambda s: (0, 0, 0, s, 0, 0))
    out_spec = pl.BlockSpec((None, 2, rows, columns), lambda s: (s, 0, 0, 0))
    points = count * energies
    outs = pl.pallas_call(
        functools.partial(convolve_body, count, energies),
        grid=(slabs,),
        in_specs=[in_spec] * count,
        out_specs=[out_spec] * points,
        out_shape=[jax.ShapeDtypeStruct((slabs, 2, rows, columns), BF16)] * points,
        scratch_shapes=[
            pltpu.VMEM((2, points, rows, columns), F32),
            pltpu.VMEM((2, points, rows, columns), F32),
            pltpu.VMEM((points, 2, rows, columns), F32),
        ],
        compiler_params=params(),
        cost_estimate=pl.CostEstimate(
            flops=8 * 200 * slabs * rows * columns * points,
            bytes_accessed=6 * points * slabs * rows * columns * 2,
            transcendentals=0,
        ),
        name="convolve",
    )(*pieces)
    return [outs[k * energies : (k + 1) * energies] for k in range(count)]


def source_body(count, *refs):
    pieces = refs[:count]
    g_ref, k_ref, b_ref, v_ref, sigma, carry = refs[count:]
    me = lax.axis_index("energy")
    rows = pieces[0].shape[1]
    order = sigma.shape[1]
    for k in range(count):
        start = pl.multiple_of((me ^ k) * rows, rows)
        for part in range(2):
            sigma[part, pl.ds(start, rows), :] = pieces[k][part]
    left = jnp.concatenate([g_ref[0], g_ref[1]], axis=1)
    mixed = dot(left, panel(sigma[0], sigma[1])).astype(BF16)
    source = dot_nt(mixed, panel(g_ref[0], g_ref[1]))

    @pl.when(pl.program_id(0) == 0)
    def _():
        carry[...] = source

    @pl.when(pl.program_id(0) > 0)
    def _():
        high, low = panels(k_ref)
        inner = times_wide(high, low, carry[...])
        carry[...] = times_adjoint(inner, high, low) + source

    b_ref[...] = carry[...]

    @pl.when(pl.program_id(0) == pl.num_programs(0) - 1)
    def _():
        v_ref[...] = carry[...].astype(BF16)


def build_sources(pieces, green, kernels, energy):
    count = len(pieces)
    slabs, _, rows, order = pieces[0].shape
    piece_spec = pl.BlockSpec((None, 2, rows, order), lambda s: (s, 0, 0, 0))
    return pl.pallas_call(
        functools.partial(source_body, count),
        grid=(slabs,),
        in_specs=[piece_spec] * count
        + [
            pl.BlockSpec((2, None, None, order, order), lambda s: (0, energy, s, 0, 0)),
            pl.BlockSpec((None, None, 2, order, 2 * order), lambda s: (energy, s, 0, 0, 0)),
        ],
        out_specs=[
            pl.BlockSpec((None, order, 2 * order), lambda s: (s, 0, 0)),
            pl.BlockSpec((order, 2 * order), lambda s: (0, 0)),
        ],
        out_shape=[
            jax.ShapeDtypeStruct((slabs, order, 2 * order), F32),
            jax.ShapeDtypeStruct((order, 2 * order), BF16),
        ],
        scratch_shapes=[
            pltpu.VMEM((2, order, order), BF16),
            pltpu.VMEM((order, 2 * order), F32),
        ],
        compiler_params=params(),
        cost_estimate=cost(32 * slabs, order, 24 * slabs * order * order),
        name="sources",
    )(*pieces, green, kernels)


def combine_body(v_ref, t_ref, base_ref, *outs):
    order = v_ref.shape[0]
    high, low = panels(t_ref)
    inner = times_narrow(high, low, v_ref[:, :order], v_ref[:, order:])
    value = times_adjoint(inner, high, low) + base_ref[...].astype(F32)
    for out in outs:
        out[...] = value.astype(out.dtype)


def combine(arrived, maps, base, base_index, energy, dtypes):
    order = arrived.shape[0]
    whole = pl.BlockSpec((order, 2 * order), lambda i: (0, 0))
    if base_index is None:
        base_spec = whole
    else:
        base_spec = pl.BlockSpec((None, order, 2 * order), lambda i: (base_index, 0, 0))
    return pl.pallas_call(
        combine_body,
        grid=(1,),
        in_specs=[
            whole,
            pl.BlockSpec((None, 2, order, 2 * order), lambda i: (energy, 0, 0, 0)),
            base_spec,
        ],
        out_specs=[whole] * len(dtypes),
        out_shape=[jax.ShapeDtypeStruct((order, 2 * order), t) for t in dtypes],
        compiler_params=params(),
        cost_estimate=cost(20, order, 20 * order * order),
        name="combine",
    )(arrived, maps, base)


def entry_body(w_ref, p_ref, b_ref, y_ref):
    high, low = panels(p_ref)
    inner = times_wide(high, low, w_ref[...].astype(F32))
    y_ref[...] = times_adjoint(inner, high, low) + b_ref[...]


def apply_entry(entry, prefixes, sums, energy):
    slabs, order, _ = sums.shape
    block = pl.BlockSpec((None, order, 2 * order), lambda s: (s, 0, 0))
    return pl.pallas_call(
        entry_body,
        grid=(slabs,),
        in_specs=[
            pl.BlockSpec((order, 2 * order), lambda s: (0, 0)),
            pl.BlockSpec((None, None, 2, order, 2 * order), lambda s: (energy, s, 0, 0, 0)),
            block,
        ],
        out_specs=block,
        out_shape=jax.ShapeDtypeStruct(sums.shape, F32),
        compiler_params=params(),
        cost_estimate=cost(24 * slabs, order, 24 * slabs * order * order),
        name="entry",
    )(entry, prefixes, sums)


def finish_body(v_ref, r_ref, y_ref, *rest):
    out = rest[-1]
    order = v_ref.shape[0]
    high, low = panels(r_ref)
    inner = times_narrow(high, low, v_ref[:, :order], v_ref[:, order:])
    value = times_adjoint(inner, high, low) + y_ref[...]
    out[0] = value[:, :order]
    out[1] = value[:, order:]


def finish(arrived, maps, partial, energy, energies, held):
    slabs, order, _ = partial.shape
    operands = [arrived, maps, partial]
    in_specs = [
        pl.BlockSpec((order, 2 * order), lambda s: (0, 0)),
        pl.BlockSpec((None, None, 2, order, 2 * order), lambda s: (energy, s, 0, 0, 0)),
        pl.BlockSpec((None, order, 2 * order), lambda s: (s, 0, 0)),
    ]
    aliases = {}
    if held is not None:
        operands.append(held)
        in_specs.append(pl.BlockSpec(memory_space=pl.ANY))
        aliases = {3: 0}
    return pl.pallas_call(
        finish_body,
        grid=(slabs,),
        in_specs=in_specs,
        out_specs=pl.BlockSpec((2, None, None, order, order), lambda s: (0, energy, s, 0, 0)),
        out_shape=jax.ShapeDtypeStruct((2, energies, slabs, order, order), F32),
        input_output_aliases=aliases,
        compiler_params=params(),
        cost_estimate=cost(20 * slabs, order, 24 * slabs * order * order),
        name="finish",
    )(*operands)


def swap(x, k):
    count = lax.axis_size("energy")
    return lax.ppermute(x, "energy", [(i, i ^ k) for i in range(count)])


def forward(x, by):
    count = lax.axis_size("slab")
    return lax.ppermute(x, "slab", [(i, i + by) for i in range(count - by)])


CHUNKS = 2


def per_device(green_lesser, screened_lesser, green_retarded, coupling):
    count = lax.axis_size("energy")
    depth = lax.axis_size("slab")
    me = lax.axis_index("energy")
    _, energies, slabs, order, _ = green_lesser.shape
    rows = order // count
    partners = [k for k in range(count) if k >= 2] + [k for k in range(min(2, count)) if k == 1]

    def piece(k, start, size):
        sizes = (2, energies, size, rows, order)
        begin = (0, 0, start, (me ^ k) * rows, 0)
        return jnp.stack(
            [
                lax.dynamic_slice(green_lesser, begin, sizes),
                lax.dynamic_slice(screened_lesser, begin, sizes),
            ]
        )

    size = slabs // CHUNKS if slabs % CHUNKS == 0 else slabs
    rounds = [[None] * count for _ in range(slabs // size)]
    for index, held in enumerate(rounds):
        for k in partners:
            held[k] = swap(piece(k, index * size, size), k)
        held[0] = piece(0, index * size, size)

    kernels, prefixes = build_maps(green_retarded, coupling)
    steps = (depth - 1).bit_length()
    step_maps = [prefixes[:, slabs - 1]]
    gap_maps = [None]
    for k in range(steps - 1):
        arrived = forward(step_maps[k], 1 << k)
        if gap_maps[k] is None:
            gap_maps.append(arrived)
        else:
            gap_maps.append(map_product(gap_maps[k][:, None], arrived)[:, 0])
        if k < steps - 2:
            step_maps.append(map_product(step_maps[k][:, None], arrived)[:, 0])
    last_gap = gap_maps[-1] if steps > 0 else None
    final_maps = prefixes if last_gap is None else map_product(prefixes, last_gap)

    sigmas = [convolve(held) for held in rounds]

    result = None
    for e in range(energies):
        pieces = [None] * count
        for k in partners + [0]:
            block = jnp.concatenate([chunk[k][e] for chunk in sigmas], axis=0)
            pieces[k] = block if k == 0 else swap(block, k)
        sums, carry = build_sources(pieces, green_retarded, kernels, e)
        running, index = sums, slabs - 1
        entry = None
        for k in range(steps):
            arrived = forward(carry, 1 << k)
            if k == steps - 1:
                break
            if k == steps - 2:
                (carry,) = combine(arrived, step_maps[k], running, index, e, (BF16,))
            else:
                running, carry = combine(arrived, step_maps[k], running, index, e, (F32, BF16))
                index = None
            if entry is None:
                entry = arrived
            else:
                (entry,) = combine(arrived, gap_maps[k], entry, None, e, (F32,))
        partial = sums if entry is None else apply_entry(entry, prefixes, sums, e)
        result = finish(arrived, final_maps, partial, e, energies, result)
    return result


def solution(mesh):
    placed = (
        P(None, "energy", "slab", None, None),
        P(None, "energy", "slab", None, None),
        P(None, "energy", "slab", None, None),
        P(None, "slab", None, None),
    )
    return jax.shard_map(
        per_device,
        mesh=mesh,
        in_specs=placed,
        out_specs=P(None, "energy", "slab", None, None),
        check_vma=False,
    )
```

time: 498 us -> 159 us (0.32); the launches traced: 489 us -> 158 us
  matrix products: 146 us -> 0 us
  waiting for transfers between devices: 201 us -> 74.4 us
  other arithmetic: 75.4 us -> 0.61 us
  Pallas kernels: 0 us -> 54.2 us
  local copies, waits for them, and re-layouts: 35.1 us -> 2.84 us
    dot_general x136 -> x0, matrix products: 146 us -> none  [the longest x68 100 us: precise(): jnp.einsum('eij,ejk->eik', first, second, precision=lax.Precision.HIGHEST...]
    ppermute x7 -> x20, waiting for transfers between devices: 160 us -> 74.4 us  [the longest x12 40.4 us: swap(): return lax.ppermute(x, 'energy', [(i, i ^ k) for i in range(count)])]
    pallas_call x0 -> x18, Pallas kernels: none -> 54.2 us  [the longest x2 11.4 us: build_sources(): pl.pallas_call(functools.partial(source_body, count), grid=(slabs,), in_s...]
    add x8 -> x0, other arithmetic: 54 us -> none  [add_offset(): imag_part = totals[1] + shifted[0] * weight[1] + shifted[1] * weight[0]]
    all_to_all x3 -> x0, waiting for transfers between devices: 40.8 us -> none  [the longest x1 18 us: per_device(): lax.all_to_all(sigma_rows, 'energy', split_axis=1, concat_axis=3, tiled=T...]
    unnamed x44 -> x4, local copies, waits for them, and re-layouts: 13.9 us -> 0.01 us
    all_to_all x3 -> x0, starting transfers between devices: 13.7 us -> none  [the longest x1 4.66 us: per_device(): lax.all_to_all(sigma_rows, 'energy', split_axis=1, concat_axis=3, tiled=T...]
    another operation x14 -> x8, other arithmetic: 12.5 us -> 0.41 us  [piece(): jnp.stack([lax.dynamic_slice(green_lesser, begin, sizes), lax.dynamic_sli...]
  transfers between devices with their start and end apart: 10 -> 20, of which waited for: 10 -> 11; matrix products, arithmetic and copies ran while one was open for 7% -> 0% of each run, Pallas kernels for 0% -> 31%
where the time goes in v1:
time: 159 us; the launch traced here: 158 us
  waiting for transfers between devices  74.4 us (47%)
  Pallas kernels  54.2 us (34%)
  starting transfers between devices  25.8 us (16%)
  local copies, waits for them, and re-layouts  2.84 us (2%)
    ppermute x12, waiting for transfers between devices, swap(): return lax.ppermute(x, 'energy', [(i, i ^ k) for i in range(count)])  40.4 us
    ppermute x8, waiting for transfers between devices, forward(): return lax.ppermute(x, 'slab', [(i, i + by) for i in range(count - by)])  34 us
    ppermute x8, starting transfers between devices, forward(): return lax.ppermute(x, 'slab', [(i, i + by) for i in range(count - by)])  16.8 us
    pallas_call x2, Pallas kernels, build_sources(): pl.pallas_call(functools.partial(source_body, count), grid=(slabs,), in_s...  11.4 us
    pallas_call x2, Pallas kernels, finish(): pl.pallas_call(finish_body, grid=(slabs,), in_specs=in_specs, out_specs=p...  9.09 us
    ppermute x12, starting transfers between devices, swap(): return lax.ppermute(x, 'energy', [(i, i ^ k) for i in range(count)])  8.99 us
    pallas_call x2, Pallas kernels, apply_entry(): pl.pallas_call(entry_body, grid=(slabs,), in_specs=[pl.BlockSpec((order,...  8.62 us
    pallas_call x3, Pallas kernels, map_product(): pl.pallas_call(map_product_body, grid=(energies, slabs), in_specs=[spec,...  7.47 us
  transfers between devices with their start and end apart: 20, of which 11 were waited for; matrix products, arithmetic and copies ran while one was open for 0% of the time, Pallas kernels for 31%

profile of v1, /device:TPU:24, one launch (start us, length us, event | category | flops | bytes accessed | tf_op | source)
XLA Modules:
  0.0 158.3 jit_solution(13573226721631243790)
XLA Ops:
  0.0 2.6 %dynamic-slice_bitcast_fusion.8 = (bf16[1,2,2,2,64,256]{5,4,3,2,1,0:T(8,128)(2,1)S(1)}, bf16[1,2,2,2,64,256]{5,4,3,2,1,0:T(8,128)(2,1)S(1)}, bf16[1,2,2,2,64,256...) fusion(bf16[2,2,4,256,256]{4,3,2,1,0:T(8,128)(2,1)} %param.5, ...), kind=kLoop, calls=%fused_computation.26 | loop fusion | bytes 8388624 | tf_op jit(solution)/shard_map/stack | solution.py:386
  2.7 0.0 copy-start
  2.7 0.0 copy-start.1
  2.7 0.1 pad_maximum_fusion.6
  2.7 1.6 %collective-permute-start.4 = (bf16[2,2,2,2,64,256]{5,4,3,2,1,0:T(8,128)(2,1)S(1)}, bf16[2,2,2,2,64,256]{5,4,3,2,1,0:T(8,128)(2,1)S(1)}, u32[]{:S(2)}, u32[]{:S(2)}) collective-permute-start(bf16[2,2,2,2,64,256]{5,4,3,2,1,0:T(8,128)(2,1)S(1)} %pad_maximum_fusion.6), channel_id=1, source_target_pairs={{0,2},{1,3},{2,0},{3,1},{4,6},{5,7},{6,4},{7,5},{8,10},{9,11},{10,... | collective-permute-start | bytes 1572872 | tf_op jit(solution)/shard_map/ppermute | solution.py:364
  4.3 0.1 pad_maximum_fusion.7
  4.4 0.1 collective-permute-start.5
  4.5 0.1 pad_maximum_fusion.1
  4.5 0.7 collective-permute-start
  5.2 0.1 pad_maximum_fusion.2
  5.2 1.6 %collective-permute-start.1 = (bf16[2,2,2,2,64,256]{5,4,3,2,1,0:T(8,128)(2,1)S(1)}, bf16[2,2,2,2,64,256]{5,4,3,2,1,0:T(8,128)(2,1)S(1)}, u32[]{:S(2)}, u32[]{:S(2)}) collective-permute-start(bf16[2,2,2,2,64,256]{5,4,3,2,1,0:T(8,128)(2,1)S(1)} %pad_maximum_fusion.2), channel_id=1, source_target_pairs={{0,2},{1,3},{2,0},{3,1},{4,6},{5,7},{6,4},{7,5},{8,10},{9,11},{10,... | collective-permute-start | bytes 1572872 | tf_op jit(solution)/shard_map/ppermute | solution.py:364
  6.8 0.1 pad_maximum_fusion.5
  6.9 0.1 collective-permute-start.3
  7.0 0.1 pad_maximum_fusion.3
  7.0 7.2 %maps.1 = (bf16[2,4,2,256,512]{4,3,2,1,0:T(8,128)(2,1)S(1)}, bf16[2,4,2,256,512]{4,3,2,1,0:T(8,128)(2,1)S(1)}) custom-call(bf16[2,2,4,256,256]{4,3,2,1,0:T(8,128)(2,1)S(1)} %copy-done, bf16[2,4,256,256]{3,2,1,0:T(8,128)(2,1)S(1)} %copy-done.1), custom_call_target="tpu_custom_call" | custom-call | flops 4294967296 | bytes 12582912 | tf_op jit(solution)/shard_map/maps/pallas_call | solution.py:100
  14.2 3.4 %collective-permute-done.4.refs_2_ = bf16[2,2,2,2,64,256]{5,4,3,2,1,0:T(8,128)(2,1)S(1)} collective-permute-done((bf16[2,2,2,2,64,256]{5,4,3,2,1,0:T(8,128)(2,1)S(1)}, bf16[2,2,2,2,64,256]{5,4,3,2,1,0:T(8,128)(2,1)S(1)}, u32[]{:S(2)}, u32[]{:S(2)}) %collective-permute-start.4) | collective-permute-done | bytes 524320 | tf_op jit(solution)/shard_map/ppermute | solution.py:364
  17.6 0.0 collective-permute-start.2
  17.6 0.1 pad_maximum_fusion.4.refs_0_
  17.7 0.1 pad_maximum_fusion.refs_0_
  17.7 0.2 slice_bitcast_fusion
  17.9 10.0 %collective-permute-done.5.refs_3_ = bf16[2,2,2,2,64,256]{5,4,3,2,1,0:T(8,128)(2,1)S(1)} collective-permute-done((bf16[2,2,2,2,64,256]{5,4,3,2,1,0:T(8,128)(2,1)S(1)}, bf16[2,2,2,2,64,256]{5,4,3,2,1,0:T(8,128)(2,1)S(1)}, u32[]{:S(2)}, u32[]{:S(2)}) %collective-permute-start.5) | collective-permute-done | bytes 524320 | tf_op jit(solution)/shard_map/ppermute | solution.py:364
  27.9 3.4 %collective-permute-start.11 = (bf16[2,2,256,512]{3,2,1,0:T(8,128)(2,1)S(1)}, bf16[2,2,256,512]{3,2,1,0:T(8,128)(2,1)S(1)}, u32[]{:S(2)}, u32[]{:S(2)}) collective-permute-start(bf16[2,2,256,512]{3,2,1,0:T(8,128)(2,1)S(1)} %get-tuple-element.58.t_ref), channel_id=1, source_target_pairs={{0,4},{4,8},{8,12},{12,16},{16,20},{20,24},{24,28},{1,5},{5,9},{9,... | collective-permute-start | bytes 3145736 | tf_op jit(solution)/shard_map/ppermute | solution.py:369
  31.3 0.0 collective-permute-done.3.refs_1_
  31.3 2.5 %convolve.3 = (bf16[2,2,64,256]{3,2,1,0:T(8,128)(2,1)S(1)}, bf16[2,2,64,256]{3,2,1,0:T(8,128)(2,1)S(1)}, bf16[2,2,64,256]{3,2,1,0:T(8,128)(2,1)S(1)}, bf16[2,2,6...) custom-call(bf16[2,2,2,2,64,256]{5,4,3,2,1,0:T(8,128)(2,1)S(1)} %pad, ...), custom_call_target="tpu_custom_call" | custom-call | flops 419430400 | bytes 3145728 | tf_op jit(solution)/shard_map/convolve/pallas_call | solution.py:186
  33.8 6.3 %collective-permute-done.1.refs_2_ = bf16[2,2,2,2,64,256]{5,4,3,2,1,0:T(8,128)(2,1)S(1)} collective-permute-done((bf16[2,2,2,2,64,256]{5,4,3,2,1,0:T(8,128)(2,1)S(1)}, bf16[2,2,2,2,64,256]{5,4,3,2,1,0:T(8,128)(2,1)S(1)}, u32[]{:S(2)}, u32[]{:S(2)}) %collective-permute-start.1) | collective-permute-done | bytes 524320 | tf_op jit(solution)/shard_map/ppermute | solution.py:364
  40.1 9.1 %collective-permute-done.2.refs_3_ = bf16[2,2,2,2,64,256]{5,4,3,2,1,0:T(8,128)(2,1)S(1)} collective-permute-done((bf16[2,2,2,2,64,256]{5,4,3,2,1,0:T(8,128)(2,1)S(1)}, bf16[2,2,2,2,64,256]{5,4,3,2,1,0:T(8,128)(2,1)S(1)}, u32[]{:S(2)}, u32[]{:S(2)}) %collective-permute-start.2) | collective-permute-done | bytes 524320 | tf_op jit(solution)/shard_map/ppermute | solution.py:364
  49.2 2.5 %convolve.2 = (bf16[2,2,64,256]{3,2,1,0:T(8,128)(2,1)S(1)}, bf16[2,2,64,256]{3,2,1,0:T(8,128)(2,1)S(1)}, bf16[2,2,64,256]{3,2,1,0:T(8,128)(2,1)S(1)}, bf16[2,2,6...) custom-call(bf16[2,2,2,2,64,256]{5,4,3,2,1,0:T(8,128)(2,1)S(1)} %pad, ...), custom_call_target="tpu_custom_call" | custom-call | flops 419430400 | bytes 3145728 | tf_op jit(solution)/shard_map/convolve/pallas_call | solution.py:186
  51.7 2.3 %collective-permute-start.16 = (bf16[4,2,64,256]{3,2,1,0:T(8,128)(2,1)S(1)}, bf16[4,2,64,256]{3,2,1,0:T(8,128)(2,1)S(1)}, u32[]{:S(2)}, u32[]{:S(2)}) collective-permute-start(bf16[4,2,64,256]{3,2,1,0:T(8,128)(2,1)S(1)} %pad_maximum_fusion.15), channel_id=1, source_target_pairs={{0,3},{1,2},{2,1},{3,0},{4,7},{5,6},{6,5},{7,4},{8,11},{9,10},{10,... | collective-permute-start | bytes 786440 | tf_op jit(solution)/shard_map/ppermute | solution.py:364
  54.0 0.6 collective-permute-start.15
  54.6 0.1 collective-permute-start.14
  54.7 1.7 %collective-permute-start.8 = (bf16[4,2,64,256]{3,2,1,0:T(8,128)(2,1)S(1)}, bf16[4,2,64,256]{3,2,1,0:T(8,128)(2,1)S(1)}, u32[]{:S(2)}, u32[]{:S(2)}) collective-permute-start(bf16[4,2,64,256]{3,2,1,0:T(8,128)(2,1)S(1)} %pad_maximum_fusion.11), channel_id=1, source_target_pairs={{0,3},{1,2},{2,1},{3,0},{4,7},{5,6},{6,5},{7,4},{8,11},{9,10},{10,... | collective-permute-start | bytes 786440 | tf_op jit(solution)/shard_map/ppermute | solution.py:364
  56.5 4.2 %collective-permute-done.16.refs_3_ = bf16[4,2,64,256]{3,2,1,0:T(8,128)(2,1)S(1)} collective-permute-done((bf16[4,2,64,256]{3,2,1,0:T(8,128)(2,1)S(1)}, bf16[4,2,64,256]{3,2,1,0:T(8,128)(2,1)S(1)}, u32[]{:S(2)}, u32[]{:S(2)}) %collective-permute-start.16) | collective-permute-done | bytes 262176 | tf_op jit(solution)/shard_map/ppermute | solution.py:364
  60.8 0.4 collective-permute-start.7
  61.2 6.1 %collective-permute-done.15.refs_2_ = bf16[4,2,64,256]{3,2,1,0:T(8,128)(2,1)S(1)} collective-permute-done((bf16[4,2,64,256]{3,2,1,0:T(8,128)(2,1)S(1)}, bf16[4,2,64,256]{3,2,1,0:T(8,128)(2,1)S(1)}, u32[]{:S(2)}, u32[]{:S(2)}) %collective-permute-start.15) | collective-permute-done | bytes 262176 | tf_op jit(solution)/shard_map/ppermute | solution.py:364
  67.2 0.0 collective-permute-start.6
  67.2 5.7 %sources.3 = (f32[4,256,512]{2,1,0:T(8,128)S(1)}, bf16[256,512]{1,0:T(8,128)(2,1)S(1)}) custom-call(bf16[4,2,64,256]{3,2,1,0:T(8,128)(2,1)S(1)} %pad_maximum_fusion.12.refs_0_, bf16[4,2,64,256]{3,2,1,0:T(8,128)(2,1)S(1)} %collective-permute-done.14.refs_1_, bf16[4,2,64,256]{3,2,1,0:T(8,128)(2,1)S(1)} %collective-permute-done.15.refs_2_, ...), custom_call_target="tpu_custom_call" | custom-call | flops 4294967296 | bytes 6291456 | tf_op jit(solution)/shard_map/sources/pallas_call | solution.py:243
  72.9 3.4 %collective-permute-start.17 = (bf16[256,512]{1,0:T(8,128)(2,1)S(1)}, bf16[256,512]{1,0:T(8,128)(2,1)S(1)}, u32[]{:S(2)}, u32[]{:S(2)}) collective-permute-start(bf16[256,512]{1,0:T(8,128)(2,1)S(1)} %get-tuple-element.53), channel_id=1, source_target_pairs={{0,4},{4,8},{8,12},{12,16},{16,20},{20,24},{24,28},{1,5},{5,9},{9,... | collective-permute-start | bytes 786440 | tf_op jit(solution)/shard_map/ppermute | solution.py:369
  76.3 0.0 collective-permute-done.8.refs_3_
  76.3 1.4 collective-permute-done.7.refs_2_
  77.7 0.0 collective-permute-done.6.refs_1_
  77.7 5.7 %sources.2 = (f32[4,256,512]{2,1,0:T(8,128)S(1)}, bf16[256,512]{1,0:T(8,128)(2,1)S(1)}) custom-call(bf16[4,2,64,256]{3,2,1,0:T(8,128)(2,1)S(1)} %pad_maximum_fusion.8.refs_0_, bf16[4,2,64,256]{3,2,1,0:T(8,128)(2,1)S(1)} %collective-permute-done.6.refs_1_, bf16[4,2,64,256]{3,2,1,0:T(8,128)(2,1)S(1)} %collective-permute-done.7.refs_2_, ...), custom_call_target="tpu_custom_call" | custom-call | flops 4294967296 | bytes 6291456 | tf_op jit(solution)/shard_map/sources/pallas_call | solution.py:243
  83.4 3.4 %collective-permute-start.9 = (bf16[256,512]{1,0:T(8,128)(2,1)S(1)}, bf16[256,512]{1,0:T(8,128)(2,1)S(1)}, u32[]{:S(2)}, u32[]{:S(2)}) collective-permute-start(bf16[256,512]{1,0:T(8,128)(2,1)S(1)} %get-tuple-element.40), channel_id=1, source_target_pairs={{0,4},{4,8},{8,12},{12,16},{16,20},{20,24},{24,28},{1,5},{5,9},{9,... | collective-permute-start | bytes 786440 | tf_op jit(solution)/shard_map/ppermute | solution.py:369
  86.8 0.9 combine.9
  87.8 1.3 collective-permute-start.18
  89.1 6.4 %collective-permute-done.9.v_ref.base_ref = bf16[256,512]{1,0:T(8,128)(2,1)S(1)} collective-permute-done((bf16[256,512]{1,0:T(8,128)(2,1)S(1)}, bf16[256,512]{1,0:T(8,128)(2,1)S(1)}, u32[]{:S(2)}, u32[]{:S(2)}) %collective-permute-start.9) | collective-permute-done | bytes 262176 | tf_op jit(solution)/shard_map/ppermute | solution.py:369
  95.4 0.9 combine.6
  96.4 1.3 collective-permute-start.10
  97.7 1.3 map_product.3
  98.9 1.3 collective-permute-start.13
  100.2 7.2 %collective-permute-done.10.v_ref = bf16[256,512]{1,0:T(8,128)(2,1)S(1)} collective-permute-done((bf16[256,512]{1,0:T(8,128)(2,1)S(1)}, bf16[256,512]{1,0:T(8,128)(2,1)S(1)}, u32[]{:S(2)}, u32[]{:S(2)}) %collective-permute-start.10) | collective-permute-done | bytes 262176 | tf_op jit(solution)/shard_map/ppermute | solution.py:369
  107.4 0.9 combine.7
  108.4 1.3 collective-permute-start.12
  109.7 0.9 combine.10
  110.6 1.5 collective-permute-start.19
  112.1 0.9 combine.8.w_ref
  113.0 0.9 combine.11.w_ref
  114.0 4.3 %entry.2.y_ref = f32[4,256,512]{2,1,0:T(8,128)S(1)} custom-call(f32[256,512]{1,0:T(8,128)S(1)} %combine.8.w_ref, bf16[2,4,2,256,512]{4,3,2,1,0:T(8,128)(2,1)S(1)} %get-tuple-element.41.a_ref.p_ref, f32[4,256,512]{2,1,0:T(8,128)S(1)} %get-tuple-element.42.base_ref.b_ref), custom_call_target="tpu_custom_call" | custom-call | flops 3221225472 | bytes 6291456 | tf_op jit(solution)/shard_map/entry/pallas_call | solution.py:310
  118.3 4.3 %entry.3.y_ref = f32[4,256,512]{2,1,0:T(8,128)S(1)} custom-call(f32[256,512]{1,0:T(8,128)S(1)} %combine.11.w_ref, bf16[2,4,2,256,512]{4,3,2,1,0:T(8,128)(2,1)S(1)} %get-tuple-element.41.a_ref.p_ref, f32[4,256,512]{2,1,0:T(8,128)S(1)} %get-tuple-element.54.base_ref.b_ref), custom_call_target="tpu_custom_call" | custom-call | flops 3221225472 | bytes 6291456 | tf_op jit(solution)/shard_map/entry/pallas_call | solution.py:310
  122.6 4.0 %collective-permute-done.13.b_ref = bf16[2,2,256,512]{3,2,1,0:T(8,128)(2,1)S(1)} collective-permute-done((bf16[2,2,256,512]{3,2,1,0:T(8,128)(2,1)S(1)}, bf16[2,2,256,512]{3,2,1,0:T(8,128)(2,1)S(1)}, u32[]{:S(2)}, u32[]{:S(2)}) %collective-permute-start.13) | collective-permute-done | bytes 1048608 | tf_op jit(solution)/shard_map/ppermute | solution.py:369
  126.6 1.2 map_product.4
  127.9 5.0 %map_product.5.r_ref = bf16[2,4,2,256,512]{4,3,2,1,0:T(8,128)(2,1)S(1)} custom-call(bf16[2,4,2,256,512]{4,3,2,1,0:T(8,128)(2,1)S(1)} %get-tuple-element.41.a_ref.p_ref, bf16[2,2,256,512]{3,2,1,0:T(8,128)(2,1)S(1)} %bitcast.45), custom_call_target="tpu_custom_call" | custom-call | flops 3221225472 | bytes 8388608 | tf_op jit(solution)/shard_map/map_product/pallas_call | solution.py:125
  132.9 16.3 %collective-permute-done.19.v_ref = bf16[256,512]{1,0:T(8,128)(2,1)S(1)} collective-permute-done((bf16[256,512]{1,0:T(8,128)(2,1)S(1)}, bf16[256,512]{1,0:T(8,128)(2,1)S(1)}, u32[]{:S(2)}, u32[]{:S(2)}) %collective-permute-start.19) | collective-permute-done | bytes 262176 | tf_op jit(solution)/shard_map/ppermute | solution.py:369
  149.2 4.5 %finish.2.rest_0_ = f32[2,2,4,256,256]{4,3,2,1,0:T(8,128)} custom-call(bf16[256,512]{1,0:T(8,128)(2,1)S(1)} %collective-permute-done.19.v_ref, bf16[2,4,2,256,512]{4,3,2,1,0:T(8,128)(2,1)S(1)} %map_product.5.r_ref, f32[4,256,512]{2,1,0:T(8,128)S(1)} %entry.3.y_ref), custom_call_target="tpu_custom_call" | custom-call | flops 2684354560 | bytes 6291456 | tf_op jit(solution)/shard_map/finish/pallas_call | solution.py:349
  153.7 4.6 %finish.3 = f32[2,2,4,256,256]{4,3,2,1,0:T(8,128)} custom-call(bf16[256,512]{1,0:T(8,128)(2,1)S(1)} %collective-permute-done.12.v_ref, bf16[2,4,2,256,512]{4,3,2,1,0:T(8,128)(2,1)S(1)} %map_product.5.r_ref, f32[4,256,512]{2,1,0:T(8,128)S(1)} %entry.2.y_ref, f32[2,2,4,256,256]{4,3,2,1,0:T(8,128)} %finish.2.rest_0_), custom_call_target="tpu_custom_call", output_to_operand_aliasing={{}: (3, {})} | custom-call | flops 2684354560 | bytes 6291456 | tf_op jit(solution)/shard_map/finish/pallas_call | solution.py:349
  (16 shorter events, 0.2 us)
Async XLA Ops:
  2.7 4.4 %copy-start = (bf16[2,2,4,256,256]{4,3,2,1,0:T(8,128)(2,1)S(1)}, bf16[2,2,4,256,256]{4,3,2,1,0:T(8,128)(2,1)}, u32[]{:S(2)}) copy-start(bf16[2,2,4,256,256]{4,3,2,1,0:T(8,128)(2,1)} %refs_4_.3) | copy-start | bytes 6291460
  2.7 4.4 %copy-start.1 = (bf16[2,4,256,256]{3,2,1,0:T(8,128)(2,1)S(1)}, bf16[2,4,256,256]{3,2,1,0:T(8,128)(2,1)}, u32[]{:S(2)}) copy-start(bf16[2,4,256,256]{3,2,1,0:T(8,128)(2,1)} %c_ref.1) | copy-start | bytes 3145732
  2.7 14.9 %collective-permute-start.4 = (bf16[2,2,2,2,64,256]{5,4,3,2,1,0:T(8,128)(2,1)S(1)}, bf16[2,2,2,2,64,256]{5,4,3,2,1,0:T(8,128)(2,1)S(1)}, u32[]{:S(2)}, u32[]{:S(2)}) collective-permute-start(bf16[2,2,2,2,64,256]{5,4,3,2,1,0:T(8,128)(2,1)S(1)} %pad_maximum_fusion.6), channel_id=1, source_target_pairs={{0,2},{1,3},{2,0},{3,1},{4,6},{5,7},{6,4},{7,5},{8,10},{9,11},{10,... | collective-permute-start | bytes 1572872 | tf_op jit(solution)/shard_map/ppermute | solution.py:364
  4.4 23.5 %collective-permute-start.5 = (bf16[2,2,2,2,64,256]{5,4,3,2,1,0:T(8,128)(2,1)S(1)}, bf16[2,2,2,2,64,256]{5,4,3,2,1,0:T(8,128)(2,1)S(1)}, u32[]{:S(2)}, u32[]{:S(2)}) collective-permute-start(bf16[2,2,2,2,64,256]{5,4,3,2,1,0:T(8,128)(2,1)S(1)} %pad_maximum_fusion.7), channel_id=1, source_target_pairs={{0,3},{1,2},{2,1},{3,0},{4,7},{5,6},{6,5},{7,4},{8,11},{9,10},{10,... | collective-permute-start | bytes 1572872 | tf_op jit(solution)/shard_map/ppermute | solution.py:364
  4.5 29.3 %collective-permute-start = (bf16[2,2,2,2,64,256]{5,4,3,2,1,0:T(8,128)(2,1)S(1)}, bf16[2,2,2,2,64,256]{5,4,3,2,1,0:T(8,128)(2,1)S(1)}, u32[]{:S(2)}, u32[]{:S(2)}) collective-permute-start(bf16[2,2,2,2,64,256]{5,4,3,2,1,0:T(8,128)(2,1)S(1)} %pad_maximum_fusion.1), channel_id=1, source_target_pairs={{0,1},{1,0},{2,3},{3,2},{4,5},{5,4},{6,7},{7,6},{8,9},{9,8},{10,11... | collective-permute-start | bytes 1572872 | tf_op jit(solution)/shard_map/ppermute | solution.py:364
  5.2 34.9 %collective-permute-start.1 = (bf16[2,2,2,2,64,256]{5,4,3,2,1,0:T(8,128)(2,1)S(1)}, bf16[2,2,2,2,64,256]{5,4,3,2,1,0:T(8,128)(2,1)S(1)}, u32[]{:S(2)}, u32[]{:S(2)}) collective-permute-start(bf16[2,2,2,2,64,256]{5,4,3,2,1,0:T(8,128)(2,1)S(1)} %pad_maximum_fusion.2), channel_id=1, source_target_pairs={{0,2},{1,3},{2,0},{3,1},{4,6},{5,7},{6,4},{7,5},{8,10},{9,11},{10,... | collective-permute-start | bytes 1572872 | tf_op jit(solution)/shard_map/ppermute | solution.py:364
  6.9 24.4 %collective-permute-start.3 = (bf16[2,2,2,2,64,256]{5,4,3,2,1,0:T(8,128)(2,1)S(1)}, bf16[2,2,2,2,64,256]{5,4,3,2,1,0:T(8,128)(2,1)S(1)}, u32[]{:S(2)}, u32[]{:S(2)}) collective-permute-start(bf16[2,2,2,2,64,256]{5,4,3,2,1,0:T(8,128)(2,1)S(1)} %pad_maximum_fusion.5), channel_id=1, source_target_pairs={{0,1},{1,0},{2,3},{3,2},{4,5},{5,4},{6,7},{7,6},{8,9},{9,8},{10,11... | collective-permute-start | bytes 1572872 | tf_op jit(solution)/shard_map/ppermute | solution.py:364
  17.6 31.6 %collective-permute-start.2 = (bf16[2,2,2,2,64,256]{5,4,3,2,1,0:T(8,128)(2,1)S(1)}, bf16[2,2,2,2,64,256]{5,4,3,2,1,0:T(8,128)(2,1)S(1)}, u32[]{:S(2)}, u32[]{:S(2)}) collective-permute-start(bf16[2,2,2,2,64,256]{5,4,3,2,1,0:T(8,128)(2,1)S(1)} %pad_maximum_fusion.3), channel_id=1, source_target_pairs={{0,3},{1,2},{2,1},{3,0},{4,7},{5,6},{6,5},{7,4},{8,11},{9,10},{10,... | collective-permute-start | bytes 1572872 | tf_op jit(solution)/shard_map/ppermute | solution.py:364
  27.9 69.8 %collective-permute-start.11 = (bf16[2,2,256,512]{3,2,1,0:T(8,128)(2,1)S(1)}, bf16[2,2,256,512]{3,2,1,0:T(8,128)(2,1)S(1)}, u32[]{:S(2)}, u32[]{:S(2)}) collective-permute-start(bf16[2,2,256,512]{3,2,1,0:T(8,128)(2,1)S(1)} %get-tuple-element.58.t_ref), channel_id=1, source_target_pairs={{0,4},{4,8},{8,12},{12,16},{16,20},{20,24},{24,28},{1,5},{5,9},{9,... | collective-permute-start | bytes 3145736 | tf_op jit(solution)/shard_map/ppermute | solution.py:369
  51.7 9.0 %collective-permute-start.16 = (bf16[4,2,64,256]{3,2,1,0:T(8,128)(2,1)S(1)}, bf16[4,2,64,256]{3,2,1,0:T(8,128)(2,1)S(1)}, u32[]{:S(2)}, u32[]{:S(2)}) collective-permute-start(bf16[4,2,64,256]{3,2,1,0:T(8,128)(2,1)S(1)} %pad_maximum_fusion.15), channel_id=1, source_target_pairs={{0,3},{1,2},{2,1},{3,0},{4,7},{5,6},{6,5},{7,4},{8,11},{9,10},{10,... | collective-permute-start | bytes 786440 | tf_op jit(solution)/shard_map/ppermute | solution.py:364
  54.0 13.2 %collective-permute-start.15 = (bf16[4,2,64,256]{3,2,1,0:T(8,128)(2,1)S(1)}, bf16[4,2,64,256]{3,2,1,0:T(8,128)(2,1)S(1)}, u32[]{:S(2)}, u32[]{:S(2)}) collective-permute-start(bf16[4,2,64,256]{3,2,1,0:T(8,128)(2,1)S(1)} %pad_maximum_fusion.14), channel_id=1, source_target_pairs={{0,2},{1,3},{2,0},{3,1},{4,6},{5,7},{6,4},{7,5},{8,10},{9,11},{10,... | collective-permute-start | bytes 786440 | tf_op jit(solution)/shard_map/ppermute | solution.py:364
  54.6 12.6 %collective-permute-start.14 = (bf16[4,2,64,256]{3,2,1,0:T(8,128)(2,1)S(1)}, bf16[4,2,64,256]{3,2,1,0:T(8,128)(2,1)S(1)}, u32[]{:S(2)}, u32[]{:S(2)}) collective-permute-start(bf16[4,2,64,256]{3,2,1,0:T(8,128)(2,1)S(1)} %pad_maximum_fusion.13), channel_id=1, source_target_pairs={{0,1},{1,0},{2,3},{3,2},{4,5},{5,4},{6,7},{7,6},{8,9},{9,8},{10,11... | collective-permute-start | bytes 786440 | tf_op jit(solution)/shard_map/ppermute | solution.py:364
  54.7 21.6 %collective-permute-start.8 = (bf16[4,2,64,256]{3,2,1,0:T(8,128)(2,1)S(1)}, bf16[4,2,64,256]{3,2,1,0:T(8,128)(2,1)S(1)}, u32[]{:S(2)}, u32[]{:S(2)}) collective-permute-start(bf16[4,2,64,256]{3,2,1,0:T(8,128)(2,1)S(1)} %pad_maximum_fusion.11), channel_id=1, source_target_pairs={{0,3},{1,2},{2,1},{3,0},{4,7},{5,6},{6,5},{7,4},{8,11},{9,10},{10,... | collective-permute-start | bytes 786440 | tf_op jit(solution)/shard_map/ppermute | solution.py:364
  60.8 17.0 %collective-permute-start.7 = (bf16[4,2,64,256]{3,2,1,0:T(8,128)(2,1)S(1)}, bf16[4,2,64,256]{3,2,1,0:T(8,128)(2,1)S(1)}, u32[]{:S(2)}, u32[]{:S(2)}) collective-permute-start(bf16[4,2,64,256]{3,2,1,0:T(8,128)(2,1)S(1)} %pad_maximum_fusion.10), channel_id=1, source_target_pairs={{0,2},{1,3},{2,0},{3,1},{4,6},{5,7},{6,4},{7,5},{8,10},{9,11},{10,... | collective-permute-start | bytes 786440 | tf_op jit(solution)/shard_map/ppermute | solution.py:364
  67.2 10.5 %collective-permute-start.6 = (bf16[4,2,64,256]{3,2,1,0:T(8,128)(2,1)S(1)}, bf16[4,2,64,256]{3,2,1,0:T(8,128)(2,1)S(1)}, u32[]{:S(2)}, u32[]{:S(2)}) collective-permute-start(bf16[4,2,64,256]{3,2,1,0:T(8,128)(2,1)S(1)} %pad_maximum_fusion.9), channel_id=1, source_target_pairs={{0,1},{1,0},{2,3},{3,2},{4,5},{5,4},{6,7},{7,6},{8,9},{9,8},{10,11... | collective-permute-start | bytes 786440 | tf_op jit(solution)/shard_map/ppermute | solution.py:364
  72.9 13.9 %collective-permute-start.17 = (bf16[256,512]{1,0:T(8,128)(2,1)S(1)}, bf16[256,512]{1,0:T(8,128)(2,1)S(1)}, u32[]{:S(2)}, u32[]{:S(2)}) collective-permute-start(bf16[256,512]{1,0:T(8,128)(2,1)S(1)} %get-tuple-element.53), channel_id=1, source_target_pairs={{0,4},{4,8},{8,12},{12,16},{16,20},{20,24},{24,28},{1,5},{5,9},{9,... | collective-permute-start | bytes 786440 | tf_op jit(solution)/shard_map/ppermute | solution.py:369
  83.4 12.0 %collective-permute-start.9 = (bf16[256,512]{1,0:T(8,128)(2,1)S(1)}, bf16[256,512]{1,0:T(8,128)(2,1)S(1)}, u32[]{:S(2)}, u32[]{:S(2)}) collective-permute-start(bf16[256,512]{1,0:T(8,128)(2,1)S(1)} %get-tuple-element.40), channel_id=1, source_target_pairs={{0,4},{4,8},{8,12},{12,16},{16,20},{20,24},{24,28},{1,5},{5,9},{9,... | collective-permute-start | bytes 786440 | tf_op jit(solution)/shard_map/ppermute | solution.py:369
  87.8 21.9 %collective-permute-start.18 = (bf16[256,512]{1,0:T(8,128)(2,1)S(1)}, bf16[256,512]{1,0:T(8,128)(2,1)S(1)}, u32[]{:S(2)}, u32[]{:S(2)}) collective-permute-start(bf16[256,512]{1,0:T(8,128)(2,1)S(1)} %get-tuple-element.55), channel_id=1, source_target_pairs={{0,8},{4,12},{8,16},{12,20},{16,24},{20,28},{1,9},{5,13},{9,17},{1... | collective-permute-start | bytes 786440 | tf_op jit(solution)/shard_map/ppermute | solution.py:369
  96.4 11.1 %collective-permute-start.10 = (bf16[256,512]{1,0:T(8,128)(2,1)S(1)}, bf16[256,512]{1,0:T(8,128)(2,1)S(1)}, u32[]{:S(2)}, u32[]{:S(2)}) collective-permute-start(bf16[256,512]{1,0:T(8,128)(2,1)S(1)} %get-tuple-element.43), channel_id=1, source_target_pairs={{0,8},{4,12},{8,16},{12,20},{16,24},{20,28},{1,9},{5,13},{9,17},{1... | collective-permute-start | bytes 786440 | tf_op jit(solution)/shard_map/ppermute | solution.py:369
  98.9 27.7 %collective-permute-start.13 = (bf16[2,2,256,512]{3,2,1,0:T(8,128)(2,1)S(1)}, bf16[2,2,256,512]{3,2,1,0:T(8,128)(2,1)S(1)}, u32[]{:S(2)}, u32[]{:S(2)}) collective-permute-start(bf16[2,2,256,512]{3,2,1,0:T(8,128)(2,1)S(1)} %bitcast.42), channel_id=1, source_target_pairs={{0,8},{4,12},{8,16},{12,20},{16,24},{20,28},{1,9},{5,13},{9,17},{1... | collective-permute-start | bytes 3145736 | tf_op jit(solution)/shard_map/ppermute | solution.py:369
  108.4 45.4 %collective-permute-start.12 = (bf16[256,512]{1,0:T(8,128)(2,1)S(1)}, bf16[256,512]{1,0:T(8,128)(2,1)S(1)}, u32[]{:S(2)}, u32[]{:S(2)}) collective-permute-start(bf16[256,512]{1,0:T(8,128)(2,1)S(1)} %combine.7), channel_id=1, source_target_pairs={{0,16},{4,20},{8,24},{12,28},{1,17},{5,21},{9,25},{13,29},{2,18},{... | collective-permute-start | bytes 786440 | tf_op jit(solution)/shard_map/ppermute | solution.py:369
  110.6 38.6 %collective-permute-start.19 = (bf16[256,512]{1,0:T(8,128)(2,1)S(1)}, bf16[256,512]{1,0:T(8,128)(2,1)S(1)}, u32[]{:S(2)}, u32[]{:S(2)}) collective-permute-start(bf16[256,512]{1,0:T(8,128)(2,1)S(1)} %combine.10), channel_id=1, source_target_pairs={{0,16},{4,20},{8,24},{12,28},{1,17},{5,21},{9,25},{13,29},{2,18},{... | collective-permute-start | bytes 786440 | tf_op jit(solution)/shard_map/ppermute | solution.py:369

commit v2 on v1

v2 whole, which is shorter than its diff:
```python
import functools

import jax
import jax.numpy as jnp
from jax import lax
from jax.experimental import pallas as pl
from jax.experimental.pallas import tpu as pltpu
from jax.sharding import PartitionSpec as P

BF16 = jnp.bfloat16
F32 = jnp.float32
VMEM_LIMIT = 24 * 1024 * 1024


def params():
    return pltpu.CompilerParams(vmem_limit_bytes=VMEM_LIMIT)


def ordered(body, count, extra=1):
    def run(*refs):
        body(*refs[:count], *refs[count + extra :])

    return run


ANYWHERE = pl.BlockSpec(memory_space=pl.ANY)


def cost():
    return pl.CostEstimate(flops=0, bytes_accessed=0, transcendentals=0)


def split(value):
    high = value.astype(BF16)
    low = (value - high.astype(F32)).astype(BF16)
    return high, low


def panel(re, im):
    return jnp.concatenate(
        [jnp.concatenate([re, im], axis=1), jnp.concatenate([-im, re], axis=1)], axis=0
    )


def dot(left, right):
    return lax.dot_general(left, right, (((1,), (0,)), ((), ())), preferred_element_type=F32)


def dot_nt(left, right):
    return lax.dot_general(left, right, (((1,), (1,)), ((), ())), preferred_element_type=F32)


def times_wide(a_high, a_low, x):
    order = x.shape[0]
    x_high, x_low = split(x)
    xh = panel(x_high[:, :order], x_high[:, order:])
    xl = panel(x_low[:, :order], x_low[:, order:])
    left = jnp.concatenate([a_high, a_high, a_low], axis=1)
    return dot(left, jnp.concatenate([xh, xl, xh], axis=0))


def times_narrow(a_high, a_low, re, im):
    xp = panel(re, im)
    left = jnp.concatenate([a_high, a_low], axis=1)
    return dot(left, jnp.concatenate([xp, xp], axis=0))


def times_adjoint(y, t_high, t_low):
    order = y.shape[0]
    y_high, y_low = split(y)
    th = panel(t_high[:, :order], t_high[:, order:])
    tl = panel(t_low[:, :order], t_low[:, order:])
    left = jnp.concatenate([y_high, y_low, y_high], axis=1)
    return dot_nt(left, jnp.concatenate([th, th, tl], axis=1))


def panels(ref):
    return ref[0], ref[1]


def store_map(ref, value):
    high, low = split(value)
    ref[0] = high
    ref[1] = low


def pack_body(wanted, *refs):
    sources, outs, sems = refs[:2], refs[-1 - len(wanted) : -1], refs[-1]
    copies = []
    for out, (k, start) in zip(outs, wanted):
        size, rows = out.shape[3:5]
        begin = pl.multiple_of((lax.axis_index("energy") ^ k) * rows, rows)
        for part in range(2):
            block = sources[part].at[:, :, pl.ds(start, size), pl.ds(begin, rows), :]
            copies.append(pltpu.make_async_copy(block, out.at[part], sems.at[len(copies)]))
    for copy in copies:
        copy.start()
    for copy in copies:
        copy.wait()


def pack(green, screen, wanted, count, *after):
    _, energies, _, order, _ = green.shape
    shapes = [(2, 2, energies, size, order // count, order) for _, _, size in wanted]
    return pl.pallas_call(
        functools.partial(pack_body, [w[:2] for w in wanted]),
        in_specs=[ANYWHERE] * (2 + len(after)),
        out_specs=[pl.BlockSpec(memory_space=pltpu.VMEM)] * len(wanted),
        out_shape=[jax.ShapeDtypeStruct(shape, BF16) for shape in shapes],
        scratch_shapes=[pltpu.SemaphoreType.DMA((2 * len(wanted),))],
        compiler_params=params(),
        cost_estimate=cost(),
        name="pack",
    )(green, screen, *after)


def maps_body(g_ref, c_ref, k_ref, p_ref, carry):
    left = jnp.concatenate([g_ref[0], g_ref[1]], axis=1)
    value = dot(left, panel(c_ref[0], c_ref[1]))
    store_map(k_ref, value)

    @pl.when(pl.program_id(1) == 0)
    def _():
        carry[...] = value

    @pl.when(pl.program_id(1) > 0)
    def _():
        high, low = panels(k_ref)
        carry[...] = times_wide(high, low, carry[...])

    store_map(p_ref, carry[...])


def build_maps(green, coupling, *after):
    _, energies, slabs, order, _ = green.shape
    shape = jax.ShapeDtypeStruct((energies, slabs, 2, order, 2 * order), BF16)
    out_spec = pl.BlockSpec((None, None, 2, order, 2 * order), lambda e, s: (e, s, 0, 0, 0))
    return pl.pallas_call(
        lambda *refs: maps_body(*refs[:2], *refs[2 + len(after) :]),
        grid=(energies, slabs),
        in_specs=[
            pl.BlockSpec((2, None, None, order, order), lambda e, s: (0, e, s, 0, 0)),
            pl.BlockSpec((2, None, order, order), lambda e, s: (0, s, 0, 0)),
        ]
        + [ANYWHERE] * len(after),
        out_specs=[out_spec, out_spec],
        out_shape=[shape, shape],
        scratch_shapes=[pltpu.VMEM((order, 2 * order), F32)],
        compiler_params=params(),
        cost_estimate=cost(),
        name="maps",
    )(green, coupling, *after)


def one_map(maps, energy):
    if isinstance(maps, list):
        return maps[energy], pl.BlockSpec(maps[energy].shape, lambda *_: (0, 0, 0))
    return maps, pl.BlockSpec((None,) + maps.shape[1:], lambda *_: (energy, 0, 0, 0))


def map_product_body(energies, *refs):
    out = refs[-1]
    for e in range(energies):
        high, low = panels(refs[2 * e])
        other = refs[2 * e + 1]
        store_map(out.at[e], times_wide(high, low, other[0].astype(F32) + other[1].astype(F32)))


def map_product(first, second, energies, after):
    pairs = [one_map(maps, e) for e in range(energies) for maps in (first, second)]
    shape = (energies,) + pairs[0][1].block_shape[-3:]
    return pl.pallas_call(
        ordered(functools.partial(map_product_body, energies), 2 * energies),
        grid=(1,),
        in_specs=[spec for _, spec in pairs] + [ANYWHERE],
        out_specs=pl.BlockSpec(shape, lambda i: (0, 0, 0, 0)),
        out_shape=jax.ShapeDtypeStruct(shape, BF16),
        compiler_params=params(),
        cost_estimate=cost(),
        name="map_product",
    )(*[maps for maps, _ in pairs], after)


def pair_maps_body(energies, *refs):
    step, plane, inner = refs[-3:]
    odd = (lax.axis_index("slab") & 1) == 1
    for e in range(energies):
        mine, other = refs[2 * e], refs[2 * e + 1]
        order = mine.shape[1]
        first = [jnp.where(odd, mine[part], other[part]) for part in range(2)]
        second = [jnp.where(odd, other[part], mine[part]).astype(F32) for part in range(2)]
        store_map(plane.at[e], times_wide(*first, second[0] + second[1]))
        row = lax.broadcasted_iota(jnp.int32, (order, 2 * order), 0)
        column = lax.broadcasted_iota(jnp.int32, (order, 2 * order), 1)
        unit = jnp.where(row == column, 1.0, 0.0)
        for part in range(2):
            step[e, part] = first[part]
            identity = unit if part == 0 else jnp.zeros_like(unit)
            inner[e, part] = jnp.where(odd, other[part].astype(F32), identity).astype(BF16)


def pair_maps(mine, other, energies, after):
    pairs = [one_map(maps, e) for e in range(energies) for maps in (mine, other)]
    shape = (energies,) + pairs[0][1].block_shape[-3:]
    return pl.pallas_call(
        ordered(functools.partial(pair_maps_body, energies), 2 * energies),
        grid=(1,),
        in_specs=[spec for _, spec in pairs] + [ANYWHERE],
        out_specs=[pl.BlockSpec(shape, lambda i: (0, 0, 0, 0))] * 3,
        out_shape=[jax.ShapeDtypeStruct(shape, BF16)] * 3,
        compiler_params=params(),
        cost_estimate=cost(),
        name="pair_maps",
    )(*[maps for maps, _ in pairs], after)


def convolve_body(count, energies, shared, *refs):
    ins, outs = refs[:count], refs[count + 1 + shared :]
    green, screen, total = refs[-3:]
    me = lax.axis_index("energy")
    points = count * energies
    middle = points // 2
    rows, columns = green.shape[2:]
    for k in range(count):
        base = (me ^ k) * energies
        for e in range(energies):
            green[:, base + e] = ins[k][0, :, e].astype(F32)
            screen[:, base + e] = ins[k][1, :, e].astype(F32)

    def tile(index, _):
        row = pl.multiple_of(index * 8, 8)
        for col in range(0, columns, 128):
            at = (pl.ds(row, 8), pl.ds(col, 128))
            gr = [green[(0, m) + at] for m in range(points)]
            gi = [green[(1, m) + at] for m in range(points)]
            wr = [screen[(0, m) + at] for m in range(points)]
            wi = [screen[(1, m) + at] for m in range(points)]
            for n in range(points):
                re = None
                im = None
                for m in range(points):
                    lag = n - m + middle
                    if 0 <= lag < points:
                        a = gr[m] * wr[lag] - gi[m] * wi[lag]
                        b = gr[m] * wi[lag] + gi[m] * wr[lag]
                        re = a if re is None else re + a
                        im = b if im is None else im + b
                total[(n, 0) + at] = -im / points
                total[(n, 1) + at] = re / points
        return 0

    lax.fori_loop(0, rows // 8, tile, 0)
    for k in range(count):
        base = (me ^ k) * energies
        for e in range(energies):
            outs[k * energies + e][...] = total[base + e].astype(BF16)


def convolve(pieces, near, start, slabs, size, held, after):
    count = len(pieces)
    _, _, energies, _, rows, columns = pieces[0].shape
    block = (2, 2, energies, None, rows, columns)
    points = count * energies
    part = pl.BlockSpec((None, 2, rows, columns), lambda s: (s, 0, 0, 0))
    whole = pl.BlockSpec((None, 2, rows, columns), lambda s: (s + start, 0, 0, 0))
    later = [index for index in range(points) if index % energies or index // energies in near]
    outs = pl.pallas_call(
        functools.partial(convolve_body, count, energies, len(held)),
        grid=(size,),
        in_specs=[
            pl.BlockSpec(block, lambda s, first=start if x.shape[3] == slabs else 0: (0, 0, 0, s + first, 0, 0))
            for x in pieces
        ]
        + [ANYWHERE] * (1 + len(held)),
        out_specs=[whole if index in later else part for index in range(points)],
        out_shape=[
            jax.ShapeDtypeStruct((slabs if index in later else size, 2, rows, columns), BF16)
            for index in range(points)
        ],
        input_output_aliases={count + 1 + i: later[i] for i in range(len(held))},
        scratch_shapes=[
            pltpu.VMEM((2, points, rows, columns), F32),
            pltpu.VMEM((2, points, rows, columns), F32),
            pltpu.VMEM((points, 2, rows, columns), F32),
        ],
        compiler_params=params(),
        cost_estimate=cost(),
        name="convolve",
    )(*pieces, after, *held)
    return [outs[k * energies : (k + 1) * energies] for k in range(count)], [outs[index] for index in later]


def source_body(owners, *refs):
    pieces = refs[: len(owners)]
    g_ref, k_ref, b_ref, v_ref, sigma, carry = refs[len(owners) :]
    me = lax.axis_index("energy")
    step = pl.program_id(0)
    for piece, (k, first) in zip(pieces, owners):
        size, _, rows, _ = piece.shape

        def place(piece=piece, k=k, first=first, rows=rows):
            start = pl.multiple_of((me ^ k) * rows, rows)
            for part in range(2):
                sigma[part, pl.ds(start, rows), :] = piece[step - first, part]

        pl.when((step >= first) & (step < first + size))(place)

    left = jnp.concatenate([g_ref[0], g_ref[1]], axis=1)
    mixed = dot(left, panel(sigma[0], sigma[1])).astype(BF16)
    source = dot_nt(mixed, panel(g_ref[0], g_ref[1]))

    @pl.when(step == 0)
    def _():
        carry[...] = source

    @pl.when(step > 0)
    def _():
        high, low = panels(k_ref)
        inner = times_wide(high, low, carry[...])
        carry[...] = times_adjoint(inner, high, low) + source

    b_ref[...] = carry[...]

    @pl.when(step == pl.num_programs(0) - 1)
    def _():
        v_ref[...] = carry[...].astype(BF16)


def build_sources(pieces, green, kernels, energy, after):
    slabs, order = green.shape[2:4]
    flat = [piece for group in pieces for piece in group]
    owners = []
    for k, group in enumerate(pieces):
        first = 0
        for piece in group:
            owners.append((k, first))
            first += piece.shape[0]
    return pl.pallas_call(
        ordered(functools.partial(source_body, owners), len(flat) + 2),
        grid=(slabs,),
        in_specs=[pl.BlockSpec(x.shape, lambda s: (0, 0, 0, 0)) for x in flat]
        + [
            pl.BlockSpec((2, None, None, order, order), lambda s: (0, energy, s, 0, 0)),
            pl.BlockSpec((None, None, 2, order, 2 * order), lambda s: (energy, s, 0, 0, 0)),
            ANYWHERE,
        ],
        out_specs=[
            pl.BlockSpec((None, order, 2 * order), lambda s: (s, 0, 0)),
            pl.BlockSpec((order, 2 * order), lambda s: (0, 0)),
        ],
        out_shape=[
            jax.ShapeDtypeStruct((slabs, order, 2 * order), F32),
            jax.ShapeDtypeStruct((order, 2 * order), BF16),
        ],
        scratch_shapes=[
            pltpu.VMEM((2, order, order), BF16),
            pltpu.VMEM((order, 2 * order), F32),
        ],
        compiler_params=params(),
        cost_estimate=cost(),
        name="sources",
    )(*flat, green, kernels, after)


def congruence(t_ref, x):
    order = x.shape[0]
    high, low = panels(t_ref)
    if x.dtype == F32:
        inner = times_wide(high, low, x)
    else:
        inner = times_narrow(high, low, x[:, :order], x[:, order:])
    return times_adjoint(inner, high, low)


def total(refs):
    value = refs[0][...]
    for ref in refs[1:]:
        value = value + ref[...]
    return value


def pair_body(v_ref, own_ref, sum_ref, t_ref, full_ref, short_ref):
    odd = (lax.axis_index("slab") & 1) == 1
    x = jnp.where(odd, v_ref[...], own_ref[...])
    base = jnp.where(odd, sum_ref[...], v_ref[...].astype(F32))
    value = base + congruence(t_ref, x)
    full_ref[...] = value
    short_ref[...] = value.astype(BF16)


def pair_sum(arrived, own, sums, maps, energy, *after):
    slabs, order, _ = sums.shape
    step, step_spec = one_map(maps, energy)
    whole = pl.BlockSpec((order, 2 * order), lambda i: (0, 0))
    return pl.pallas_call(
        ordered(pair_body, 4, len(after)),
        grid=(1,),
        in_specs=[whole, whole, pl.BlockSpec((None, order, 2 * order), lambda i: (slabs - 1, 0, 0)), step_spec]
        + [ANYWHERE] * len(after),
        out_specs=[whole] * 2,
        out_shape=[jax.ShapeDtypeStruct((order, 2 * order), t) for t in (F32, BF16)],
        compiler_params=params(),
        cost_estimate=cost(),
        name="pair_sum",
    )(arrived, own, sums, step, *after)


def combine_body(arrivals, t_ref, base_ref, outs):
    value = congruence(t_ref, total(arrivals)) + base_ref[...].astype(F32)
    for out in outs:
        out[...] = value.astype(out.dtype)


def combine(arrived, maps, base, energy, dtypes, *after):
    order = arrived[0].shape[0]
    if isinstance(base, list):
        base = functools.reduce(jnp.add, base)
    step, step_spec = one_map(maps, energy)
    whole = pl.BlockSpec((order, 2 * order), lambda i: (0, 0))
    count = len(arrived)

    def body(*refs):
        combine_body(refs[:count], refs[count], refs[count + 1], refs[count + 2 + len(after) :])

    return pl.pallas_call(
        body,
        grid=(1,),
        in_specs=[whole] * count + [step_spec, whole] + [ANYWHERE] * len(after),
        out_specs=[whole] * len(dtypes),
        out_shape=[jax.ShapeDtypeStruct((order, 2 * order), t) for t in dtypes],
        compiler_params=params(),
        cost_estimate=cost(),
        name="combine",
    )(*arrived, step, base, *after)


def entry_body(arrivals, t_ref, base_ref, out):
    odd = (lax.axis_index("slab") & 1) == 1
    base = jnp.where(odd, base_ref[...].astype(F32), 0.0)
    out[...] = base + congruence(t_ref, total(arrivals))


def pair_entry(arrived, maps, before, energy, *after):
    order = arrived[0].shape[0]
    step, step_spec = one_map(maps, energy)
    whole = pl.BlockSpec((order, 2 * order), lambda i: (0, 0))
    count = len(arrived)

    def body(*refs):
        entry_body(refs[:count], refs[count], refs[count + 1], refs[-1])

    return pl.pallas_call(
        body,
        grid=(1,),
        in_specs=[whole] * count + [step_spec, whole] + [ANYWHERE] * len(after),
        out_specs=whole,
        out_shape=jax.ShapeDtypeStruct((order, 2 * order), F32),
        compiler_params=params(),
        cost_estimate=cost(),
        name="pair_entry",
    )(*arrived, step, before, *after)


def finish_body(arrivals, q_ref, w_ref, p_ref, b_ref, *rest):
    out, entry = rest[-2:]
    order = entry.shape[0]

    @pl.when(pl.program_id(0) == 0)
    def _():
        value = total(arrivals)
        if q_ref is None:
            entry[...] = value.astype(F32)
        else:
            entry[...] = congruence(q_ref, value) + w_ref[...].astype(F32)

    high, low = panels(p_ref)
    inner = times_wide(high, low, entry[...])
    value = times_adjoint(inner, high, low) + b_ref[...]
    out[0] = value[:, :order]
    out[1] = value[:, order:]


def finish(arrived, gap, entry, prefixes, sums, energy, held, after):
    energies, slabs, _, order, _ = prefixes.shape
    whole = pl.BlockSpec((order, 2 * order), lambda s: (0, 0))
    operands = list(arrived)
    in_specs = [whole] * len(arrived)
    if gap is not None:
        step, step_spec = one_map(gap, energy)
        operands += [step, entry]
        in_specs += [step_spec, whole]
    operands += [prefixes, sums, after]
    in_specs += [
        pl.BlockSpec((None, None, 2, order, 2 * order), lambda s: (energy, s, 0, 0, 0)),
        pl.BlockSpec((None, order, 2 * order), lambda s: (s, 0, 0)),
        ANYWHERE,
    ]
    aliases = {}
    if held is not None:
        aliases = {len(operands): 0}
        operands.append(held)
        in_specs.append(ANYWHERE)

    def body(*refs):
        arrivals, rest = refs[: len(arrived)], refs[len(arrived) :]
        finish_body(arrivals, *((None, None) if gap is None else ()), *rest)

    return pl.pallas_call(
        body,
        grid=(slabs,),
        in_specs=in_specs,
        out_specs=pl.BlockSpec((2, None, None, order, order), lambda s: (0, energy, s, 0, 0)),
        out_shape=jax.ShapeDtypeStruct((2, energies, slabs, order, order), F32),
        input_output_aliases=aliases,
        scratch_shapes=[pltpu.VMEM((order, 2 * order), F32)],
        compiler_params=params(),
        cost_estimate=cost(),
        name="finish",
    )(*operands)


def swap(x, k):
    count = lax.axis_size("energy")
    return lax.ppermute(x, "energy", [(i, i ^ k) for i in range(count)])


def other_of_pair(x):
    return lax.ppermute(x, "slab", [(i, i ^ 1) for i in range(lax.axis_size("slab"))])


def forward(x, by, chosen):
    count = lax.axis_size("slab")
    return lax.ppermute(x, "slab", [(i, i + 2 * by) for i in range(count - 2 * by) if chosen(i // 2)])


def cut(slabs):
    return [(0, slabs - 1), (slabs - 1, 1)] if slabs > 1 else [(0, slabs)]


def per_device(green_lesser, screened_lesser, green_retarded, coupling):
    count = lax.axis_size("energy")
    depth = lax.axis_size("slab")
    if depth % 2 or count & (count - 1):
        raise ValueError("mesh axes")
    _, energies, slabs, order, _ = green_lesser.shape
    far = [k for k in range(count) if k >= 2]
    near = [k for k in range(min(2, count))]
    parts = cut(slabs)

    def first_rows(k, size):
        rows = order // count
        begin = (0, 0, 0, (lax.axis_index("energy") ^ k) * rows, 0)
        sizes = (2, energies, size, rows, order)
        return jnp.stack([lax.dynamic_slice(x, begin, sizes) for x in (green_lesser, screened_lesser)])

    pieces = [[None] * count for _ in parts]
    for k in near[1:]:
        for group in pieces:
            group[k] = swap(first_rows(k, slabs), k) if group is pieces[0] else pieces[0][k]
    for k in far:
        pieces[0][k] = swap(first_rows(k, parts[0][1]), k)
    tokens = [pieces[0][k] for k in near[1:]]
    places = [(chunk, k) for chunk in range(1, len(parts)) for k in far]
    wanted = [(k,) + parts[chunk] for chunk, k in places] + [(0, 0, slabs)]
    packed = pack(green_lesser, screened_lesser, wanted, count, *tokens)
    for (chunk, k), block in zip(places, packed):
        pieces[chunk][k] = swap(block, k)
    for group in pieces:
        group[0] = packed[-1]

    kernels, prefixes = build_maps(green_retarded, coupling, packed[-1])
    token = kernels
    mine = [prefixes[e, slabs - 1] for e in range(energies)]
    other = [other_of_pair(x) for x in mine]

    sigma = [[[] for _ in range(count)] for _ in range(energies)]
    held = []
    for chunk, (start, size) in enumerate(parts):
        if chunk == len(parts) - 1:
            pair_step, plane, inner = pair_maps(mine, other, energies, token)
            token = plane
        blocks, held = convolve(pieces[chunk], near, start, slabs, size, held, token)
        token = blocks[0][0]
        for k in far:
            sigma[0][k].append(swap(blocks[k][0], k))
    for e in range(energies):
        for k in near + far:
            if e > 0 or k in near:
                sigma[e][k].append(swap(blocks[k][e], k) if k else blocks[k][e])

    steps = (depth // 2 - 1).bit_length()
    step_maps, gap_maps = [plane], [None]

    def extend(k, token):
        least = 1 << k if k == steps - 2 else 0
        arrived = forward(step_maps[k], 1 << k, lambda pair: pair >= least)
        if k < steps - 2:
            token = map_product(step_maps[k], arrived, energies, token)
            step_maps.append(token)
        if gap_maps[k] is None:
            gap_maps.append(arrived)
        else:
            token = map_product(gap_maps[k], arrived, energies, token)
            gap_maps.append(token)
        return token

    for k in range(steps - 2):
        token = extend(k, token)
    nothing = jnp.zeros((order, 2 * order), BF16)
    sums, own, before = [None] * energies, [None] * energies, [None] * energies
    running, carry = [None] * energies, [None] * energies
    entry, arrived = [[nothing]] * energies, [None] * energies
    final = [[] for _ in range(energies)]

    def send(e, k):
        if k < steps - 1:
            arrived[e] = [
                forward(carry[e], 1 << k, lambda pair, bit=bit: (pair >> k) & 1 == bit) for bit in range(2)
            ]
        if steps > 0:
            final[e].append(forward(carry[e], 1 << (steps - 1), lambda pair: pair.bit_length() == k))

    for e in range(energies):
        sums[e], own[e] = build_sources(sigma[e], green_retarded, kernels, e, token)
        token = own[e]
        before[e] = other_of_pair(own[e])
    for e in range(energies):
        running[e], carry[e] = pair_sum(before[e], own[e], sums[e], pair_step, e, token)
        token = carry[e]
        send(e, 0)
    gap = inner
    for k in range(steps - 1):
        if k == steps - 2:
            token = extend(k, token)
            gap = token = map_product(inner, gap_maps[-1], energies, token)
        for e in range(energies):
            last = k == steps - 2
            made = combine(
                arrived[e][:1] if last else arrived[e],
                step_maps[k],
                running[e],
                e,
                (BF16,) if last else (F32, BF16),
                token,
                final[e][k],
            )
            token = carry[e] = made[-1]
            got, running[e] = arrived[e], made[0]
            send(e, k + 1)
            if k == 0:
                entry[e] = got
            else:
                entry[e] = list(combine(got, gap_maps[k], entry[e], e, (F32,), token))
                token = entry[e][0]
    for e in range(energies):
        entry[e] = token = pair_entry(entry[e], inner, before[e], e, token)
    result = None
    for e in range(energies):
        result = finish(final[e] or [nothing], gap, entry[e], prefixes, sums[e], e, result, token)
    return result


def solution(mesh):
    placed = (
        P(None, "energy", "slab", None, None),
        P(None, "energy", "slab", None, None),
        P(None, "energy", "slab", None, None),
        P(None, "slab", None, None),
    )
    return jax.shard_map(
        per_device,
        mesh=mesh,
        in_specs=placed,
        out_specs=P(None, "energy", "slab", None, None),
        check_vma=False,
    )
```

time: 159 us -> 134 us (0.84)
  waiting for transfers between devices: 74.4 us -> 59 us
  Pallas kernels: 54.2 us -> 43.9 us
    pallas_call x18 -> x16, Pallas kernels: 54.2 us -> 43.9 us  [the longest x2 12.1 us: finish(): pl.pallas_call(body, grid=(slabs,), in_specs=in_specs, out_specs=pl.Block...]
    ppermute x8 -> x13, waiting for transfers between devices: 34 us -> 24.9 us  [the longest x9 20.2 us: forward(): lax.ppermute(x, 'slab', [(i, i + 2 * by) for i in range(count - 2 * by) i...]
    ppermute x12 -> x13, waiting for transfers between devices: 40.4 us -> 34.1 us  [swap(): return lax.ppermute(x, 'energy', [(i, i ^ k) for i in range(count)])]
    ppermute x8 -> x13, starting transfers between devices: 16.8 us -> 14.6 us  [the longest x9 9.35 us: forward(): lax.ppermute(x, 'slab', [(i, i + 2 * by) for i in range(count - 2 * by) i...]
    ppermute x12 -> x13, starting transfers between devices: 8.99 us -> 10.6 us  [swap(): return lax.ppermute(x, 'energy', [(i, i ^ k) for i in range(count)])]
  transfers between devices with their start and end apart: 20 -> 26, of which waited for: 11 -> 10; matrix products, arithmetic and copies ran while one was open for 0% -> 1% of each run, Pallas kernels for 31% -> 28%
where the time goes in v2:
time: 134 us; the launch traced here: 133 us
  waiting for transfers between devices  59 us (44%)
  Pallas kernels  43.9 us (33%)
  starting transfers between devices  25.1 us (19%)
  local copies, waits for them, and re-layouts  3.87 us (3%)
    ppermute x13, waiting for transfers between devices, swap(): return lax.ppermute(x, 'energy', [(i, i ^ k) for i in range(count)])  34.1 us
    ppermute x9, waiting for transfers between devices, forward(): lax.ppermute(x, 'slab', [(i, i + 2 * by) for i in range(count - 2 * by) i...  20.2 us
    pallas_call x2, Pallas kernels, finish(): pl.pallas_call(body, grid=(slabs,), in_specs=in_specs, out_specs=pl.Block...  12.1 us
    pallas_call x2, Pallas kernels, build_sources(): pl.pallas_call(ordered(functools.partial(source_body, owners), len(flat)...  11.4 us
    ppermute x13, starting transfers between devices, swap(): return lax.ppermute(x, 'energy', [(i, i ^ k) for i in range(count)])  10.6 us
    ppermute x9, starting transfers between devices, forward(): lax.ppermute(x, 'slab', [(i, i + 2 * by) for i in range(count - 2 * by) i...  9.35 us
    pallas_call x1, Pallas kernels, build_maps(): pl.pallas_call(lambda *refs: maps_body(*refs[:2], *refs[2 + len(after):])...  7.16 us
    ppermute x4, starting transfers between devices, other_of_pair(): lax.ppermute(x, 'slab', [(i, i ^ 1) for i in range(lax.axis_size('slab'))])  5.2 us
  transfers between devices with their start and end apart: 26, of which 10 were waited for; matrix products, arithmetic and copies ran while one was open for 1% of the time, Pallas kernels for 28%

profile of v2, /device:TPU:24, one launch (start us, length us, event | category | flops | bytes accessed | tf_op | source)
XLA Modules:
  0.0 133.4 jit_solution(15964205057826141564)
XLA Ops:
  0.0 1.4 %dynamic-slice_bitcast_fusion = (bf16[1,2,2,4,64,256]{5,4,3,2,1,0:T(8,128)(2,1)S(1)}, bf16[1,2,2,4,64,256]{5,4,3,2,1,0:T(8,128)(2,1)S(1)}) fusion(bf16[2,2,4,256,256]{4,3,2,1,0:T(8,128)(2,1)} %refs_1_.2, s32[]{:T(128)S(6)} %select_n.12, bf16[2,2,4,256,256]{4,3,2,1,0:T(8,128)(2,1)} %refs_0_.2), kind=kLoop, calls=%fused_computation.5 | loop fusion | bytes 2097156 | tf_op jit(solution)/shard_map/stack | solution.py:554
  1.4 1.1 pad_maximum_fusion
  2.5 1.2 dynamic-slice_bitcast_fusion.2
  3.7 0.0 copy-start.2
  3.8 0.1 pad_maximum_fusion.1
  3.8 1.6 %collective-permute-start.5 = (bf16[2,2,2,3,64,256]{5,4,3,2,1,0:T(8,128)(2,1)S(1)}, bf16[2,2,2,3,64,256]{5,4,3,2,1,0:T(8,128)(2,1)S(1)}, u32[]{:S(2)}, u32[]{:S(2)}) collective-permute-start(bf16[2,2,2,3,64,256]{5,4,3,2,1,0:T(8,128)(2,1)S(1)} %pad_maximum_fusion.1), channel_id=1, source_target_pairs={{0,2},{1,3},{2,0},{3,1},{4,6},{5,7},{6,4},{7,5},{8,10},{9,11},{10,... | collective-permute-start | bytes 2359304 | tf_op jit(solution)/shard_map/ppermute | solution.py:524
  5.4 0.1 pad_maximum_fusion.2
  5.5 0.0 copy-start
  5.5 0.0 copy-start.3
  5.5 0.4 collective-permute-start.6
  5.9 0.0 collective-permute-done.refs_2_.refs_1_
  5.9 0.3 pack.1
  6.2 0.9 copy-done
  7.1 0.3 copy-done.3
  7.4 7.2 %maps.1 = (bf16[2,4,2,256,512]{4,3,2,1,0:T(8,128)(2,1)S(1)}, bf16[2,4,2,256,512]{4,3,2,1,0:T(8,128)(2,1)S(1)}) custom-call(bf16[2,2,4,256,256]{4,3,2,1,0:T(8,128)(2,1)S(1)} %copy-done, bf16[2,4,256,256]{3,2,1,0:T(8,128)(2,1)S(1)} %copy-done.3, bf16[2,2,2,4,64,256]{5,4,3,2,1,0:T(8,128)(2,1)S(1)} %get-tuple-element.37.refs_2_.refs_0_), custom_call_target="tpu_custom_call" | custom-call | tf_op jit(solution)/shard_map/maps/pallas_call | solution.py:138
  14.5 0.1 slice_bitcast_fusion
  14.6 1.6 %collective-permute-start.3 = (bf16[2,256,512]{2,1,0:T(8,128)(2,1)S(1)}, bf16[2,256,512]{2,1,0:T(8,128)(2,1)S(1)}, u32[]{:S(2)}, u32[]{:S(2)}) collective-permute-start(bf16[2,256,512]{2,1,0:T(8,128)(2,1)S(1)} %get-tuple-element.70.refs_0_), channel_id=1, source_target_pairs={{0,4},{4,0},{8,12},{12,8},{16,20},{20,16},{24,28},{28,24},{1,5},{5... | collective-permute-start | bytes 1572872 | tf_op jit(solution)/shard_map/ppermute | solution.py:528
  16.2 0.5 collective-permute-start.4
  16.7 0.7 collective-permute-start.1
  17.4 6.9 %collective-permute-done.5.refs_2_ = bf16[2,2,2,3,64,256]{5,4,3,2,1,0:T(8,128)(2,1)S(1)} collective-permute-done((bf16[2,2,2,3,64,256]{5,4,3,2,1,0:T(8,128)(2,1)S(1)}, bf16[2,2,2,3,64,256]{5,4,3,2,1,0:T(8,128)(2,1)S(1)}, u32[]{:S(2)}, u32[]{:S(2)}) %collective-permute-start.5) | collective-permute-done | bytes 786464 | tf_op jit(solution)/shard_map/ppermute | solution.py:524
  24.2 0.5 collective-permute-start.2
  24.7 15.6 %collective-permute-done.6.refs_3_ = bf16[2,2,2,3,64,256]{5,4,3,2,1,0:T(8,128)(2,1)S(1)} collective-permute-done((bf16[2,2,2,3,64,256]{5,4,3,2,1,0:T(8,128)(2,1)S(1)}, bf16[2,2,2,3,64,256]{5,4,3,2,1,0:T(8,128)(2,1)S(1)}, u32[]{:S(2)}, u32[]{:S(2)}) %collective-permute-start.6) | collective-permute-done | bytes 786464 | tf_op jit(solution)/shard_map/ppermute | solution.py:524
  40.3 3.7 %convolve.2 = (bf16[4,2,64,256]{3,2,1,0:T(8,128)(2,1)S(1)}, bf16[4,2,64,256]{3,2,1,0:T(8,128)(2,1)S(1)}, bf16[4,2,64,256]{3,2,1,0:T(8,128)(2,1)S(1)}, bf16[4,2,6...) custom-call(bf16[2,2,2,4,64,256]{5,4,3,2,1,0:T(8,128)(2,1)S(1)} %get, ...), custom_call_target="tpu_custom_call" | custom-call | tf_op jit(solution)/shard_map/convolve/pallas_call | solution.py:267
  44.0 1.5 %pair_maps.1 = (bf16[2,2,256,512]{3,2,1,0:T(8,128)(2,1)S(1)}, bf16[2,2,256,512]{3,2,1,0:T(8,128)(2,1)S(1)}, bf16[2,2,256,512]{3,2,1,0:T(8,128)(2,1)S(1)}) custom-call(bf16[2,256,512]{2,1,0:T(8,128)(2,1)S(1)} %get-tuple-element.70.refs_0_, bf16[2,256,512]{2,1,0:T(8,128)(2,1)S(1)} %collective-permute-done.3.refs_1_, ...), custom_call_target="tpu_custom_call" | custom-call | tf_op jit(solution)/shard_map/pair_maps/pallas_call | solution.py:205
  45.6 1.3 collective-permute-start.20
  46.9 1.6 %collective-permute-start.11 = (bf16[3,2,64,256]{3,2,1,0:T(8,128)(2,1)S(1)}, bf16[3,2,64,256]{3,2,1,0:T(8,128)(2,1)S(1)}, u32[]{:S(2)}, u32[]{:S(2)}) collective-permute-start(bf16[3,2,64,256]{3,2,1,0:T(8,128)(2,1)S(1)} %get-tuple-element.55), channel_id=1, source_target_pairs={{0,2},{1,3},{2,0},{3,1},{4,6},{5,7},{6,4},{7,5},{8,10},{9,11},{10,... | collective-permute-start | bytes 589832 | tf_op jit(solution)/shard_map/ppermute | solution.py:524
  48.4 0.4 collective-permute-start.13
  48.9 2.7 %collective-permute-done.2.refs_3_ = bf16[2,2,2,1,64,256]{5,4,3,2,1,0:T(8,128)(2,1)S(1)} collective-permute-done((bf16[2,2,2,1,64,256]{5,4,3,2,1,0:T(8,128)(2,1)S(1)}, bf16[2,2,2,1,64,256]{5,4,3,2,1,0:T(8,128)(2,1)S(1)}, u32[]{:S(2)}, u32[]{:S(2)}) %collective-permute-start.2) | collective-permute-done | bytes 262176 | tf_op jit(solution)/shard_map/ppermute | solution.py:524
  51.6 1.1 convolve.3
  52.7 1.6 %collective-permute-start.12 = (bf16[1,2,64,256]{3,2,1,0:T(8,128)(2,1)S(1)}, bf16[1,2,64,256]{3,2,1,0:T(8,128)(2,1)S(1)}, u32[]{:S(2)}, u32[]{:S(2)}) collective-permute-start(bf16[1,2,64,256]{3,2,1,0:T(8,128)(2,1)S(1)} %get-tuple-element.56), channel_id=1, source_target_pairs={{0,2},{1,3},{2,0},{3,1},{4,6},{5,7},{6,4},{7,5},{8,10},{9,11},{10,... | collective-permute-start | bytes 196616 | tf_op jit(solution)/shard_map/ppermute | solution.py:524
  54.3 0.7 collective-permute-start.14
  55.0 1.5 %collective-permute-done.11.refs_2_ = bf16[3,2,64,256]{3,2,1,0:T(8,128)(2,1)S(1)} collective-permute-done((bf16[3,2,64,256]{3,2,1,0:T(8,128)(2,1)S(1)}, bf16[3,2,64,256]{3,2,1,0:T(8,128)(2,1)S(1)}, u32[]{:S(2)}, u32[]{:S(2)}) %collective-permute-start.11) | collective-permute-done | bytes 196640 | tf_op jit(solution)/shard_map/ppermute | solution.py:524
  56.5 0.0 collective-permute-start.10
  56.5 3.4 %collective-permute-done.13.refs_4_ = bf16[3,2,64,256]{3,2,1,0:T(8,128)(2,1)S(1)} collective-permute-done((bf16[3,2,64,256]{3,2,1,0:T(8,128)(2,1)S(1)}, bf16[3,2,64,256]{3,2,1,0:T(8,128)(2,1)S(1)}, u32[]{:S(2)}, u32[]{:S(2)}) %collective-permute-start.13) | collective-permute-done | bytes 196640 | tf_op jit(solution)/shard_map/ppermute | solution.py:524
  60.0 0.9 collective-permute-start.7
  60.9 1.3 collective-permute-done.12.refs_3_
  62.2 1.5 %collective-permute-start.8 = (bf16[4,2,64,256]{3,2,1,0:T(8,128)(2,1)S(1)}, bf16[4,2,64,256]{3,2,1,0:T(8,128)(2,1)S(1)}, u32[]{:S(2)}, u32[]{:S(2)}) collective-permute-start(bf16[4,2,64,256]{3,2,1,0:T(8,128)(2,1)S(1)} %get-tuple-element.51), channel_id=1, source_target_pairs={{0,2},{1,3},{2,0},{3,1},{4,6},{5,7},{6,4},{7,5},{8,10},{9,11},{10,... | collective-permute-start | bytes 786440 | tf_op jit(solution)/shard_map/ppermute | solution.py:524
  63.7 0.0 collective-permute-done.14.refs_5_
  63.7 0.7 collective-permute-start.9
  64.4 5.7 %sources.2 = (f32[4,256,512]{2,1,0:T(8,128)S(1)}, bf16[256,512]{1,0:T(8,128)(2,1)S(1)}) custom-call(bf16[4,2,64,256]{3,2,1,0:T(8,128)(2,1)S(1)} %get-tuple-element.53.refs_0_.refs_8_, bf16[4,2,64,256]{3,2,1,0:T(8,128)(2,1)S(1)} %collective-permute-done.10.refs_1_, bf16[3,2,64,256]{3,2,1,0:T(8,128)(2,1)S(1)} %collective-permute-done.11.refs_2_, ...), custom_call_target="tpu_custom_call" | custom-call | tf_op jit(solution)/shard_map/sources/pallas_call | solution.py:338
  70.2 1.6 %collective-permute-start.16 = (bf16[256,512]{1,0:T(8,128)(2,1)S(1)}, bf16[256,512]{1,0:T(8,128)(2,1)S(1)}, u32[]{:S(2)}, u32[]{:S(2)}) collective-permute-start(bf16[256,512]{1,0:T(8,128)(2,1)S(1)} %get-tuple-element.59.refs_6_.refs_1_), channel_id=1, source_target_pairs={{0,4},{4,0},{8,12},{12,8},{16,20},{20,16},{24,28},{28,24},{1,5},{5... | collective-permute-start | bytes 786440 | tf_op jit(solution)/shard_map/ppermute | solution.py:528
  71.7 2.6 %collective-permute-done.9.refs_3_ = bf16[4,2,64,256]{3,2,1,0:T(8,128)(2,1)S(1)} collective-permute-done((bf16[4,2,64,256]{3,2,1,0:T(8,128)(2,1)S(1)}, bf16[4,2,64,256]{3,2,1,0:T(8,128)(2,1)S(1)}, u32[]{:S(2)}, u32[]{:S(2)}) %collective-permute-start.9) | collective-permute-done | bytes 262176 | tf_op jit(solution)/shard_map/ppermute | solution.py:524
  74.4 5.7 %sources.3 = (f32[4,256,512]{2,1,0:T(8,128)S(1)}, bf16[256,512]{1,0:T(8,128)(2,1)S(1)}) custom-call(bf16[4,2,64,256]{3,2,1,0:T(8,128)(2,1)S(1)} %get-tuple-element.49.refs_0_, bf16[4,2,64,256]{3,2,1,0:T(8,128)(2,1)S(1)} %collective-permute-done.7.refs_1_, bf16[4,2,64,256]{3,2,1,0:T(8,128)(2,1)S(1)} %collective-permute-done.8.refs_2_, ...), custom_call_target="tpu_custom_call" | custom-call | tf_op jit(solution)/shard_map/sources/pallas_call | solution.py:338
  80.1 1.6 %collective-permute-start.15 = (bf16[256,512]{1,0:T(8,128)(2,1)S(1)}, bf16[256,512]{1,0:T(8,128)(2,1)S(1)}, u32[]{:S(2)}, u32[]{:S(2)}) collective-permute-start(bf16[256,512]{1,0:T(8,128)(2,1)S(1)} %get-tuple-element.60.refs_4_.refs_1_), channel_id=1, source_target_pairs={{0,4},{4,0},{8,12},{12,8},{16,20},{20,16},{24,28},{28,24},{1,5},{5... | collective-permute-start | bytes 786440 | tf_op jit(solution)/shard_map/ppermute | solution.py:528
  81.6 0.9 pair_sum.2
  82.6 1.3 collective-permute-start.19
  83.9 0.7 collective-permute-start.21
  84.6 4.7 %collective-permute-done.15.refs_0_.refs_3_ = bf16[256,512]{1,0:T(8,128)(2,1)S(1)} collective-permute-done((bf16[256,512]{1,0:T(8,128)(2,1)S(1)}, bf16[256,512]{1,0:T(8,128)(2,1)S(1)}, u32[]{:S(2)}, u32[]{:S(2)}) %collective-permute-start.15) | collective-permute-done | bytes 262176 | tf_op jit(solution)/shard_map/ppermute | solution.py:528
  89.2 0.9 pair_sum.3
  90.1 0.7 collective-permute-start.17
  90.8 1.3 collective-permute-start.18
  92.1 0.7 collective-permute-start.23
  92.8 1.0 map_product.1.refs_3_.refs_2_
  93.9 0.7 collective-permute-start.24
  94.6 0.9 combine.2.refs_3_
  95.5 1.3 collective-permute-start.25
  96.8 4.3 %collective-permute-done.18.refs_0_ = bf16[256,512]{1,0:T(8,128)(2,1)S(1)} collective-permute-done((bf16[256,512]{1,0:T(8,128)(2,1)S(1)}, bf16[256,512]{1,0:T(8,128)(2,1)S(1)}, u32[]{:S(2)}, u32[]{:S(2)}) %collective-permute-start.18) | collective-permute-done | bytes 262176 | tf_op jit(solution)/shard_map/ppermute | solution.py:533
  101.2 0.9 combine.3.refs_4_
  102.1 1.5 %collective-permute-start.22 = (bf16[256,512]{1,0:T(8,128)(2,1)S(1)}, bf16[256,512]{1,0:T(8,128)(2,1)S(1)}, u32[]{:S(2)}, u32[]{:S(2)}) collective-permute-start(bf16[256,512]{1,0:T(8,128)(2,1)S(1)} %combine.3.refs_4_), channel_id=1, source_target_pairs={{8,24},{12,28},{9,25},{13,29},{10,26},{14,30},{11,27},{15,31}} | collective-permute-start | bytes 786440 | tf_op jit(solution)/shard_map/ppermute | solution.py:533
  103.6 0.9 pair_entry.2.refs_4_.refs_3_
  104.5 0.9 pair_entry.3.refs_6_.refs_3_
  105.5 15.9 %collective-permute-done.25.refs_1_ = bf16[256,512]{1,0:T(8,128)(2,1)S(1)} collective-permute-done((bf16[256,512]{1,0:T(8,128)(2,1)S(1)}, bf16[256,512]{1,0:T(8,128)(2,1)S(1)}, u32[]{:S(2)}, u32[]{:S(2)}) %collective-permute-start.25) | collective-permute-done | bytes 262176 | tf_op jit(solution)/shard_map/ppermute | solution.py:533
  121.3 6.0 %finish.2.refs_7_ = f32[2,2,4,256,256]{4,3,2,1,0:T(8,128)} custom-call(bf16[256,512]{1,0:T(8,128)(2,1)S(1)} %collective-permute-done.21.refs_4_.refs_0_, bf16[256,512]{1,0:T(8,128)(2,1)S(1)} %collective-permute-done.25.refs_1_, bf16[2,2,256,512]{3,2,1,0:T(8,128)(2,1)S(1)} %map_product.1.refs_3_.refs_2_, f32[256,512]{1,0:T(8,128)S(1)} %pair_entry.2.refs_4_.refs_3_, ...), custom_call_target="tpu_custom_call" | custom-call | tf_op jit(solution)/shard_map/finish/pallas_call | solution.py:508
  127.4 6.1 %finish.3 = f32[2,2,4,256,256]{4,3,2,1,0:T(8,128)} custom-call(bf16[256,512]{1,0:T(8,128)(2,1)S(1)} %collective-permute-done.17.refs_4_.refs_0_, bf16[256,512]{1,0:T(8,128)(2,1)S(1)} %collective-permute-done.22.refs_1_, bf16[2,2,256,512]{3,2,1,0:T(8,128)(2,1)S(1)} %map_product.1.refs_3_.refs_2_, ...), custom_call_target="tpu_custom_call", output_to_operand_aliasing={{}: (7, {})} | custom-call | tf_op jit(solution)/shard_map/finish/pallas_call | solution.py:508
  (18 shorter events, 0.0 us)
Async XLA Ops:
  0.0 2.5 %copy-start.1 = (bf16[2,2,4,256,256]{4,3,2,1,0:T(8,128)(2,1)S(1)}, bf16[2,2,4,256,256]{4,3,2,1,0:T(8,128)(2,1)}, u32[]{:S(2)}) copy-start(bf16[2,2,4,256,256]{4,3,2,1,0:T(8,128)(2,1)} %refs_0_.2) | copy-start | bytes 6291460
  2.5 3.4 %collective-permute-start = (bf16[2,2,2,4,64,256]{5,4,3,2,1,0:T(8,128)(2,1)}, bf16[2,2,2,4,64,256]{5,4,3,2,1,0:T(8,128)(2,1)S(1)}, u32[]{:S(2)}, u32[]{:S(2)}) collective-permute-start(bf16[2,2,2,4,64,256]{5,4,3,2,1,0:T(8,128)(2,1)} %pad_maximum_fusion), channel_id=1, source_target_pairs={{0,1},{1,0},{2,3},{3,2},{4,5},{5,4},{6,7},{7,6},{8,9},{9,8},{10,11... | collective-permute-start | bytes 3145736 | tf_op jit(solution)/shard_map/ppermute | solution.py:524
  3.7 2.2 %copy-start.2 = (bf16[2,2,4,256,256]{4,3,2,1,0:T(8,128)(2,1)S(1)}, bf16[2,2,4,256,256]{4,3,2,1,0:T(8,128)(2,1)}, u32[]{:S(2)}) copy-start(bf16[2,2,4,256,256]{4,3,2,1,0:T(8,128)(2,1)} %refs_1_.2) | copy-start | bytes 6291460
  3.8 20.4 %collective-permute-start.5 = (bf16[2,2,2,3,64,256]{5,4,3,2,1,0:T(8,128)(2,1)S(1)}, bf16[2,2,2,3,64,256]{5,4,3,2,1,0:T(8,128)(2,1)S(1)}, u32[]{:S(2)}, u32[]{:S(2)}) collective-permute-start(bf16[2,2,2,3,64,256]{5,4,3,2,1,0:T(8,128)(2,1)S(1)} %pad_maximum_fusion.1), channel_id=1, source_target_pairs={{0,2},{1,3},{2,0},{3,1},{4,6},{5,7},{6,4},{7,5},{8,10},{9,11},{10,... | collective-permute-start | bytes 2359304 | tf_op jit(solution)/shard_map/ppermute | solution.py:524
  5.5 1.6 %copy-start = (bf16[2,2,4,256,256]{4,3,2,1,0:T(8,128)(2,1)S(1)}, bf16[2,2,4,256,256]{4,3,2,1,0:T(8,128)(2,1)}, u32[]{:S(2)}) copy-start(bf16[2,2,4,256,256]{4,3,2,1,0:T(8,128)(2,1)} %refs_4_.1) | copy-start | bytes 6291460
  5.5 1.8 %copy-start.3 = (bf16[2,4,256,256]{3,2,1,0:T(8,128)(2,1)S(1)}, bf16[2,4,256,256]{3,2,1,0:T(8,128)(2,1)}, u32[]{:S(2)}) copy-start(bf16[2,4,256,256]{3,2,1,0:T(8,128)(2,1)} %refs_1_.3) | copy-start | bytes 3145732
  5.5 34.8 %collective-permute-start.6 = (bf16[2,2,2,3,64,256]{5,4,3,2,1,0:T(8,128)(2,1)S(1)}, bf16[2,2,2,3,64,256]{5,4,3,2,1,0:T(8,128)(2,1)S(1)}, u32[]{:S(2)}, u32[]{:S(2)}) collective-permute-start(bf16[2,2,2,3,64,256]{5,4,3,2,1,0:T(8,128)(2,1)S(1)} %pad_maximum_fusion.2), channel_id=1, source_target_pairs={{0,3},{1,2},{2,1},{3,0},{4,7},{5,6},{6,5},{7,4},{8,11},{9,10},{10,... | collective-permute-start | bytes 2359304 | tf_op jit(solution)/shard_map/ppermute | solution.py:524
  14.6 29.4 %collective-permute-start.3 = (bf16[2,256,512]{2,1,0:T(8,128)(2,1)S(1)}, bf16[2,256,512]{2,1,0:T(8,128)(2,1)S(1)}, u32[]{:S(2)}, u32[]{:S(2)}) collective-permute-start(bf16[2,256,512]{2,1,0:T(8,128)(2,1)S(1)} %get-tuple-element.70.refs_0_), channel_id=1, source_target_pairs={{0,4},{4,0},{8,12},{12,8},{16,20},{20,16},{24,28},{28,24},{1,5},{5... | collective-permute-start | bytes 1572872 | tf_op jit(solution)/shard_map/ppermute | solution.py:528
  16.2 27.9 %collective-permute-start.4 = (bf16[2,256,512]{2,1,0:T(8,128)(2,1)S(1)}, bf16[2,256,512]{2,1,0:T(8,128)(2,1)S(1)}, u32[]{:S(2)}, u32[]{:S(2)}) collective-permute-start(bf16[2,256,512]{2,1,0:T(8,128)(2,1)S(1)} %get-tuple-element.69.refs_2_), channel_id=1, source_target_pairs={{0,4},{4,0},{8,12},{12,8},{16,20},{20,16},{24,28},{28,24},{1,5},{5... | collective-permute-start | bytes 1572872 | tf_op jit(solution)/shard_map/ppermute | solution.py:528
  16.7 32.2 %collective-permute-start.1 = (bf16[2,2,2,1,64,256]{5,4,3,2,1,0:T(8,128)(2,1)S(1)}, bf16[2,2,2,1,64,256]{5,4,3,2,1,0:T(8,128)(2,1)S(1)}, u32[]{:S(2)}, u32[]{:S(2)}) collective-permute-start(bf16[2,2,2,1,64,256]{5,4,3,2,1,0:T(8,128)(2,1)S(1)} %get-tuple-element.38), channel_id=1, source_target_pairs={{0,2},{1,3},{2,0},{3,1},{4,6},{5,7},{6,4},{7,5},{8,10},{9,11},{10,... | collective-permute-start | bytes 786440 | tf_op jit(solution)/shard_map/ppermute | solution.py:524
  24.2 27.3 %collective-permute-start.2 = (bf16[2,2,2,1,64,256]{5,4,3,2,1,0:T(8,128)(2,1)S(1)}, bf16[2,2,2,1,64,256]{5,4,3,2,1,0:T(8,128)(2,1)S(1)}, u32[]{:S(2)}, u32[]{:S(2)}) collective-permute-start(bf16[2,2,2,1,64,256]{5,4,3,2,1,0:T(8,128)(2,1)S(1)} %get-tuple-element.39), channel_id=1, source_target_pairs={{0,3},{1,2},{2,1},{3,0},{4,7},{5,6},{6,5},{7,4},{8,11},{9,10},{10,... | collective-permute-start | bytes 786440 | tf_op jit(solution)/shard_map/ppermute | solution.py:524
  45.6 46.6 %collective-permute-start.20 = (bf16[2,2,256,512]{3,2,1,0:T(8,128)(2,1)S(1)}, bf16[2,2,256,512]{3,2,1,0:T(8,128)(2,1)S(1)}, u32[]{:S(2)}, u32[]{:S(2)}) collective-permute-start(bf16[2,2,256,512]{3,2,1,0:T(8,128)(2,1)S(1)} %get-tuple-element.43.refs_4_.refs_1_), channel_id=1, source_target_pairs={{8,16},{12,20},{16,24},{20,28},{9,17},{13,21},{17,25},{21,29},{10,... | collective-permute-start | bytes 3145736 | tf_op jit(solution)/shard_map/ppermute | solution.py:533
  46.9 9.7 %collective-permute-start.11 = (bf16[3,2,64,256]{3,2,1,0:T(8,128)(2,1)S(1)}, bf16[3,2,64,256]{3,2,1,0:T(8,128)(2,1)S(1)}, u32[]{:S(2)}, u32[]{:S(2)}) collective-permute-start(bf16[3,2,64,256]{3,2,1,0:T(8,128)(2,1)S(1)} %get-tuple-element.55), channel_id=1, source_target_pairs={{0,2},{1,3},{2,0},{3,1},{4,6},{5,7},{6,4},{7,5},{8,10},{9,11},{10,... | collective-permute-start | bytes 589832 | tf_op jit(solution)/shard_map/ppermute | solution.py:524
  48.4 11.5 %collective-permute-start.13 = (bf16[3,2,64,256]{3,2,1,0:T(8,128)(2,1)S(1)}, bf16[3,2,64,256]{3,2,1,0:T(8,128)(2,1)S(1)}, u32[]{:S(2)}, u32[]{:S(2)}) collective-permute-start(bf16[3,2,64,256]{3,2,1,0:T(8,128)(2,1)S(1)} %get-tuple-element.57), channel_id=1, source_target_pairs={{0,3},{1,2},{2,1},{3,0},{4,7},{5,6},{6,5},{7,4},{8,11},{9,10},{10,... | collective-permute-start | bytes 589832 | tf_op jit(solution)/shard_map/ppermute | solution.py:524
  52.7 9.5 %collective-permute-start.12 = (bf16[1,2,64,256]{3,2,1,0:T(8,128)(2,1)S(1)}, bf16[1,2,64,256]{3,2,1,0:T(8,128)(2,1)S(1)}, u32[]{:S(2)}, u32[]{:S(2)}) collective-permute-start(bf16[1,2,64,256]{3,2,1,0:T(8,128)(2,1)S(1)} %get-tuple-element.56), channel_id=1, source_target_pairs={{0,2},{1,3},{2,0},{3,1},{4,6},{5,7},{6,4},{7,5},{8,10},{9,11},{10,... | collective-permute-start | bytes 196616 | tf_op jit(solution)/shard_map/ppermute | solution.py:524
  54.3 9.4 %collective-permute-start.14 = (bf16[1,2,64,256]{3,2,1,0:T(8,128)(2,1)S(1)}, bf16[1,2,64,256]{3,2,1,0:T(8,128)(2,1)S(1)}, u32[]{:S(2)}, u32[]{:S(2)}) collective-permute-start(bf16[1,2,64,256]{3,2,1,0:T(8,128)(2,1)S(1)} %get-tuple-element.58), channel_id=1, source_target_pairs={{0,3},{1,2},{2,1},{3,0},{4,7},{5,6},{6,5},{7,4},{8,11},{9,10},{10,... | collective-permute-start | bytes 196616 | tf_op jit(solution)/shard_map/ppermute | solution.py:524
  56.5 7.9 %collective-permute-start.10 = (bf16[4,2,64,256]{3,2,1,0:T(8,128)(2,1)S(1)}, bf16[4,2,64,256]{3,2,1,0:T(8,128)(2,1)S(1)}, u32[]{:S(2)}, u32[]{:S(2)}) collective-permute-start(bf16[4,2,64,256]{3,2,1,0:T(8,128)(2,1)S(1)} %get-tuple-element.54), channel_id=1, source_target_pairs={{0,1},{1,0},{2,3},{3,2},{4,5},{5,4},{6,7},{7,6},{8,9},{9,8},{10,11... | collective-permute-start | bytes 786440 | tf_op jit(solution)/shard_map/ppermute | solution.py:524
  60.0 11.7 %collective-permute-start.7 = (bf16[4,2,64,256]{3,2,1,0:T(8,128)(2,1)S(1)}, bf16[4,2,64,256]{3,2,1,0:T(8,128)(2,1)S(1)}, u32[]{:S(2)}, u32[]{:S(2)}) collective-permute-start(bf16[4,2,64,256]{3,2,1,0:T(8,128)(2,1)S(1)} %get-tuple-element.50), channel_id=1, source_target_pairs={{0,1},{1,0},{2,3},{3,2},{4,5},{5,4},{6,7},{7,6},{8,9},{9,8},{10,11... | collective-permute-start | bytes 786440 | tf_op jit(solution)/shard_map/ppermute | solution.py:524
  62.2 9.6 %collective-permute-start.8 = (bf16[4,2,64,256]{3,2,1,0:T(8,128)(2,1)S(1)}, bf16[4,2,64,256]{3,2,1,0:T(8,128)(2,1)S(1)}, u32[]{:S(2)}, u32[]{:S(2)}) collective-permute-start(bf16[4,2,64,256]{3,2,1,0:T(8,128)(2,1)S(1)} %get-tuple-element.51), channel_id=1, source_target_pairs={{0,2},{1,3},{2,0},{3,1},{4,6},{5,7},{6,4},{7,5},{8,10},{9,11},{10,... | collective-permute-start | bytes 786440 | tf_op jit(solution)/shard_map/ppermute | solution.py:524
  63.7 10.7 %collective-permute-start.9 = (bf16[4,2,64,256]{3,2,1,0:T(8,128)(2,1)S(1)}, bf16[4,2,64,256]{3,2,1,0:T(8,128)(2,1)S(1)}, u32[]{:S(2)}, u32[]{:S(2)}) collective-permute-start(bf16[4,2,64,256]{3,2,1,0:T(8,128)(2,1)S(1)} %get-tuple-element.52), channel_id=1, source_target_pairs={{0,3},{1,2},{2,1},{3,0},{4,7},{5,6},{6,5},{7,4},{8,11},{9,10},{10,... | collective-permute-start | bytes 786440 | tf_op jit(solution)/shard_map/ppermute | solution.py:524
  70.2 11.5 %collective-permute-start.16 = (bf16[256,512]{1,0:T(8,128)(2,1)S(1)}, bf16[256,512]{1,0:T(8,128)(2,1)S(1)}, u32[]{:S(2)}, u32[]{:S(2)}) collective-permute-start(bf16[256,512]{1,0:T(8,128)(2,1)S(1)} %get-tuple-element.59.refs_6_.refs_1_), channel_id=1, source_target_pairs={{0,4},{4,0},{8,12},{12,8},{16,20},{20,16},{24,28},{28,24},{1,5},{5... | collective-permute-start | bytes 786440 | tf_op jit(solution)/shard_map/ppermute | solution.py:528
  80.1 9.1 %collective-permute-start.15 = (bf16[256,512]{1,0:T(8,128)(2,1)S(1)}, bf16[256,512]{1,0:T(8,128)(2,1)S(1)}, u32[]{:S(2)}, u32[]{:S(2)}) collective-permute-start(bf16[256,512]{1,0:T(8,128)(2,1)S(1)} %get-tuple-element.60.refs_4_.refs_1_), channel_id=1, source_target_pairs={{0,4},{4,0},{8,12},{12,8},{16,20},{20,16},{24,28},{28,24},{1,5},{5... | collective-permute-start | bytes 786440 | tf_op jit(solution)/shard_map/ppermute | solution.py:528
  82.6 11.3 %collective-permute-start.19 = (bf16[256,512]{1,0:T(8,128)(2,1)S(1)}, bf16[256,512]{1,0:T(8,128)(2,1)S(1)}, u32[]{:S(2)}, u32[]{:S(2)}) collective-permute-start(bf16[256,512]{1,0:T(8,128)(2,1)S(1)} %get-tuple-element.64.refs_4_), channel_id=1, source_target_pairs={{0,8},{4,12},{16,24},{20,28},{1,9},{5,13},{17,25},{21,29},{2,10},{... | collective-permute-start | bytes 786440 | tf_op jit(solution)/shard_map/ppermute | solution.py:533
  83.9 10.7 %collective-permute-start.21 = (bf16[256,512]{1,0:T(8,128)(2,1)S(1)}, bf16[256,512]{1,0:T(8,128)(2,1)S(1)}, u32[]{:S(2)}, u32[]{:S(2)}) collective-permute-start(bf16[256,512]{1,0:T(8,128)(2,1)S(1)} %get-tuple-element.64.refs_4_), channel_id=1, source_target_pairs={{0,16},{4,20},{1,17},{5,21},{2,18},{6,22},{3,19},{7,23}} | collective-permute-start | bytes 786440 | tf_op jit(solution)/shard_map/ppermute | solution.py:533
  90.1 6.7 %collective-permute-start.17 = (bf16[256,512]{1,0:T(8,128)(2,1)S(1)}, bf16[256,512]{1,0:T(8,128)(2,1)S(1)}, u32[]{:S(2)}, u32[]{:S(2)}) collective-permute-start(bf16[256,512]{1,0:T(8,128)(2,1)S(1)} %get-tuple-element.65.refs_4_), channel_id=1, source_target_pairs={{0,16},{4,20},{1,17},{5,21},{2,18},{6,22},{3,19},{7,23}} | collective-permute-start | bytes 786440 | tf_op jit(solution)/shard_map/ppermute | solution.py:533
  90.8 10.3 %collective-permute-start.18 = (bf16[256,512]{1,0:T(8,128)(2,1)S(1)}, bf16[256,512]{1,0:T(8,128)(2,1)S(1)}, u32[]{:S(2)}, u32[]{:S(2)}) collective-permute-start(bf16[256,512]{1,0:T(8,128)(2,1)S(1)} %get-tuple-element.65.refs_4_), channel_id=1, source_target_pairs={{0,8},{4,12},{16,24},{20,28},{1,9},{5,13},{17,25},{21,29},{2,10},{... | collective-permute-start | bytes 786440 | tf_op jit(solution)/shard_map/ppermute | solution.py:533
  92.1 12.4 %collective-permute-start.23 = (bf16[256,512]{1,0:T(8,128)(2,1)S(1)}, bf16[256,512]{1,0:T(8,128)(2,1)S(1)}, u32[]{:S(2)}, u32[]{:S(2)}) collective-permute-start(bf16[256,512]{1,0:T(8,128)(2,1)S(1)} %get-tuple-element.65.refs_4_), channel_id=1, source_target_pairs={{8,16},{12,20},{9,17},{13,21},{10,18},{14,22},{11,19},{15,23}} | collective-permute-start | bytes 786440 | tf_op jit(solution)/shard_map/ppermute | solution.py:533
  93.9 9.7 %collective-permute-start.24 = (bf16[256,512]{1,0:T(8,128)(2,1)S(1)}, bf16[256,512]{1,0:T(8,128)(2,1)S(1)}, u32[]{:S(2)}, u32[]{:S(2)}) collective-permute-start(bf16[256,512]{1,0:T(8,128)(2,1)S(1)} %get-tuple-element.64.refs_4_), channel_id=1, source_target_pairs={{8,16},{12,20},{9,17},{13,21},{10,18},{14,22},{11,19},{15,23}} | collective-permute-start | bytes 786440 | tf_op jit(solution)/shard_map/ppermute | solution.py:533
  95.5 25.8 %collective-permute-start.25 = (bf16[256,512]{1,0:T(8,128)(2,1)S(1)}, bf16[256,512]{1,0:T(8,128)(2,1)S(1)}, u32[]{:S(2)}, u32[]{:S(2)}) collective-permute-start(bf16[256,512]{1,0:T(8,128)(2,1)S(1)} %combine.2.refs_3_), channel_id=1, source_target_pairs={{8,24},{12,28},{9,25},{13,29},{10,26},{14,30},{11,27},{15,31}} | collective-permute-start | bytes 786440 | tf_op jit(solution)/shard_map/ppermute | solution.py:533
  102.1 25.3 %collective-permute-start.22 = (bf16[256,512]{1,0:T(8,128)(2,1)S(1)}, bf16[256,512]{1,0:T(8,128)(2,1)S(1)}, u32[]{:S(2)}, u32[]{:S(2)}) collective-permute-start(bf16[256,512]{1,0:T(8,128)(2,1)S(1)} %combine.3.refs_4_), channel_id=1, source_target_pairs={{8,24},{12,28},{9,25},{13,29},{10,26},{14,30},{11,27},{15,31}} | collective-permute-start | bytes 786440 | tf_op jit(solution)/shard_map/ppermute | solution.py:533

commit v3 on v2

v3 whole, which is shorter than its diff:
```python
import functools

import jax
import jax.numpy as jnp
from jax import lax
from jax.experimental import pallas as pl
from jax.experimental.pallas import tpu as pltpu
from jax.sharding import PartitionSpec as P

BF16 = jnp.bfloat16
F32 = jnp.float32
VMEM_LIMIT = 24 * 1024 * 1024


def params():
    return pltpu.CompilerParams(vmem_limit_bytes=VMEM_LIMIT)


def ordered(body, count, extra=1):
    def run(*refs):
        body(*refs[:count], *refs[count + extra :])

    return run


ANYWHERE = pl.BlockSpec(memory_space=pl.ANY)


def cost():
    return pl.CostEstimate(flops=0, bytes_accessed=0, transcendentals=0)


def split(value):
    high = value.astype(BF16)
    low = (value - high.astype(F32)).astype(BF16)
    return high, low


def panel(re, im):
    return jnp.concatenate(
        [jnp.concatenate([re, im], axis=1), jnp.concatenate([-im, re], axis=1)], axis=0
    )


def dot(left, right):
    return lax.dot_general(left, right, (((1,), (0,)), ((), ())), preferred_element_type=F32)


def dot_nt(left, right):
    return lax.dot_general(left, right, (((1,), (1,)), ((), ())), preferred_element_type=F32)


def times_wide(a_high, a_low, x):
    order = x.shape[0]
    x_high, x_low = split(x)
    xh = panel(x_high[:, :order], x_high[:, order:])
    xl = panel(x_low[:, :order], x_low[:, order:])
    left = jnp.concatenate([a_high, a_high, a_low], axis=1)
    return dot(left, jnp.concatenate([xh, xl, xh], axis=0))


def times_narrow(a_high, a_low, re, im):
    xp = panel(re, im)
    left = jnp.concatenate([a_high, a_low], axis=1)
    return dot(left, jnp.concatenate([xp, xp], axis=0))


def times_adjoint(y, t_high, t_low):
    order = y.shape[0]
    y_high, y_low = split(y)
    th = panel(t_high[:, :order], t_high[:, order:])
    tl = panel(t_low[:, :order], t_low[:, order:])
    left = jnp.concatenate([y_high, y_low, y_high], axis=1)
    return dot_nt(left, jnp.concatenate([th, th, tl], axis=1))


def panels(ref):
    return ref[0], ref[1]


def store_map(ref, value):
    high, low = split(value)
    ref[0] = high
    ref[1] = low


def pack_body(wanted, *refs):
    sources, outs, sems = refs[:2], refs[-1 - len(wanted) : -1], refs[-1]
    copies = []
    for out, (parts, k, start) in zip(outs, wanted):
        size, rows = out.shape[-4 + 1 : -1]
        begin = pl.multiple_of((lax.axis_index("energy") ^ k) * rows, rows)
        for part in parts:
            block = sources[part].at[:, :, pl.ds(start, size), pl.ds(begin, rows), :]
            target = out if len(parts) == 1 else out.at[part]
            copies.append(pltpu.make_async_copy(block, target, sems.at[len(copies)]))
    for copy in copies:
        copy.start()
    for copy in copies:
        copy.wait()


def pack(green, screen, wanted, count, *after):
    _, energies, _, order, _ = green.shape
    shapes = [
        (len(parts),) * (len(parts) > 1) + (2, energies, size, order // count, order)
        for parts, _, _, size in wanted
    ]
    return pl.pallas_call(
        functools.partial(pack_body, [w[:3] for w in wanted]),
        in_specs=[ANYWHERE] * (2 + len(after)),
        out_specs=[pl.BlockSpec(memory_space=pltpu.VMEM)] * len(wanted),
        out_shape=[jax.ShapeDtypeStruct(shape, BF16) for shape in shapes],
        scratch_shapes=[pltpu.SemaphoreType.DMA((sum(len(w[0]) for w in wanted),))],
        compiler_params=params(),
        cost_estimate=cost(),
        name="pack",
    )(green, screen, *after)


def maps_body(g_ref, c_ref, k_ref, p_ref, carry):
    left = jnp.concatenate([g_ref[0], g_ref[1]], axis=1)
    value = dot(left, panel(c_ref[0], c_ref[1]))
    store_map(k_ref, value)

    @pl.when(pl.program_id(1) == 0)
    def _():
        carry[...] = value

    @pl.when(pl.program_id(1) > 0)
    def _():
        high, low = panels(k_ref)
        carry[...] = times_wide(high, low, carry[...])

    store_map(p_ref, carry[...])


def build_maps(green, coupling, *after):
    _, energies, slabs, order, _ = green.shape
    shape = jax.ShapeDtypeStruct((energies, slabs, 2, order, 2 * order), BF16)
    out_spec = pl.BlockSpec((None, None, 2, order, 2 * order), lambda e, s: (e, s, 0, 0, 0))
    return pl.pallas_call(
        lambda *refs: maps_body(*refs[:2], *refs[2 + len(after) :]),
        grid=(energies, slabs),
        in_specs=[
            pl.BlockSpec((2, None, None, order, order), lambda e, s: (0, e, s, 0, 0)),
            pl.BlockSpec((2, None, order, order), lambda e, s: (0, s, 0, 0)),
        ]
        + [ANYWHERE] * len(after),
        out_specs=[out_spec, out_spec],
        out_shape=[shape, shape],
        scratch_shapes=[pltpu.VMEM((order, 2 * order), F32)],
        compiler_params=params(),
        cost_estimate=cost(),
        name="maps",
    )(green, coupling, *after)


def one_map(maps, energy):
    if isinstance(maps, list):
        return maps[energy], pl.BlockSpec(maps[energy].shape, lambda *_: (0, 0, 0))
    return maps, pl.BlockSpec((None,) + maps.shape[1:], lambda *_: (energy, 0, 0, 0))


def pair_maps_body(energies, *refs):
    step, plane, inner = refs[-3:]
    odd = (lax.axis_index("slab") & 1) == 1
    for e in range(energies):
        mine, other = refs[2 * e], refs[2 * e + 1]
        order = mine.shape[1]
        first = [jnp.where(odd, mine[part], other[part]) for part in range(2)]
        second = [jnp.where(odd, other[part], mine[part]).astype(F32) for part in range(2)]
        store_map(plane.at[e], times_wide(*first, second[0] + second[1]))
        row = lax.broadcasted_iota(jnp.int32, (order, 2 * order), 0)
        column = lax.broadcasted_iota(jnp.int32, (order, 2 * order), 1)
        unit = jnp.where(row == column, 1.0, 0.0)
        for part in range(2):
            step[e, part] = first[part]
            identity = unit if part == 0 else jnp.zeros_like(unit)
            inner[e, part] = jnp.where(odd, other[part].astype(F32), identity).astype(BF16)


def pair_maps(mine, other, energies, after):
    pairs = [one_map(maps, e) for e in range(energies) for maps in (mine, other)]
    shape = (energies,) + pairs[0][1].block_shape[-3:]
    return pl.pallas_call(
        ordered(functools.partial(pair_maps_body, energies), 2 * energies),
        grid=(1,),
        in_specs=[spec for _, spec in pairs] + [ANYWHERE],
        out_specs=[pl.BlockSpec(shape, lambda i: (0, 0, 0, 0))] * 3,
        out_shape=[jax.ShapeDtypeStruct(shape, BF16)] * 3,
        compiler_params=params(),
        cost_estimate=cost(),
        name="pair_maps",
    )(*[maps for maps, _ in pairs], after)


def convolve_body(pairs, energies, shared, *refs):
    count = len(pairs)
    taken = sum(1 + pair for pair in pairs)
    ins, outs = list(refs[:taken]), refs[taken + 1 + shared :]
    green, screen, total = refs[-3:]
    me = lax.axis_index("energy")
    points = count * energies
    middle = points // 2
    rows, columns = green.shape[2:]
    for k in range(count):
        base = (me ^ k) * energies
        piece = ins.pop(0)
        halves = (piece, ins.pop(0)) if pairs[k] else (piece.at[0], piece.at[1])
        for e in range(energies):
            green[:, base + e] = halves[0][:, e].astype(F32)
            screen[:, base + e] = halves[1][:, e].astype(F32)

    def tile(index, _):
        row = pl.multiple_of(index * 8, 8)
        for col in range(0, columns, 128):
            at = (pl.ds(row, 8), pl.ds(col, 128))
            gr = [green[(0, m) + at] for m in range(points)]
            gi = [green[(1, m) + at] for m in range(points)]
            wr = [screen[(0, m) + at] for m in range(points)]
            wi = [screen[(1, m) + at] for m in range(points)]
            for n in range(points):
                re = None
                im = None
                for m in range(points):
                    lag = n - m + middle
                    if 0 <= lag < points:
                        a = gr[m] * wr[lag] - gi[m] * wi[lag]
                        b = gr[m] * wi[lag] + gi[m] * wr[lag]
                        re = a if re is None else re + a
                        im = b if im is None else im + b
                total[(n, 0) + at] = -im / points
                total[(n, 1) + at] = re / points
        return 0

    lax.fori_loop(0, rows // 8, tile, 0)
    for k in range(count):
        base = (me ^ k) * energies
        for e in range(energies):
            outs[k * energies + e][...] = total[base + e].astype(BF16)


def convolve(pieces, start, slabs, size, held, after):
    count = len(pieces)
    pairs = [isinstance(piece, tuple) for piece in pieces]
    operands, in_specs = [], []
    for piece, pair in zip(pieces, pairs):
        if pair:
            operands += piece
            energies, _, rows, columns = piece[0].shape[1:]
            in_specs += [pl.BlockSpec((2, energies, None, rows, columns), lambda s: (0, 0, s + start, 0, 0))] * 2
        else:
            operands.append(piece)
            energies, _, rows, columns = piece.shape[2:]
            first = start if piece.shape[3] == slabs else 0
            block = (2, 2, energies, None, rows, columns)
            in_specs.append(pl.BlockSpec(block, lambda s, first=first: (0, 0, 0, s + first, 0, 0)))
    points = count * energies
    whole = pl.BlockSpec((None, 2, rows, columns), lambda s: (s + start, 0, 0, 0))
    outs = pl.pallas_call(
        functools.partial(convolve_body, pairs, energies, len(held)),
        grid=(size,),
        in_specs=in_specs + [ANYWHERE] * (1 + len(held)),
        out_specs=[whole] * points,
        out_shape=[jax.ShapeDtypeStruct((slabs, 2, rows, columns), BF16)] * points,
        input_output_aliases={len(operands) + 1 + i: i for i in range(len(held))},
        scratch_shapes=[
            pltpu.VMEM((2, points, rows, columns), F32),
            pltpu.VMEM((2, points, rows, columns), F32),
            pltpu.VMEM((points, 2, rows, columns), F32),
        ],
        compiler_params=params(),
        cost_estimate=cost(),
        name="convolve",
    )(*operands, after, *held)
    return outs


def source_body(owners, *refs):
    pieces = refs[: len(owners)]
    g_ref, k_ref, b_ref, v_ref, sigma = refs[len(owners) :]
    me = lax.axis_index("energy")
    for piece, k in zip(pieces, owners):
        slabs, _, rows, _ = piece.shape
        start = pl.multiple_of((me ^ k) * rows, rows)
        for s in range(slabs):
            for part in range(2):
                sigma[s, part, pl.ds(start, rows), :] = piece[s, part]

    carry = None
    for s in range(sigma.shape[0]):
        left = jnp.concatenate([g_ref[0, s], g_ref[1, s]], axis=1)
        mixed = dot(left, panel(sigma[s, 0], sigma[s, 1])).astype(BF16)
        source = dot_nt(mixed, panel(g_ref[0, s], g_ref[1, s]))
        if carry is not None:
            high, low = k_ref[s, 0], k_ref[s, 1]
            source = times_adjoint(times_wide(high, low, carry), high, low) + source
        carry = source
        b_ref[s] = carry
    v_ref[...] = carry.astype(BF16)


def build_sources(pieces, green, kernels, energy, after):
    slabs, order = green.shape[2:4]
    return pl.pallas_call(
        ordered(functools.partial(source_body, range(len(pieces))), len(pieces) + 2),
        grid=(1,),
        in_specs=[pl.BlockSpec(x.shape, lambda i: (0, 0, 0, 0)) for x in pieces]
        + [
            pl.BlockSpec((2, None, slabs, order, order), lambda i: (0, energy, 0, 0, 0)),
            pl.BlockSpec((None, slabs, 2, order, 2 * order), lambda i: (energy, 0, 0, 0, 0)),
            ANYWHERE,
        ],
        out_specs=[
            pl.BlockSpec((slabs, order, 2 * order), lambda i: (0, 0, 0)),
            pl.BlockSpec((order, 2 * order), lambda i: (0, 0)),
        ],
        out_shape=[
            jax.ShapeDtypeStruct((slabs, order, 2 * order), F32),
            jax.ShapeDtypeStruct((order, 2 * order), BF16),
        ],
        scratch_shapes=[pltpu.VMEM((slabs, 2, order, order), BF16)],
        compiler_params=params(),
        cost_estimate=cost(),
        name="sources",
    )(*pieces, green, kernels, after)


def congruence(t_ref, x):
    order = x.shape[0]
    high, low = panels(t_ref)
    if x.dtype == F32:
        inner = times_wide(high, low, x)
    else:
        inner = times_narrow(high, low, x[:, :order], x[:, order:])
    return times_adjoint(inner, high, low)


def total(refs):
    value = refs[0][...]
    for ref in refs[1:]:
        value = value + ref[...]
    return value


def pair_body(v_ref, own_ref, sum_ref, t_ref, full_ref, short_ref):
    odd = (lax.axis_index("slab") & 1) == 1
    x = jnp.where(odd, v_ref[...], own_ref[...])
    base = jnp.where(odd, sum_ref[...], v_ref[...].astype(F32))
    value = base + congruence(t_ref, x)
    full_ref[...] = value
    short_ref[...] = value.astype(BF16)


def pair_sum(arrived, own, sums, maps, energy, *after):
    slabs, order, _ = sums.shape
    step, step_spec = one_map(maps, energy)
    whole = pl.BlockSpec((order, 2 * order), lambda i: (0, 0))
    return pl.pallas_call(
        ordered(pair_body, 4, len(after)),
        grid=(1,),
        in_specs=[whole, whole, pl.BlockSpec((None, order, 2 * order), lambda i: (slabs - 1, 0, 0)), step_spec]
        + [ANYWHERE] * len(after),
        out_specs=[whole] * 2,
        out_shape=[jax.ShapeDtypeStruct((order, 2 * order), t) for t in (F32, BF16)],
        compiler_params=params(),
        cost_estimate=cost(),
        name="pair_sum",
    )(arrived, own, sums, step, *after)


def combine(arrived, maps, base, energy, after):
    order = base.shape[0]
    step, step_spec = one_map(maps, energy)
    whole = pl.BlockSpec((order, 2 * order), lambda i: (0, 0))
    count = len(arrived)

    def body(*refs):
        t_ref, base_ref, _, out = refs[count:]
        out[...] = (base_ref[...] + congruence(t_ref, total(refs[:count]))).astype(BF16)

    return pl.pallas_call(
        body,
        grid=(1,),
        in_specs=[whole] * count + [step_spec, whole, ANYWHERE],
        out_specs=whole,
        out_shape=jax.ShapeDtypeStruct((order, 2 * order), BF16),
        compiler_params=params(),
        cost_estimate=cost(),
        name="combine",
    )(*arrived, step, base, after)


def keep(blocks, after):
    count = len(blocks)
    shape = (count,) + blocks[0].shape

    def body(*refs):
        for index in range(count):
            refs[-1][index] = refs[index][...]

    return pl.pallas_call(
        body,
        grid=(1,),
        in_specs=[pl.BlockSpec(shape[1:], lambda i: (0, 0))] * count + [ANYWHERE],
        out_specs=pl.BlockSpec(shape, lambda i: (0, 0, 0)),
        out_shape=jax.ShapeDtypeStruct(shape, BF16),
        compiler_params=params(),
        cost_estimate=cost(),
        name="keep",
    )(*blocks, after)


def finish_body(arrivals, ours, kept_ref, t_ref, m_ref, base_ref, out, entry):
    group, _, order, _ = m_ref.shape

    @pl.when(pl.program_id(0) == 0)
    def _():
        odd = (lax.axis_index("slab") & 1) == 1
        before = jnp.where(odd, ours[...].astype(F32) + kept_ref[...].astype(F32), 0.0)
        entry[...] = before + congruence(t_ref, total(arrivals))

    x_high, x_low = split(entry[...])
    xh = panel(x_high[:, :order], x_high[:, order:])
    xl = panel(x_low[:, :order], x_low[:, order:])
    both = dot(m_ref[...].reshape(group * 2 * order, 2 * order), xh)
    for index in range(group):
        first = 2 * index * order
        inner = both[first : first + order] + both[first + order : first + 2 * order] + dot(m_ref[index, 0], xl)
        value = times_adjoint(inner, m_ref[index, 0], m_ref[index, 1]) + base_ref[index]
        out[0, index] = value[:, :order]
        out[1, index] = value[:, order:]


def finish(arrived, ours, kept, inner, prefixes, sums, energy, held, after):
    energies, slabs, _, order, _ = prefixes.shape
    group = 2 if slabs % 2 == 0 else 1
    whole = pl.BlockSpec((order, 2 * order), lambda s: (0, 0))
    step, step_spec = one_map(inner, energy)
    operands = list(arrived) + [ours, kept, step, prefixes, sums, after]
    in_specs = [whole] * (len(arrived) + 1) + [
        pl.BlockSpec((None, order, 2 * order), lambda s: (energy, 0, 0)),
        step_spec,
        pl.BlockSpec((None, group, 2, order, 2 * order), lambda s: (energy, s, 0, 0, 0)),
        pl.BlockSpec((group, order, 2 * order), lambda s: (s, 0, 0)),
        ANYWHERE,
    ]
    aliases = {}
    if held is not None:
        aliases = {len(operands): 0}
        operands.append(held)
        in_specs.append(ANYWHERE)

    def body(*refs):
        fixed = refs[len(arrived) : len(arrived) + 5]
        finish_body(refs[: len(arrived)], *fixed, *refs[-2:])

    return pl.pallas_call(
        body,
        grid=(slabs // group,),
        in_specs=in_specs,
        out_specs=pl.BlockSpec((2, None, group, order, order), lambda s: (0, energy, s, 0, 0)),
        out_shape=jax.ShapeDtypeStruct((2, energies, slabs, order, order), F32),
        input_output_aliases=aliases,
        scratch_shapes=[pltpu.VMEM((order, 2 * order), F32)],
        compiler_params=params(),
        cost_estimate=cost(),
        name="finish",
    )(*operands)


def swap(x, k):
    count = lax.axis_size("energy")
    return lax.ppermute(x, "energy", [(i, i ^ k) for i in range(count)])


def other_of_pair(x):
    return lax.ppermute(x, "slab", [(i, i ^ 1) for i in range(lax.axis_size("slab"))])


def along(x, moves):
    count = lax.axis_size("energy")
    pairs = [(i * count + n, j * count + n) for n in range(count) for i, j in moves(n & 1)]
    return lax.ppermute(x, ("slab", "energy"), pairs)


def cut(slabs):
    return [(0, slabs - 1), (slabs - 1, 1)] if slabs > 1 else [(0, slabs)]


def per_device(green_lesser, screened_lesser, green_retarded, coupling):
    count = lax.axis_size("energy")
    depth = lax.axis_size("slab")
    if depth % 2 or count & (count - 1):
        raise ValueError("mesh axes")
    _, energies, slabs, order, _ = green_lesser.shape
    far = [k for k in range(count) if k >= 2]
    near = [k for k in range(min(2, count))]
    parts = cut(slabs)

    def first_rows(k, start, size):
        rows = order // count
        begin = (0, 0, start, (lax.axis_index("energy") ^ k) * rows, 0)
        sizes = (2, energies, size, rows, order)
        return [lax.dynamic_slice(x, begin, sizes) for x in (green_lesser, screened_lesser)]

    pieces = [[None] * count for _ in parts]
    for chunk, (start, size) in enumerate(parts):
        for k in far + near:
            block = jnp.stack(first_rows(k, start, size))
            pieces[chunk][k] = swap(block, k) if k else block
    token = pieces[0][0]

    kernels, prefixes = build_maps(green_retarded, coupling, token)
    token = kernels
    mine = [prefixes[e, slabs - 1] for e in range(energies)]
    other = [other_of_pair(x) for x in mine]

    blocks = ()
    for chunk, (start, size) in enumerate(parts):
        if chunk == len(parts) - 1:
            pair_step, plane, inner = pair_maps(mine, other, energies, token)
            token = plane
        blocks = convolve(pieces[chunk], start, slabs, size, blocks, token)
        token = blocks[0]
    sigma = [[None] * count for _ in range(energies)]
    for e in range(energies):
        for k in range(count):
            block = blocks[k * energies + e]
            sigma[e][k] = swap(block, k) if k else block

    pairs = depth // 2
    sums, own, ours = ([None] * energies for _ in range(3))
    running, carry = [None] * energies, [None] * energies
    arrived = [[] for _ in range(energies)]

    def to_carrier(lane):
        return [(2 * z + 1 - lane, 2 * z + lane) for z in range(pairs)]

    def to_second(lane):
        return [(2 * z, 2 * z + 1) for z in range(pairs)] if lane == 0 else []

    def onward(step):
        def moves(lane):
            ahead = [(2 * step + lane, 2 * step + 2 + lane)] if step < pairs - 1 else []
            aside = [(2 * step - 2 + lane, 2 * step + 1 - lane)] if step > 0 else []
            return ahead + aside

        return moves

    kept = None

    def stage(e, step):
        nonlocal token, kept
        if step == 0:
            sums[e], own[e] = build_sources(sigma[e], green_retarded, kernels, e, token)
            token = own[e]
            ours[e] = along(own[e], to_carrier)
        elif step == 1:
            running[e], carry[e] = pair_sum(ours[e], own[e], sums[e], pair_step, e, token)
            token = carry[e]
            arrived[e].append(along(carry[e], onward(0)))
            if e == energies - 1:
                token = keep(own, token)
                kept = along(token, to_second)
        else:
            carry[e] = token = combine(arrived[e], plane, running[e], e, token)
            arrived[e].append(along(carry[e], onward(step - 1)))
        if step == last:
            arrived[e].append(along(carry[e], onward(pairs - 1)))

    last = max(pairs - 1, 1)
    for step in range(last + 1):
        for e in range(energies):
            stage(e, step)
    result = None
    for e in range(energies):
        result = finish(arrived[e], ours[e], kept, inner, prefixes, sums[e], e, result, token)
    return result


def solution(mesh):
    placed = (
        P(None, "energy", "slab", None, None),
        P(None, "energy", "slab", None, None),
        P(None, "energy", "slab", None, None),
        P(None, "slab", None, None),
    )
    return jax.shard_map(
        per_device,
        mesh=mesh,
        in_specs=placed,
        out_specs=P(None, "energy", "slab", None, None),
        check_vma=False,
    )
```

time: 134 us -> 122 us (0.910)
  waiting for transfers between devices: 59 us -> 53.5 us
  Pallas kernels: 43.9 us -> 39.5 us
  starting transfers between devices: 25.1 us -> 23.3 us
    pallas_call x10 -> x7, Pallas kernels: 31.5 us -> 25.2 us  [the longest x2 11.7 us: finish(): pl.pallas_call(body, grid=(slabs // group,), in_specs=in_specs, out_specs...]
    ppermute x9 -> x11, waiting for transfers between devices: 20.2 us -> 15.1 us  [along(): return lax.ppermute(x, ('slab', 'energy'), pairs)]
    ppermute x4 -> x2, waiting for transfers between devices: 4.66 us -> 0.01 us  [other_of_pair(): lax.ppermute(x, 'slab', [(i, i ^ 1) for i in range(lax.axis_size('slab'))])]
    ppermute x13 -> x12, waiting for transfers between devices: 34.1 us -> 38.4 us  [swap(): return lax.ppermute(x, 'energy', [(i, i ^ k) for i in range(count)])]
    ppermute x4 -> x2, starting transfers between devices: 5.2 us -> 2.09 us  [other_of_pair(): lax.ppermute(x, 'slab', [(i, i ^ 1) for i in range(lax.axis_size('slab'))])]
    pallas_call x2 -> x4, Pallas kernels: 1.86 us -> 3.71 us  [combine(): pl.pallas_call(body, grid=(1,), in_specs=[whole] * count + [step_spec, wh...]
    ppermute x9 -> x11, starting transfers between devices: 9.35 us -> 10.9 us  [along(): return lax.ppermute(x, ('slab', 'energy'), pairs)]
    ppermute x13 -> x12, starting transfers between devices: 10.6 us -> 10.3 us  [swap(): return lax.ppermute(x, 'energy', [(i, i ^ k) for i in range(count)])]
  transfers between devices with their start and end apart: 26 -> 25, of which waited for: 10 -> 9; matrix products, arithmetic and copies ran while one was open for 1% -> 1% of each run, Pallas kernels for 28% -> 27%
where the time goes in v3:
time: 122 us
  waiting for transfers between devices  53.5 us (44%)
  Pallas kernels  39.5 us (32%)
  starting transfers between devices  23.3 us (19%)
  local copies, waits for them, and re-layouts  4.5 us (4%)
    ppermute x12, waiting for transfers between devices, swap(): return lax.ppermute(x, 'energy', [(i, i ^ k) for i in range(count)])  38.4 us
    ppermute x11, waiting for transfers between devices, along(): return lax.ppermute(x, ('slab', 'energy'), pairs)  15.1 us
    pallas_call x2, Pallas kernels, finish(): pl.pallas_call(body, grid=(slabs // group,), in_specs=in_specs, out_specs...  11.7 us
    ppermute x11, starting transfers between devices, along(): return lax.ppermute(x, ('slab', 'energy'), pairs)  10.9 us
    ppermute x12, starting transfers between devices, swap(): return lax.ppermute(x, 'energy', [(i, i ^ k) for i in range(count)])  10.3 us
    pallas_call x2, Pallas kernels, build_sources(): pl.pallas_call(ordered(functools.partial(source_body, range(len(pieces)))...  8.65 us
    pallas_call x1, Pallas kernels, build_maps(): pl.pallas_call(lambda *refs: maps_body(*refs[:2], *refs[2 + len(after):])...  7.15 us
    pallas_call x2, Pallas kernels, convolve(): pl.pallas_call(functools.partial(convolve_body, pairs, energies, len(held...  4.83 us
  transfers between devices with their start and end apart: 25, of which 9 were waited for; matrix products, arithmetic and copies ran while one was open for 1% of the time, Pallas kernels for 27%

profile of v3, /device:TPU:24, one launch (start us, length us, event | category | flops | bytes accessed | tf_op | source)
XLA Modules:
  0.0 121.5 jit_solution(3121040235421042193)
XLA Ops:
  0.0 2.2 %dynamic-slice_bitcast_fusion = (bf16[1,2,2,3,64,256]{5,4,3,2,1,0:T(8,128)(2,1)S(1)}, bf16[1,2,2,3,64,256]{5,4,3,2,1,0:T(8,128)(2,1)S(1)}, bf16[1,2,2,3,64,256]{...) fusion(bf16[2,2,4,256,256]{4,3,2,1,0:T(8,128)(2,1)} %param.5, ...), kind=kLoop, calls=%fused_computation.6 | loop fusion | bytes 6291472 | tf_op jit(solution)/shard_map/stack | solution.py:511
  2.2 0.1 pad_maximum_fusion.2
  2.3 1.6 %collective-permute-start.6 = (bf16[2,2,2,3,64,256]{5,4,3,2,1,0:T(8,128)(2,1)S(1)}, bf16[2,2,2,3,64,256]{5,4,3,2,1,0:T(8,128)(2,1)S(1)}, u32[]{:S(2)}, u32[]{:S(2)}) collective-permute-start(bf16[2,2,2,3,64,256]{5,4,3,2,1,0:T(8,128)(2,1)S(1)} %pad_maximum_fusion.2), channel_id=1, source_target_pairs={{0,2},{1,3},{2,0},{3,1},{4,6},{5,7},{6,4},{7,5},{8,10},{9,11},{10,... | collective-permute-start | bytes 2359304 | tf_op jit(solution)/shard_map/ppermute | solution.py:475
  3.9 0.1 pad_maximum_fusion.1
  3.9 0.1 collective-permute-start.5
  4.0 0.1 pad_maximum_fusion.3
  4.1 0.7 collective-permute-start.7
  4.8 0.1 pad_maximum_fusion.refs_2_.refs_0_
  4.8 0.6 copy-done
  5.4 0.3 copy-done.1
  5.7 7.2 %maps.1 = (bf16[2,4,2,256,512]{4,3,2,1,0:T(8,128)(2,1)S(1)}, bf16[2,4,2,256,512]{4,3,2,1,0:T(8,128)(2,1)S(1)}) custom-call(bf16[2,2,4,256,256]{4,3,2,1,0:T(8,128)(2,1)S(1)} %copy-done, bf16[2,4,256,256]{3,2,1,0:T(8,128)(2,1)S(1)} %copy-done.1, bf16[2,2,2,3,64,256]{5,4,3,2,1,0:T(8,128)(2,1)S(1)} %pad_maximum_fusion.refs_2_.refs_0_), custom_call_target="tpu_custom_call" | custom-call | tf_op jit(solution)/shard_map/maps/pallas_call | solution.py:142
  12.9 0.1 slice_bitcast_fusion
  12.9 1.6 %collective-permute-start.4 = (bf16[2,256,512]{2,1,0:T(8,128)(2,1)S(1)}, bf16[2,256,512]{2,1,0:T(8,128)(2,1)S(1)}, u32[]{:S(2)}, u32[]{:S(2)}) collective-permute-start(bf16[2,256,512]{2,1,0:T(8,128)(2,1)S(1)} %get-tuple-element.63.refs_2_), channel_id=1, source_target_pairs={{0,4},{4,0},{8,12},{12,8},{16,20},{20,16},{24,28},{28,24},{1,5},{5... | collective-permute-start | bytes 1572872 | tf_op jit(solution)/shard_map/ppermute | solution.py:479
  14.5 0.5 collective-permute-start.3
  15.0 1.4 %dynamic-slice_bitcast_fusion.8 = (bf16[1,2,2,1,64,256]{5,4,3,2,1,0:T(8,128)(2,1)S(1)}, bf16[1,2,2,1,64,256]{5,4,3,2,1,0:T(8,128)(2,1)S(1)}, bf16[1,2,2,1,64,256...) fusion(bf16[2,2,4,256,256]{4,3,2,1,0:T(8,128)(2,1)} %param.5, ...), kind=kLoop, calls=%fused_computation.18 | loop fusion | bytes 2097168 | tf_op jit(solution)/shard_map/stack | solution.py:511
  16.5 6.2 %collective-permute-done.6.refs_2_ = bf16[2,2,2,3,64,256]{5,4,3,2,1,0:T(8,128)(2,1)S(1)} collective-permute-done((bf16[2,2,2,3,64,256]{5,4,3,2,1,0:T(8,128)(2,1)S(1)}, bf16[2,2,2,3,64,256]{5,4,3,2,1,0:T(8,128)(2,1)S(1)}, u32[]{:S(2)}, u32[]{:S(2)}) %collective-permute-start.6) | collective-permute-done | bytes 786464 | tf_op jit(solution)/shard_map/ppermute | solution.py:475
  22.8 0.0 collective-permute-start
  22.8 0.0 collective-permute-done.5.refs_1_
  22.8 1.5 %collective-permute-start.1 = (bf16[2,2,2,1,64,256]{5,4,3,2,1,0:T(8,128)(2,1)S(1)}, bf16[2,2,2,1,64,256]{5,4,3,2,1,0:T(8,128)(2,1)S(1)}, u32[]{:S(2)}, u32[]{:S(2)}) collective-permute-start(bf16[2,2,2,1,64,256]{5,4,3,2,1,0:T(8,128)(2,1)S(1)} %pad_maximum_fusion.6), channel_id=1, source_target_pairs={{0,2},{1,3},{2,0},{3,1},{4,6},{5,7},{6,4},{7,5},{8,10},{9,11},{10,... | collective-permute-start | bytes 786440 | tf_op jit(solution)/shard_map/ppermute | solution.py:475
  24.3 14.4 %collective-permute-done.7.refs_3_ = bf16[2,2,2,3,64,256]{5,4,3,2,1,0:T(8,128)(2,1)S(1)} collective-permute-done((bf16[2,2,2,3,64,256]{5,4,3,2,1,0:T(8,128)(2,1)S(1)}, bf16[2,2,2,3,64,256]{5,4,3,2,1,0:T(8,128)(2,1)S(1)}, u32[]{:S(2)}, u32[]{:S(2)}) %collective-permute-start.7) | collective-permute-done | bytes 786464 | tf_op jit(solution)/shard_map/ppermute | solution.py:475
  38.7 1.9 %collective-permute-start.2 = (bf16[2,2,2,1,64,256]{5,4,3,2,1,0:T(8,128)(2,1)S(1)}, bf16[2,2,2,1,64,256]{5,4,3,2,1,0:T(8,128)(2,1)S(1)}, u32[]{:S(2)}, u32[]{:S(2)}) collective-permute-start(bf16[2,2,2,1,64,256]{5,4,3,2,1,0:T(8,128)(2,1)S(1)} %pad_maximum_fusion.7), channel_id=1, source_target_pairs={{0,3},{1,2},{2,1},{3,0},{4,7},{5,6},{6,5},{7,4},{8,11},{9,10},{10,... | collective-permute-start | bytes 786440 | tf_op jit(solution)/shard_map/ppermute | solution.py:475
  40.6 3.7 %convolve.2 = (bf16[4,2,64,256]{3,2,1,0:T(8,128)(2,1)S(1)}, bf16[4,2,64,256]{3,2,1,0:T(8,128)(2,1)S(1)}, bf16[4,2,64,256]{3,2,1,0:T(8,128)(2,1)S(1)}, bf16[4,2,6...) custom-call(bf16[2,2,2,3,64,256]{5,4,3,2,1,0:T(8,128)(2,1)S(1)} %pad, ...), custom_call_target="tpu_custom_call" | custom-call | tf_op jit(solution)/shard_map/convolve/pallas_call | solution.py:261
  44.3 1.5 %pair_maps.1 = (bf16[2,2,256,512]{3,2,1,0:T(8,128)(2,1)S(1)}, bf16[2,2,256,512]{3,2,1,0:T(8,128)(2,1)S(1)}, bf16[2,2,256,512]{3,2,1,0:T(8,128)(2,1)S(1)}) custom-call(bf16[2,256,512]{2,1,0:T(8,128)(2,1)S(1)} %get-tuple-element.64.refs_0_, bf16[2,256,512]{2,1,0:T(8,128)(2,1)S(1)} %collective-permute-done.3.refs_1_, ...), custom_call_target="tpu_custom_call" | custom-call | tf_op jit(solution)/shard_map/pair_maps/pallas_call | solution.py:186
  45.8 0.0 collective-permute-done.refs_1_
  45.8 0.0 collective-permute-done.1.refs_2_
  45.9 2.9 %collective-permute-done.2.refs_3_ = bf16[2,2,2,1,64,256]{5,4,3,2,1,0:T(8,128)(2,1)S(1)} collective-permute-done((bf16[2,2,2,1,64,256]{5,4,3,2,1,0:T(8,128)(2,1)S(1)}, bf16[2,2,2,1,64,256]{5,4,3,2,1,0:T(8,128)(2,1)S(1)}, u32[]{:S(2)}, u32[]{:S(2)}) %collective-permute-start.2) | collective-permute-done | bytes 262176 | tf_op jit(solution)/shard_map/ppermute | solution.py:475
  48.7 1.1 convolve.3
  49.9 0.8 collective-permute-start.11
  50.7 1.5 %collective-permute-start.12 = (bf16[4,2,64,256]{3,2,1,0:T(8,128)(2,1)S(1)}, bf16[4,2,64,256]{3,2,1,0:T(8,128)(2,1)S(1)}, u32[]{:S(2)}, u32[]{:S(2)}) collective-permute-start(bf16[4,2,64,256]{3,2,1,0:T(8,128)(2,1)S(1)} %get-tuple-element.51), channel_id=1, source_target_pairs={{0,2},{1,3},{2,0},{3,1},{4,6},{5,7},{6,4},{7,5},{8,10},{9,11},{10,... | collective-permute-start | bytes 786440 | tf_op jit(solution)/shard_map/ppermute | solution.py:475
  52.2 0.6 collective-permute-start.8
  52.9 1.5 %collective-permute-start.9 = (bf16[4,2,64,256]{3,2,1,0:T(8,128)(2,1)S(1)}, bf16[4,2,64,256]{3,2,1,0:T(8,128)(2,1)S(1)}, u32[]{:S(2)}, u32[]{:S(2)}) collective-permute-start(bf16[4,2,64,256]{3,2,1,0:T(8,128)(2,1)S(1)} %get-tuple-element.47), channel_id=1, source_target_pairs={{0,2},{1,3},{2,0},{3,1},{4,6},{5,7},{6,4},{7,5},{8,10},{9,11},{10,... | collective-permute-start | bytes 786440 | tf_op jit(solution)/shard_map/ppermute | solution.py:475
  54.4 0.0 collective-permute-done.11.refs_1_
  54.4 0.0 collective-permute-start.10
  54.4 5.5 %collective-permute-done.12.refs_2_ = bf16[4,2,64,256]{3,2,1,0:T(8,128)(2,1)S(1)} collective-permute-done((bf16[4,2,64,256]{3,2,1,0:T(8,128)(2,1)S(1)}, bf16[4,2,64,256]{3,2,1,0:T(8,128)(2,1)S(1)}, u32[]{:S(2)}, u32[]{:S(2)}) %collective-permute-start.12) | collective-permute-done | bytes 262176 | tf_op jit(solution)/shard_map/ppermute | solution.py:475
  59.9 4.7 %collective-permute-done.13.refs_3_ = bf16[4,2,64,256]{3,2,1,0:T(8,128)(2,1)S(1)} collective-permute-done((bf16[4,2,64,256]{3,2,1,0:T(8,128)(2,1)S(1)}, bf16[4,2,64,256]{3,2,1,0:T(8,128)(2,1)S(1)}, u32[]{:S(2)}, u32[]{:S(2)}) %collective-permute-start.13) | collective-permute-done | bytes 262176 | tf_op jit(solution)/shard_map/ppermute | solution.py:475
  64.5 4.3 %sources.2 = (f32[4,256,512]{2,1,0:T(8,128)S(1)}, bf16[256,512]{1,0:T(8,128)(2,1)S(1)}) custom-call(bf16[4,2,64,256]{3,2,1,0:T(8,128)(2,1)S(1)} %get-tuple-element.49.refs_0_.refs_6_, bf16[4,2,64,256]{3,2,1,0:T(8,128)(2,1)S(1)} %collective-permute-done.11.refs_1_, bf16[4,2,64,256]{3,2,1,0:T(8,128)(2,1)S(1)} %collective-permute-done.12.refs_2_, ...), custom_call_target="tpu_custom_call" | custom-call | tf_op jit(solution)/shard_map/sources/pallas_call | solution.py:306
  68.9 1.3 %collective-permute-start.15 = (bf16[256,512]{1,0:T(8,128)(2,1)S(1)}, bf16[256,512]{1,0:T(8,128)(2,1)S(1)}, u32[]{:S(2)}, u32[]{:S(2)}) collective-permute-start(bf16[256,512]{1,0:T(8,128)(2,1)S(1)} %get-tuple-element.53.refs_6_.refs_1_.refs_0_), channel_id=1, source_target_pairs={{4,0},{12,8},{20,16},{28,24},{1,5},{9,13},{17,21},{25,29},{6,2},{1... | collective-permute-start | bytes 786440 | tf_op jit(solution)/shard_map/ppermute | solution.py:485
  70.2 0.0 collective-permute-done.8.refs_1_
  70.2 0.9 collective-permute-done.9.refs_2_
  71.1 3.9 %collective-permute-done.10.refs_3_ = bf16[4,2,64,256]{3,2,1,0:T(8,128)(2,1)S(1)} collective-permute-done((bf16[4,2,64,256]{3,2,1,0:T(8,128)(2,1)S(1)}, bf16[4,2,64,256]{3,2,1,0:T(8,128)(2,1)S(1)}, u32[]{:S(2)}, u32[]{:S(2)}) %collective-permute-start.10) | collective-permute-done | bytes 262176 | tf_op jit(solution)/shard_map/ppermute | solution.py:475
  75.0 4.3 %sources.3 = (f32[4,256,512]{2,1,0:T(8,128)S(1)}, bf16[256,512]{1,0:T(8,128)(2,1)S(1)}) custom-call(bf16[4,2,64,256]{3,2,1,0:T(8,128)(2,1)S(1)} %get-tuple-element.45.refs_0_, bf16[4,2,64,256]{3,2,1,0:T(8,128)(2,1)S(1)} %collective-permute-done.8.refs_1_, bf16[4,2,64,256]{3,2,1,0:T(8,128)(2,1)S(1)} %collective-permute-done.9.refs_2_, ...), custom_call_target="tpu_custom_call" | custom-call | tf_op jit(solution)/shard_map/sources/pallas_call | solution.py:306
  79.3 1.3 %collective-permute-start.14 = (bf16[256,512]{1,0:T(8,128)(2,1)S(1)}, bf16[256,512]{1,0:T(8,128)(2,1)S(1)}, u32[]{:S(2)}, u32[]{:S(2)}) collective-permute-start(bf16[256,512]{1,0:T(8,128)(2,1)S(1)} %get-tuple-element.54.refs_4_.refs_1_), channel_id=1, source_target_pairs={{4,0},{12,8},{20,16},{28,24},{1,5},{9,13},{17,21},{25,29},{6,2},{1... | collective-permute-start | bytes 786440 | tf_op jit(solution)/shard_map/ppermute | solution.py:485
  80.6 0.9 pair_sum.2
  81.6 0.9 collective-permute-start.17
  82.4 5.1 %collective-permute-done.14.refs_0_.refs_4_ = bf16[256,512]{1,0:T(8,128)(2,1)S(1)} collective-permute-done((bf16[256,512]{1,0:T(8,128)(2,1)S(1)}, bf16[256,512]{1,0:T(8,128)(2,1)S(1)}, u32[]{:S(2)}, u32[]{:S(2)}) %collective-permute-start.14) | collective-permute-done | bytes 262176 | tf_op jit(solution)/shard_map/ppermute | solution.py:485
  87.6 0.9 pair_sum.3
  88.5 0.7 collective-permute-start.16
  89.3 1.5 %collective-permute-start.22 = (bf16[2,256,512]{2,1,0:T(8,128)(2,1)S(1)}, bf16[2,256,512]{2,1,0:T(8,128)(2,1)S(1)}, u32[]{:S(2)}, u32[]{:S(2)}) collective-permute-start(bf16[2,256,512]{2,1,0:T(8,128)(2,1)S(1)} %keep.1.refs_3_), channel_id=1, source_target_pairs={{0,4},{8,12},{16,20},{24,28},{2,6},{10,14},{18,22},{26,30}} | collective-permute-start | bytes 1572872 | tf_op jit(solution)/shard_map/ppermute | solution.py:485
  90.8 0.9 combine.4.refs_3_
  91.7 0.7 collective-permute-start.19
  92.4 0.0 collective-permute-done.16.refs_0_
  92.4 0.9 combine.5.refs_4_
  93.3 0.7 collective-permute-start.18
  94.0 0.9 combine.6.refs_4_
  95.0 0.7 collective-permute-start.24
  95.6 1.3 %collective-permute-start.23 = (bf16[256,512]{1,0:T(8,128)(2,1)S(1)}, bf16[256,512]{1,0:T(8,128)(2,1)S(1)}, u32[]{:S(2)}, u32[]{:S(2)}) collective-permute-start(bf16[256,512]{1,0:T(8,128)(2,1)S(1)} %combine.6.refs_4_), channel_id=1, source_target_pairs={{16,24},{8,20},{21,29},{13,17},{18,26},{10,22},{23,31},{15,19}} | collective-permute-start | bytes 786440 | tf_op jit(solution)/shard_map/ppermute | solution.py:485
  96.9 0.0 collective-permute-done.18.refs_1_
  97.0 0.9 combine.7.refs_9_
  97.9 0.7 collective-permute-start.21
  98.6 1.3 %collective-permute-start.20 = (bf16[256,512]{1,0:T(8,128)(2,1)S(1)}, bf16[256,512]{1,0:T(8,128)(2,1)S(1)}, u32[]{:S(2)}, u32[]{:S(2)}) collective-permute-start(bf16[256,512]{1,0:T(8,128)(2,1)S(1)} %combine.7.refs_9_), channel_id=1, source_target_pairs={{16,24},{8,20},{21,29},{13,17},{18,26},{10,22},{23,31},{15,19}} | collective-permute-start | bytes 786440 | tf_op jit(solution)/shard_map/ppermute | solution.py:485
  99.9 0.0 collective-permute-done.22.refs_5_
  99.9 9.9 %collective-permute-done.23.refs_2_ = bf16[256,512]{1,0:T(8,128)(2,1)S(1)} collective-permute-done((bf16[256,512]{1,0:T(8,128)(2,1)S(1)}, bf16[256,512]{1,0:T(8,128)(2,1)S(1)}, u32[]{:S(2)}, u32[]{:S(2)}) %collective-permute-start.23) | collective-permute-done | bytes 262176 | tf_op jit(solution)/shard_map/ppermute | solution.py:485
  109.8 5.8 %finish.2.refs_10_ = f32[2,2,4,256,256]{4,3,2,1,0:T(8,128)} custom-call(bf16[256,512]{1,0:T(8,128)(2,1)S(1)} %collective-permute-done.17.refs_0_, bf16[256,512]{1,0:T(8,128)(2,1)S(1)} %collective-permute-done.19.refs_1_, bf16[256,512]{1,0:T(8,128)(2,1)S(1)} %collective-permute-done.23.refs_2_, bf16[256,512]{1,0:T(8,128)(2,1)S(1)} %collective-permute-done.24.refs_3_, ...), custom_call_target="tpu_custom_call" | custom-call | tf_op jit(solution)/shard_map/finish/pallas_call | solution.py:459
  115.6 5.9 %finish.3 = f32[2,2,4,256,256]{4,3,2,1,0:T(8,128)} custom-call(bf16[256,512]{1,0:T(8,128)(2,1)S(1)} %collective-permute-done.16.refs_0_, bf16[256,512]{1,0:T(8,128)(2,1)S(1)} %collective-permute-done.18.refs_1_, bf16[256,512]{1,0:T(8,128)(2,1)S(1)} %collective-permute-done.20.refs_2_, ...), custom_call_target="tpu_custom_call", output_to_operand_aliasing={{}: (10, {})} | custom-call | tf_op jit(solution)/shard_map/finish/pallas_call | solution.py:459
  (16 shorter events, 0.2 us)
Async XLA Ops:
  2.3 20.5 %collective-permute-start.6 = (bf16[2,2,2,3,64,256]{5,4,3,2,1,0:T(8,128)(2,1)S(1)}, bf16[2,2,2,3,64,256]{5,4,3,2,1,0:T(8,128)(2,1)S(1)}, u32[]{:S(2)}, u32[]{:S(2)}) collective-permute-start(bf16[2,2,2,3,64,256]{5,4,3,2,1,0:T(8,128)(2,1)S(1)} %pad_maximum_fusion.2), channel_id=1, source_target_pairs={{0,2},{1,3},{2,0},{3,1},{4,6},{5,7},{6,4},{7,5},{8,10},{9,11},{10,... | collective-permute-start | bytes 2359304 | tf_op jit(solution)/shard_map/ppermute | solution.py:475
  3.9 1.6 %copy-start = (bf16[2,2,4,256,256]{4,3,2,1,0:T(8,128)(2,1)S(1)}, bf16[2,2,4,256,256]{4,3,2,1,0:T(8,128)(2,1)}, u32[]{:S(2)}) copy-start(bf16[2,2,4,256,256]{4,3,2,1,0:T(8,128)(2,1)} %refs_4_.3) | copy-start | bytes 6291460
  3.9 1.9 %copy-start.1 = (bf16[2,4,256,256]{3,2,1,0:T(8,128)(2,1)S(1)}, bf16[2,4,256,256]{3,2,1,0:T(8,128)(2,1)}, u32[]{:S(2)}) copy-start(bf16[2,4,256,256]{3,2,1,0:T(8,128)(2,1)} %refs_1_.1) | copy-start | bytes 3145732
  3.9 18.8 %collective-permute-start.5 = (bf16[2,2,2,3,64,256]{5,4,3,2,1,0:T(8,128)(2,1)S(1)}, bf16[2,2,2,3,64,256]{5,4,3,2,1,0:T(8,128)(2,1)S(1)}, u32[]{:S(2)}, u32[]{:S(2)}) collective-permute-start(bf16[2,2,2,3,64,256]{5,4,3,2,1,0:T(8,128)(2,1)S(1)} %pad_maximum_fusion.1), channel_id=1, source_target_pairs={{0,1},{1,0},{2,3},{3,2},{4,5},{5,4},{6,7},{7,6},{8,9},{9,8},{10,11... | collective-permute-start | bytes 2359304 | tf_op jit(solution)/shard_map/ppermute | solution.py:475
  4.1 34.6 %collective-permute-start.7 = (bf16[2,2,2,3,64,256]{5,4,3,2,1,0:T(8,128)(2,1)S(1)}, bf16[2,2,2,3,64,256]{5,4,3,2,1,0:T(8,128)(2,1)S(1)}, u32[]{:S(2)}, u32[]{:S(2)}) collective-permute-start(bf16[2,2,2,3,64,256]{5,4,3,2,1,0:T(8,128)(2,1)S(1)} %pad_maximum_fusion.3), channel_id=1, source_target_pairs={{0,3},{1,2},{2,1},{3,0},{4,7},{5,6},{6,5},{7,4},{8,11},{9,10},{10,... | collective-permute-start | bytes 2359304 | tf_op jit(solution)/shard_map/ppermute | solution.py:475
  12.9 31.4 %collective-permute-start.4 = (bf16[2,256,512]{2,1,0:T(8,128)(2,1)S(1)}, bf16[2,256,512]{2,1,0:T(8,128)(2,1)S(1)}, u32[]{:S(2)}, u32[]{:S(2)}) collective-permute-start(bf16[2,256,512]{2,1,0:T(8,128)(2,1)S(1)} %get-tuple-element.63.refs_2_), channel_id=1, source_target_pairs={{0,4},{4,0},{8,12},{12,8},{16,20},{20,16},{24,28},{28,24},{1,5},{5... | collective-permute-start | bytes 1572872 | tf_op jit(solution)/shard_map/ppermute | solution.py:479
  14.5 29.8 %collective-permute-start.3 = (bf16[2,256,512]{2,1,0:T(8,128)(2,1)S(1)}, bf16[2,256,512]{2,1,0:T(8,128)(2,1)S(1)}, u32[]{:S(2)}, u32[]{:S(2)}) collective-permute-start(bf16[2,256,512]{2,1,0:T(8,128)(2,1)S(1)} %get-tuple-element.64.refs_0_), channel_id=1, source_target_pairs={{0,4},{4,0},{8,12},{12,8},{16,20},{20,16},{24,28},{28,24},{1,5},{5... | collective-permute-start | bytes 1572872 | tf_op jit(solution)/shard_map/ppermute | solution.py:479
  22.8 23.1 %collective-permute-start = (bf16[2,2,2,1,64,256]{5,4,3,2,1,0:T(8,128)(2,1)S(1)}, bf16[2,2,2,1,64,256]{5,4,3,2,1,0:T(8,128)(2,1)S(1)}, u32[]{:S(2)}, u32[]{:S(2)}) collective-permute-start(bf16[2,2,2,1,64,256]{5,4,3,2,1,0:T(8,128)(2,1)S(1)} %pad_maximum_fusion.5), channel_id=1, source_target_pairs={{0,1},{1,0},{2,3},{3,2},{4,5},{5,4},{6,7},{7,6},{8,9},{9,8},{10,11... | collective-permute-start | bytes 786440 | tf_op jit(solution)/shard_map/ppermute | solution.py:475
  22.8 23.1 %collective-permute-start.1 = (bf16[2,2,2,1,64,256]{5,4,3,2,1,0:T(8,128)(2,1)S(1)}, bf16[2,2,2,1,64,256]{5,4,3,2,1,0:T(8,128)(2,1)S(1)}, u32[]{:S(2)}, u32[]{:S(2)}) collective-permute-start(bf16[2,2,2,1,64,256]{5,4,3,2,1,0:T(8,128)(2,1)S(1)} %pad_maximum_fusion.6), channel_id=1, source_target_pairs={{0,2},{1,3},{2,0},{3,1},{4,6},{5,7},{6,4},{7,5},{8,10},{9,11},{10,... | collective-permute-start | bytes 786440 | tf_op jit(solution)/shard_map/ppermute | solution.py:475
  38.7 10.1 %collective-permute-start.2 = (bf16[2,2,2,1,64,256]{5,4,3,2,1,0:T(8,128)(2,1)S(1)}, bf16[2,2,2,1,64,256]{5,4,3,2,1,0:T(8,128)(2,1)S(1)}, u32[]{:S(2)}, u32[]{:S(2)}) collective-permute-start(bf16[2,2,2,1,64,256]{5,4,3,2,1,0:T(8,128)(2,1)S(1)} %pad_maximum_fusion.7), channel_id=1, source_target_pairs={{0,3},{1,2},{2,1},{3,0},{4,7},{5,6},{6,5},{7,4},{8,11},{9,10},{10,... | collective-permute-start | bytes 786440 | tf_op jit(solution)/shard_map/ppermute | solution.py:475
  49.9 4.5 %collective-permute-start.11 = (bf16[4,2,64,256]{3,2,1,0:T(8,128)(2,1)S(1)}, bf16[4,2,64,256]{3,2,1,0:T(8,128)(2,1)S(1)}, u32[]{:S(2)}, u32[]{:S(2)}) collective-permute-start(bf16[4,2,64,256]{3,2,1,0:T(8,128)(2,1)S(1)} %get-tuple-element.50), channel_id=1, source_target_pairs={{0,1},{1,0},{2,3},{3,2},{4,5},{5,4},{6,7},{7,6},{8,9},{9,8},{10,11... | collective-permute-start | bytes 786440 | tf_op jit(solution)/shard_map/ppermute | solution.py:475
  50.7 9.2 %collective-permute-start.12 = (bf16[4,2,64,256]{3,2,1,0:T(8,128)(2,1)S(1)}, bf16[4,2,64,256]{3,2,1,0:T(8,128)(2,1)S(1)}, u32[]{:S(2)}, u32[]{:S(2)}) collective-permute-start(bf16[4,2,64,256]{3,2,1,0:T(8,128)(2,1)S(1)} %get-tuple-element.51), channel_id=1, source_target_pairs={{0,2},{1,3},{2,0},{3,1},{4,6},{5,7},{6,4},{7,5},{8,10},{9,11},{10,... | collective-permute-start | bytes 786440 | tf_op jit(solution)/shard_map/ppermute | solution.py:475
  52.2 12.3 %collective-permute-start.13 = (bf16[4,2,64,256]{3,2,1,0:T(8,128)(2,1)S(1)}, bf16[4,2,64,256]{3,2,1,0:T(8,128)(2,1)S(1)}, u32[]{:S(2)}, u32[]{:S(2)}) collective-permute-start(bf16[4,2,64,256]{3,2,1,0:T(8,128)(2,1)S(1)} %get-tuple-element.52), channel_id=1, source_target_pairs={{0,3},{1,2},{2,1},{3,0},{4,7},{5,6},{6,5},{7,4},{8,11},{9,10},{10,... | collective-permute-start | bytes 786440 | tf_op jit(solution)/shard_map/ppermute | solution.py:475
  52.2 17.9 %collective-permute-start.8 = (bf16[4,2,64,256]{3,2,1,0:T(8,128)(2,1)S(1)}, bf16[4,2,64,256]{3,2,1,0:T(8,128)(2,1)S(1)}, u32[]{:S(2)}, u32[]{:S(2)}) collective-permute-start(bf16[4,2,64,256]{3,2,1,0:T(8,128)(2,1)S(1)} %get-tuple-element.46), channel_id=1, source_target_pairs={{0,1},{1,0},{2,3},{3,2},{4,5},{5,4},{6,7},{7,6},{8,9},{9,8},{10,11... | collective-permute-start | bytes 786440 | tf_op jit(solution)/shard_map/ppermute | solution.py:475
  52.9 18.3 %collective-permute-start.9 = (bf16[4,2,64,256]{3,2,1,0:T(8,128)(2,1)S(1)}, bf16[4,2,64,256]{3,2,1,0:T(8,128)(2,1)S(1)}, u32[]{:S(2)}, u32[]{:S(2)}) collective-permute-start(bf16[4,2,64,256]{3,2,1,0:T(8,128)(2,1)S(1)} %get-tuple-element.47), channel_id=1, source_target_pairs={{0,2},{1,3},{2,0},{3,1},{4,6},{5,7},{6,4},{7,5},{8,10},{9,11},{10,... | collective-permute-start | bytes 786440 | tf_op jit(solution)/shard_map/ppermute | solution.py:475
  54.4 20.6 %collective-permute-start.10 = (bf16[4,2,64,256]{3,2,1,0:T(8,128)(2,1)S(1)}, bf16[4,2,64,256]{3,2,1,0:T(8,128)(2,1)S(1)}, u32[]{:S(2)}, u32[]{:S(2)}) collective-permute-start(bf16[4,2,64,256]{3,2,1,0:T(8,128)(2,1)S(1)} %get-tuple-element.48), channel_id=1, source_target_pairs={{0,3},{1,2},{2,1},{3,0},{4,7},{5,6},{6,5},{7,4},{8,11},{9,10},{10,... | collective-permute-start | bytes 786440 | tf_op jit(solution)/shard_map/ppermute | solution.py:475
  68.9 11.7 %collective-permute-start.15 = (bf16[256,512]{1,0:T(8,128)(2,1)S(1)}, bf16[256,512]{1,0:T(8,128)(2,1)S(1)}, u32[]{:S(2)}, u32[]{:S(2)}) collective-permute-start(bf16[256,512]{1,0:T(8,128)(2,1)S(1)} %get-tuple-element.53.refs_6_.refs_1_.refs_0_), channel_id=1, source_target_pairs={{4,0},{12,8},{20,16},{28,24},{1,5},{9,13},{17,21},{25,29},{6,2},{1... | collective-permute-start | bytes 786440 | tf_op jit(solution)/shard_map/ppermute | solution.py:485
  79.3 8.3 %collective-permute-start.14 = (bf16[256,512]{1,0:T(8,128)(2,1)S(1)}, bf16[256,512]{1,0:T(8,128)(2,1)S(1)}, u32[]{:S(2)}, u32[]{:S(2)}) collective-permute-start(bf16[256,512]{1,0:T(8,128)(2,1)S(1)} %get-tuple-element.54.refs_4_.refs_1_), channel_id=1, source_target_pairs={{4,0},{12,8},{20,16},{28,24},{1,5},{9,13},{17,21},{25,29},{6,2},{1... | collective-permute-start | bytes 786440 | tf_op jit(solution)/shard_map/ppermute | solution.py:485
  81.6 9.2 %collective-permute-start.17 = (bf16[256,512]{1,0:T(8,128)(2,1)S(1)}, bf16[256,512]{1,0:T(8,128)(2,1)S(1)}, u32[]{:S(2)}, u32[]{:S(2)}) collective-permute-start(bf16[256,512]{1,0:T(8,128)(2,1)S(1)} %get-tuple-element.58.refs_4_), channel_id=1, source_target_pairs={{0,8},{5,13},{2,10},{7,15}} | collective-permute-start | bytes 786440 | tf_op jit(solution)/shard_map/ppermute | solution.py:485
  88.5 3.9 %collective-permute-start.16 = (bf16[256,512]{1,0:T(8,128)(2,1)S(1)}, bf16[256,512]{1,0:T(8,128)(2,1)S(1)}, u32[]{:S(2)}, u32[]{:S(2)}) collective-permute-start(bf16[256,512]{1,0:T(8,128)(2,1)S(1)} %get-tuple-element.59.refs_2_), channel_id=1, source_target_pairs={{0,8},{5,13},{2,10},{7,15}} | collective-permute-start | bytes 786440 | tf_op jit(solution)/shard_map/ppermute | solution.py:485
  89.3 10.6 %collective-permute-start.22 = (bf16[2,256,512]{2,1,0:T(8,128)(2,1)S(1)}, bf16[2,256,512]{2,1,0:T(8,128)(2,1)S(1)}, u32[]{:S(2)}, u32[]{:S(2)}) collective-permute-start(bf16[2,256,512]{2,1,0:T(8,128)(2,1)S(1)} %keep.1.refs_3_), channel_id=1, source_target_pairs={{0,4},{8,12},{16,20},{24,28},{2,6},{10,14},{18,22},{26,30}} | collective-permute-start | bytes 1572872 | tf_op jit(solution)/shard_map/ppermute | solution.py:485
  91.7 2.3 %collective-permute-start.19 = (bf16[256,512]{1,0:T(8,128)(2,1)S(1)}, bf16[256,512]{1,0:T(8,128)(2,1)S(1)}, u32[]{:S(2)}, u32[]{:S(2)}) collective-permute-start(bf16[256,512]{1,0:T(8,128)(2,1)S(1)} %combine.4.refs_3_), channel_id=1, source_target_pairs={{8,16},{0,12},{13,21},{5,9},{10,18},{2,14},{15,23},{7,11}} | collective-permute-start | bytes 786440 | tf_op jit(solution)/shard_map/ppermute | solution.py:485
  93.3 3.6 %collective-permute-start.18 = (bf16[256,512]{1,0:T(8,128)(2,1)S(1)}, bf16[256,512]{1,0:T(8,128)(2,1)S(1)}, u32[]{:S(2)}, u32[]{:S(2)}) collective-permute-start(bf16[256,512]{1,0:T(8,128)(2,1)S(1)} %combine.5.refs_4_), channel_id=1, source_target_pairs={{8,16},{0,12},{13,21},{5,9},{10,18},{2,14},{15,23},{7,11}} | collective-permute-start | bytes 786440 | tf_op jit(solution)/shard_map/ppermute | solution.py:485
  95.0 4.9 %collective-permute-start.24 = (bf16[256,512]{1,0:T(8,128)(2,1)S(1)}, bf16[256,512]{1,0:T(8,128)(2,1)S(1)}, u32[]{:S(2)}, u32[]{:S(2)}) collective-permute-start(bf16[256,512]{1,0:T(8,128)(2,1)S(1)} %combine.6.refs_4_), channel_id=1, source_target_pairs={{16,28},{21,25},{18,30},{23,27}} | collective-permute-start | bytes 786440 | tf_op jit(solution)/shard_map/ppermute | solution.py:485
  95.6 14.1 %collective-permute-start.23 = (bf16[256,512]{1,0:T(8,128)(2,1)S(1)}, bf16[256,512]{1,0:T(8,128)(2,1)S(1)}, u32[]{:S(2)}, u32[]{:S(2)}) collective-permute-start(bf16[256,512]{1,0:T(8,128)(2,1)S(1)} %combine.6.refs_4_), channel_id=1, source_target_pairs={{16,24},{8,20},{21,29},{13,17},{18,26},{10,22},{23,31},{15,19}} | collective-permute-start | bytes 786440 | tf_op jit(solution)/shard_map/ppermute | solution.py:485
  97.9 17.7 %collective-permute-start.21 = (bf16[256,512]{1,0:T(8,128)(2,1)S(1)}, bf16[256,512]{1,0:T(8,128)(2,1)S(1)}, u32[]{:S(2)}, u32[]{:S(2)}) collective-permute-start(bf16[256,512]{1,0:T(8,128)(2,1)S(1)} %combine.7.refs_9_), channel_id=1, source_target_pairs={{16,28},{21,25},{18,30},{23,27}} | collective-permute-start | bytes 786440 | tf_op jit(solution)/shard_map/ppermute | solution.py:485
  98.6 17.1 %collective-permute-start.20 = (bf16[256,512]{1,0:T(8,128)(2,1)S(1)}, bf16[256,512]{1,0:T(8,128)(2,1)S(1)}, u32[]{:S(2)}, u32[]{:S(2)}) collective-permute-start(bf16[256,512]{1,0:T(8,128)(2,1)S(1)} %combine.7.refs_9_), channel_id=1, source_target_pairs={{16,24},{8,20},{21,29},{13,17},{18,26},{10,22},{23,31},{15,19}} | collective-permute-start | bytes 786440 | tf_op jit(solution)/shard_map/ppermute | solution.py:485

commit v4 on v3

--- a/solution.py
+++ b/solution.py
@@ -303,8 +303,10 @@
 
 def build_sources(pieces, green, kernels, energy, after):
     slabs, order = green.shape[2:4]
-    return pl.pallas_call(
-        ordered(functools.partial(source_body, range(len(pieces))), len(pieces) + 2),
+    owners = [k for k in range(len(pieces)) if k >= 2] + [k for k in (1, 0) if k < len(pieces)]
+    pieces = [pieces[k] for k in owners]
+    return pl.pallas_call(
+        ordered(functools.partial(source_body, owners), len(pieces) + 2),
         grid=(1,),
         in_specs=[pl.BlockSpec(x.shape, lambda i: (0, 0, 0, 0)) for x in pieces]
         + [
@@ -346,8 +348,9 @@
 
 def pair_body(v_ref, own_ref, sum_ref, t_ref, full_ref, short_ref):
     odd = (lax.axis_index("slab") & 1) == 1
-    x = jnp.where(odd, v_ref[...], own_ref[...])
-    base = jnp.where(odd, sum_ref[...], v_ref[...].astype(F32))
+    theirs = v_ref[...]
+    x = jnp.where(odd, theirs, own_ref[...])
+    base = jnp.where(odd, sum_ref[...], theirs.astype(F32))
     value = base + congruence(t_ref, x)
     full_ref[...] = value
     short_ref[...] = value.astype(BF16)
@@ -392,42 +395,36 @@
     )(*arrived, step, base, after)
 
 
-def keep(blocks, after):
-    count = len(blocks)
-    shape = (count,) + blocks[0].shape
-
-    def body(*refs):
-        for index in range(count):
-            refs[-1][index] = refs[index][...]
-
+def keep(block, after):
+    def body(source, _, out):
+        out[...] = source[...]
+
+    whole = pl.BlockSpec(block.shape, lambda i: (0, 0))
     return pl.pallas_call(
         body,
         grid=(1,),
-        in_specs=[pl.BlockSpec(shape[1:], lambda i: (0, 0))] * count + [ANYWHERE],
-        out_specs=pl.BlockSpec(shape, lambda i: (0, 0, 0)),
-        out_shape=jax.ShapeDtypeStruct(shape, BF16),
+        in_specs=[whole, ANYWHERE],
+        out_specs=whole,
+        out_shape=jax.ShapeDtypeStruct(block.shape, BF16),
         compiler_params=params(),
         cost_estimate=cost(),
         name="keep",
-    )(*blocks, after)
-
-
-def finish_body(arrivals, ours, kept_ref, t_ref, m_ref, base_ref, out, entry):
+    )(block, after)
+
+
+def finish_body(arrivals, ours_ref, kept_ref, t_ref, m_ref, base_ref, out, entry):
     group, _, order, _ = m_ref.shape
 
     @pl.when(pl.program_id(0) == 0)
     def _():
         odd = (lax.axis_index("slab") & 1) == 1
-        before = jnp.where(odd, ours[...].astype(F32) + kept_ref[...].astype(F32), 0.0)
-        entry[...] = before + congruence(t_ref, total(arrivals))
-
-    x_high, x_low = split(entry[...])
-    xh = panel(x_high[:, :order], x_high[:, order:])
-    xl = panel(x_low[:, :order], x_low[:, order:])
-    both = dot(m_ref[...].reshape(group * 2 * order, 2 * order), xh)
+        before = jnp.where(odd, ours_ref[...].astype(F32) + kept_ref[...].astype(F32), 0.0)
+        entry[...] = (before + congruence(t_ref, total(arrivals))).astype(BF16)
+
+    both = dot(m_ref[...].reshape(group * 2 * order, 2 * order), panel(entry[:, :order], entry[:, order:]))
     for index in range(group):
         first = 2 * index * order
-        inner = both[first : first + order] + both[first + order : first + 2 * order] + dot(m_ref[index, 0], xl)
+        inner = both[first : first + order] + both[first + order : first + 2 * order]
         value = times_adjoint(inner, m_ref[index, 0], m_ref[index, 1]) + base_ref[index]
         out[0, index] = value[:, :order]
         out[1, index] = value[:, order:]
@@ -439,8 +436,7 @@
     whole = pl.BlockSpec((order, 2 * order), lambda s: (0, 0))
     step, step_spec = one_map(inner, energy)
     operands = list(arrived) + [ours, kept, step, prefixes, sums, after]
-    in_specs = [whole] * (len(arrived) + 1) + [
-        pl.BlockSpec((None, order, 2 * order), lambda s: (energy, 0, 0)),
+    in_specs = [whole] * (len(arrived) + 2) + [
         step_spec,
         pl.BlockSpec((None, group, 2, order, 2 * order), lambda s: (energy, s, 0, 0, 0)),
         pl.BlockSpec((group, order, 2 * order), lambda s: (s, 0, 0)),
@@ -453,8 +449,7 @@
         in_specs.append(ANYWHERE)
 
     def body(*refs):
-        fixed = refs[len(arrived) : len(arrived) + 5]
-        finish_body(refs[: len(arrived)], *fixed, *refs[-2:])
+        finish_body(refs[: len(arrived)], *refs[len(arrived) : len(arrived) + 5], *refs[-2:])
 
     return pl.pallas_call(
         body,
@@ -463,7 +458,7 @@
         out_specs=pl.BlockSpec((2, None, group, order, order), lambda s: (0, energy, s, 0, 0)),
         out_shape=jax.ShapeDtypeStruct((2, energies, slabs, order, order), F32),
         input_output_aliases=aliases,
-        scratch_shapes=[pltpu.VMEM((order, 2 * order), F32)],
+        scratch_shapes=[pltpu.VMEM((order, 2 * order), BF16)],
         compiler_params=params(),
         cost_estimate=cost(),
         name="finish",
@@ -549,21 +544,24 @@
 
         return moves
 
-    kept = None
+    kept = [None] * energies
 
     def stage(e, step):
-        nonlocal token, kept
+        nonlocal token
         if step == 0:
             sums[e], own[e] = build_sources(sigma[e], green_retarded, kernels, e, token)
             token = own[e]
             ours[e] = along(own[e], to_carrier)
+            if e < energies - 1:
+                kept[e] = along(own[e], to_second)
         elif step == 1:
-            running[e], carry[e] = pair_sum(ours[e], own[e], sums[e], pair_step, e, token)
+            early = [kept[e]] if kept[e] is not None else []
+            running[e], carry[e] = pair_sum(ours[e], own[e], sums[e], pair_step, e, token, *early)
             token = carry[e]
             arrived[e].append(along(carry[e], onward(0)))
             if e == energies - 1:
-                token = keep(own, token)
-                kept = along(token, to_second)
+                token = keep(own[e], token)
+                kept[e] = along(token, to_second)
         else:
             carry[e] = token = combine(arrived[e], plane, running[e], e, token)
             arrived[e].append(along(carry[e], onward(step - 1)))
@@ -576,7 +574,7 @@
             stage(e, step)
     result = None
     for e in range(energies):
-        result = finish(arrived[e], ours[e], kept, inner, prefixes, sums[e], e, result, token)
+        result = finish(arrived[e], ours[e], kept[e], inner, prefixes, sums[e], e, result, token)
     return result
 
 

time: 122 us -> 120 us (0.984)
  waiting for transfers between devices: 53.5 us -> 50.3 us
  starting transfers between devices: 23.3 us -> 26.2 us
  Pallas kernels: 39.5 us -> 37.7 us
    ppermute x11 -> x12, starting transfers between devices: 10.9 us -> 14.3 us  [along(): return lax.ppermute(x, ('slab', 'energy'), pairs)]
    ppermute x12, waiting for transfers between devices: 38.4 us -> 36.1 us  [swap(): return lax.ppermute(x, 'energy', [(i, i ^ k) for i in range(count)])]
    pallas_call x2, Pallas kernels: 11.7 us -> 9.96 us  [finish(): pl.pallas_call(body, grid=(slabs // group,), in_specs=in_specs, out_specs...]
    ppermute x11 -> x12, waiting for transfers between devices: 15.1 us -> 14.2 us  [along(): return lax.ppermute(x, ('slab', 'energy'), pairs)]
  transfers between devices with their start and end apart: 25 -> 26, of which waited for: 9 -> 9; matrix products, arithmetic and copies ran while one was open for 1% -> 1% of each run, Pallas kernels for 27% -> 26%
where the time goes in v4:
time: 120 us; the launch traced here: 119 us
  waiting for transfers between devices  50.3 us (42%)
  Pallas kernels  37.7 us (31%)
  starting transfers between devices  26.2 us (22%)
  local copies, waits for them, and re-layouts  4.5 us (4%)
    ppermute x12, waiting for transfers between devices, swap(): return lax.ppermute(x, 'energy', [(i, i ^ k) for i in range(count)])  36.1 us
    ppermute x12, starting transfers between devices, along(): return lax.ppermute(x, ('slab', 'energy'), pairs)  14.3 us
    ppermute x12, waiting for transfers between devices, along(): return lax.ppermute(x, ('slab', 'energy'), pairs)  14.2 us
    pallas_call x2, Pallas kernels, finish(): pl.pallas_call(body, grid=(slabs // group,), in_specs=in_specs, out_specs...  9.96 us
    ppermute x12, starting transfers between devices, swap(): return lax.ppermute(x, 'energy', [(i, i ^ k) for i in range(count)])  9.81 us
    pallas_call x2, Pallas kernels, build_sources(): pl.pallas_call(ordered(functools.partial(source_body, owners), len(pieces...  8.65 us
    pallas_call x1, Pallas kernels, build_maps(): pl.pallas_call(lambda *refs: maps_body(*refs[:2], *refs[2 + len(after):])...  7.15 us
    pallas_call x2, Pallas kernels, convolve(): pl.pallas_call(functools.partial(convolve_body, pairs, energies, len(held...  4.83 us
  transfers between devices with their start and end apart: 26, of which 9 were waited for; matrix products, arithmetic and copies ran while one was open for 1% of the time, Pallas kernels for 26%

profile of v4, /device:TPU:24, one launch (start us, length us, event | category | flops | bytes accessed | tf_op | source)
XLA Modules:
  0.0 119.5 jit_solution(14629120771649673196)
XLA Ops:
  0.0 2.2 %dynamic-slice_bitcast_fusion = (bf16[1,2,2,3,64,256]{5,4,3,2,1,0:T(8,128)(2,1)S(1)}, bf16[1,2,2,3,64,256]{5,4,3,2,1,0:T(8,128)(2,1)S(1)}, bf16[1,2,2,3,64,256]{...) fusion(bf16[2,2,4,256,256]{4,3,2,1,0:T(8,128)(2,1)} %param.5, ...), kind=kLoop, calls=%fused_computation.6 | loop fusion | bytes 6291472 | tf_op jit(solution)/shard_map/stack | solution.py:506
  2.2 0.1 pad_maximum_fusion.2
  2.3 1.6 %collective-permute-start.6 = (bf16[2,2,2,3,64,256]{5,4,3,2,1,0:T(8,128)(2,1)S(1)}, bf16[2,2,2,3,64,256]{5,4,3,2,1,0:T(8,128)(2,1)S(1)}, u32[]{:S(2)}, u32[]{:S(2)}) collective-permute-start(bf16[2,2,2,3,64,256]{5,4,3,2,1,0:T(8,128)(2,1)S(1)} %pad_maximum_fusion.2), channel_id=1, source_target_pairs={{0,2},{1,3},{2,0},{3,1},{4,6},{5,7},{6,4},{7,5},{8,10},{9,11},{10,... | collective-permute-start | bytes 2359304 | tf_op jit(solution)/shard_map/ppermute | solution.py:470
  3.9 0.1 pad_maximum_fusion.1
  3.9 0.1 collective-permute-start.5
  4.0 0.1 pad_maximum_fusion.3
  4.1 0.7 collective-permute-start.7
  4.8 0.1 pad_maximum_fusion.refs_2_.refs_0_
  4.8 0.6 copy-done
  5.4 0.3 copy-done.1
  5.7 7.2 %maps.1 = (bf16[2,4,2,256,512]{4,3,2,1,0:T(8,128)(2,1)S(1)}, bf16[2,4,2,256,512]{4,3,2,1,0:T(8,128)(2,1)S(1)}) custom-call(bf16[2,2,4,256,256]{4,3,2,1,0:T(8,128)(2,1)S(1)} %copy-done, bf16[2,4,256,256]{3,2,1,0:T(8,128)(2,1)S(1)} %copy-done.1, bf16[2,2,2,3,64,256]{5,4,3,2,1,0:T(8,128)(2,1)S(1)} %pad_maximum_fusion.refs_2_.refs_0_), custom_call_target="tpu_custom_call" | custom-call | tf_op jit(solution)/shard_map/maps/pallas_call | solution.py:142
  12.9 0.1 slice_bitcast_fusion
  12.9 1.6 %collective-permute-start.4 = (bf16[2,256,512]{2,1,0:T(8,128)(2,1)S(1)}, bf16[2,256,512]{2,1,0:T(8,128)(2,1)S(1)}, u32[]{:S(2)}, u32[]{:S(2)}) collective-permute-start(bf16[2,256,512]{2,1,0:T(8,128)(2,1)S(1)} %get-tuple-element.63.refs_2_), channel_id=1, source_target_pairs={{0,4},{4,0},{8,12},{12,8},{16,20},{20,16},{24,28},{28,24},{1,5},{5... | collective-permute-start | bytes 1572872 | tf_op jit(solution)/shard_map/ppermute | solution.py:474
  14.5 0.5 collective-permute-start.3
  15.0 1.4 %dynamic-slice_bitcast_fusion.8 = (bf16[1,2,2,1,64,256]{5,4,3,2,1,0:T(8,128)(2,1)S(1)}, bf16[1,2,2,1,64,256]{5,4,3,2,1,0:T(8,128)(2,1)S(1)}, bf16[1,2,2,1,64,256...) fusion(bf16[2,2,4,256,256]{4,3,2,1,0:T(8,128)(2,1)} %param.5, ...), kind=kLoop, calls=%fused_computation.18 | loop fusion | bytes 2097168 | tf_op jit(solution)/shard_map/stack | solution.py:506
  16.5 6.2 %collective-permute-done.6.refs_2_ = bf16[2,2,2,3,64,256]{5,4,3,2,1,0:T(8,128)(2,1)S(1)} collective-permute-done((bf16[2,2,2,3,64,256]{5,4,3,2,1,0:T(8,128)(2,1)S(1)}, bf16[2,2,2,3,64,256]{5,4,3,2,1,0:T(8,128)(2,1)S(1)}, u32[]{:S(2)}, u32[]{:S(2)}) %collective-permute-start.6) | collective-permute-done | bytes 786464 | tf_op jit(solution)/shard_map/ppermute | solution.py:470
  22.8 0.0 collective-permute-start
  22.8 0.0 collective-permute-done.5.refs_1_
  22.8 1.5 %collective-permute-start.1 = (bf16[2,2,2,1,64,256]{5,4,3,2,1,0:T(8,128)(2,1)S(1)}, bf16[2,2,2,1,64,256]{5,4,3,2,1,0:T(8,128)(2,1)S(1)}, u32[]{:S(2)}, u32[]{:S(2)}) collective-permute-start(bf16[2,2,2,1,64,256]{5,4,3,2,1,0:T(8,128)(2,1)S(1)} %pad_maximum_fusion.6), channel_id=1, source_target_pairs={{0,2},{1,3},{2,0},{3,1},{4,6},{5,7},{6,4},{7,5},{8,10},{9,11},{10,... | collective-permute-start | bytes 786440 | tf_op jit(solution)/shard_map/ppermute | solution.py:470
  24.3 14.4 %collective-permute-done.7.refs_3_ = bf16[2,2,2,3,64,256]{5,4,3,2,1,0:T(8,128)(2,1)S(1)} collective-permute-done((bf16[2,2,2,3,64,256]{5,4,3,2,1,0:T(8,128)(2,1)S(1)}, bf16[2,2,2,3,64,256]{5,4,3,2,1,0:T(8,128)(2,1)S(1)}, u32[]{:S(2)}, u32[]{:S(2)}) %collective-permute-start.7) | collective-permute-done | bytes 786464 | tf_op jit(solution)/shard_map/ppermute | solution.py:470
  38.7 1.9 %collective-permute-start.2 = (bf16[2,2,2,1,64,256]{5,4,3,2,1,0:T(8,128)(2,1)S(1)}, bf16[2,2,2,1,64,256]{5,4,3,2,1,0:T(8,128)(2,1)S(1)}, u32[]{:S(2)}, u32[]{:S(2)}) collective-permute-start(bf16[2,2,2,1,64,256]{5,4,3,2,1,0:T(8,128)(2,1)S(1)} %pad_maximum_fusion.7), channel_id=1, source_target_pairs={{0,3},{1,2},{2,1},{3,0},{4,7},{5,6},{6,5},{7,4},{8,11},{9,10},{10,... | collective-permute-start | bytes 786440 | tf_op jit(solution)/shard_map/ppermute | solution.py:470
  40.6 3.7 %convolve.2 = (bf16[4,2,64,256]{3,2,1,0:T(8,128)(2,1)S(1)}, bf16[4,2,64,256]{3,2,1,0:T(8,128)(2,1)S(1)}, bf16[4,2,64,256]{3,2,1,0:T(8,128)(2,1)S(1)}, bf16[4,2,6...) custom-call(bf16[2,2,2,3,64,256]{5,4,3,2,1,0:T(8,128)(2,1)S(1)} %pad, ...), custom_call_target="tpu_custom_call" | custom-call | tf_op jit(solution)/shard_map/convolve/pallas_call | solution.py:261
  44.3 0.0 collective-permute-done.3.refs_1_
  44.3 1.5 %pair_maps.1 = (bf16[2,2,256,512]{3,2,1,0:T(8,128)(2,1)S(1)}, bf16[2,2,256,512]{3,2,1,0:T(8,128)(2,1)S(1)}, bf16[2,2,256,512]{3,2,1,0:T(8,128)(2,1)S(1)}) custom-call(bf16[2,256,512]{2,1,0:T(8,128)(2,1)S(1)} %get-tuple-element.64.refs_0_, bf16[2,256,512]{2,1,0:T(8,128)(2,1)S(1)} %collective-permute-done.3.refs_1_, ...), custom_call_target="tpu_custom_call" | custom-call | tf_op jit(solution)/shard_map/pair_maps/pallas_call | solution.py:186
  45.8 0.0 collective-permute-done.refs_1_
  45.9 2.9 %collective-permute-done.2.refs_3_ = bf16[2,2,2,1,64,256]{5,4,3,2,1,0:T(8,128)(2,1)S(1)} collective-permute-done((bf16[2,2,2,1,64,256]{5,4,3,2,1,0:T(8,128)(2,1)S(1)}, bf16[2,2,2,1,64,256]{5,4,3,2,1,0:T(8,128)(2,1)S(1)}, u32[]{:S(2)}, u32[]{:S(2)}) %collective-permute-start.2) | collective-permute-done | bytes 262176 | tf_op jit(solution)/shard_map/ppermute | solution.py:470
  48.7 1.1 convolve.3
  49.9 1.4 %collective-permute-start.11 = (bf16[4,2,64,256]{3,2,1,0:T(8,128)(2,1)S(1)}, bf16[4,2,64,256]{3,2,1,0:T(8,128)(2,1)S(1)}, u32[]{:S(2)}, u32[]{:S(2)}) collective-permute-start(bf16[4,2,64,256]{3,2,1,0:T(8,128)(2,1)S(1)} %get-tuple-element.49), channel_id=1, source_target_pairs={{0,2},{1,3},{2,0},{3,1},{4,6},{5,7},{6,4},{7,5},{8,10},{9,11},{10,... | collective-permute-start | bytes 786440 | tf_op jit(solution)/shard_map/ppermute | solution.py:470
  51.3 0.8 collective-permute-start.12
  52.1 0.0 collective-permute-start.13
  52.1 1.5 %collective-permute-start.8 = (bf16[4,2,64,256]{3,2,1,0:T(8,128)(2,1)S(1)}, bf16[4,2,64,256]{3,2,1,0:T(8,128)(2,1)S(1)}, u32[]{:S(2)}, u32[]{:S(2)}) collective-permute-start(bf16[4,2,64,256]{3,2,1,0:T(8,128)(2,1)S(1)} %get-tuple-element.45), channel_id=1, source_target_pairs={{0,2},{1,3},{2,0},{3,1},{4,6},{5,7},{6,4},{7,5},{8,10},{9,11},{10,... | collective-permute-start | bytes 786440 | tf_op jit(solution)/shard_map/ppermute | solution.py:470
  53.6 0.3 collective-permute-start.9
  53.9 5.2 %collective-permute-done.11.refs_0_ = bf16[4,2,64,256]{3,2,1,0:T(8,128)(2,1)S(1)} collective-permute-done((bf16[4,2,64,256]{3,2,1,0:T(8,128)(2,1)S(1)}, bf16[4,2,64,256]{3,2,1,0:T(8,128)(2,1)S(1)}, u32[]{:S(2)}, u32[]{:S(2)}) %collective-permute-start.11) | collective-permute-done | bytes 262176 | tf_op jit(solution)/shard_map/ppermute | solution.py:470
  59.1 5.2 %collective-permute-done.12.refs_1_ = bf16[4,2,64,256]{3,2,1,0:T(8,128)(2,1)S(1)} collective-permute-done((bf16[4,2,64,256]{3,2,1,0:T(8,128)(2,1)S(1)}, bf16[4,2,64,256]{3,2,1,0:T(8,128)(2,1)S(1)}, u32[]{:S(2)}, u32[]{:S(2)}) %collective-permute-start.12) | collective-permute-done | bytes 262176 | tf_op jit(solution)/shard_map/ppermute | solution.py:470
  64.4 0.0 collective-permute-done.13.refs_2_
  64.4 4.3 %sources.2 = (f32[4,256,512]{2,1,0:T(8,128)S(1)}, bf16[256,512]{1,0:T(8,128)(2,1)S(1)}) custom-call(bf16[4,2,64,256]{3,2,1,0:T(8,128)(2,1)S(1)} %collective-permute-done.11.refs_0_, bf16[4,2,64,256]{3,2,1,0:T(8,128)(2,1)S(1)} %collective-permute-done.12.refs_1_, bf16[4,2,64,256]{3,2,1,0:T(8,128)(2,1)S(1)} %collective-permute-done.13.refs_2_, ...), custom_call_target="tpu_custom_call" | custom-call | tf_op jit(solution)/shard_map/sources/pallas_call | solution.py:308
  68.7 3.4 %collective-permute-start.16 = (bf16[256,512]{1,0:T(8,128)(2,1)S(1)}, bf16[256,512]{1,0:T(8,128)(2,1)S(1)}, u32[]{:S(2)}, u32[]{:S(2)}) collective-permute-start(bf16[256,512]{1,0:T(8,128)(2,1)S(1)} %get-tuple-element.53.refs_6_.refs_1_), channel_id=1, source_target_pairs={{0,4},{8,12},{16,20},{24,28},{2,6},{10,14},{18,22},{26,30}} | collective-permute-start | bytes 786440 | tf_op jit(solution)/shard_map/ppermute | solution.py:480
  72.1 1.3 %collective-permute-start.15 = (bf16[256,512]{1,0:T(8,128)(2,1)S(1)}, bf16[256,512]{1,0:T(8,128)(2,1)S(1)}, u32[]{:S(2)}, u32[]{:S(2)}) collective-permute-start(bf16[256,512]{1,0:T(8,128)(2,1)S(1)} %get-tuple-element.53.refs_6_.refs_1_), channel_id=1, source_target_pairs={{4,0},{12,8},{20,16},{28,24},{1,5},{9,13},{17,21},{25,29},{6,2},{1... | collective-permute-start | bytes 786440 | tf_op jit(solution)/shard_map/ppermute | solution.py:480
  73.4 2.2 %collective-permute-done.9.refs_1_ = bf16[4,2,64,256]{3,2,1,0:T(8,128)(2,1)S(1)} collective-permute-done((bf16[4,2,64,256]{3,2,1,0:T(8,128)(2,1)S(1)}, bf16[4,2,64,256]{3,2,1,0:T(8,128)(2,1)S(1)}, u32[]{:S(2)}, u32[]{:S(2)}) %collective-permute-start.9) | collective-permute-done | bytes 262176 | tf_op jit(solution)/shard_map/ppermute | solution.py:470
  75.6 0.0 collective-permute-done.10.refs_2_
  75.6 4.3 %sources.3 = (f32[4,256,512]{2,1,0:T(8,128)S(1)}, bf16[256,512]{1,0:T(8,128)(2,1)S(1)}) custom-call(bf16[4,2,64,256]{3,2,1,0:T(8,128)(2,1)S(1)} %collective-permute-done.8.refs_0_, bf16[4,2,64,256]{3,2,1,0:T(8,128)(2,1)S(1)} %collective-permute-done.9.refs_1_, bf16[4,2,64,256]{3,2,1,0:T(8,128)(2,1)S(1)} %collective-permute-done.10.refs_2_, ...), custom_call_target="tpu_custom_call" | custom-call | tf_op jit(solution)/shard_map/sources/pallas_call | solution.py:308
  79.9 1.3 %collective-permute-start.14 = (bf16[256,512]{1,0:T(8,128)(2,1)S(1)}, bf16[256,512]{1,0:T(8,128)(2,1)S(1)}, u32[]{:S(2)}, u32[]{:S(2)}) collective-permute-start(bf16[256,512]{1,0:T(8,128)(2,1)S(1)} %get-tuple-element.54.refs_4_.refs_1_.source), channel_id=1, source_target_pairs={{4,0},{12,8},{20,16},{28,24},{1,5},{9,13},{17,21},{25,29},{6,2},{1... | collective-permute-start | bytes 786440 | tf_op jit(solution)/shard_map/ppermute | solution.py:480
  81.2 0.0 collective-permute-done.15.refs_0_.refs_4_
  81.2 0.9 pair_sum.2
  82.2 0.9 collective-permute-start.18
  83.1 5.1 %collective-permute-done.14.refs_0_.refs_4_ = bf16[256,512]{1,0:T(8,128)(2,1)S(1)} collective-permute-done((bf16[256,512]{1,0:T(8,128)(2,1)S(1)}, bf16[256,512]{1,0:T(8,128)(2,1)S(1)}, u32[]{:S(2)}, u32[]{:S(2)}) %collective-permute-start.14) | collective-permute-done | bytes 262176 | tf_op jit(solution)/shard_map/ppermute | solution.py:480
  88.2 0.9 pair_sum.3
  89.1 0.7 collective-permute-start.17
  89.9 0.9 combine.4.refs_3_
  90.8 0.7 collective-permute-start.20
  91.5 0.9 combine.5.refs_4_
  92.4 0.7 collective-permute-start.19
  93.1 0.9 combine.6.refs_4_
  94.0 0.7 collective-permute-start.25
  94.7 1.3 %collective-permute-start.24 = (bf16[256,512]{1,0:T(8,128)(2,1)S(1)}, bf16[256,512]{1,0:T(8,128)(2,1)S(1)}, u32[]{:S(2)}, u32[]{:S(2)}) collective-permute-start(bf16[256,512]{1,0:T(8,128)(2,1)S(1)} %combine.6.refs_4_), channel_id=1, source_target_pairs={{16,24},{8,20},{21,29},{13,17},{18,26},{10,22},{23,31},{15,19}} | collective-permute-start | bytes 786440 | tf_op jit(solution)/shard_map/ppermute | solution.py:480
  96.0 1.5 %collective-permute-start.23 = (bf16[256,512]{1,0:T(8,128)(2,1)S(1)}, bf16[256,512]{1,0:T(8,128)(2,1)S(1)}, u32[]{:S(2)}, u32[]{:S(2)}) collective-permute-start(bf16[256,512]{1,0:T(8,128)(2,1)S(1)} %keep.1.refs_3_), channel_id=1, source_target_pairs={{0,4},{8,12},{16,20},{24,28},{2,6},{10,14},{18,22},{26,30}} | collective-permute-start | bytes 786440 | tf_op jit(solution)/shard_map/ppermute | solution.py:480
  97.5 0.9 combine.7.refs_9_
  98.4 0.7 collective-permute-start.22
  99.1 1.3 %collective-permute-start.21 = (bf16[256,512]{1,0:T(8,128)(2,1)S(1)}, bf16[256,512]{1,0:T(8,128)(2,1)S(1)}, u32[]{:S(2)}, u32[]{:S(2)}) collective-permute-start(bf16[256,512]{1,0:T(8,128)(2,1)S(1)} %combine.7.refs_9_), channel_id=1, source_target_pairs={{16,24},{8,20},{21,29},{13,17},{18,26},{10,22},{23,31},{15,19}} | collective-permute-start | bytes 786440 | tf_op jit(solution)/shard_map/ppermute | solution.py:480
  100.4 0.0 collective-permute-done.25.refs_3_
  100.4 8.4 %collective-permute-done.24.refs_2_ = bf16[256,512]{1,0:T(8,128)(2,1)S(1)} collective-permute-done((bf16[256,512]{1,0:T(8,128)(2,1)S(1)}, bf16[256,512]{1,0:T(8,128)(2,1)S(1)}, u32[]{:S(2)}, u32[]{:S(2)}) %collective-permute-start.24) | collective-permute-done | bytes 262176 | tf_op jit(solution)/shard_map/ppermute | solution.py:480
  108.9 5.0 %finish.2.refs_10_ = f32[2,2,4,256,256]{4,3,2,1,0:T(8,128)} custom-call(bf16[256,512]{1,0:T(8,128)(2,1)S(1)} %collective-permute-done.18.refs_0_, bf16[256,512]{1,0:T(8,128)(2,1)S(1)} %collective-permute-done.20.refs_1_, bf16[256,512]{1,0:T(8,128)(2,1)S(1)} %collective-permute-done.24.refs_2_, bf16[256,512]{1,0:T(8,128)(2,1)S(1)} %collective-permute-done.25.refs_3_, ...), custom_call_target="tpu_custom_call" | custom-call | tf_op jit(solution)/shard_map/finish/pallas_call | solution.py:454
  113.9 0.6 collective-permute-done.21.refs_2_
  114.5 5.0 %finish.3 = f32[2,2,4,256,256]{4,3,2,1,0:T(8,128)} custom-call(bf16[256,512]{1,0:T(8,128)(2,1)S(1)} %collective-permute-done.17.refs_0_, bf16[256,512]{1,0:T(8,128)(2,1)S(1)} %collective-permute-done.19.refs_1_, bf16[256,512]{1,0:T(8,128)(2,1)S(1)} %collective-permute-done.21.refs_2_, ...), custom_call_target="tpu_custom_call", output_to_operand_aliasing={{}: (10, {})} | custom-call | tf_op jit(solution)/shard_map/finish/pallas_call | solution.py:454
  (18 shorter events, 0.2 us)
Async XLA Ops:
  2.3 20.5 %collective-permute-start.6 = (bf16[2,2,2,3,64,256]{5,4,3,2,1,0:T(8,128)(2,1)S(1)}, bf16[2,2,2,3,64,256]{5,4,3,2,1,0:T(8,128)(2,1)S(1)}, u32[]{:S(2)}, u32[]{:S(2)}) collective-permute-start(bf16[2,2,2,3,64,256]{5,4,3,2,1,0:T(8,128)(2,1)S(1)} %pad_maximum_fusion.2), channel_id=1, source_target_pairs={{0,2},{1,3},{2,0},{3,1},{4,6},{5,7},{6,4},{7,5},{8,10},{9,11},{10,... | collective-permute-start | bytes 2359304 | tf_op jit(solution)/shard_map/ppermute | solution.py:470
  3.9 1.6 %copy-start = (bf16[2,2,4,256,256]{4,3,2,1,0:T(8,128)(2,1)S(1)}, bf16[2,2,4,256,256]{4,3,2,1,0:T(8,128)(2,1)}, u32[]{:S(2)}) copy-start(bf16[2,2,4,256,256]{4,3,2,1,0:T(8,128)(2,1)} %refs_4_.3) | copy-start | bytes 6291460
  3.9 1.9 %copy-start.1 = (bf16[2,4,256,256]{3,2,1,0:T(8,128)(2,1)S(1)}, bf16[2,4,256,256]{3,2,1,0:T(8,128)(2,1)}, u32[]{:S(2)}) copy-start(bf16[2,4,256,256]{3,2,1,0:T(8,128)(2,1)} %refs_1_.1) | copy-start | bytes 3145732
  3.9 18.8 %collective-permute-start.5 = (bf16[2,2,2,3,64,256]{5,4,3,2,1,0:T(8,128)(2,1)S(1)}, bf16[2,2,2,3,64,256]{5,4,3,2,1,0:T(8,128)(2,1)S(1)}, u32[]{:S(2)}, u32[]{:S(2)}) collective-permute-start(bf16[2,2,2,3,64,256]{5,4,3,2,1,0:T(8,128)(2,1)S(1)} %pad_maximum_fusion.1), channel_id=1, source_target_pairs={{0,1},{1,0},{2,3},{3,2},{4,5},{5,4},{6,7},{7,6},{8,9},{9,8},{10,11... | collective-permute-start | bytes 2359304 | tf_op jit(solution)/shard_map/ppermute | solution.py:470
  4.1 34.6 %collective-permute-start.7 = (bf16[2,2,2,3,64,256]{5,4,3,2,1,0:T(8,128)(2,1)S(1)}, bf16[2,2,2,3,64,256]{5,4,3,2,1,0:T(8,128)(2,1)S(1)}, u32[]{:S(2)}, u32[]{:S(2)}) collective-permute-start(bf16[2,2,2,3,64,256]{5,4,3,2,1,0:T(8,128)(2,1)S(1)} %pad_maximum_fusion.3), channel_id=1, source_target_pairs={{0,3},{1,2},{2,1},{3,0},{4,7},{5,6},{6,5},{7,4},{8,11},{9,10},{10,... | collective-permute-start | bytes 2359304 | tf_op jit(solution)/shard_map/ppermute | solution.py:470
  12.9 31.4 %collective-permute-start.4 = (bf16[2,256,512]{2,1,0:T(8,128)(2,1)S(1)}, bf16[2,256,512]{2,1,0:T(8,128)(2,1)S(1)}, u32[]{:S(2)}, u32[]{:S(2)}) collective-permute-start(bf16[2,256,512]{2,1,0:T(8,128)(2,1)S(1)} %get-tuple-element.63.refs_2_), channel_id=1, source_target_pairs={{0,4},{4,0},{8,12},{12,8},{16,20},{20,16},{24,28},{28,24},{1,5},{5... | collective-permute-start | bytes 1572872 | tf_op jit(solution)/shard_map/ppermute | solution.py:474
  14.5 29.8 %collective-permute-start.3 = (bf16[2,256,512]{2,1,0:T(8,128)(2,1)S(1)}, bf16[2,256,512]{2,1,0:T(8,128)(2,1)S(1)}, u32[]{:S(2)}, u32[]{:S(2)}) collective-permute-start(bf16[2,256,512]{2,1,0:T(8,128)(2,1)S(1)} %get-tuple-element.64.refs_0_), channel_id=1, source_target_pairs={{0,4},{4,0},{8,12},{12,8},{16,20},{20,16},{24,28},{28,24},{1,5},{5... | collective-permute-start | bytes 1572872 | tf_op jit(solution)/shard_map/ppermute | solution.py:474
  22.8 23.1 %collective-permute-start = (bf16[2,2,2,1,64,256]{5,4,3,2,1,0:T(8,128)(2,1)S(1)}, bf16[2,2,2,1,64,256]{5,4,3,2,1,0:T(8,128)(2,1)S(1)}, u32[]{:S(2)}, u32[]{:S(2)}) collective-permute-start(bf16[2,2,2,1,64,256]{5,4,3,2,1,0:T(8,128)(2,1)S(1)} %pad_maximum_fusion.5), channel_id=1, source_target_pairs={{0,1},{1,0},{2,3},{3,2},{4,5},{5,4},{6,7},{7,6},{8,9},{9,8},{10,11... | collective-permute-start | bytes 786440 | tf_op jit(solution)/shard_map/ppermute | solution.py:470
  22.8 23.1 %collective-permute-start.1 = (bf16[2,2,2,1,64,256]{5,4,3,2,1,0:T(8,128)(2,1)S(1)}, bf16[2,2,2,1,64,256]{5,4,3,2,1,0:T(8,128)(2,1)S(1)}, u32[]{:S(2)}, u32[]{:S(2)}) collective-permute-start(bf16[2,2,2,1,64,256]{5,4,3,2,1,0:T(8,128)(2,1)S(1)} %pad_maximum_fusion.6), channel_id=1, source_target_pairs={{0,2},{1,3},{2,0},{3,1},{4,6},{5,7},{6,4},{7,5},{8,10},{9,11},{10,... | collective-permute-start | bytes 786440 | tf_op jit(solution)/shard_map/ppermute | solution.py:470
  38.7 10.1 %collective-permute-start.2 = (bf16[2,2,2,1,64,256]{5,4,3,2,1,0:T(8,128)(2,1)S(1)}, bf16[2,2,2,1,64,256]{5,4,3,2,1,0:T(8,128)(2,1)S(1)}, u32[]{:S(2)}, u32[]{:S(2)}) collective-permute-start(bf16[2,2,2,1,64,256]{5,4,3,2,1,0:T(8,128)(2,1)S(1)} %pad_maximum_fusion.7), channel_id=1, source_target_pairs={{0,3},{1,2},{2,1},{3,0},{4,7},{5,6},{6,5},{7,4},{8,11},{9,10},{10,... | collective-permute-start | bytes 786440 | tf_op jit(solution)/shard_map/ppermute | solution.py:470
  49.9 9.2 %collective-permute-start.11 = (bf16[4,2,64,256]{3,2,1,0:T(8,128)(2,1)S(1)}, bf16[4,2,64,256]{3,2,1,0:T(8,128)(2,1)S(1)}, u32[]{:S(2)}, u32[]{:S(2)}) collective-permute-start(bf16[4,2,64,256]{3,2,1,0:T(8,128)(2,1)S(1)} %get-tuple-element.49), channel_id=1, source_target_pairs={{0,2},{1,3},{2,0},{3,1},{4,6},{5,7},{6,4},{7,5},{8,10},{9,11},{10,... | collective-permute-start | bytes 786440 | tf_op jit(solution)/shard_map/ppermute | solution.py:470
  51.3 13.1 %collective-permute-start.12 = (bf16[4,2,64,256]{3,2,1,0:T(8,128)(2,1)S(1)}, bf16[4,2,64,256]{3,2,1,0:T(8,128)(2,1)S(1)}, u32[]{:S(2)}, u32[]{:S(2)}) collective-permute-start(bf16[4,2,64,256]{3,2,1,0:T(8,128)(2,1)S(1)} %get-tuple-element.50), channel_id=1, source_target_pairs={{0,3},{1,2},{2,1},{3,0},{4,7},{5,6},{6,5},{7,4},{8,11},{9,10},{10,... | collective-permute-start | bytes 786440 | tf_op jit(solution)/shard_map/ppermute | solution.py:470
  52.1 12.3 %collective-permute-start.13 = (bf16[4,2,64,256]{3,2,1,0:T(8,128)(2,1)S(1)}, bf16[4,2,64,256]{3,2,1,0:T(8,128)(2,1)S(1)}, u32[]{:S(2)}, u32[]{:S(2)}) collective-permute-start(bf16[4,2,64,256]{3,2,1,0:T(8,128)(2,1)S(1)} %get-tuple-element.51), channel_id=1, source_target_pairs={{0,1},{1,0},{2,3},{3,2},{4,5},{5,4},{6,7},{7,6},{8,9},{9,8},{10,11... | collective-permute-start | bytes 786440 | tf_op jit(solution)/shard_map/ppermute | solution.py:470
  52.1 21.3 %collective-permute-start.8 = (bf16[4,2,64,256]{3,2,1,0:T(8,128)(2,1)S(1)}, bf16[4,2,64,256]{3,2,1,0:T(8,128)(2,1)S(1)}, u32[]{:S(2)}, u32[]{:S(2)}) collective-permute-start(bf16[4,2,64,256]{3,2,1,0:T(8,128)(2,1)S(1)} %get-tuple-element.45), channel_id=1, source_target_pairs={{0,2},{1,3},{2,0},{3,1},{4,6},{5,7},{6,4},{7,5},{8,10},{9,11},{10,... | collective-permute-start | bytes 786440 | tf_op jit(solution)/shard_map/ppermute | solution.py:470
  53.6 22.0 %collective-permute-start.9 = (bf16[4,2,64,256]{3,2,1,0:T(8,128)(2,1)S(1)}, bf16[4,2,64,256]{3,2,1,0:T(8,128)(2,1)S(1)}, u32[]{:S(2)}, u32[]{:S(2)}) collective-permute-start(bf16[4,2,64,256]{3,2,1,0:T(8,128)(2,1)S(1)} %get-tuple-element.46), channel_id=1, source_target_pairs={{0,3},{1,2},{2,1},{3,0},{4,7},{5,6},{6,5},{7,4},{8,11},{9,10},{10,... | collective-permute-start | bytes 786440 | tf_op jit(solution)/shard_map/ppermute | solution.py:470
  59.1 16.5 %collective-permute-start.10 = (bf16[4,2,64,256]{3,2,1,0:T(8,128)(2,1)S(1)}, bf16[4,2,64,256]{3,2,1,0:T(8,128)(2,1)S(1)}, u32[]{:S(2)}, u32[]{:S(2)}) collective-permute-start(bf16[4,2,64,256]{3,2,1,0:T(8,128)(2,1)S(1)} %get-tuple-element.47), channel_id=1, source_target_pairs={{0,1},{1,0},{2,3},{3,2},{4,5},{5,4},{6,7},{7,6},{8,9},{9,8},{10,11... | collective-permute-start | bytes 786440 | tf_op jit(solution)/shard_map/ppermute | solution.py:470
  68.7 12.5 %collective-permute-start.16 = (bf16[256,512]{1,0:T(8,128)(2,1)S(1)}, bf16[256,512]{1,0:T(8,128)(2,1)S(1)}, u32[]{:S(2)}, u32[]{:S(2)}) collective-permute-start(bf16[256,512]{1,0:T(8,128)(2,1)S(1)} %get-tuple-element.53.refs_6_.refs_1_), channel_id=1, source_target_pairs={{0,4},{8,12},{16,20},{24,28},{2,6},{10,14},{18,22},{26,30}} | collective-permute-start | bytes 786440 | tf_op jit(solution)/shard_map/ppermute | solution.py:480
  72.1 9.1 %collective-permute-start.15 = (bf16[256,512]{1,0:T(8,128)(2,1)S(1)}, bf16[256,512]{1,0:T(8,128)(2,1)S(1)}, u32[]{:S(2)}, u32[]{:S(2)}) collective-permute-start(bf16[256,512]{1,0:T(8,128)(2,1)S(1)} %get-tuple-element.53.refs_6_.refs_1_), channel_id=1, source_target_pairs={{4,0},{12,8},{20,16},{28,24},{1,5},{9,13},{17,21},{25,29},{6,2},{1... | collective-permute-start | bytes 786440 | tf_op jit(solution)/shard_map/ppermute | solution.py:480
  79.9 8.3 %collective-permute-start.14 = (bf16[256,512]{1,0:T(8,128)(2,1)S(1)}, bf16[256,512]{1,0:T(8,128)(2,1)S(1)}, u32[]{:S(2)}, u32[]{:S(2)}) collective-permute-start(bf16[256,512]{1,0:T(8,128)(2,1)S(1)} %get-tuple-element.54.refs_4_.refs_1_.source), channel_id=1, source_target_pairs={{4,0},{12,8},{20,16},{28,24},{1,5},{9,13},{17,21},{25,29},{6,2},{1... | collective-permute-start | bytes 786440 | tf_op jit(solution)/shard_map/ppermute | solution.py:480
  82.2 7.7 %collective-permute-start.18 = (bf16[256,512]{1,0:T(8,128)(2,1)S(1)}, bf16[256,512]{1,0:T(8,128)(2,1)S(1)}, u32[]{:S(2)}, u32[]{:S(2)}) collective-permute-start(bf16[256,512]{1,0:T(8,128)(2,1)S(1)} %get-tuple-element.58.refs_4_), channel_id=1, source_target_pairs={{0,8},{5,13},{2,10},{7,15}} | collective-permute-start | bytes 786440 | tf_op jit(solution)/shard_map/ppermute | solution.py:480
  89.1 2.3 %collective-permute-start.17 = (bf16[256,512]{1,0:T(8,128)(2,1)S(1)}, bf16[256,512]{1,0:T(8,128)(2,1)S(1)}, u32[]{:S(2)}, u32[]{:S(2)}) collective-permute-start(bf16[256,512]{1,0:T(8,128)(2,1)S(1)} %get-tuple-element.59._), channel_id=1, source_target_pairs={{0,8},{5,13},{2,10},{7,15}} | collective-permute-start | bytes 786440 | tf_op jit(solution)/shard_map/ppermute | solution.py:480
  90.8 2.3 %collective-permute-start.20 = (bf16[256,512]{1,0:T(8,128)(2,1)S(1)}, bf16[256,512]{1,0:T(8,128)(2,1)S(1)}, u32[]{:S(2)}, u32[]{:S(2)}) collective-permute-start(bf16[256,512]{1,0:T(8,128)(2,1)S(1)} %combine.4.refs_3_), channel_id=1, source_target_pairs={{8,16},{0,12},{13,21},{5,9},{10,18},{2,14},{15,23},{7,11}} | collective-permute-start | bytes 786440 | tf_op jit(solution)/shard_map/ppermute | solution.py:480
  92.4 5.1 %collective-permute-start.19 = (bf16[256,512]{1,0:T(8,128)(2,1)S(1)}, bf16[256,512]{1,0:T(8,128)(2,1)S(1)}, u32[]{:S(2)}, u32[]{:S(2)}) collective-permute-start(bf16[256,512]{1,0:T(8,128)(2,1)S(1)} %combine.5.refs_4_), channel_id=1, source_target_pairs={{8,16},{0,12},{13,21},{5,9},{10,18},{2,14},{15,23},{7,11}} | collective-permute-start | bytes 786440 | tf_op jit(solution)/shard_map/ppermute | solution.py:480
  94.0 6.4 %collective-permute-start.25 = (bf16[256,512]{1,0:T(8,128)(2,1)S(1)}, bf16[256,512]{1,0:T(8,128)(2,1)S(1)}, u32[]{:S(2)}, u32[]{:S(2)}) collective-permute-start(bf16[256,512]{1,0:T(8,128)(2,1)S(1)} %combine.6.refs_4_), channel_id=1, source_target_pairs={{16,28},{21,25},{18,30},{23,27}} | collective-permute-start | bytes 786440 | tf_op jit(solution)/shard_map/ppermute | solution.py:480
  94.7 14.1 %collective-permute-start.24 = (bf16[256,512]{1,0:T(8,128)(2,1)S(1)}, bf16[256,512]{1,0:T(8,128)(2,1)S(1)}, u32[]{:S(2)}, u32[]{:S(2)}) collective-permute-start(bf16[256,512]{1,0:T(8,128)(2,1)S(1)} %combine.6.refs_4_), channel_id=1, source_target_pairs={{16,24},{8,20},{21,29},{13,17},{18,26},{10,22},{23,31},{15,19}} | collective-permute-start | bytes 786440 | tf_op jit(solution)/shard_map/ppermute | solution.py:480
  96.0 17.8 %collective-permute-start.23 = (bf16[256,512]{1,0:T(8,128)(2,1)S(1)}, bf16[256,512]{1,0:T(8,128)(2,1)S(1)}, u32[]{:S(2)}, u32[]{:S(2)}) collective-permute-start(bf16[256,512]{1,0:T(8,128)(2,1)S(1)} %keep.1.refs_3_), channel_id=1, source_target_pairs={{0,4},{8,12},{16,20},{24,28},{2,6},{10,14},{18,22},{26,30}} | collective-permute-start | bytes 786440 | tf_op jit(solution)/shard_map/ppermute | solution.py:480
  98.4 15.4 %collective-permute-start.22 = (bf16[256,512]{1,0:T(8,128)(2,1)S(1)}, bf16[256,512]{1,0:T(8,128)(2,1)S(1)}, u32[]{:S(2)}, u32[]{:S(2)}) collective-permute-start(bf16[256,512]{1,0:T(8,128)(2,1)S(1)} %combine.7.refs_9_), channel_id=1, source_target_pairs={{16,28},{21,25},{18,30},{23,27}} | collective-permute-start | bytes 786440 | tf_op jit(solution)/shard_map/ppermute | solution.py:480
  99.1 15.4 %collective-permute-start.21 = (bf16[256,512]{1,0:T(8,128)(2,1)S(1)}, bf16[256,512]{1,0:T(8,128)(2,1)S(1)}, u32[]{:S(2)}, u32[]{:S(2)}) collective-permute-start(bf16[256,512]{1,0:T(8,128)(2,1)S(1)} %combine.7.refs_9_), channel_id=1, source_target_pairs={{16,24},{8,20},{21,29},{13,17},{18,26},{10,22},{23,31},{15,19}} | collective-permute-start | bytes 786440 | tf_op jit(solution)/shard_map/ppermute | solution.py:480

commit v5 on v4

--- a/solution.py
+++ b/solution.py
@@ -24,6 +24,7 @@
 
 
 ANYWHERE = pl.BlockSpec(memory_space=pl.ANY)
+WHOLE = pl.BlockSpec(memory_space=pltpu.VMEM)
 
 
 def cost():
@@ -277,7 +278,7 @@
     return outs
 
 
-def source_body(owners, *refs):
+def source_body(energy, owners, *refs):
     pieces = refs[: len(owners)]
     g_ref, k_ref, b_ref, v_ref, sigma = refs[len(owners) :]
     me = lax.axis_index("energy")
@@ -290,11 +291,12 @@
 
     carry = None
     for s in range(sigma.shape[0]):
-        left = jnp.concatenate([g_ref[0, s], g_ref[1, s]], axis=1)
+        green_re, green_im = g_ref[0, energy, s], g_ref[1, energy, s]
+        left = jnp.concatenate([green_re, green_im], axis=1)
         mixed = dot(left, panel(sigma[s, 0], sigma[s, 1])).astype(BF16)
-        source = dot_nt(mixed, panel(g_ref[0, s], g_ref[1, s]))
+        source = dot_nt(mixed, panel(green_re, green_im))
         if carry is not None:
-            high, low = k_ref[s, 0], k_ref[s, 1]
+            high, low = k_ref[energy, s, 0], k_ref[energy, s, 1]
             source = times_adjoint(times_wide(high, low, carry), high, low) + source
         carry = source
         b_ref[s] = carry
@@ -306,18 +308,9 @@
     owners = [k for k in range(len(pieces)) if k >= 2] + [k for k in (1, 0) if k < len(pieces)]
     pieces = [pieces[k] for k in owners]
     return pl.pallas_call(
-        ordered(functools.partial(source_body, owners), len(pieces) + 2),
-        grid=(1,),
-        in_specs=[pl.BlockSpec(x.shape, lambda i: (0, 0, 0, 0)) for x in pieces]
-        + [
-            pl.BlockSpec((2, None, slabs, order, order), lambda i: (0, energy, 0, 0, 0)),
-            pl.BlockSpec((None, slabs, 2, order, 2 * order), lambda i: (energy, 0, 0, 0, 0)),
-            ANYWHERE,
-        ],
-        out_specs=[
-            pl.BlockSpec((slabs, order, 2 * order), lambda i: (0, 0, 0)),
-            pl.BlockSpec((order, 2 * order), lambda i: (0, 0)),
-        ],
+        ordered(functools.partial(source_body, energy, owners), len(pieces) + 2),
+        in_specs=[WHOLE] * (len(pieces) + 2) + [ANYWHERE],
+        out_specs=[WHOLE] * 2,
         out_shape=[
             jax.ShapeDtypeStruct((slabs, order, 2 * order), F32),
             jax.ShapeDtypeStruct((order, 2 * order), BF16),
@@ -339,109 +332,82 @@
     return times_adjoint(inner, high, low)
 
 
-def total(refs):
-    value = refs[0][...]
-    for ref in refs[1:]:
-        value = value + ref[...]
+def entered(refs):
+    pair = lax.axis_index("slab") >> 1
+    value = jnp.zeros(refs[0].shape, refs[0].dtype)
+    for step, ref in enumerate(refs):
+        value = jnp.where(pair == step + 1, ref[...], value)
     return value
 
 
-def pair_body(v_ref, own_ref, sum_ref, t_ref, full_ref, short_ref):
+def pair_body(energy, v_ref, own_ref, sum_ref, t_ref, full_ref, short_ref):
     odd = (lax.axis_index("slab") & 1) == 1
     theirs = v_ref[...]
     x = jnp.where(odd, theirs, own_ref[...])
-    base = jnp.where(odd, sum_ref[...], theirs.astype(F32))
-    value = base + congruence(t_ref, x)
+    base = jnp.where(odd, sum_ref[sum_ref.shape[0] - 1], theirs.astype(F32))
+    value = base + congruence(t_ref.at[energy], x)
     full_ref[...] = value
     short_ref[...] = value.astype(BF16)
 
 
-def pair_sum(arrived, own, sums, maps, energy, *after):
-    slabs, order, _ = sums.shape
-    step, step_spec = one_map(maps, energy)
-    whole = pl.BlockSpec((order, 2 * order), lambda i: (0, 0))
-    return pl.pallas_call(
-        ordered(pair_body, 4, len(after)),
-        grid=(1,),
-        in_specs=[whole, whole, pl.BlockSpec((None, order, 2 * order), lambda i: (slabs - 1, 0, 0)), step_spec]
-        + [ANYWHERE] * len(after),
-        out_specs=[whole] * 2,
+def pair_sum(arrived, own, sums, maps, energy, after):
+    _, order, _ = sums.shape
+    return pl.pallas_call(
+        ordered(functools.partial(pair_body, energy), 4),
+        in_specs=[WHOLE] * 4 + [ANYWHERE],
+        out_specs=[WHOLE] * 2,
         out_shape=[jax.ShapeDtypeStruct((order, 2 * order), t) for t in (F32, BF16)],
         compiler_params=params(),
         cost_estimate=cost(),
         name="pair_sum",
-    )(arrived, own, sums, step, *after)
+    )(arrived, own, sums, maps, after)
 
 
 def combine(arrived, maps, base, energy, after):
-    order = base.shape[0]
-    step, step_spec = one_map(maps, energy)
-    whole = pl.BlockSpec((order, 2 * order), lambda i: (0, 0))
     count = len(arrived)
 
     def body(*refs):
         t_ref, base_ref, _, out = refs[count:]
-        out[...] = (base_ref[...] + congruence(t_ref, total(refs[:count]))).astype(BF16)
+        out[...] = (base_ref[...] + congruence(t_ref.at[energy], entered(refs[:count]))).astype(BF16)
 
     return pl.pallas_call(
         body,
-        grid=(1,),
-        in_specs=[whole] * count + [step_spec, whole, ANYWHERE],
-        out_specs=whole,
-        out_shape=jax.ShapeDtypeStruct((order, 2 * order), BF16),
+        in_specs=[WHOLE] * (count + 2) + [ANYWHERE],
+        out_specs=WHOLE,
+        out_shape=jax.ShapeDtypeStruct(base.shape, BF16),
         compiler_params=params(),
         cost_estimate=cost(),
         name="combine",
-    )(*arrived, step, base, after)
-
-
-def keep(block, after):
-    def body(source, _, out):
-        out[...] = source[...]
-
-    whole = pl.BlockSpec(block.shape, lambda i: (0, 0))
-    return pl.pallas_call(
-        body,
-        grid=(1,),
-        in_specs=[whole, ANYWHERE],
-        out_specs=whole,
-        out_shape=jax.ShapeDtypeStruct(block.shape, BF16),
-        compiler_params=params(),
-        cost_estimate=cost(),
-        name="keep",
-    )(block, after)
-
-
-def finish_body(arrivals, ours_ref, kept_ref, t_ref, m_ref, base_ref, out, entry):
-    group, _, order, _ = m_ref.shape
-
-    @pl.when(pl.program_id(0) == 0)
-    def _():
-        odd = (lax.axis_index("slab") & 1) == 1
-        before = jnp.where(odd, ours_ref[...].astype(F32) + kept_ref[...].astype(F32), 0.0)
-        entry[...] = (before + congruence(t_ref, total(arrivals))).astype(BF16)
-
-    both = dot(m_ref[...].reshape(group * 2 * order, 2 * order), panel(entry[:, :order], entry[:, order:]))
-    for index in range(group):
-        first = 2 * index * order
+    )(*arrived, maps, base, after)
+
+
+def finish_body(energy, arrivals, before_ref, t_ref, m_ref, base_ref, out, blocks, sems):
+    slabs, order, _ = base_ref.shape
+    odd = (lax.axis_index("slab") & 1) == 1
+    before = jnp.where(odd, before_ref[...].astype(F32), 0.0)
+    entry = (before + congruence(t_ref.at[energy], entered(arrivals))).astype(BF16)
+    maps = m_ref.at[energy]
+    rows = maps[...].reshape(slabs * 2 * order, 2 * order)
+    both = dot(rows, panel(entry[:, :order], entry[:, order:]))
+    copies = []
+    for s in range(slabs):
+        first = 2 * s * order
         inner = both[first : first + order] + both[first + order : first + 2 * order]
-        value = times_adjoint(inner, m_ref[index, 0], m_ref[index, 1]) + base_ref[index]
-        out[0, index] = value[:, :order]
-        out[1, index] = value[:, order:]
-
-
-def finish(arrived, ours, kept, inner, prefixes, sums, energy, held, after):
+        value = times_adjoint(inner, maps[s, 0], maps[s, 1]) + base_ref[s]
+        blocks[s, 0] = value[:, :order]
+        blocks[s, 1] = value[:, order:]
+        copies.append(pltpu.make_async_copy(blocks.at[s], out.at[:, energy, s], sems.at[s]))
+        copies[-1].start()
+    for copy in copies:
+        copy.wait()
+
+
+def finish(arrived, before, inner, prefixes, sums, energy, held, after):
     energies, slabs, _, order, _ = prefixes.shape
-    group = 2 if slabs % 2 == 0 else 1
-    whole = pl.BlockSpec((order, 2 * order), lambda s: (0, 0))
-    step, step_spec = one_map(inner, energy)
-    operands = list(arrived) + [ours, kept, step, prefixes, sums, after]
-    in_specs = [whole] * (len(arrived) + 2) + [
-        step_spec,
-        pl.BlockSpec((None, group, 2, order, 2 * order), lambda s: (energy, s, 0, 0, 0)),
-        pl.BlockSpec((group, order, 2 * order), lambda s: (s, 0, 0)),
-        ANYWHERE,
-    ]
+    operands = list(arrived) + [before, inner, prefixes, sums]
+    count = len(operands)
+    in_specs = [WHOLE] * count + [ANYWHERE]
+    operands.append(after)
     aliases = {}
     if held is not None:
         aliases = {len(operands): 0}
@@ -449,16 +415,15 @@
         in_specs.append(ANYWHERE)
 
     def body(*refs):
-        finish_body(refs[: len(arrived)], *refs[len(arrived) : len(arrived) + 5], *refs[-2:])
+        finish_body(energy, refs[: len(arrived)], *refs[len(arrived) : count], *refs[-3:])
 
     return pl.pallas_call(
         body,
-        grid=(slabs // group,),
         in_specs=in_specs,
-        out_specs=pl.BlockSpec((2, None, group, order, order), lambda s: (0, energy, s, 0, 0)),
+        out_specs=ANYWHERE,
         out_shape=jax.ShapeDtypeStruct((2, energies, slabs, order, order), F32),
         input_output_aliases=aliases,
-        scratch_shapes=[pltpu.VMEM((order, 2 * order), BF16)],
+        scratch_shapes=[pltpu.VMEM((slabs, 2, order, order), F32), pltpu.SemaphoreType.DMA((slabs,))],
         compiler_params=params(),
         cost_estimate=cost(),
         name="finish",
@@ -474,10 +439,8 @@
     return lax.ppermute(x, "slab", [(i, i ^ 1) for i in range(lax.axis_size("slab"))])
 
 
-def along(x, moves):
-    count = lax.axis_size("energy")
-    pairs = [(i * count + n, j * count + n) for n in range(count) for i, j in moves(n & 1)]
-    return lax.ppermute(x, ("slab", "energy"), pairs)
+def forward(x, pair):
+    return lax.ppermute(x, "slab", [(2 * pair + i, 2 * pair + 2 + i) for i in range(2)])
 
 
 def cut(slabs):
@@ -530,43 +493,19 @@
     running, carry = [None] * energies, [None] * energies
     arrived = [[] for _ in range(energies)]
 
-    def to_carrier(lane):
-        return [(2 * z + 1 - lane, 2 * z + lane) for z in range(pairs)]
-
-    def to_second(lane):
-        return [(2 * z, 2 * z + 1) for z in range(pairs)] if lane == 0 else []
-
-    def onward(step):
-        def moves(lane):
-            ahead = [(2 * step + lane, 2 * step + 2 + lane)] if step < pairs - 1 else []
-            aside = [(2 * step - 2 + lane, 2 * step + 1 - lane)] if step > 0 else []
-            return ahead + aside
-
-        return moves
-
-    kept = [None] * energies
-
     def stage(e, step):
         nonlocal token
         if step == 0:
             sums[e], own[e] = build_sources(sigma[e], green_retarded, kernels, e, token)
             token = own[e]
-            ours[e] = along(own[e], to_carrier)
-            if e < energies - 1:
-                kept[e] = along(own[e], to_second)
+            ours[e] = other_of_pair(own[e])
         elif step == 1:
-            early = [kept[e]] if kept[e] is not None else []
-            running[e], carry[e] = pair_sum(ours[e], own[e], sums[e], pair_step, e, token, *early)
+            running[e], carry[e] = pair_sum(ours[e], own[e], sums[e], pair_step, e, token)
             token = carry[e]
-            arrived[e].append(along(carry[e], onward(0)))
-            if e == energies - 1:
-                token = keep(own[e], token)
-                kept[e] = along(token, to_second)
+            arrived[e].append(forward(carry[e], 0))
         else:
             carry[e] = token = combine(arrived[e], plane, running[e], e, token)
-            arrived[e].append(along(carry[e], onward(step - 1)))
-        if step == last:
-            arrived[e].append(along(carry[e], onward(pairs - 1)))
+            arrived[e].append(forward(carry[e], step - 1))
 
     last = max(pairs - 1, 1)
     for step in range(last + 1):
@@ -574,7 +513,7 @@
             stage(e, step)
     result = None
     for e in range(energies):
-        result = finish(arrived[e], ours[e], kept[e], inner, prefixes, sums[e], e, result, token)
+        result = finish(arrived[e], ours[e], inner, prefixes, sums[e], e, result, token)
     return result
 
 

time: 120 us -> 119 us (level)
  waiting for transfers between devices: 50.3 us -> 56.1 us
  starting transfers between devices: 26.2 us -> 20.5 us
    ppermute x12 -> x6, starting transfers between devices: 14.3 us -> 5.47 us  [forward(): lax.ppermute(x, 'slab', [(2 * pair + i, 2 * pair + 2 + i) for i in range(...]
    ppermute x2 -> x4, waiting for transfers between devices: 0.01 us -> 5.23 us  [other_of_pair(): lax.ppermute(x, 'slab', [(i, i ^ 1) for i in range(lax.axis_size('slab'))])]
    ppermute x12, waiting for transfers between devices: 36.1 us -> 39.3 us  [swap(): return lax.ppermute(x, 'energy', [(i, i ^ k) for i in range(count)])]
    ppermute x2 -> x4, starting transfers between devices: 2.09 us -> 5.19 us  [other_of_pair(): lax.ppermute(x, 'slab', [(i, i ^ 1) for i in range(lax.axis_size('slab'))])]
    ppermute x12 -> x6, waiting for transfers between devices: 14.2 us -> 11.6 us  [forward(): lax.ppermute(x, 'slab', [(2 * pair + i, 2 * pair + 2 + i) for i in range(...]
    pallas_call x11 -> x10, Pallas kernels: 24.2 us -> 23.5 us  [the longest x2 9.23 us: finish(): pl.pallas_call(body, in_specs=in_specs, out_specs=ANYWHERE, out_shape=jax...]
  transfers between devices with their start and end apart: 26 -> 22, of which waited for: 9 -> 10; matrix products, arithmetic and copies ran while one was open for 1% -> 2% of each run, Pallas kernels for 26% -> 26%
where the time goes in v5:
time: 119 us
  waiting for transfers between devices  56.1 us (47%)
  Pallas kernels  37 us (31%)
  starting transfers between devices  20.5 us (17%)
  local copies, waits for them, and re-layouts  4.5 us (4%)
    ppermute x12, waiting for transfers between devices, swap(): return lax.ppermute(x, 'energy', [(i, i ^ k) for i in range(count)])  39.3 us
    ppermute x6, waiting for transfers between devices, forward(): lax.ppermute(x, 'slab', [(2 * pair + i, 2 * pair + 2 + i) for i in range(...  11.6 us
    ppermute x12, starting transfers between devices, swap(): return lax.ppermute(x, 'energy', [(i, i ^ k) for i in range(count)])  9.81 us
    pallas_call x2, Pallas kernels, finish(): pl.pallas_call(body, in_specs=in_specs, out_specs=ANYWHERE, out_shape=jax...  9.23 us
    pallas_call x2, Pallas kernels, build_sources(): pl.pallas_call(ordered(functools.partial(source_body, energy, owners), le...  8.65 us
    pallas_call x1, Pallas kernels, build_maps(): pl.pallas_call(lambda *refs: maps_body(*refs[:2], *refs[2 + len(after):])...  7.15 us
    ppermute x6, starting transfers between devices, forward(): lax.ppermute(x, 'slab', [(2 * pair + i, 2 * pair + 2 + i) for i in range(...  5.47 us
    ppermute x4, waiting for transfers between devices, other_of_pair(): lax.ppermute(x, 'slab', [(i, i ^ 1) for i in range(lax.axis_size('slab'))])  5.23 us
  transfers between devices with their start and end apart: 22, of which 10 were waited for; matrix products, arithmetic and copies ran while one was open for 2% of the time, Pallas kernels for 26%

profile of v5, /device:TPU:24, one launch (start us, length us, event | category | flops | bytes accessed | tf_op | source)
XLA Modules:
  0.0 118.9 jit_solution(6796969996623988058)
XLA Ops:
  0.0 2.2 %dynamic-slice_bitcast_fusion = (bf16[1,2,2,3,64,256]{5,4,3,2,1,0:T(8,128)(2,1)S(1)}, bf16[1,2,2,3,64,256]{5,4,3,2,1,0:T(8,128)(2,1)S(1)}, bf16[1,2,2,3,64,256]{...) fusion(bf16[2,2,4,256,256]{4,3,2,1,0:T(8,128)(2,1)} %param.5, ...), kind=kLoop, calls=%fused_computation.6 | loop fusion | bytes 6291472 | tf_op jit(solution)/shard_map/stack | solution.py:469
  2.2 0.1 pad_maximum_fusion.2
  2.3 1.6 %collective-permute-start.6 = (bf16[2,2,2,3,64,256]{5,4,3,2,1,0:T(8,128)(2,1)S(1)}, bf16[2,2,2,3,64,256]{5,4,3,2,1,0:T(8,128)(2,1)S(1)}, u32[]{:S(2)}, u32[]{:S(2)}) collective-permute-start(bf16[2,2,2,3,64,256]{5,4,3,2,1,0:T(8,128)(2,1)S(1)} %pad_maximum_fusion.2), channel_id=1, source_target_pairs={{0,2},{1,3},{2,0},{3,1},{4,6},{5,7},{6,4},{7,5},{8,10},{9,11},{10,... | collective-permute-start | bytes 2359304 | tf_op jit(solution)/shard_map/ppermute | solution.py:435
  3.9 0.1 pad_maximum_fusion.1
  3.9 0.1 collective-permute-start.5
  4.0 0.1 pad_maximum_fusion.3
  4.1 0.7 collective-permute-start.7
  4.8 0.1 pad_maximum_fusion.refs_2_.refs_0_
  4.8 0.6 copy-done
  5.4 0.3 copy-done.1
  5.7 7.2 %maps.1 = (bf16[2,4,2,256,512]{4,3,2,1,0:T(8,128)(2,1)S(1)}, bf16[2,4,2,256,512]{4,3,2,1,0:T(8,128)(2,1)S(1)}) custom-call(bf16[2,2,4,256,256]{4,3,2,1,0:T(8,128)(2,1)S(1)} %copy-done, bf16[2,4,256,256]{3,2,1,0:T(8,128)(2,1)S(1)} %copy-done.1, bf16[2,2,2,3,64,256]{5,4,3,2,1,0:T(8,128)(2,1)S(1)} %pad_maximum_fusion.refs_2_.refs_0_), custom_call_target="tpu_custom_call" | custom-call | tf_op jit(solution)/shard_map/maps/pallas_call | solution.py:143
  12.9 0.1 slice_bitcast_fusion
  12.9 1.6 %collective-permute-start.4 = (bf16[2,256,512]{2,1,0:T(8,128)(2,1)S(1)}, bf16[2,256,512]{2,1,0:T(8,128)(2,1)S(1)}, u32[]{:S(2)}, u32[]{:S(2)}) collective-permute-start(bf16[2,256,512]{2,1,0:T(8,128)(2,1)S(1)} %get-tuple-element.63.refs_2_), channel_id=1, source_target_pairs={{0,4},{4,0},{8,12},{12,8},{16,20},{20,16},{24,28},{28,24},{1,5},{5... | collective-permute-start | bytes 1572872 | tf_op jit(solution)/shard_map/ppermute | solution.py:439
  14.5 0.5 collective-permute-start.3
  15.0 1.4 %dynamic-slice_bitcast_fusion.8 = (bf16[1,2,2,1,64,256]{5,4,3,2,1,0:T(8,128)(2,1)S(1)}, bf16[1,2,2,1,64,256]{5,4,3,2,1,0:T(8,128)(2,1)S(1)}, bf16[1,2,2,1,64,256...) fusion(bf16[2,2,4,256,256]{4,3,2,1,0:T(8,128)(2,1)} %param.5, ...), kind=kLoop, calls=%fused_computation.18 | loop fusion | bytes 2097168 | tf_op jit(solution)/shard_map/stack | solution.py:469
  16.5 6.2 %collective-permute-done.6.refs_2_ = bf16[2,2,2,3,64,256]{5,4,3,2,1,0:T(8,128)(2,1)S(1)} collective-permute-done((bf16[2,2,2,3,64,256]{5,4,3,2,1,0:T(8,128)(2,1)S(1)}, bf16[2,2,2,3,64,256]{5,4,3,2,1,0:T(8,128)(2,1)S(1)}, u32[]{:S(2)}, u32[]{:S(2)}) %collective-permute-start.6) | collective-permute-done | bytes 786464 | tf_op jit(solution)/shard_map/ppermute | solution.py:435
  22.8 0.0 collective-permute-start
  22.8 0.0 collective-permute-done.5.refs_1_
  22.8 1.5 %collective-permute-start.1 = (bf16[2,2,2,1,64,256]{5,4,3,2,1,0:T(8,128)(2,1)S(1)}, bf16[2,2,2,1,64,256]{5,4,3,2,1,0:T(8,128)(2,1)S(1)}, u32[]{:S(2)}, u32[]{:S(2)}) collective-permute-start(bf16[2,2,2,1,64,256]{5,4,3,2,1,0:T(8,128)(2,1)S(1)} %pad_maximum_fusion.6), channel_id=1, source_target_pairs={{0,2},{1,3},{2,0},{3,1},{4,6},{5,7},{6,4},{7,5},{8,10},{9,11},{10,... | collective-permute-start | bytes 786440 | tf_op jit(solution)/shard_map/ppermute | solution.py:435
  24.3 14.4 %collective-permute-done.7.refs_3_ = bf16[2,2,2,3,64,256]{5,4,3,2,1,0:T(8,128)(2,1)S(1)} collective-permute-done((bf16[2,2,2,3,64,256]{5,4,3,2,1,0:T(8,128)(2,1)S(1)}, bf16[2,2,2,3,64,256]{5,4,3,2,1,0:T(8,128)(2,1)S(1)}, u32[]{:S(2)}, u32[]{:S(2)}) %collective-permute-start.7) | collective-permute-done | bytes 786464 | tf_op jit(solution)/shard_map/ppermute | solution.py:435
  38.7 1.9 %collective-permute-start.2 = (bf16[2,2,2,1,64,256]{5,4,3,2,1,0:T(8,128)(2,1)S(1)}, bf16[2,2,2,1,64,256]{5,4,3,2,1,0:T(8,128)(2,1)S(1)}, u32[]{:S(2)}, u32[]{:S(2)}) collective-permute-start(bf16[2,2,2,1,64,256]{5,4,3,2,1,0:T(8,128)(2,1)S(1)} %pad_maximum_fusion.7), channel_id=1, source_target_pairs={{0,3},{1,2},{2,1},{3,0},{4,7},{5,6},{6,5},{7,4},{8,11},{9,10},{10,... | collective-permute-start | bytes 786440 | tf_op jit(solution)/shard_map/ppermute | solution.py:435
  40.6 3.7 %convolve.2 = (bf16[4,2,64,256]{3,2,1,0:T(8,128)(2,1)S(1)}, bf16[4,2,64,256]{3,2,1,0:T(8,128)(2,1)S(1)}, bf16[4,2,64,256]{3,2,1,0:T(8,128)(2,1)S(1)}, bf16[4,2,6...) custom-call(bf16[2,2,2,3,64,256]{5,4,3,2,1,0:T(8,128)(2,1)S(1)} %pad, ...), custom_call_target="tpu_custom_call" | custom-call | tf_op jit(solution)/shard_map/convolve/pallas_call | solution.py:262
  44.3 0.0 collective-permute-done.4.refs_3_
  44.3 0.0 collective-permute-done.3.refs_1_
  44.3 1.5 %pair_maps.1 = (bf16[2,2,256,512]{3,2,1,0:T(8,128)(2,1)S(1)}, bf16[2,2,256,512]{3,2,1,0:T(8,128)(2,1)S(1)}, bf16[2,2,256,512]{3,2,1,0:T(8,128)(2,1)S(1)}) custom-call(bf16[2,256,512]{2,1,0:T(8,128)(2,1)S(1)} %get-tuple-element.64.refs_0_, bf16[2,256,512]{2,1,0:T(8,128)(2,1)S(1)} %collective-permute-done.3.refs_1_, ...), custom_call_target="tpu_custom_call" | custom-call | tf_op jit(solution)/shard_map/pair_maps/pallas_call | solution.py:187
  45.8 0.0 collective-permute-done.refs_1_
  45.8 0.0 collective-permute-done.1.refs_2_
  45.9 2.9 %collective-permute-done.2.refs_3_ = bf16[2,2,2,1,64,256]{5,4,3,2,1,0:T(8,128)(2,1)S(1)} collective-permute-done((bf16[2,2,2,1,64,256]{5,4,3,2,1,0:T(8,128)(2,1)S(1)}, bf16[2,2,2,1,64,256]{5,4,3,2,1,0:T(8,128)(2,1)S(1)}, u32[]{:S(2)}, u32[]{:S(2)}) %collective-permute-start.2) | collective-permute-done | bytes 262176 | tf_op jit(solution)/shard_map/ppermute | solution.py:435
  48.7 1.1 convolve.3
  49.9 1.4 %collective-permute-start.11 = (bf16[4,2,64,256]{3,2,1,0:T(8,128)(2,1)S(1)}, bf16[4,2,64,256]{3,2,1,0:T(8,128)(2,1)S(1)}, u32[]{:S(2)}, u32[]{:S(2)}) collective-permute-start(bf16[4,2,64,256]{3,2,1,0:T(8,128)(2,1)S(1)} %get-tuple-element.49), channel_id=1, source_target_pairs={{0,2},{1,3},{2,0},{3,1},{4,6},{5,7},{6,4},{7,5},{8,10},{9,11},{10,... | collective-permute-start | bytes 786440 | tf_op jit(solution)/shard_map/ppermute | solution.py:435
  51.3 0.8 collective-permute-start.12
  52.1 0.0 collective-permute-start.13
  52.1 1.5 %collective-permute-start.8 = (bf16[4,2,64,256]{3,2,1,0:T(8,128)(2,1)S(1)}, bf16[4,2,64,256]{3,2,1,0:T(8,128)(2,1)S(1)}, u32[]{:S(2)}, u32[]{:S(2)}) collective-permute-start(bf16[4,2,64,256]{3,2,1,0:T(8,128)(2,1)S(1)} %get-tuple-element.45), channel_id=1, source_target_pairs={{0,2},{1,3},{2,0},{3,1},{4,6},{5,7},{6,4},{7,5},{8,10},{9,11},{10,... | collective-permute-start | bytes 786440 | tf_op jit(solution)/shard_map/ppermute | solution.py:435
  53.6 0.3 collective-permute-start.9
  53.9 5.2 %collective-permute-done.11.refs_0_ = bf16[4,2,64,256]{3,2,1,0:T(8,128)(2,1)S(1)} collective-permute-done((bf16[4,2,64,256]{3,2,1,0:T(8,128)(2,1)S(1)}, bf16[4,2,64,256]{3,2,1,0:T(8,128)(2,1)S(1)}, u32[]{:S(2)}, u32[]{:S(2)}) %collective-permute-start.11) | collective-permute-done | bytes 262176 | tf_op jit(solution)/shard_map/ppermute | solution.py:435
  59.1 0.0 collective-permute-start.10
  59.1 5.2 %collective-permute-done.12.refs_1_ = bf16[4,2,64,256]{3,2,1,0:T(8,128)(2,1)S(1)} collective-permute-done((bf16[4,2,64,256]{3,2,1,0:T(8,128)(2,1)S(1)}, bf16[4,2,64,256]{3,2,1,0:T(8,128)(2,1)S(1)}, u32[]{:S(2)}, u32[]{:S(2)}) %collective-permute-start.12) | collective-permute-done | bytes 262176 | tf_op jit(solution)/shard_map/ppermute | solution.py:435
  64.4 0.0 collective-permute-done.13.refs_2_
  64.4 4.3 %sources.2 = (f32[4,256,512]{2,1,0:T(8,128)S(1)}, bf16[256,512]{1,0:T(8,128)(2,1)S(1)}) custom-call(bf16[4,2,64,256]{3,2,1,0:T(8,128)(2,1)S(1)} %collective-permute-done.11.refs_0_, bf16[4,2,64,256]{3,2,1,0:T(8,128)(2,1)S(1)} %collective-permute-done.12.refs_1_, bf16[4,2,64,256]{3,2,1,0:T(8,128)(2,1)S(1)} %collective-permute-done.13.refs_2_, ...), custom_call_target="tpu_custom_call" | custom-call | tf_op jit(solution)/shard_map/sources/pallas_call | solution.py:310
  68.7 1.5 %collective-permute-start.15 = (bf16[256,512]{1,0:T(8,128)(2,1)S(1)}, bf16[256,512]{1,0:T(8,128)(2,1)S(1)}, u32[]{:S(2)}, u32[]{:S(2)}) collective-permute-start(bf16[256,512]{1,0:T(8,128)(2,1)S(1)} %get-tuple-element.53.refs_6_.refs_1_), channel_id=1, source_target_pairs={{0,4},{4,0},{8,12},{12,8},{16,20},{20,16},{24,28},{28,24},{1,5},{5... | collective-permute-start | bytes 786440 | tf_op jit(solution)/shard_map/ppermute | solution.py:439
  70.2 0.1 collective-permute-done.8.refs_0_
  70.4 5.2 %collective-permute-done.9.refs_1_ = bf16[4,2,64,256]{3,2,1,0:T(8,128)(2,1)S(1)} collective-permute-done((bf16[4,2,64,256]{3,2,1,0:T(8,128)(2,1)S(1)}, bf16[4,2,64,256]{3,2,1,0:T(8,128)(2,1)S(1)}, u32[]{:S(2)}, u32[]{:S(2)}) %collective-permute-start.9) | collective-permute-done | bytes 262176 | tf_op jit(solution)/shard_map/ppermute | solution.py:435
  75.6 4.3 %sources.3 = (f32[4,256,512]{2,1,0:T(8,128)S(1)}, bf16[256,512]{1,0:T(8,128)(2,1)S(1)}) custom-call(bf16[4,2,64,256]{3,2,1,0:T(8,128)(2,1)S(1)} %collective-permute-done.8.refs_0_, bf16[4,2,64,256]{3,2,1,0:T(8,128)(2,1)S(1)} %collective-permute-done.9.refs_1_, bf16[4,2,64,256]{3,2,1,0:T(8,128)(2,1)S(1)} %collective-permute-done.10.refs_2_, ...), custom_call_target="tpu_custom_call" | custom-call | tf_op jit(solution)/shard_map/sources/pallas_call | solution.py:310
  79.9 1.5 %collective-permute-start.14 = (bf16[256,512]{1,0:T(8,128)(2,1)S(1)}, bf16[256,512]{1,0:T(8,128)(2,1)S(1)}, u32[]{:S(2)}, u32[]{:S(2)}) collective-permute-start(bf16[256,512]{1,0:T(8,128)(2,1)S(1)} %get-tuple-element.54.refs_4_.refs_1_), channel_id=1, source_target_pairs={{0,4},{4,0},{8,12},{12,8},{16,20},{20,16},{24,28},{28,24},{1,5},{5... | collective-permute-start | bytes 786440 | tf_op jit(solution)/shard_map/ppermute | solution.py:439
  81.5 0.0 collective-permute-done.15.refs_0_.refs_3_
  81.5 0.9 pair_sum.2
  82.4 0.9 collective-permute-start.17
  83.3 5.2 %collective-permute-done.14.refs_0_.refs_3_ = bf16[256,512]{1,0:T(8,128)(2,1)S(1)} collective-permute-done((bf16[256,512]{1,0:T(8,128)(2,1)S(1)}, bf16[256,512]{1,0:T(8,128)(2,1)S(1)}, u32[]{:S(2)}, u32[]{:S(2)}) %collective-permute-start.14) | collective-permute-done | bytes 262176 | tf_op jit(solution)/shard_map/ppermute | solution.py:439
  88.5 0.9 pair_sum.3
  89.5 0.7 collective-permute-start.16
  90.1 0.0 collective-permute-done.17.refs_0_
  90.1 0.9 combine.4.refs_3_
  91.1 0.7 collective-permute-start.19
  91.8 0.0 collective-permute-done.16.refs_0_
  91.8 0.9 combine.5.refs_4_
  92.7 0.7 collective-permute-start.18
  93.4 0.9 combine.6.refs_4_
  94.4 1.3 %collective-permute-start.21 = (bf16[256,512]{1,0:T(8,128)(2,1)S(1)}, bf16[256,512]{1,0:T(8,128)(2,1)S(1)}, u32[]{:S(2)}, u32[]{:S(2)}) collective-permute-start(bf16[256,512]{1,0:T(8,128)(2,1)S(1)} %combine.6.refs_4_), channel_id=1, source_target_pairs={{16,24},{20,28},{17,25},{21,29},{18,26},{22,30},{19,27},{23,31}} | collective-permute-start | bytes 786440 | tf_op jit(solution)/shard_map/ppermute | solution.py:443
  95.7 0.9 combine.7.refs_7_
  96.6 1.3 %collective-permute-start.20 = (bf16[256,512]{1,0:T(8,128)(2,1)S(1)}, bf16[256,512]{1,0:T(8,128)(2,1)S(1)}, u32[]{:S(2)}, u32[]{:S(2)}) collective-permute-start(bf16[256,512]{1,0:T(8,128)(2,1)S(1)} %combine.7.refs_7_), channel_id=1, source_target_pairs={{16,24},{20,28},{17,25},{21,29},{18,26},{22,30},{19,27},{23,31}} | collective-permute-start | bytes 786440 | tf_op jit(solution)/shard_map/ppermute | solution.py:443
  97.9 10.9 %collective-permute-done.21.refs_2_ = bf16[256,512]{1,0:T(8,128)(2,1)S(1)} collective-permute-done((bf16[256,512]{1,0:T(8,128)(2,1)S(1)}, bf16[256,512]{1,0:T(8,128)(2,1)S(1)}, u32[]{:S(2)}, u32[]{:S(2)}) %collective-permute-start.21) | collective-permute-done | bytes 262176 | tf_op jit(solution)/shard_map/ppermute | solution.py:443
  108.8 4.6 %finish.2.refs_8_ = f32[2,2,4,256,256]{4,3,2,1,0:T(8,128)} custom-call(bf16[256,512]{1,0:T(8,128)(2,1)S(1)} %collective-permute-done.17.refs_0_, bf16[256,512]{1,0:T(8,128)(2,1)S(1)} %collective-permute-done.19.refs_1_, bf16[256,512]{1,0:T(8,128)(2,1)S(1)} %collective-permute-done.21.refs_2_, bf16[256,512]{1,0:T(8,128)(2,1)S(1)} %collective-permute-done.15.refs_0_.refs_3_, ...), custom_call_target="tpu_custom_call" | custom-call | tf_op jit(solution)/shard_map/finish/pallas_call | solution.py:420
  113.4 0.7 collective-permute-done.20.refs_2_
  114.2 4.6 %finish.3 = f32[2,2,4,256,256]{4,3,2,1,0:T(8,128)} custom-call(bf16[256,512]{1,0:T(8,128)(2,1)S(1)} %collective-permute-done.16.refs_0_, bf16[256,512]{1,0:T(8,128)(2,1)S(1)} %collective-permute-done.18.refs_1_, bf16[256,512]{1,0:T(8,128)(2,1)S(1)} %collective-permute-done.20.refs_2_, ...), custom_call_target="tpu_custom_call", output_to_operand_aliasing={{}: (8, {})} | custom-call | tf_op jit(solution)/shard_map/finish/pallas_call | solution.py:420
  (9 shorter events, 0.1 us)
Async XLA Ops:
  2.3 20.5 %collective-permute-start.6 = (bf16[2,2,2,3,64,256]{5,4,3,2,1,0:T(8,128)(2,1)S(1)}, bf16[2,2,2,3,64,256]{5,4,3,2,1,0:T(8,128)(2,1)S(1)}, u32[]{:S(2)}, u32[]{:S(2)}) collective-permute-start(bf16[2,2,2,3,64,256]{5,4,3,2,1,0:T(8,128)(2,1)S(1)} %pad_maximum_fusion.2), channel_id=1, source_target_pairs={{0,2},{1,3},{2,0},{3,1},{4,6},{5,7},{6,4},{7,5},{8,10},{9,11},{10,... | collective-permute-start | bytes 2359304 | tf_op jit(solution)/shard_map/ppermute | solution.py:435
  3.9 1.6 %copy-start = (bf16[2,2,4,256,256]{4,3,2,1,0:T(8,128)(2,1)S(1)}, bf16[2,2,4,256,256]{4,3,2,1,0:T(8,128)(2,1)}, u32[]{:S(2)}) copy-start(bf16[2,2,4,256,256]{4,3,2,1,0:T(8,128)(2,1)} %refs_4_.3) | copy-start | bytes 6291460
  3.9 1.9 %copy-start.1 = (bf16[2,4,256,256]{3,2,1,0:T(8,128)(2,1)S(1)}, bf16[2,4,256,256]{3,2,1,0:T(8,128)(2,1)}, u32[]{:S(2)}) copy-start(bf16[2,4,256,256]{3,2,1,0:T(8,128)(2,1)} %refs_1_.1) | copy-start | bytes 3145732
  3.9 18.8 %collective-permute-start.5 = (bf16[2,2,2,3,64,256]{5,4,3,2,1,0:T(8,128)(2,1)S(1)}, bf16[2,2,2,3,64,256]{5,4,3,2,1,0:T(8,128)(2,1)S(1)}, u32[]{:S(2)}, u32[]{:S(2)}) collective-permute-start(bf16[2,2,2,3,64,256]{5,4,3,2,1,0:T(8,128)(2,1)S(1)} %pad_maximum_fusion.1), channel_id=1, source_target_pairs={{0,1},{1,0},{2,3},{3,2},{4,5},{5,4},{6,7},{7,6},{8,9},{9,8},{10,11... | collective-permute-start | bytes 2359304 | tf_op jit(solution)/shard_map/ppermute | solution.py:435
  4.1 34.6 %collective-permute-start.7 = (bf16[2,2,2,3,64,256]{5,4,3,2,1,0:T(8,128)(2,1)S(1)}, bf16[2,2,2,3,64,256]{5,4,3,2,1,0:T(8,128)(2,1)S(1)}, u32[]{:S(2)}, u32[]{:S(2)}) collective-permute-start(bf16[2,2,2,3,64,256]{5,4,3,2,1,0:T(8,128)(2,1)S(1)} %pad_maximum_fusion.3), channel_id=1, source_target_pairs={{0,3},{1,2},{2,1},{3,0},{4,7},{5,6},{6,5},{7,4},{8,11},{9,10},{10,... | collective-permute-start | bytes 2359304 | tf_op jit(solution)/shard_map/ppermute | solution.py:435
  12.9 31.4 %collective-permute-start.4 = (bf16[2,256,512]{2,1,0:T(8,128)(2,1)S(1)}, bf16[2,256,512]{2,1,0:T(8,128)(2,1)S(1)}, u32[]{:S(2)}, u32[]{:S(2)}) collective-permute-start(bf16[2,256,512]{2,1,0:T(8,128)(2,1)S(1)} %get-tuple-element.63.refs_2_), channel_id=1, source_target_pairs={{0,4},{4,0},{8,12},{12,8},{16,20},{20,16},{24,28},{28,24},{1,5},{5... | collective-permute-start | bytes 1572872 | tf_op jit(solution)/shard_map/ppermute | solution.py:439
  14.5 29.8 %collective-permute-start.3 = (bf16[2,256,512]{2,1,0:T(8,128)(2,1)S(1)}, bf16[2,256,512]{2,1,0:T(8,128)(2,1)S(1)}, u32[]{:S(2)}, u32[]{:S(2)}) collective-permute-start(bf16[2,256,512]{2,1,0:T(8,128)(2,1)S(1)} %get-tuple-element.64.refs_0_), channel_id=1, source_target_pairs={{0,4},{4,0},{8,12},{12,8},{16,20},{20,16},{24,28},{28,24},{1,5},{5... | collective-permute-start | bytes 1572872 | tf_op jit(solution)/shard_map/ppermute | solution.py:439
  22.8 23.1 %collective-permute-start = (bf16[2,2,2,1,64,256]{5,4,3,2,1,0:T(8,128)(2,1)S(1)}, bf16[2,2,2,1,64,256]{5,4,3,2,1,0:T(8,128)(2,1)S(1)}, u32[]{:S(2)}, u32[]{:S(2)}) collective-permute-start(bf16[2,2,2,1,64,256]{5,4,3,2,1,0:T(8,128)(2,1)S(1)} %pad_maximum_fusion.5), channel_id=1, source_target_pairs={{0,1},{1,0},{2,3},{3,2},{4,5},{5,4},{6,7},{7,6},{8,9},{9,8},{10,11... | collective-permute-start | bytes 786440 | tf_op jit(solution)/shard_map/ppermute | solution.py:435
  22.8 23.1 %collective-permute-start.1 = (bf16[2,2,2,1,64,256]{5,4,3,2,1,0:T(8,128)(2,1)S(1)}, bf16[2,2,2,1,64,256]{5,4,3,2,1,0:T(8,128)(2,1)S(1)}, u32[]{:S(2)}, u32[]{:S(2)}) collective-permute-start(bf16[2,2,2,1,64,256]{5,4,3,2,1,0:T(8,128)(2,1)S(1)} %pad_maximum_fusion.6), channel_id=1, source_target_pairs={{0,2},{1,3},{2,0},{3,1},{4,6},{5,7},{6,4},{7,5},{8,10},{9,11},{10,... | collective-permute-start | bytes 786440 | tf_op jit(solution)/shard_map/ppermute | solution.py:435
  38.7 10.1 %collective-permute-start.2 = (bf16[2,2,2,1,64,256]{5,4,3,2,1,0:T(8,128)(2,1)S(1)}, bf16[2,2,2,1,64,256]{5,4,3,2,1,0:T(8,128)(2,1)S(1)}, u32[]{:S(2)}, u32[]{:S(2)}) collective-permute-start(bf16[2,2,2,1,64,256]{5,4,3,2,1,0:T(8,128)(2,1)S(1)} %pad_maximum_fusion.7), channel_id=1, source_target_pairs={{0,3},{1,2},{2,1},{3,0},{4,7},{5,6},{6,5},{7,4},{8,11},{9,10},{10,... | collective-permute-start | bytes 786440 | tf_op jit(solution)/shard_map/ppermute | solution.py:435
  49.9 9.2 %collective-permute-start.11 = (bf16[4,2,64,256]{3,2,1,0:T(8,128)(2,1)S(1)}, bf16[4,2,64,256]{3,2,1,0:T(8,128)(2,1)S(1)}, u32[]{:S(2)}, u32[]{:S(2)}) collective-permute-start(bf16[4,2,64,256]{3,2,1,0:T(8,128)(2,1)S(1)} %get-tuple-element.49), channel_id=1, source_target_pairs={{0,2},{1,3},{2,0},{3,1},{4,6},{5,7},{6,4},{7,5},{8,10},{9,11},{10,... | collective-permute-start | bytes 786440 | tf_op jit(solution)/shard_map/ppermute | solution.py:435
  51.3 13.1 %collective-permute-start.12 = (bf16[4,2,64,256]{3,2,1,0:T(8,128)(2,1)S(1)}, bf16[4,2,64,256]{3,2,1,0:T(8,128)(2,1)S(1)}, u32[]{:S(2)}, u32[]{:S(2)}) collective-permute-start(bf16[4,2,64,256]{3,2,1,0:T(8,128)(2,1)S(1)} %get-tuple-element.50), channel_id=1, source_target_pairs={{0,3},{1,2},{2,1},{3,0},{4,7},{5,6},{6,5},{7,4},{8,11},{9,10},{10,... | collective-permute-start | bytes 786440 | tf_op jit(solution)/shard_map/ppermute | solution.py:435
  52.1 12.3 %collective-permute-start.13 = (bf16[4,2,64,256]{3,2,1,0:T(8,128)(2,1)S(1)}, bf16[4,2,64,256]{3,2,1,0:T(8,128)(2,1)S(1)}, u32[]{:S(2)}, u32[]{:S(2)}) collective-permute-start(bf16[4,2,64,256]{3,2,1,0:T(8,128)(2,1)S(1)} %get-tuple-element.51), channel_id=1, source_target_pairs={{0,1},{1,0},{2,3},{3,2},{4,5},{5,4},{6,7},{7,6},{8,9},{9,8},{10,11... | collective-permute-start | bytes 786440 | tf_op jit(solution)/shard_map/ppermute | solution.py:435
  52.1 18.3 %collective-permute-start.8 = (bf16[4,2,64,256]{3,2,1,0:T(8,128)(2,1)S(1)}, bf16[4,2,64,256]{3,2,1,0:T(8,128)(2,1)S(1)}, u32[]{:S(2)}, u32[]{:S(2)}) collective-permute-start(bf16[4,2,64,256]{3,2,1,0:T(8,128)(2,1)S(1)} %get-tuple-element.45), channel_id=1, source_target_pairs={{0,2},{1,3},{2,0},{3,1},{4,6},{5,7},{6,4},{7,5},{8,10},{9,11},{10,... | collective-permute-start | bytes 786440 | tf_op jit(solution)/shard_map/ppermute | solution.py:435
  53.6 22.0 %collective-permute-start.9 = (bf16[4,2,64,256]{3,2,1,0:T(8,128)(2,1)S(1)}, bf16[4,2,64,256]{3,2,1,0:T(8,128)(2,1)S(1)}, u32[]{:S(2)}, u32[]{:S(2)}) collective-permute-start(bf16[4,2,64,256]{3,2,1,0:T(8,128)(2,1)S(1)} %get-tuple-element.46), channel_id=1, source_target_pairs={{0,3},{1,2},{2,1},{3,0},{4,7},{5,6},{6,5},{7,4},{8,11},{9,10},{10,... | collective-permute-start | bytes 786440 | tf_op jit(solution)/shard_map/ppermute | solution.py:435
  59.1 16.5 %collective-permute-start.10 = (bf16[4,2,64,256]{3,2,1,0:T(8,128)(2,1)S(1)}, bf16[4,2,64,256]{3,2,1,0:T(8,128)(2,1)S(1)}, u32[]{:S(2)}, u32[]{:S(2)}) collective-permute-start(bf16[4,2,64,256]{3,2,1,0:T(8,128)(2,1)S(1)} %get-tuple-element.47), channel_id=1, source_target_pairs={{0,1},{1,0},{2,3},{3,2},{4,5},{5,4},{6,7},{7,6},{8,9},{9,8},{10,11... | collective-permute-start | bytes 786440 | tf_op jit(solution)/shard_map/ppermute | solution.py:435
  68.7 12.8 %collective-permute-start.15 = (bf16[256,512]{1,0:T(8,128)(2,1)S(1)}, bf16[256,512]{1,0:T(8,128)(2,1)S(1)}, u32[]{:S(2)}, u32[]{:S(2)}) collective-permute-start(bf16[256,512]{1,0:T(8,128)(2,1)S(1)} %get-tuple-element.53.refs_6_.refs_1_), channel_id=1, source_target_pairs={{0,4},{4,0},{8,12},{12,8},{16,20},{20,16},{24,28},{28,24},{1,5},{5... | collective-permute-start | bytes 786440 | tf_op jit(solution)/shard_map/ppermute | solution.py:439
  79.9 8.6 %collective-permute-start.14 = (bf16[256,512]{1,0:T(8,128)(2,1)S(1)}, bf16[256,512]{1,0:T(8,128)(2,1)S(1)}, u32[]{:S(2)}, u32[]{:S(2)}) collective-permute-start(bf16[256,512]{1,0:T(8,128)(2,1)S(1)} %get-tuple-element.54.refs_4_.refs_1_), channel_id=1, source_target_pairs={{0,4},{4,0},{8,12},{12,8},{16,20},{20,16},{24,28},{28,24},{1,5},{5... | collective-permute-start | bytes 786440 | tf_op jit(solution)/shard_map/ppermute | solution.py:439
  82.4 7.7 %collective-permute-start.17 = (bf16[256,512]{1,0:T(8,128)(2,1)S(1)}, bf16[256,512]{1,0:T(8,128)(2,1)S(1)}, u32[]{:S(2)}, u32[]{:S(2)}) collective-permute-start(bf16[256,512]{1,0:T(8,128)(2,1)S(1)} %get-tuple-element.58.refs_4_), channel_id=1, source_target_pairs={{0,8},{4,12},{1,9},{5,13},{2,10},{6,14},{3,11},{7,15}} | collective-permute-start | bytes 786440 | tf_op jit(solution)/shard_map/ppermute | solution.py:443
  89.5 2.3 %collective-permute-start.16 = (bf16[256,512]{1,0:T(8,128)(2,1)S(1)}, bf16[256,512]{1,0:T(8,128)(2,1)S(1)}, u32[]{:S(2)}, u32[]{:S(2)}) collective-permute-start(bf16[256,512]{1,0:T(8,128)(2,1)S(1)} %get-tuple-element.59.refs_3_), channel_id=1, source_target_pairs={{0,8},{4,12},{1,9},{5,13},{2,10},{6,14},{3,11},{7,15}} | collective-permute-start | bytes 786440 | tf_op jit(solution)/shard_map/ppermute | solution.py:443
  91.1 2.3 %collective-permute-start.19 = (bf16[256,512]{1,0:T(8,128)(2,1)S(1)}, bf16[256,512]{1,0:T(8,128)(2,1)S(1)}, u32[]{:S(2)}, u32[]{:S(2)}) collective-permute-start(bf16[256,512]{1,0:T(8,128)(2,1)S(1)} %combine.4.refs_3_), channel_id=1, source_target_pairs={{8,16},{12,20},{9,17},{13,21},{10,18},{14,22},{11,19},{15,23}} | collective-permute-start | bytes 786440 | tf_op jit(solution)/shard_map/ppermute | solution.py:443
  92.7 2.9 %collective-permute-start.18 = (bf16[256,512]{1,0:T(8,128)(2,1)S(1)}, bf16[256,512]{1,0:T(8,128)(2,1)S(1)}, u32[]{:S(2)}, u32[]{:S(2)}) collective-permute-start(bf16[256,512]{1,0:T(8,128)(2,1)S(1)} %combine.5.refs_4_), channel_id=1, source_target_pairs={{8,16},{12,20},{9,17},{13,21},{10,18},{14,22},{11,19},{15,23}} | collective-permute-start | bytes 786440 | tf_op jit(solution)/shard_map/ppermute | solution.py:443
  94.4 14.5 %collective-permute-start.21 = (bf16[256,512]{1,0:T(8,128)(2,1)S(1)}, bf16[256,512]{1,0:T(8,128)(2,1)S(1)}, u32[]{:S(2)}, u32[]{:S(2)}) collective-permute-start(bf16[256,512]{1,0:T(8,128)(2,1)S(1)} %combine.6.refs_4_), channel_id=1, source_target_pairs={{16,24},{20,28},{17,25},{21,29},{18,26},{22,30},{19,27},{23,31}} | collective-permute-start | bytes 786440 | tf_op jit(solution)/shard_map/ppermute | solution.py:443
  96.6 17.5 %collective-permute-start.20 = (bf16[256,512]{1,0:T(8,128)(2,1)S(1)}, bf16[256,512]{1,0:T(8,128)(2,1)S(1)}, u32[]{:S(2)}, u32[]{:S(2)}) collective-permute-start(bf16[256,512]{1,0:T(8,128)(2,1)S(1)} %combine.7.refs_7_), channel_id=1, source_target_pairs={{16,24},{20,28},{17,25},{21,29},{18,26},{22,30},{19,27},{23,31}} | collective-permute-start | bytes 786440 | tf_op jit(solution)/shard_map/ppermute | solution.py:443

commit v6 on v5

--- a/solution.py
+++ b/solution.py
@@ -88,35 +88,32 @@
 def pack_body(wanted, *refs):
     sources, outs, sems = refs[:2], refs[-1 - len(wanted) : -1], refs[-1]
     copies = []
-    for out, (parts, k, start) in zip(outs, wanted):
-        size, rows = out.shape[-4 + 1 : -1]
+    for out, (k, start) in zip(outs, wanted):
+        size, rows = out.shape[3:5]
         begin = pl.multiple_of((lax.axis_index("energy") ^ k) * rows, rows)
-        for part in parts:
+        for part in range(2):
             block = sources[part].at[:, :, pl.ds(start, size), pl.ds(begin, rows), :]
-            target = out if len(parts) == 1 else out.at[part]
-            copies.append(pltpu.make_async_copy(block, target, sems.at[len(copies)]))
+            copies.append(pltpu.make_async_copy(block, out.at[part], sems.at[len(copies)]))
     for copy in copies:
         copy.start()
     for copy in copies:
         copy.wait()
 
 
-def pack(green, screen, wanted, count, *after):
+def pack(green, screen, wanted, count, after):
     _, energies, _, order, _ = green.shape
-    shapes = [
-        (len(parts),) * (len(parts) > 1) + (2, energies, size, order // count, order)
-        for parts, _, _, size in wanted
-    ]
-    return pl.pallas_call(
-        functools.partial(pack_body, [w[:3] for w in wanted]),
-        in_specs=[ANYWHERE] * (2 + len(after)),
-        out_specs=[pl.BlockSpec(memory_space=pltpu.VMEM)] * len(wanted),
-        out_shape=[jax.ShapeDtypeStruct(shape, BF16) for shape in shapes],
-        scratch_shapes=[pltpu.SemaphoreType.DMA((sum(len(w[0]) for w in wanted),))],
+    return pl.pallas_call(
+        functools.partial(pack_body, [w[:2] for w in wanted]),
+        in_specs=[ANYWHERE] * 3,
+        out_specs=[WHOLE] * len(wanted),
+        out_shape=[
+            jax.ShapeDtypeStruct((2, 2, energies, size, order // count, order), BF16) for _, _, size in wanted
+        ],
+        scratch_shapes=[pltpu.SemaphoreType.DMA((2 * len(wanted),))],
         compiler_params=params(),
         cost_estimate=cost(),
         name="pack",
-    )(green, screen, *after)
+    )(green, screen, after)
 
 
 def maps_body(g_ref, c_ref, k_ref, p_ref, carry):
@@ -381,32 +378,87 @@
     )(*arrived, maps, base, after)
 
 
-def finish_body(energy, arrivals, before_ref, t_ref, m_ref, base_ref, out, blocks, sems):
-    slabs, order, _ = base_ref.shape
-    odd = (lax.axis_index("slab") & 1) == 1
-    before = jnp.where(odd, before_ref[...].astype(F32), 0.0)
-    entry = (before + congruence(t_ref.at[energy], entered(arrivals))).astype(BF16)
-    maps = m_ref.at[energy]
+def spread(maps, entry, sums, store):
+    slabs, order, _ = sums.shape
     rows = maps[...].reshape(slabs * 2 * order, 2 * order)
     both = dot(rows, panel(entry[:, :order], entry[:, order:]))
-    copies = []
     for s in range(slabs):
         first = 2 * s * order
         inner = both[first : first + order] + both[first + order : first + 2 * order]
-        value = times_adjoint(inner, maps[s, 0], maps[s, 1]) + base_ref[s]
+        store(s, times_adjoint(inner, maps[s, 0], maps[s, 1]) + sums[s])
+
+
+def from_partner(before_ref):
+    odd = (lax.axis_index("slab") & 1) == 1
+    return jnp.where(odd, before_ref[...], jnp.zeros_like(before_ref))
+
+
+def entry_maps(prefixes, inner, energy, after):
+    _, slabs, _, order, _ = prefixes.shape
+
+    def body(p_ref, i_ref, _, out):
+        high, low = panels(i_ref.at[energy])
+        ih = panel(high[:, :order], high[:, order:])
+        il = panel(low[:, :order], low[:, order:])
+        for s in range(slabs):
+            both = dot(p_ref[energy, s].reshape(2 * order, 2 * order), ih)
+            store_map(out.at[0, s], both[:order] + both[order:] + dot(p_ref[energy, s, 0], il))
+
+    return pl.pallas_call(
+        body,
+        in_specs=[WHOLE] * 2 + [ANYWHERE],
+        out_specs=WHOLE,
+        out_shape=jax.ShapeDtypeStruct((1,) + prefixes.shape[1:], BF16),
+        compiler_params=params(),
+        cost_estimate=cost(),
+        name="entry_maps",
+    )(prefixes, inner, after)
+
+
+def part_known(before, prefixes, sums, energy, after):
+    def body(before_ref, p_ref, sum_ref, _, out):
+        def store(s, value):
+            out[s] = value
+
+        spread(p_ref.at[energy], from_partner(before_ref), sum_ref, store)
+
+    return pl.pallas_call(
+        body,
+        in_specs=[WHOLE] * 3 + [ANYWHERE],
+        out_specs=WHOLE,
+        out_shape=jax.ShapeDtypeStruct(sums.shape, F32),
+        compiler_params=params(),
+        cost_estimate=cost(),
+        name="part_known",
+    )(before, prefixes, sums, after)
+
+
+def finish_body(energy, maps_index, arrivals, before, m_ref, base_ref, out, blocks, sems):
+    order = base_ref.shape[1]
+    entry = entered(arrivals)
+    if before is not None:
+        before_ref, t_ref = before
+        whole = from_partner(before_ref).astype(F32) + congruence(t_ref.at[energy], entry)
+        entry = whole.astype(BF16)
+    copies = []
+
+    def store(s, value):
         blocks[s, 0] = value[:, :order]
         blocks[s, 1] = value[:, order:]
         copies.append(pltpu.make_async_copy(blocks.at[s], out.at[:, energy, s], sems.at[s]))
         copies[-1].start()
+
+    spread(m_ref.at[maps_index], entry, base_ref, store)
     for copy in copies:
         copy.wait()
 
 
-def finish(arrived, before, inner, prefixes, sums, energy, held, after):
-    energies, slabs, _, order, _ = prefixes.shape
-    operands = list(arrived) + [before, inner, prefixes, sums]
-    count = len(operands)
-    in_specs = [WHOLE] * count + [ANYWHERE]
+def finish(arrived, before, maps, maps_index, sums, energy, energies, held, after):
+    slabs, order, _ = sums.shape
+    count = len(arrived)
+    extra = [] if before is None else list(before)
+    operands = list(arrived) + extra + [maps, sums]
+    in_specs = [WHOLE] * len(operands) + [ANYWHERE]
     operands.append(after)
     aliases = {}
     if held is not None:
@@ -415,7 +467,15 @@
         in_specs.append(ANYWHERE)
 
     def body(*refs):
-        finish_body(energy, refs[: len(arrived)], *refs[len(arrived) : count], *refs[-3:])
+        second = count + len(extra)
+        finish_body(
+            energy,
+            maps_index,
+            refs[:count],
+            refs[count:second] if extra else None,
+            *refs[second : second + 2],
+            *refs[-3:],
+        )
 
     return pl.pallas_call(
         body,
@@ -464,11 +524,17 @@
         return [lax.dynamic_slice(x, begin, sizes) for x in (green_lesser, screened_lesser)]
 
     pieces = [[None] * count for _ in parts]
-    for chunk, (start, size) in enumerate(parts):
-        for k in far + near:
-            block = jnp.stack(first_rows(k, start, size))
-            pieces[chunk][k] = swap(block, k) if k else block
-    token = pieces[0][0]
+    places = [(chunk, k) for chunk in range(len(parts)) for k in far + near]
+    chunk, k = places[0]
+    token = jnp.stack(first_rows(k, *parts[chunk]))
+    pieces[chunk][k] = swap(token, k) if k else token
+    urgent = [place for place in places[1:] if place[0] == 0 and place[1]]
+    for group in (urgent, [place for place in places[1:] if place not in urgent]):
+        if group:
+            packed = pack(green_lesser, screened_lesser, [(k,) + parts[chunk] for chunk, k in group], count, token)
+            for (chunk, k), block in zip(group, packed):
+                pieces[chunk][k] = swap(block, k) if k else block
+            token = packed[0]
 
     kernels, prefixes = build_maps(green_retarded, coupling, token)
     token = kernels
@@ -489,6 +555,9 @@
             sigma[e][k] = swap(block, k) if k else block
 
     pairs = depth // 2
+    final = energies - 1
+    entries = token = entry_maps(prefixes, inner, final, token)
+    known = None
     sums, own, ours = ([None] * energies for _ in range(3))
     running, carry = [None] * energies, [None] * energies
     arrived = [[] for _ in range(energies)]
@@ -511,10 +580,14 @@
     for step in range(last + 1):
         for e in range(energies):
             stage(e, step)
+        if step == min(2, last):
+            known = token = part_known(ours[final], prefixes, sums[final], final, token)
     result = None
-    for e in range(energies):
-        result = finish(arrived[e], ours[e], inner, prefixes, sums[e], e, result, token)
-    return result
+    for e in range(final):
+        result = finish(
+            arrived[e], (ours[e], inner), prefixes, e, sums[e], e, energies, result, token
+        )
+    return finish(arrived[final], None, entries, 0, known, final, energies, result, token)
 
 
 def solution(mesh):

time: 119 us -> 118 us (level)
  waiting for transfers between devices: 56.1 us -> 51 us
  Pallas kernels: 37 us -> 41.6 us
    pallas_call x0 -> x4, Pallas kernels: none -> 5.33 us  [the longest x1 2.9 us: part_known(): pl.pallas_call(body, in_specs=[WHOLE] * 3 + [ANYWHERE], out_specs=WHOLE,...]
    ppermute x6, waiting for transfers between devices: 11.6 us -> 8.5 us  [forward(): lax.ppermute(x, 'slab', [(2 * pair + i, 2 * pair + 2 + i) for i in range(...]
    another operation x2 -> x1, local copies, waits for them, and re-layouts: 3.56 us -> 1.33 us  [per_device(): token = jnp.stack(first_rows(k, *parts[chunk]))]
    ppermute x12, waiting for transfers between devices: 39.3 us -> 37.1 us  [swap(): return lax.ppermute(x, 'energy', [(i, i ^ k) for i in range(count)])]
    unnamed x4 -> x8, local copies, waits for them, and re-layouts: 0.87 us -> 2.33 us
  transfers between devices with their start and end apart: 22 -> 22, of which waited for: 10 -> 10; matrix products, arithmetic and copies ran while one was open for 2% -> 0% of each run, Pallas kernels for 26% -> 31%
where the time goes in v6:
time: 118 us; the launch traced here: 117 us
  waiting for transfers between devices  51 us (43%)
  Pallas kernels  41.6 us (35%)
  starting transfers between devices  20.6 us (17%)
  local copies, waits for them, and re-layouts  3.73 us (3%)
    ppermute x12, waiting for transfers between devices, swap(): return lax.ppermute(x, 'energy', [(i, i ^ k) for i in range(count)])  37.1 us
    ppermute x12, starting transfers between devices, swap(): return lax.ppermute(x, 'energy', [(i, i ^ k) for i in range(count)])  9.83 us
    pallas_call x2, Pallas kernels, build_sources(): pl.pallas_call(ordered(functools.partial(source_body, energy, owners), le...  8.63 us
    ppermute x6, waiting for transfers between devices, forward(): lax.ppermute(x, 'slab', [(2 * pair + i, 2 * pair + 2 + i) for i in range(...  8.5 us
    pallas_call x2, Pallas kernels, finish(): pl.pallas_call(body, in_specs=in_specs, out_specs=ANYWHERE, out_shape=jax...  8.33 us
    pallas_call x1, Pallas kernels, build_maps(): pl.pallas_call(lambda *refs: maps_body(*refs[:2], *refs[2 + len(after):])...  7.16 us
    ppermute x6, starting transfers between devices, forward(): lax.ppermute(x, 'slab', [(2 * pair + i, 2 * pair + 2 + i) for i in range(...  5.51 us
    ppermute x4, waiting for transfers between devices, other_of_pair(): lax.ppermute(x, 'slab', [(i, i ^ 1) for i in range(lax.axis_size('slab'))])  5.4 us
  transfers between devices with their start and end apart: 22, of which 10 were waited for; matrix products, arithmetic and copies ran while one was open for 0% of the time, Pallas kernels for 31%

profile of v6, /device:TPU:24, one launch (start us, length us, event | category | flops | bytes accessed | tf_op | source)
XLA Modules:
  0.0 117.4 jit_solution(2658676966047909711)
XLA Ops:
  0.0 1.3 %dynamic-slice_bitcast_fusion = (bf16[1,2,2,3,64,256]{5,4,3,2,1,0:T(8,128)(2,1)S(1)}, bf16[1,2,2,3,64,256]{5,4,3,2,1,0:T(8,128)(2,1)S(1)}) fusion(bf16[2,2,4,256,256]{4,3,2,1,0:T(8,128)(2,1)} %refs_1_.4, s32[]{:T(128)S(6)} %select_n.4, bf16[2,2,4,256,256]{4,3,2,1,0:T(8,128)(2,1)} %refs_0_.4), kind=kLoop, calls=%fused_computation.3 | loop fusion | bytes 1572868 | tf_op jit(solution)/shard_map/stack | solution.py:529
  1.3 0.1 pad_maximum_fusion.refs_2_
  1.4 1.6 %collective-permute-start.6 = (bf16[2,2,2,3,64,256]{5,4,3,2,1,0:T(8,128)(2,1)S(1)}, bf16[2,2,2,3,64,256]{5,4,3,2,1,0:T(8,128)(2,1)S(1)}, u32[]{:S(2)}, u32[]{:S(2)}) collective-permute-start(bf16[2,2,2,3,64,256]{5,4,3,2,1,0:T(8,128)(2,1)S(1)} %pad_maximum_fusion.refs_2_), channel_id=1, source_target_pairs={{0,2},{1,3},{2,0},{3,1},{4,6},{5,7},{6,4},{7,5},{8,10},{9,11},{10,... | collective-permute-start | bytes 2359304 | tf_op jit(solution)/shard_map/ppermute | solution.py:495
  3.0 1.6 %copy-done.2 = bf16[2,2,4,256,256]{4,3,2,1,0:T(8,128)(2,1)S(1)} copy-done((bf16[2,2,4,256,256]{4,3,2,1,0:T(8,128)(2,1)S(1)}, bf16[2,2,4,256,256]{4,3,2,1,0:T(8,128)(2,1)}, u32[]{:S(2)}) %copy-start.2) | copy-done | bytes 2097176
  4.6 0.1 pack.2
  4.8 0.1 collective-permute-start.5
  4.8 0.0 copy-start
  4.9 0.0 copy-start.3
  4.9 0.6 collective-permute-start.7
  5.5 0.5 pack.3
  6.0 0.5 copy-done
  6.4 0.3 copy-done.3
  6.7 7.2 %maps.1 = (bf16[2,4,2,256,512]{4,3,2,1,0:T(8,128)(2,1)S(1)}, bf16[2,4,2,256,512]{4,3,2,1,0:T(8,128)(2,1)S(1)}) custom-call(bf16[2,2,4,256,256]{4,3,2,1,0:T(8,128)(2,1)S(1)} %copy-done, bf16[2,4,256,256]{3,2,1,0:T(8,128)(2,1)S(1)} %copy-done.3, bf16[2,2,2,3,64,256]{5,4,3,2,1,0:T(8,128)(2,1)S(1)} %get-tuple-element.46.refs_2_.refs_0_), custom_call_target="tpu_custom_call" | custom-call | tf_op jit(solution)/shard_map/maps/pallas_call | solution.py:140
  13.9 0.1 slice_bitcast_fusion
  13.9 1.6 %collective-permute-start.4 = (bf16[2,256,512]{2,1,0:T(8,128)(2,1)S(1)}, bf16[2,256,512]{2,1,0:T(8,128)(2,1)S(1)}, u32[]{:S(2)}, u32[]{:S(2)}) collective-permute-start(bf16[2,256,512]{2,1,0:T(8,128)(2,1)S(1)} %get-tuple-element.77.refs_2_), channel_id=1, source_target_pairs={{0,4},{4,0},{8,12},{12,8},{16,20},{20,16},{24,28},{28,24},{1,5},{5... | collective-permute-start | bytes 1572872 | tf_op jit(solution)/shard_map/ppermute | solution.py:499
  15.5 0.5 collective-permute-start.3
  16.0 5.9 %collective-permute-done.6.refs_2_ = bf16[2,2,2,3,64,256]{5,4,3,2,1,0:T(8,128)(2,1)S(1)} collective-permute-done((bf16[2,2,2,3,64,256]{5,4,3,2,1,0:T(8,128)(2,1)S(1)}, bf16[2,2,2,3,64,256]{5,4,3,2,1,0:T(8,128)(2,1)S(1)}, u32[]{:S(2)}, u32[]{:S(2)}) %collective-permute-start.6) | collective-permute-done | bytes 786464 | tf_op jit(solution)/shard_map/ppermute | solution.py:495
  21.9 0.0 collective-permute-start
  21.9 0.0 collective-permute-done.5.refs_1_
  21.9 1.5 %collective-permute-start.1 = (bf16[2,2,2,1,64,256]{5,4,3,2,1,0:T(8,128)(2,1)S(1)}, bf16[2,2,2,1,64,256]{5,4,3,2,1,0:T(8,128)(2,1)S(1)}, u32[]{:S(2)}, u32[]{:S(2)}) collective-permute-start(bf16[2,2,2,1,64,256]{5,4,3,2,1,0:T(8,128)(2,1)S(1)} %get-tuple-element.44), channel_id=1, source_target_pairs={{0,2},{1,3},{2,0},{3,1},{4,6},{5,7},{6,4},{7,5},{8,10},{9,11},{10,... | collective-permute-start | bytes 786440 | tf_op jit(solution)/shard_map/ppermute | solution.py:495
  23.4 14.4 %collective-permute-done.7.refs_3_ = bf16[2,2,2,3,64,256]{5,4,3,2,1,0:T(8,128)(2,1)S(1)} collective-permute-done((bf16[2,2,2,3,64,256]{5,4,3,2,1,0:T(8,128)(2,1)S(1)}, bf16[2,2,2,3,64,256]{5,4,3,2,1,0:T(8,128)(2,1)S(1)}, u32[]{:S(2)}, u32[]{:S(2)}) %collective-permute-start.7) | collective-permute-done | bytes 786464 | tf_op jit(solution)/shard_map/ppermute | solution.py:495
  37.8 2.0 %collective-permute-start.2 = (bf16[2,2,2,1,64,256]{5,4,3,2,1,0:T(8,128)(2,1)S(1)}, bf16[2,2,2,1,64,256]{5,4,3,2,1,0:T(8,128)(2,1)S(1)}, u32[]{:S(2)}, u32[]{:S(2)}) collective-permute-start(bf16[2,2,2,1,64,256]{5,4,3,2,1,0:T(8,128)(2,1)S(1)} %get-tuple-element.45), channel_id=1, source_target_pairs={{0,3},{1,2},{2,1},{3,0},{4,7},{5,6},{6,5},{7,4},{8,11},{9,10},{10,... | collective-permute-start | bytes 786440 | tf_op jit(solution)/shard_map/ppermute | solution.py:495
  39.8 3.7 %convolve.2 = (bf16[4,2,64,256]{3,2,1,0:T(8,128)(2,1)S(1)}, bf16[4,2,64,256]{3,2,1,0:T(8,128)(2,1)S(1)}, bf16[4,2,64,256]{3,2,1,0:T(8,128)(2,1)S(1)}, bf16[4,2,6...) custom-call(bf16[2,2,2,3,64,256]{5,4,3,2,1,0:T(8,128)(2,1)S(1)} %get, ...), custom_call_target="tpu_custom_call" | custom-call | tf_op jit(solution)/shard_map/convolve/pallas_call | solution.py:259
  43.5 0.0 collective-permute-done.3.refs_1_
  43.5 1.5 %pair_maps.1 = (bf16[2,2,256,512]{3,2,1,0:T(8,128)(2,1)S(1)}, bf16[2,2,256,512]{3,2,1,0:T(8,128)(2,1)S(1)}, bf16[2,2,256,512]{3,2,1,0:T(8,128)(2,1)S(1)}) custom-call(bf16[2,256,512]{2,1,0:T(8,128)(2,1)S(1)} %get-tuple-element.78.refs_0_, bf16[2,256,512]{2,1,0:T(8,128)(2,1)S(1)} %collective-permute-done.3.refs_1_, ...), custom_call_target="tpu_custom_call" | custom-call | tf_op jit(solution)/shard_map/pair_maps/pallas_call | solution.py:184
  45.0 0.0 collective-permute-done.1.refs_2_
  45.0 2.9 %collective-permute-done.2.refs_3_ = bf16[2,2,2,1,64,256]{5,4,3,2,1,0:T(8,128)(2,1)S(1)} collective-permute-done((bf16[2,2,2,1,64,256]{5,4,3,2,1,0:T(8,128)(2,1)S(1)}, bf16[2,2,2,1,64,256]{5,4,3,2,1,0:T(8,128)(2,1)S(1)}, u32[]{:S(2)}, u32[]{:S(2)}) %collective-permute-start.2) | collective-permute-done | bytes 262176 | tf_op jit(solution)/shard_map/ppermute | solution.py:495
  47.9 1.3 %convolve.3 = (bf16[4,2,64,256]{3,2,1,0:T(8,128)(2,1)S(1)}, bf16[4,2,64,256]{3,2,1,0:T(8,128)(2,1)S(1)}, bf16[4,2,64,256]{3,2,1,0:T(8,128)(2,1)S(1)}, bf16[4,2,6...) custom-call(bf16[2,2,2,1,64,256]{5,4,3,2,1,0:T(8,128)(2,1)S(1)} %get, ...), custom_call_target="tpu_custom_call", output_to_operand_aliasing={{0}: (5, {}), {1}: (6, {}), {2}: (7, {}), {3}: (8, {}), {4}... | custom-call | tf_op jit(solution)/shard_map/convolve/pallas_call | solution.py:259
  49.2 1.4 %collective-permute-start.11 = (bf16[4,2,64,256]{3,2,1,0:T(8,128)(2,1)S(1)}, bf16[4,2,64,256]{3,2,1,0:T(8,128)(2,1)S(1)}, u32[]{:S(2)}, u32[]{:S(2)}) collective-permute-start(bf16[4,2,64,256]{3,2,1,0:T(8,128)(2,1)S(1)} %get-tuple-element.63), channel_id=1, source_target_pairs={{0,2},{1,3},{2,0},{3,1},{4,6},{5,7},{6,4},{7,5},{8,10},{9,11},{10,... | collective-permute-start | bytes 786440 | tf_op jit(solution)/shard_map/ppermute | solution.py:495
  50.6 0.8 collective-permute-start.12
  51.4 0.0 collective-permute-start.13
  51.4 1.5 %collective-permute-start.8 = (bf16[4,2,64,256]{3,2,1,0:T(8,128)(2,1)S(1)}, bf16[4,2,64,256]{3,2,1,0:T(8,128)(2,1)S(1)}, u32[]{:S(2)}, u32[]{:S(2)}) collective-permute-start(bf16[4,2,64,256]{3,2,1,0:T(8,128)(2,1)S(1)} %get-tuple-element.59), channel_id=1, source_target_pairs={{0,2},{1,3},{2,0},{3,1},{4,6},{5,7},{6,4},{7,5},{8,10},{9,11},{10,... | collective-permute-start | bytes 786440 | tf_op jit(solution)/shard_map/ppermute | solution.py:495
  52.9 0.3 collective-permute-start.9
  53.3 5.2 %collective-permute-done.11.refs_0_ = bf16[4,2,64,256]{3,2,1,0:T(8,128)(2,1)S(1)} collective-permute-done((bf16[4,2,64,256]{3,2,1,0:T(8,128)(2,1)S(1)}, bf16[4,2,64,256]{3,2,1,0:T(8,128)(2,1)S(1)}, u32[]{:S(2)}, u32[]{:S(2)}) %collective-permute-start.11) | collective-permute-done | bytes 262176 | tf_op jit(solution)/shard_map/ppermute | solution.py:495
  58.5 1.8 %entry_maps.1.refs_6_.refs_3_ = bf16[1,4,2,256,512]{4,3,2,1,0:T(8,128)(2,1)S(1)} custom-call(bf16[2,4,2,256,512]{4,3,2,1,0:T(8,128)(2,1)S(1)} %get-tuple-element.47.p_ref.refs_5_, bf16[2,2,256,512]{3,2,1,0:T(8,128)(2,1)S(1)} %get-tuple-element.67.i_ref.refs_4_, bf16[4,2,64,256]{3,2,1,0:T(8,128)(2,1)S(1)} %get-tuple-element.66._.refs_3_), custom_call_target="tpu_custom_call" | custom-call | tf_op jit(solution)/shard_map/entry_maps/pallas_call | solution.py:407
  60.3 3.4 %collective-permute-done.12.refs_1_ = bf16[4,2,64,256]{3,2,1,0:T(8,128)(2,1)S(1)} collective-permute-done((bf16[4,2,64,256]{3,2,1,0:T(8,128)(2,1)S(1)}, bf16[4,2,64,256]{3,2,1,0:T(8,128)(2,1)S(1)}, u32[]{:S(2)}, u32[]{:S(2)}) %collective-permute-start.12) | collective-permute-done | bytes 262176 | tf_op jit(solution)/shard_map/ppermute | solution.py:495
  63.7 0.0 collective-permute-done.13.refs_2_
  63.7 4.3 %sources.2 = (f32[4,256,512]{2,1,0:T(8,128)S(1)}, bf16[256,512]{1,0:T(8,128)(2,1)S(1)}) custom-call(bf16[4,2,64,256]{3,2,1,0:T(8,128)(2,1)S(1)} %collective-permute-done.11.refs_0_, bf16[4,2,64,256]{3,2,1,0:T(8,128)(2,1)S(1)} %collective-permute-done.12.refs_1_, bf16[4,2,64,256]{3,2,1,0:T(8,128)(2,1)S(1)} %collective-permute-done.13.refs_2_, ...), custom_call_target="tpu_custom_call" | custom-call | tf_op jit(solution)/shard_map/sources/pallas_call | solution.py:307
  68.0 1.6 %collective-permute-start.15 = (bf16[256,512]{1,0:T(8,128)(2,1)S(1)}, bf16[256,512]{1,0:T(8,128)(2,1)S(1)}, u32[]{:S(2)}, u32[]{:S(2)}) collective-permute-start(bf16[256,512]{1,0:T(8,128)(2,1)S(1)} %get-tuple-element.68.refs_6_.refs_1_), channel_id=1, source_target_pairs={{0,4},{4,0},{8,12},{12,8},{16,20},{20,16},{24,28},{28,24},{1,5},{5... | collective-permute-start | bytes 786440 | tf_op jit(solution)/shard_map/ppermute | solution.py:499
  69.6 0.1 collective-permute-done.8.refs_0_
  69.7 5.2 %collective-permute-done.9.refs_1_ = bf16[4,2,64,256]{3,2,1,0:T(8,128)(2,1)S(1)} collective-permute-done((bf16[4,2,64,256]{3,2,1,0:T(8,128)(2,1)S(1)}, bf16[4,2,64,256]{3,2,1,0:T(8,128)(2,1)S(1)}, u32[]{:S(2)}, u32[]{:S(2)}) %collective-permute-start.9) | collective-permute-done | bytes 262176 | tf_op jit(solution)/shard_map/ppermute | solution.py:495
  74.9 0.0 collective-permute-done.10.refs_2_
  74.9 4.3 %sources.3 = (f32[4,256,512]{2,1,0:T(8,128)S(1)}, bf16[256,512]{1,0:T(8,128)(2,1)S(1)}) custom-call(bf16[4,2,64,256]{3,2,1,0:T(8,128)(2,1)S(1)} %collective-permute-done.8.refs_0_, bf16[4,2,64,256]{3,2,1,0:T(8,128)(2,1)S(1)} %collective-permute-done.9.refs_1_, bf16[4,2,64,256]{3,2,1,0:T(8,128)(2,1)S(1)} %collective-permute-done.10.refs_2_, ...), custom_call_target="tpu_custom_call" | custom-call | tf_op jit(solution)/shard_map/sources/pallas_call | solution.py:307
  79.3 1.6 %collective-permute-start.14 = (bf16[256,512]{1,0:T(8,128)(2,1)S(1)}, bf16[256,512]{1,0:T(8,128)(2,1)S(1)}, u32[]{:S(2)}, u32[]{:S(2)}) collective-permute-start(bf16[256,512]{1,0:T(8,128)(2,1)S(1)} %get-tuple-element.69.refs_4_.refs_1_), channel_id=1, source_target_pairs={{0,4},{4,0},{8,12},{12,8},{16,20},{20,16},{24,28},{28,24},{1,5},{5... | collective-permute-start | bytes 786440 | tf_op jit(solution)/shard_map/ppermute | solution.py:499
  80.8 0.0 collective-permute-done.15.refs_0_.refs_3_
  80.8 0.9 pair_sum.2
  81.8 0.7 collective-permute-start.17
  82.5 5.4 %collective-permute-done.14.refs_0_.before_ref = bf16[256,512]{1,0:T(8,128)(2,1)S(1)} collective-permute-done((bf16[256,512]{1,0:T(8,128)(2,1)S(1)}, bf16[256,512]{1,0:T(8,128)(2,1)S(1)}, u32[]{:S(2)}, u32[]{:S(2)}) %collective-permute-start.14) | collective-permute-done | bytes 262176 | tf_op jit(solution)/shard_map/ppermute | solution.py:499
  87.8 0.9 pair_sum.3
  88.8 0.7 collective-permute-start.16
  89.5 0.9 combine.4.refs_3_
  90.4 0.7 collective-permute-start.19
  91.1 0.9 combine.5._
  92.1 0.9 collective-permute-start.18
  93.0 2.9 %part_known.1.refs_4_ = f32[4,256,512]{2,1,0:T(8,128)S(1)} custom-call(bf16[256,512]{1,0:T(8,128)(2,1)S(1)} %collective-permute-done.14.refs_0_.before_ref, bf16[2,4,2,256,512]{4,3,2,1,0:T(8,128)(2,1)S(1)} %get-tuple-element.47.p_ref.refs_5_, f32[4,256,512]{2,1,0:T(8,128)S(1)} %get-tuple-element.70.refs_2_.sum_ref, bf16[256,512]{1,0:T(8,128)(2,1)S(1)} %combine.5._), custom_call_target="tpu_custom_call" | custom-call | tf_op jit(solution)/shard_map/part_known/pallas_call | solution.py:425
  95.9 0.9 combine.6.refs_4_
  96.8 1.3 %collective-permute-start.21 = (bf16[256,512]{1,0:T(8,128)(2,1)S(1)}, bf16[256,512]{1,0:T(8,128)(2,1)S(1)}, u32[]{:S(2)}, u32[]{:S(2)}) collective-permute-start(bf16[256,512]{1,0:T(8,128)(2,1)S(1)} %combine.6.refs_4_), channel_id=1, source_target_pairs={{16,24},{20,28},{17,25},{21,29},{18,26},{22,30},{19,27},{23,31}} | collective-permute-start | bytes 786440 | tf_op jit(solution)/shard_map/ppermute | solution.py:503
  98.1 0.0 collective-permute-done.18.refs_1_
  98.2 0.9 combine.7.refs_7_.refs_5_
  99.1 1.3 %collective-permute-start.20 = (bf16[256,512]{1,0:T(8,128)(2,1)S(1)}, bf16[256,512]{1,0:T(8,128)(2,1)S(1)}, u32[]{:S(2)}, u32[]{:S(2)}) collective-permute-start(bf16[256,512]{1,0:T(8,128)(2,1)S(1)} %combine.7.refs_7_.refs_5_), channel_id=1, source_target_pairs={{16,24},{20,28},{17,25},{21,29},{18,26},{22,30},{19,27},{23,31}} | collective-permute-start | bytes 786440 | tf_op jit(solution)/shard_map/ppermute | solution.py:503
  100.4 7.8 %collective-permute-done.21.refs_2_ = bf16[256,512]{1,0:T(8,128)(2,1)S(1)} collective-permute-done((bf16[256,512]{1,0:T(8,128)(2,1)S(1)}, bf16[256,512]{1,0:T(8,128)(2,1)S(1)}, u32[]{:S(2)}, u32[]{:S(2)}) %collective-permute-start.21) | collective-permute-done | bytes 262176 | tf_op jit(solution)/shard_map/ppermute | solution.py:503
  108.2 4.6 %finish.2.refs_6_ = f32[2,2,4,256,256]{4,3,2,1,0:T(8,128)} custom-call(bf16[256,512]{1,0:T(8,128)(2,1)S(1)} %collective-permute-done.17.refs_0_, bf16[256,512]{1,0:T(8,128)(2,1)S(1)} %collective-permute-done.19.refs_1_, bf16[256,512]{1,0:T(8,128)(2,1)S(1)} %collective-permute-done.21.refs_2_, bf16[256,512]{1,0:T(8,128)(2,1)S(1)} %collective-permute-done.15.refs_0_.refs_3_, ...), custom_call_target="tpu_custom_call" | custom-call | tf_op jit(solution)/shard_map/finish/pallas_call | solution.py:480
  112.8 0.7 collective-permute-done.20.refs_2_
  113.5 3.7 %finish.3 = f32[2,2,4,256,256]{4,3,2,1,0:T(8,128)} custom-call(bf16[256,512]{1,0:T(8,128)(2,1)S(1)} %collective-permute-done.16.refs_0_, bf16[256,512]{1,0:T(8,128)(2,1)S(1)} %collective-permute-done.18.refs_1_, bf16[256,512]{1,0:T(8,128)(2,1)S(1)} %collective-permute-done.20.refs_2_, ...), custom_call_target="tpu_custom_call", output_to_operand_aliasing={{}: (6, {})} | custom-call | tf_op jit(solution)/shard_map/finish/pallas_call | solution.py:480
  (9 shorter events, 0.0 us)
Async XLA Ops:
  0.0 3.0 %copy-start.1 = (bf16[2,2,4,256,256]{4,3,2,1,0:T(8,128)(2,1)S(1)}, bf16[2,2,4,256,256]{4,3,2,1,0:T(8,128)(2,1)}, u32[]{:S(2)}) copy-start(bf16[2,2,4,256,256]{4,3,2,1,0:T(8,128)(2,1)} %refs_0_.4) | copy-start | bytes 6291460
  1.4 20.5 %collective-permute-start.6 = (bf16[2,2,2,3,64,256]{5,4,3,2,1,0:T(8,128)(2,1)S(1)}, bf16[2,2,2,3,64,256]{5,4,3,2,1,0:T(8,128)(2,1)S(1)}, u32[]{:S(2)}, u32[]{:S(2)}) collective-permute-start(bf16[2,2,2,3,64,256]{5,4,3,2,1,0:T(8,128)(2,1)S(1)} %pad_maximum_fusion.refs_2_), channel_id=1, source_target_pairs={{0,2},{1,3},{2,0},{3,1},{4,6},{5,7},{6,4},{7,5},{8,10},{9,11},{10,... | collective-permute-start | bytes 2359304 | tf_op jit(solution)/shard_map/ppermute | solution.py:495
  3.0 1.6 %copy-start.2 = (bf16[2,2,4,256,256]{4,3,2,1,0:T(8,128)(2,1)S(1)}, bf16[2,2,4,256,256]{4,3,2,1,0:T(8,128)(2,1)}, u32[]{:S(2)}) copy-start(bf16[2,2,4,256,256]{4,3,2,1,0:T(8,128)(2,1)} %refs_1_.4) | copy-start | bytes 6291460
  4.8 17.2 %collective-permute-start.5 = (bf16[2,2,2,3,64,256]{5,4,3,2,1,0:T(8,128)(2,1)S(1)}, bf16[2,2,2,3,64,256]{5,4,3,2,1,0:T(8,128)(2,1)S(1)}, u32[]{:S(2)}, u32[]{:S(2)}) collective-permute-start(bf16[2,2,2,3,64,256]{5,4,3,2,1,0:T(8,128)(2,1)S(1)} %get-tuple-element.48), channel_id=1, source_target_pairs={{0,1},{1,0},{2,3},{3,2},{4,5},{5,4},{6,7},{7,6},{8,9},{9,8},{10,11... | collective-permute-start | bytes 2359304 | tf_op jit(solution)/shard_map/ppermute | solution.py:495
  4.8 1.6 %copy-start = (bf16[2,2,4,256,256]{4,3,2,1,0:T(8,128)(2,1)S(1)}, bf16[2,2,4,256,256]{4,3,2,1,0:T(8,128)(2,1)}, u32[]{:S(2)}) copy-start(bf16[2,2,4,256,256]{4,3,2,1,0:T(8,128)(2,1)} %refs_4_.3) | copy-start | bytes 6291460
  4.9 1.8 %copy-start.3 = (bf16[2,4,256,256]{3,2,1,0:T(8,128)(2,1)S(1)}, bf16[2,4,256,256]{3,2,1,0:T(8,128)(2,1)}, u32[]{:S(2)}) copy-start(bf16[2,4,256,256]{3,2,1,0:T(8,128)(2,1)} %refs_1_.5) | copy-start | bytes 3145732
  4.9 32.9 %collective-permute-start.7 = (bf16[2,2,2,3,64,256]{5,4,3,2,1,0:T(8,128)(2,1)S(1)}, bf16[2,2,2,3,64,256]{5,4,3,2,1,0:T(8,128)(2,1)S(1)}, u32[]{:S(2)}, u32[]{:S(2)}) collective-permute-start(bf16[2,2,2,3,64,256]{5,4,3,2,1,0:T(8,128)(2,1)S(1)} %get-tuple-element.41.refs_2_), channel_id=1, source_target_pairs={{0,3},{1,2},{2,1},{3,0},{4,7},{5,6},{6,5},{7,4},{8,11},{9,10},{10,... | collective-permute-start | bytes 2359304 | tf_op jit(solution)/shard_map/ppermute | solution.py:495
  13.9 29.6 %collective-permute-start.4 = (bf16[2,256,512]{2,1,0:T(8,128)(2,1)S(1)}, bf16[2,256,512]{2,1,0:T(8,128)(2,1)S(1)}, u32[]{:S(2)}, u32[]{:S(2)}) collective-permute-start(bf16[2,256,512]{2,1,0:T(8,128)(2,1)S(1)} %get-tuple-element.77.refs_2_), channel_id=1, source_target_pairs={{0,4},{4,0},{8,12},{12,8},{16,20},{20,16},{24,28},{28,24},{1,5},{5... | collective-permute-start | bytes 1572872 | tf_op jit(solution)/shard_map/ppermute | solution.py:499
  15.5 28.0 %collective-permute-start.3 = (bf16[2,256,512]{2,1,0:T(8,128)(2,1)S(1)}, bf16[2,256,512]{2,1,0:T(8,128)(2,1)S(1)}, u32[]{:S(2)}, u32[]{:S(2)}) collective-permute-start(bf16[2,256,512]{2,1,0:T(8,128)(2,1)S(1)} %get-tuple-element.78.refs_0_), channel_id=1, source_target_pairs={{0,4},{4,0},{8,12},{12,8},{16,20},{20,16},{24,28},{28,24},{1,5},{5... | collective-permute-start | bytes 1572872 | tf_op jit(solution)/shard_map/ppermute | solution.py:499
  21.9 23.1 %collective-permute-start = (bf16[2,2,2,1,64,256]{5,4,3,2,1,0:T(8,128)(2,1)S(1)}, bf16[2,2,2,1,64,256]{5,4,3,2,1,0:T(8,128)(2,1)S(1)}, u32[]{:S(2)}, u32[]{:S(2)}) collective-permute-start(bf16[2,2,2,1,64,256]{5,4,3,2,1,0:T(8,128)(2,1)S(1)} %get-tuple-element.43), channel_id=1, source_target_pairs={{0,1},{1,0},{2,3},{3,2},{4,5},{5,4},{6,7},{7,6},{8,9},{9,8},{10,11... | collective-permute-start | bytes 786440 | tf_op jit(solution)/shard_map/ppermute | solution.py:495
  21.9 23.1 %collective-permute-start.1 = (bf16[2,2,2,1,64,256]{5,4,3,2,1,0:T(8,128)(2,1)S(1)}, bf16[2,2,2,1,64,256]{5,4,3,2,1,0:T(8,128)(2,1)S(1)}, u32[]{:S(2)}, u32[]{:S(2)}) collective-permute-start(bf16[2,2,2,1,64,256]{5,4,3,2,1,0:T(8,128)(2,1)S(1)} %get-tuple-element.44), channel_id=1, source_target_pairs={{0,2},{1,3},{2,0},{3,1},{4,6},{5,7},{6,4},{7,5},{8,10},{9,11},{10,... | collective-permute-start | bytes 786440 | tf_op jit(solution)/shard_map/ppermute | solution.py:495
  37.8 10.1 %collective-permute-start.2 = (bf16[2,2,2,1,64,256]{5,4,3,2,1,0:T(8,128)(2,1)S(1)}, bf16[2,2,2,1,64,256]{5,4,3,2,1,0:T(8,128)(2,1)S(1)}, u32[]{:S(2)}, u32[]{:S(2)}) collective-permute-start(bf16[2,2,2,1,64,256]{5,4,3,2,1,0:T(8,128)(2,1)S(1)} %get-tuple-element.45), channel_id=1, source_target_pairs={{0,3},{1,2},{2,1},{3,0},{4,7},{5,6},{6,5},{7,4},{8,11},{9,10},{10,... | collective-permute-start | bytes 786440 | tf_op jit(solution)/shard_map/ppermute | solution.py:495
  49.2 9.2 %collective-permute-start.11 = (bf16[4,2,64,256]{3,2,1,0:T(8,128)(2,1)S(1)}, bf16[4,2,64,256]{3,2,1,0:T(8,128)(2,1)S(1)}, u32[]{:S(2)}, u32[]{:S(2)}) collective-permute-start(bf16[4,2,64,256]{3,2,1,0:T(8,128)(2,1)S(1)} %get-tuple-element.63), channel_id=1, source_target_pairs={{0,2},{1,3},{2,0},{3,1},{4,6},{5,7},{6,4},{7,5},{8,10},{9,11},{10,... | collective-permute-start | bytes 786440 | tf_op jit(solution)/shard_map/ppermute | solution.py:495
  50.6 13.1 %collective-permute-start.12 = (bf16[4,2,64,256]{3,2,1,0:T(8,128)(2,1)S(1)}, bf16[4,2,64,256]{3,2,1,0:T(8,128)(2,1)S(1)}, u32[]{:S(2)}, u32[]{:S(2)}) collective-permute-start(bf16[4,2,64,256]{3,2,1,0:T(8,128)(2,1)S(1)} %get-tuple-element.64), channel_id=1, source_target_pairs={{0,3},{1,2},{2,1},{3,0},{4,7},{5,6},{6,5},{7,4},{8,11},{9,10},{10,... | collective-permute-start | bytes 786440 | tf_op jit(solution)/shard_map/ppermute | solution.py:495
  51.4 12.3 %collective-permute-start.13 = (bf16[4,2,64,256]{3,2,1,0:T(8,128)(2,1)S(1)}, bf16[4,2,64,256]{3,2,1,0:T(8,128)(2,1)S(1)}, u32[]{:S(2)}, u32[]{:S(2)}) collective-permute-start(bf16[4,2,64,256]{3,2,1,0:T(8,128)(2,1)S(1)} %get-tuple-element.65), channel_id=1, source_target_pairs={{0,1},{1,0},{2,3},{3,2},{4,5},{5,4},{6,7},{7,6},{8,9},{9,8},{10,11... | collective-permute-start | bytes 786440 | tf_op jit(solution)/shard_map/ppermute | solution.py:495
  51.4 18.3 %collective-permute-start.8 = (bf16[4,2,64,256]{3,2,1,0:T(8,128)(2,1)S(1)}, bf16[4,2,64,256]{3,2,1,0:T(8,128)(2,1)S(1)}, u32[]{:S(2)}, u32[]{:S(2)}) collective-permute-start(bf16[4,2,64,256]{3,2,1,0:T(8,128)(2,1)S(1)} %get-tuple-element.59), channel_id=1, source_target_pairs={{0,2},{1,3},{2,0},{3,1},{4,6},{5,7},{6,4},{7,5},{8,10},{9,11},{10,... | collective-permute-start | bytes 786440 | tf_op jit(solution)/shard_map/ppermute | solution.py:495
  52.9 22.0 %collective-permute-start.9 = (bf16[4,2,64,256]{3,2,1,0:T(8,128)(2,1)S(1)}, bf16[4,2,64,256]{3,2,1,0:T(8,128)(2,1)S(1)}, u32[]{:S(2)}, u32[]{:S(2)}) collective-permute-start(bf16[4,2,64,256]{3,2,1,0:T(8,128)(2,1)S(1)} %get-tuple-element.60), channel_id=1, source_target_pairs={{0,3},{1,2},{2,1},{3,0},{4,7},{5,6},{6,5},{7,4},{8,11},{9,10},{10,... | collective-permute-start | bytes 786440 | tf_op jit(solution)/shard_map/ppermute | solution.py:495
  58.5 16.5 %collective-permute-start.10 = (bf16[4,2,64,256]{3,2,1,0:T(8,128)(2,1)S(1)}, bf16[4,2,64,256]{3,2,1,0:T(8,128)(2,1)S(1)}, u32[]{:S(2)}, u32[]{:S(2)}) collective-permute-start(bf16[4,2,64,256]{3,2,1,0:T(8,128)(2,1)S(1)} %get-tuple-element.61), channel_id=1, source_target_pairs={{0,1},{1,0},{2,3},{3,2},{4,5},{5,4},{6,7},{7,6},{8,9},{9,8},{10,11... | collective-permute-start | bytes 786440 | tf_op jit(solution)/shard_map/ppermute | solution.py:495
  68.0 12.8 %collective-permute-start.15 = (bf16[256,512]{1,0:T(8,128)(2,1)S(1)}, bf16[256,512]{1,0:T(8,128)(2,1)S(1)}, u32[]{:S(2)}, u32[]{:S(2)}) collective-permute-start(bf16[256,512]{1,0:T(8,128)(2,1)S(1)} %get-tuple-element.68.refs_6_.refs_1_), channel_id=1, source_target_pairs={{0,4},{4,0},{8,12},{12,8},{16,20},{20,16},{24,28},{28,24},{1,5},{5... | collective-permute-start | bytes 786440 | tf_op jit(solution)/shard_map/ppermute | solution.py:499
  79.3 8.6 %collective-permute-start.14 = (bf16[256,512]{1,0:T(8,128)(2,1)S(1)}, bf16[256,512]{1,0:T(8,128)(2,1)S(1)}, u32[]{:S(2)}, u32[]{:S(2)}) collective-permute-start(bf16[256,512]{1,0:T(8,128)(2,1)S(1)} %get-tuple-element.69.refs_4_.refs_1_), channel_id=1, source_target_pairs={{0,4},{4,0},{8,12},{12,8},{16,20},{20,16},{24,28},{28,24},{1,5},{5... | collective-permute-start | bytes 786440 | tf_op jit(solution)/shard_map/ppermute | solution.py:499
  81.8 7.7 %collective-permute-start.17 = (bf16[256,512]{1,0:T(8,128)(2,1)S(1)}, bf16[256,512]{1,0:T(8,128)(2,1)S(1)}, u32[]{:S(2)}, u32[]{:S(2)}) collective-permute-start(bf16[256,512]{1,0:T(8,128)(2,1)S(1)} %get-tuple-element.73.refs_4_), channel_id=1, source_target_pairs={{0,8},{4,12},{1,9},{5,13},{2,10},{6,14},{3,11},{7,15}} | collective-permute-start | bytes 786440 | tf_op jit(solution)/shard_map/ppermute | solution.py:503
  88.8 2.3 %collective-permute-start.16 = (bf16[256,512]{1,0:T(8,128)(2,1)S(1)}, bf16[256,512]{1,0:T(8,128)(2,1)S(1)}, u32[]{:S(2)}, u32[]{:S(2)}) collective-permute-start(bf16[256,512]{1,0:T(8,128)(2,1)S(1)} %get-tuple-element.74.refs_3_), channel_id=1, source_target_pairs={{0,8},{4,12},{1,9},{5,13},{2,10},{6,14},{3,11},{7,15}} | collective-permute-start | bytes 786440 | tf_op jit(solution)/shard_map/ppermute | solution.py:503
  90.4 5.5 %collective-permute-start.19 = (bf16[256,512]{1,0:T(8,128)(2,1)S(1)}, bf16[256,512]{1,0:T(8,128)(2,1)S(1)}, u32[]{:S(2)}, u32[]{:S(2)}) collective-permute-start(bf16[256,512]{1,0:T(8,128)(2,1)S(1)} %combine.4.refs_3_), channel_id=1, source_target_pairs={{8,16},{12,20},{9,17},{13,21},{10,18},{14,22},{11,19},{15,23}} | collective-permute-start | bytes 786440 | tf_op jit(solution)/shard_map/ppermute | solution.py:503
  92.1 6.1 %collective-permute-start.18 = (bf16[256,512]{1,0:T(8,128)(2,1)S(1)}, bf16[256,512]{1,0:T(8,128)(2,1)S(1)}, u32[]{:S(2)}, u32[]{:S(2)}) collective-permute-start(bf16[256,512]{1,0:T(8,128)(2,1)S(1)} %combine.5._), channel_id=1, source_target_pairs={{8,16},{12,20},{9,17},{13,21},{10,18},{14,22},{11,19},{15,23}} | collective-permute-start | bytes 786440 | tf_op jit(solution)/shard_map/ppermute | solution.py:503
  96.8 11.3 %collective-permute-start.21 = (bf16[256,512]{1,0:T(8,128)(2,1)S(1)}, bf16[256,512]{1,0:T(8,128)(2,1)S(1)}, u32[]{:S(2)}, u32[]{:S(2)}) collective-permute-start(bf16[256,512]{1,0:T(8,128)(2,1)S(1)} %combine.6.refs_4_), channel_id=1, source_target_pairs={{16,24},{20,28},{17,25},{21,29},{18,26},{22,30},{19,27},{23,31}} | collective-permute-start | bytes 786440 | tf_op jit(solution)/shard_map/ppermute | solution.py:503
  99.1 14.4 %collective-permute-start.20 = (bf16[256,512]{1,0:T(8,128)(2,1)S(1)}, bf16[256,512]{1,0:T(8,128)(2,1)S(1)}, u32[]{:S(2)}, u32[]{:S(2)}) collective-permute-start(bf16[256,512]{1,0:T(8,128)(2,1)S(1)} %combine.7.refs_7_.refs_5_), channel_id=1, source_target_pairs={{16,24},{20,28},{17,25},{21,29},{18,26},{22,30},{19,27},{23,31}} | collective-permute-start | bytes 786440 | tf_op jit(solution)/shard_map/ppermute | solution.py:503

commit v7 on v6

--- a/solution.py
+++ b/solution.py
@@ -9,7 +9,7 @@
 
 BF16 = jnp.bfloat16
 F32 = jnp.float32
-VMEM_LIMIT = 24 * 1024 * 1024
+VMEM_LIMIT = 36 * 1024 * 1024
 
 
 def params():
@@ -54,16 +54,14 @@
 def times_wide(a_high, a_low, x):
     order = x.shape[0]
     x_high, x_low = split(x)
-    xh = panel(x_high[:, :order], x_high[:, order:])
-    xl = panel(x_low[:, :order], x_low[:, order:])
-    left = jnp.concatenate([a_high, a_high, a_low], axis=1)
-    return dot(left, jnp.concatenate([xh, xl, xh], axis=0))
+    both = dot(jnp.concatenate([a_high, a_low], axis=0), panel(x_high[:, :order], x_high[:, order:]))
+    return both[:order] + both[order:] + dot(a_high, panel(x_low[:, :order], x_low[:, order:]))
 
 
 def times_narrow(a_high, a_low, re, im):
-    xp = panel(re, im)
-    left = jnp.concatenate([a_high, a_low], axis=1)
-    return dot(left, jnp.concatenate([xp, xp], axis=0))
+    order = re.shape[0]
+    both = dot(jnp.concatenate([a_high, a_low], axis=0), panel(re, im))
+    return both[:order] + both[order:]
 
 
 def times_adjoint(y, t_high, t_low):
@@ -71,8 +69,8 @@
     y_high, y_low = split(y)
     th = panel(t_high[:, :order], t_high[:, order:])
     tl = panel(t_low[:, :order], t_low[:, order:])
-    left = jnp.concatenate([y_high, y_low, y_high], axis=1)
-    return dot_nt(left, jnp.concatenate([th, th, tl], axis=1))
+    both = dot_nt(jnp.concatenate([y_high, y_low], axis=0), th)
+    return both[:order] + both[order:] + dot_nt(y_high, tl)
 
 
 def panels(ref):

time: 118 us -> 117 us (level)
  no operation moved by 1% of the time
where the time goes in v7:
time: 117 us
  waiting for transfers between devices  51.1 us (44%)
  Pallas kernels  41.3 us (35%)
  starting transfers between devices  20.5 us (18%)
  local copies, waits for them, and re-layouts  3.74 us (3%)
    ppermute x12, waiting for transfers between devices, swap(): return lax.ppermute(x, 'energy', [(i, i ^ k) for i in range(count)])  37.2 us
    ppermute x12, starting transfers between devices, swap(): return lax.ppermute(x, 'energy', [(i, i ^ k) for i in range(count)])  9.78 us
    ppermute x6, waiting for transfers between devices, forward(): lax.ppermute(x, 'slab', [(2 * pair + i, 2 * pair + 2 + i) for i in range(...  8.71 us
    pallas_call x2, Pallas kernels, build_sources(): pl.pallas_call(ordered(functools.partial(source_body, energy, owners), le...  8.63 us
    pallas_call x2, Pallas kernels, finish(): pl.pallas_call(body, in_specs=in_specs, out_specs=ANYWHERE, out_shape=jax...  8.32 us
    pallas_call x1, Pallas kernels, build_maps(): pl.pallas_call(lambda *refs: maps_body(*refs[:2], *refs[2 + len(after):])...  7.11 us
    ppermute x6, starting transfers between devices, forward(): lax.ppermute(x, 'slab', [(2 * pair + i, 2 * pair + 2 + i) for i in range(...  5.47 us
    ppermute x4, waiting for transfers between devices, other_of_pair(): lax.ppermute(x, 'slab', [(i, i ^ 1) for i in range(lax.axis_size('slab'))])  5.23 us
  transfers between devices with their start and end apart: 22, of which 10 were waited for; matrix products, arithmetic and copies ran while one was open for 0% of the time, Pallas kernels for 31%

profile of v7, /device:TPU:24, one launch (start us, length us, event | category | flops | bytes accessed | tf_op | source)
XLA Modules:
  0.0 117.2 jit_solution(14979766678676658279)
XLA Ops:
  0.0 1.3 %dynamic-slice_bitcast_fusion = (bf16[1,2,2,3,64,256]{5,4,3,2,1,0:T(8,128)(2,1)S(1)}, bf16[1,2,2,3,64,256]{5,4,3,2,1,0:T(8,128)(2,1)S(1)}) fusion(bf16[2,2,4,256,256]{4,3,2,1,0:T(8,128)(2,1)} %refs_1_.4, s32[]{:T(128)S(6)} %select_n.4, bf16[2,2,4,256,256]{4,3,2,1,0:T(8,128)(2,1)} %refs_0_.4), kind=kLoop, calls=%fused_computation.3 | loop fusion | bytes 1572868 | tf_op jit(solution)/shard_map/stack | solution.py:527
  1.3 0.1 pad_maximum_fusion.refs_2_
  1.4 1.6 %collective-permute-start.6 = (bf16[2,2,2,3,64,256]{5,4,3,2,1,0:T(8,128)(2,1)S(1)}, bf16[2,2,2,3,64,256]{5,4,3,2,1,0:T(8,128)(2,1)S(1)}, u32[]{:S(2)}, u32[]{:S(2)}) collective-permute-start(bf16[2,2,2,3,64,256]{5,4,3,2,1,0:T(8,128)(2,1)S(1)} %pad_maximum_fusion.refs_2_), channel_id=1, source_target_pairs={{0,2},{1,3},{2,0},{3,1},{4,6},{5,7},{6,4},{7,5},{8,10},{9,11},{10,... | collective-permute-start | bytes 2359304 | tf_op jit(solution)/shard_map/ppermute | solution.py:493
  3.0 1.6 %copy-done.2 = bf16[2,2,4,256,256]{4,3,2,1,0:T(8,128)(2,1)S(1)} copy-done((bf16[2,2,4,256,256]{4,3,2,1,0:T(8,128)(2,1)S(1)}, bf16[2,2,4,256,256]{4,3,2,1,0:T(8,128)(2,1)}, u32[]{:S(2)}) %copy-start.2) | copy-done | bytes 2097176
  4.6 0.1 pack.2
  4.8 0.1 collective-permute-start.5
  4.8 0.0 copy-start
  4.9 0.0 copy-start.5
  4.9 0.6 collective-permute-start.7
  5.5 0.5 pack.3
  6.0 0.5 copy-done
  6.4 0.3 copy-done.5
  6.7 7.1 %maps.1 = (bf16[2,4,2,256,512]{4,3,2,1,0:T(8,128)(2,1)S(1)}, bf16[2,4,2,256,512]{4,3,2,1,0:T(8,128)(2,1)S(1)}) custom-call(bf16[2,2,4,256,256]{4,3,2,1,0:T(8,128)(2,1)S(1)} %copy-done, bf16[2,4,256,256]{3,2,1,0:T(8,128)(2,1)S(1)} %copy-done.5, bf16[2,2,2,3,64,256]{5,4,3,2,1,0:T(8,128)(2,1)S(1)} %get-tuple-element.46.refs_2_.refs_0_), custom_call_target="tpu_custom_call" | custom-call | tf_op jit(solution)/shard_map/maps/pallas_call | solution.py:138
  13.8 0.1 slice_bitcast_fusion
  13.9 1.6 %collective-permute-start.4 = (bf16[2,256,512]{2,1,0:T(8,128)(2,1)S(1)}, bf16[2,256,512]{2,1,0:T(8,128)(2,1)S(1)}, u32[]{:S(2)}, u32[]{:S(2)}) collective-permute-start(bf16[2,256,512]{2,1,0:T(8,128)(2,1)S(1)} %get-tuple-element.77.refs_2_), channel_id=1, source_target_pairs={{0,4},{4,0},{8,12},{12,8},{16,20},{20,16},{24,28},{28,24},{1,5},{5... | collective-permute-start | bytes 1572872 | tf_op jit(solution)/shard_map/ppermute | solution.py:497
  15.5 0.5 collective-permute-start.3
  16.0 5.9 %collective-permute-done.6.refs_2_ = bf16[2,2,2,3,64,256]{5,4,3,2,1,0:T(8,128)(2,1)S(1)} collective-permute-done((bf16[2,2,2,3,64,256]{5,4,3,2,1,0:T(8,128)(2,1)S(1)}, bf16[2,2,2,3,64,256]{5,4,3,2,1,0:T(8,128)(2,1)S(1)}, u32[]{:S(2)}, u32[]{:S(2)}) %collective-permute-start.6) | collective-permute-done | bytes 786464 | tf_op jit(solution)/shard_map/ppermute | solution.py:493
  21.9 1.5 %collective-permute-start.1 = (bf16[2,2,2,1,64,256]{5,4,3,2,1,0:T(8,128)(2,1)S(1)}, bf16[2,2,2,1,64,256]{5,4,3,2,1,0:T(8,128)(2,1)S(1)}, u32[]{:S(2)}, u32[]{:S(2)}) collective-permute-start(bf16[2,2,2,1,64,256]{5,4,3,2,1,0:T(8,128)(2,1)S(1)} %get-tuple-element.44), channel_id=1, source_target_pairs={{0,2},{1,3},{2,0},{3,1},{4,6},{5,7},{6,4},{7,5},{8,10},{9,11},{10,... | collective-permute-start | bytes 786440 | tf_op jit(solution)/shard_map/ppermute | solution.py:493
  23.4 14.4 %collective-permute-done.7.refs_3_ = bf16[2,2,2,3,64,256]{5,4,3,2,1,0:T(8,128)(2,1)S(1)} collective-permute-done((bf16[2,2,2,3,64,256]{5,4,3,2,1,0:T(8,128)(2,1)S(1)}, bf16[2,2,2,3,64,256]{5,4,3,2,1,0:T(8,128)(2,1)S(1)}, u32[]{:S(2)}, u32[]{:S(2)}) %collective-permute-start.7) | collective-permute-done | bytes 786464 | tf_op jit(solution)/shard_map/ppermute | solution.py:493
  37.8 1.9 %collective-permute-start.2 = (bf16[2,2,2,1,64,256]{5,4,3,2,1,0:T(8,128)(2,1)S(1)}, bf16[2,2,2,1,64,256]{5,4,3,2,1,0:T(8,128)(2,1)S(1)}, u32[]{:S(2)}, u32[]{:S(2)}) collective-permute-start(bf16[2,2,2,1,64,256]{5,4,3,2,1,0:T(8,128)(2,1)S(1)} %get-tuple-element.45), channel_id=1, source_target_pairs={{0,3},{1,2},{2,1},{3,0},{4,7},{5,6},{6,5},{7,4},{8,11},{9,10},{10,... | collective-permute-start | bytes 786440 | tf_op jit(solution)/shard_map/ppermute | solution.py:493
  39.7 3.7 %convolve.2 = (bf16[4,2,64,256]{3,2,1,0:T(8,128)(2,1)S(1)}, bf16[4,2,64,256]{3,2,1,0:T(8,128)(2,1)S(1)}, bf16[4,2,64,256]{3,2,1,0:T(8,128)(2,1)S(1)}, bf16[4,2,6...) custom-call(bf16[2,2,2,3,64,256]{5,4,3,2,1,0:T(8,128)(2,1)S(1)} %get, ...), custom_call_target="tpu_custom_call" | custom-call | tf_op jit(solution)/shard_map/convolve/pallas_call | solution.py:257
  43.4 0.0 collective-permute-done.4.refs_3_
  43.5 0.0 collective-permute-done.3.refs_1_
  43.5 1.5 %pair_maps.1 = (bf16[2,2,256,512]{3,2,1,0:T(8,128)(2,1)S(1)}, bf16[2,2,256,512]{3,2,1,0:T(8,128)(2,1)S(1)}, bf16[2,2,256,512]{3,2,1,0:T(8,128)(2,1)S(1)}) custom-call(bf16[2,256,512]{2,1,0:T(8,128)(2,1)S(1)} %get-tuple-element.78.refs_0_, bf16[2,256,512]{2,1,0:T(8,128)(2,1)S(1)} %collective-permute-done.3.refs_1_, ...), custom_call_target="tpu_custom_call" | custom-call | tf_op jit(solution)/shard_map/pair_maps/pallas_call | solution.py:182
  45.0 0.0 collective-permute-done.refs_1_
  45.0 2.9 %collective-permute-done.2.refs_3_ = bf16[2,2,2,1,64,256]{5,4,3,2,1,0:T(8,128)(2,1)S(1)} collective-permute-done((bf16[2,2,2,1,64,256]{5,4,3,2,1,0:T(8,128)(2,1)S(1)}, bf16[2,2,2,1,64,256]{5,4,3,2,1,0:T(8,128)(2,1)S(1)}, u32[]{:S(2)}, u32[]{:S(2)}) %collective-permute-start.2) | collective-permute-done | bytes 262176 | tf_op jit(solution)/shard_map/ppermute | solution.py:493
  47.9 1.1 convolve.3
  49.0 1.4 %collective-permute-start.11 = (bf16[4,2,64,256]{3,2,1,0:T(8,128)(2,1)S(1)}, bf16[4,2,64,256]{3,2,1,0:T(8,128)(2,1)S(1)}, u32[]{:S(2)}, u32[]{:S(2)}) collective-permute-start(bf16[4,2,64,256]{3,2,1,0:T(8,128)(2,1)S(1)} %get-tuple-element.63), channel_id=1, source_target_pairs={{0,2},{1,3},{2,0},{3,1},{4,6},{5,7},{6,4},{7,5},{8,10},{9,11},{10,... | collective-permute-start | bytes 786440 | tf_op jit(solution)/shard_map/ppermute | solution.py:493
  50.4 0.8 collective-permute-start.12
  51.2 0.0 collective-permute-start.13
  51.2 1.5 %collective-permute-start.8 = (bf16[4,2,64,256]{3,2,1,0:T(8,128)(2,1)S(1)}, bf16[4,2,64,256]{3,2,1,0:T(8,128)(2,1)S(1)}, u32[]{:S(2)}, u32[]{:S(2)}) collective-permute-start(bf16[4,2,64,256]{3,2,1,0:T(8,128)(2,1)S(1)} %get-tuple-element.59), channel_id=1, source_target_pairs={{0,2},{1,3},{2,0},{3,1},{4,6},{5,7},{6,4},{7,5},{8,10},{9,11},{10,... | collective-permute-start | bytes 786440 | tf_op jit(solution)/shard_map/ppermute | solution.py:493
  52.8 0.3 collective-permute-start.9
  53.1 5.2 %collective-permute-done.11.refs_0_ = bf16[4,2,64,256]{3,2,1,0:T(8,128)(2,1)S(1)} collective-permute-done((bf16[4,2,64,256]{3,2,1,0:T(8,128)(2,1)S(1)}, bf16[4,2,64,256]{3,2,1,0:T(8,128)(2,1)S(1)}, u32[]{:S(2)}, u32[]{:S(2)}) %collective-permute-start.11) | collective-permute-done | bytes 262176 | tf_op jit(solution)/shard_map/ppermute | solution.py:493
  58.3 1.8 %entry_maps.1.refs_6_.refs_3_ = bf16[1,4,2,256,512]{4,3,2,1,0:T(8,128)(2,1)S(1)} custom-call(bf16[2,4,2,256,512]{4,3,2,1,0:T(8,128)(2,1)S(1)} %get-tuple-element.47.p_ref.refs_5_, bf16[2,2,256,512]{3,2,1,0:T(8,128)(2,1)S(1)} %get-tuple-element.67.i_ref.refs_4_, bf16[4,2,64,256]{3,2,1,0:T(8,128)(2,1)S(1)} %get-tuple-element.66._.refs_3_), custom_call_target="tpu_custom_call" | custom-call | tf_op jit(solution)/shard_map/entry_maps/pallas_call | solution.py:405
  60.1 3.4 %collective-permute-done.12.refs_1_ = bf16[4,2,64,256]{3,2,1,0:T(8,128)(2,1)S(1)} collective-permute-done((bf16[4,2,64,256]{3,2,1,0:T(8,128)(2,1)S(1)}, bf16[4,2,64,256]{3,2,1,0:T(8,128)(2,1)S(1)}, u32[]{:S(2)}, u32[]{:S(2)}) %collective-permute-start.12) | collective-permute-done | bytes 262176 | tf_op jit(solution)/shard_map/ppermute | solution.py:493
  63.5 4.3 %sources.2 = (f32[4,256,512]{2,1,0:T(8,128)S(1)}, bf16[256,512]{1,0:T(8,128)(2,1)S(1)}) custom-call(bf16[4,2,64,256]{3,2,1,0:T(8,128)(2,1)S(1)} %collective-permute-done.11.refs_0_, bf16[4,2,64,256]{3,2,1,0:T(8,128)(2,1)S(1)} %collective-permute-done.12.refs_1_, bf16[4,2,64,256]{3,2,1,0:T(8,128)(2,1)S(1)} %collective-permute-done.13.refs_2_, ...), custom_call_target="tpu_custom_call" | custom-call | tf_op jit(solution)/shard_map/sources/pallas_call | solution.py:305
  67.9 1.5 %collective-permute-start.15 = (bf16[256,512]{1,0:T(8,128)(2,1)S(1)}, bf16[256,512]{1,0:T(8,128)(2,1)S(1)}, u32[]{:S(2)}, u32[]{:S(2)}) collective-permute-start(bf16[256,512]{1,0:T(8,128)(2,1)S(1)} %get-tuple-element.68.refs_6_.refs_1_), channel_id=1, source_target_pairs={{0,4},{4,0},{8,12},{12,8},{16,20},{20,16},{24,28},{28,24},{1,5},{5... | collective-permute-start | bytes 786440 | tf_op jit(solution)/shard_map/ppermute | solution.py:497
  69.4 0.1 collective-permute-done.8.refs_0_
  69.5 5.2 %collective-permute-done.9.refs_1_ = bf16[4,2,64,256]{3,2,1,0:T(8,128)(2,1)S(1)} collective-permute-done((bf16[4,2,64,256]{3,2,1,0:T(8,128)(2,1)S(1)}, bf16[4,2,64,256]{3,2,1,0:T(8,128)(2,1)S(1)}, u32[]{:S(2)}, u32[]{:S(2)}) %collective-permute-start.9) | collective-permute-done | bytes 262176 | tf_op jit(solution)/shard_map/ppermute | solution.py:493
  74.8 0.0 collective-permute-done.10.refs_2_
  74.8 4.3 %sources.3 = (f32[4,256,512]{2,1,0:T(8,128)S(1)}, bf16[256,512]{1,0:T(8,128)(2,1)S(1)}) custom-call(bf16[4,2,64,256]{3,2,1,0:T(8,128)(2,1)S(1)} %collective-permute-done.8.refs_0_, bf16[4,2,64,256]{3,2,1,0:T(8,128)(2,1)S(1)} %collective-permute-done.9.refs_1_, bf16[4,2,64,256]{3,2,1,0:T(8,128)(2,1)S(1)} %collective-permute-done.10.refs_2_, ...), custom_call_target="tpu_custom_call" | custom-call | tf_op jit(solution)/shard_map/sources/pallas_call | solution.py:305
  79.1 0.0 copy-start.3
  79.1 1.6 %collective-permute-start.14 = (bf16[256,512]{1,0:T(8,128)(2,1)S(1)}, bf16[256,512]{1,0:T(8,128)(2,1)S(1)}, u32[]{:S(2)}, u32[]{:S(2)}) collective-permute-start(bf16[256,512]{1,0:T(8,128)(2,1)S(1)} %get-tuple-element.69.refs_4_.refs_1_), channel_id=1, source_target_pairs={{0,4},{4,0},{8,12},{12,8},{16,20},{20,16},{24,28},{28,24},{1,5},{5... | collective-permute-start | bytes 786440 | tf_op jit(solution)/shard_map/ppermute | solution.py:497
  80.6 0.0 collective-permute-done.15.refs_0_.refs_3_
  80.6 0.9 pair_sum.2
  81.6 0.9 collective-permute-start.17
  82.4 5.2 %collective-permute-done.14.refs_0_.before_ref = bf16[256,512]{1,0:T(8,128)(2,1)S(1)} collective-permute-done((bf16[256,512]{1,0:T(8,128)(2,1)S(1)}, bf16[256,512]{1,0:T(8,128)(2,1)S(1)}, u32[]{:S(2)}, u32[]{:S(2)}) %collective-permute-start.14) | collective-permute-done | bytes 262176 | tf_op jit(solution)/shard_map/ppermute | solution.py:497
  87.7 0.9 pair_sum.3
  88.6 0.7 collective-permute-start.16
  89.3 0.0 copy-start.4
  89.3 0.9 combine.4.refs_3_
  90.3 0.7 collective-permute-start.19
  90.9 0.0 collective-permute-done.16.refs_0_
  91.0 0.9 combine.5._
  91.9 0.7 collective-permute-start.18
  92.6 2.9 %part_known.1.refs_4_ = f32[4,256,512]{2,1,0:T(8,128)S(1)} custom-call(bf16[256,512]{1,0:T(8,128)(2,1)S(1)} %collective-permute-done.14.refs_0_.before_ref, bf16[2,4,2,256,512]{4,3,2,1,0:T(8,128)(2,1)S(1)} %get-tuple-element.47.p_ref.refs_5_, f32[4,256,512]{2,1,0:T(8,128)S(1)} %copy-done.4, bf16[256,512]{1,0:T(8,128)(2,1)S(1)} %combine.5._), custom_call_target="tpu_custom_call" | custom-call | tf_op jit(solution)/shard_map/part_known/pallas_call | solution.py:423
  95.5 0.9 combine.6.refs_4_
  96.5 1.3 %collective-permute-start.21 = (bf16[256,512]{1,0:T(8,128)(2,1)S(1)}, bf16[256,512]{1,0:T(8,128)(2,1)S(1)}, u32[]{:S(2)}, u32[]{:S(2)}) collective-permute-start(bf16[256,512]{1,0:T(8,128)(2,1)S(1)} %combine.6.refs_4_), channel_id=1, source_target_pairs={{16,24},{20,28},{17,25},{21,29},{18,26},{22,30},{19,27},{23,31}} | collective-permute-start | bytes 786440 | tf_op jit(solution)/shard_map/ppermute | solution.py:501
  97.8 0.9 combine.7.refs_7_.refs_5_
  98.7 1.3 %collective-permute-start.20 = (bf16[256,512]{1,0:T(8,128)(2,1)S(1)}, bf16[256,512]{1,0:T(8,128)(2,1)S(1)}, u32[]{:S(2)}, u32[]{:S(2)}) collective-permute-start(bf16[256,512]{1,0:T(8,128)(2,1)S(1)} %combine.7.refs_7_.refs_5_), channel_id=1, source_target_pairs={{16,24},{20,28},{17,25},{21,29},{18,26},{22,30},{19,27},{23,31}} | collective-permute-start | bytes 786440 | tf_op jit(solution)/shard_map/ppermute | solution.py:501
  100.0 8.0 %collective-permute-done.21.refs_2_ = bf16[256,512]{1,0:T(8,128)(2,1)S(1)} collective-permute-done((bf16[256,512]{1,0:T(8,128)(2,1)S(1)}, bf16[256,512]{1,0:T(8,128)(2,1)S(1)}, u32[]{:S(2)}, u32[]{:S(2)}) %collective-permute-start.21) | collective-permute-done | bytes 262176 | tf_op jit(solution)/shard_map/ppermute | solution.py:501
  108.0 4.6 %finish.2.refs_6_ = f32[2,2,4,256,256]{4,3,2,1,0:T(8,128)} custom-call(bf16[256,512]{1,0:T(8,128)(2,1)S(1)} %collective-permute-done.17.refs_0_, bf16[256,512]{1,0:T(8,128)(2,1)S(1)} %collective-permute-done.19.refs_1_, bf16[256,512]{1,0:T(8,128)(2,1)S(1)} %collective-permute-done.21.refs_2_, bf16[256,512]{1,0:T(8,128)(2,1)S(1)} %collective-permute-done.15.refs_0_.refs_3_, ...), custom_call_target="tpu_custom_call" | custom-call | tf_op jit(solution)/shard_map/finish/pallas_call | solution.py:478
  112.6 0.7 collective-permute-done.20.refs_2_
  113.3 3.7 %finish.3 = f32[2,2,4,256,256]{4,3,2,1,0:T(8,128)} custom-call(bf16[256,512]{1,0:T(8,128)(2,1)S(1)} %collective-permute-done.16.refs_0_, bf16[256,512]{1,0:T(8,128)(2,1)S(1)} %collective-permute-done.18.refs_1_, bf16[256,512]{1,0:T(8,128)(2,1)S(1)} %collective-permute-done.20.refs_2_, ...), custom_call_target="tpu_custom_call", output_to_operand_aliasing={{}: (6, {})} | custom-call | tf_op jit(solution)/shard_map/finish/pallas_call | solution.py:478
  (13 shorter events, 0.0 us)
Async XLA Ops:
  0.0 3.0 %copy-start.1 = (bf16[2,2,4,256,256]{4,3,2,1,0:T(8,128)(2,1)S(1)}, bf16[2,2,4,256,256]{4,3,2,1,0:T(8,128)(2,1)}, u32[]{:S(2)}) copy-start(bf16[2,2,4,256,256]{4,3,2,1,0:T(8,128)(2,1)} %refs_0_.4) | copy-start | bytes 6291460
  1.4 20.5 %collective-permute-start.6 = (bf16[2,2,2,3,64,256]{5,4,3,2,1,0:T(8,128)(2,1)S(1)}, bf16[2,2,2,3,64,256]{5,4,3,2,1,0:T(8,128)(2,1)S(1)}, u32[]{:S(2)}, u32[]{:S(2)}) collective-permute-start(bf16[2,2,2,3,64,256]{5,4,3,2,1,0:T(8,128)(2,1)S(1)} %pad_maximum_fusion.refs_2_), channel_id=1, source_target_pairs={{0,2},{1,3},{2,0},{3,1},{4,6},{5,7},{6,4},{7,5},{8,10},{9,11},{10,... | collective-permute-start | bytes 2359304 | tf_op jit(solution)/shard_map/ppermute | solution.py:493
  3.0 1.6 %copy-start.2 = (bf16[2,2,4,256,256]{4,3,2,1,0:T(8,128)(2,1)S(1)}, bf16[2,2,4,256,256]{4,3,2,1,0:T(8,128)(2,1)}, u32[]{:S(2)}) copy-start(bf16[2,2,4,256,256]{4,3,2,1,0:T(8,128)(2,1)} %refs_1_.4) | copy-start | bytes 6291460
  4.8 17.2 %collective-permute-start.5 = (bf16[2,2,2,3,64,256]{5,4,3,2,1,0:T(8,128)(2,1)S(1)}, bf16[2,2,2,3,64,256]{5,4,3,2,1,0:T(8,128)(2,1)S(1)}, u32[]{:S(2)}, u32[]{:S(2)}) collective-permute-start(bf16[2,2,2,3,64,256]{5,4,3,2,1,0:T(8,128)(2,1)S(1)} %get-tuple-element.48), channel_id=1, source_target_pairs={{0,1},{1,0},{2,3},{3,2},{4,5},{5,4},{6,7},{7,6},{8,9},{9,8},{10,11... | collective-permute-start | bytes 2359304 | tf_op jit(solution)/shard_map/ppermute | solution.py:493
  4.8 1.6 %copy-start = (bf16[2,2,4,256,256]{4,3,2,1,0:T(8,128)(2,1)S(1)}, bf16[2,2,4,256,256]{4,3,2,1,0:T(8,128)(2,1)}, u32[]{:S(2)}) copy-start(bf16[2,2,4,256,256]{4,3,2,1,0:T(8,128)(2,1)} %refs_4_.3) | copy-start | bytes 6291460
  4.9 1.8 %copy-start.5 = (bf16[2,4,256,256]{3,2,1,0:T(8,128)(2,1)S(1)}, bf16[2,4,256,256]{3,2,1,0:T(8,128)(2,1)}, u32[]{:S(2)}) copy-start(bf16[2,4,256,256]{3,2,1,0:T(8,128)(2,1)} %refs_1_.5) | copy-start | bytes 3145732
  4.9 32.9 %collective-permute-start.7 = (bf16[2,2,2,3,64,256]{5,4,3,2,1,0:T(8,128)(2,1)S(1)}, bf16[2,2,2,3,64,256]{5,4,3,2,1,0:T(8,128)(2,1)S(1)}, u32[]{:S(2)}, u32[]{:S(2)}) collective-permute-start(bf16[2,2,2,3,64,256]{5,4,3,2,1,0:T(8,128)(2,1)S(1)} %get-tuple-element.41.refs_2_), channel_id=1, source_target_pairs={{0,3},{1,2},{2,1},{3,0},{4,7},{5,6},{6,5},{7,4},{8,11},{9,10},{10,... | collective-permute-start | bytes 2359304 | tf_op jit(solution)/shard_map/ppermute | solution.py:493
  13.9 29.6 %collective-permute-start.4 = (bf16[2,256,512]{2,1,0:T(8,128)(2,1)S(1)}, bf16[2,256,512]{2,1,0:T(8,128)(2,1)S(1)}, u32[]{:S(2)}, u32[]{:S(2)}) collective-permute-start(bf16[2,256,512]{2,1,0:T(8,128)(2,1)S(1)} %get-tuple-element.77.refs_2_), channel_id=1, source_target_pairs={{0,4},{4,0},{8,12},{12,8},{16,20},{20,16},{24,28},{28,24},{1,5},{5... | collective-permute-start | bytes 1572872 | tf_op jit(solution)/shard_map/ppermute | solution.py:497
  15.5 28.0 %collective-permute-start.3 = (bf16[2,256,512]{2,1,0:T(8,128)(2,1)S(1)}, bf16[2,256,512]{2,1,0:T(8,128)(2,1)S(1)}, u32[]{:S(2)}, u32[]{:S(2)}) collective-permute-start(bf16[2,256,512]{2,1,0:T(8,128)(2,1)S(1)} %get-tuple-element.78.refs_0_), channel_id=1, source_target_pairs={{0,4},{4,0},{8,12},{12,8},{16,20},{20,16},{24,28},{28,24},{1,5},{5... | collective-permute-start | bytes 1572872 | tf_op jit(solution)/shard_map/ppermute | solution.py:497
  21.9 23.0 %collective-permute-start = (bf16[2,2,2,1,64,256]{5,4,3,2,1,0:T(8,128)(2,1)S(1)}, bf16[2,2,2,1,64,256]{5,4,3,2,1,0:T(8,128)(2,1)S(1)}, u32[]{:S(2)}, u32[]{:S(2)}) collective-permute-start(bf16[2,2,2,1,64,256]{5,4,3,2,1,0:T(8,128)(2,1)S(1)} %get-tuple-element.43), channel_id=1, source_target_pairs={{0,1},{1,0},{2,3},{3,2},{4,5},{5,4},{6,7},{7,6},{8,9},{9,8},{10,11... | collective-permute-start | bytes 786440 | tf_op jit(solution)/shard_map/ppermute | solution.py:493
  21.9 23.0 %collective-permute-start.1 = (bf16[2,2,2,1,64,256]{5,4,3,2,1,0:T(8,128)(2,1)S(1)}, bf16[2,2,2,1,64,256]{5,4,3,2,1,0:T(8,128)(2,1)S(1)}, u32[]{:S(2)}, u32[]{:S(2)}) collective-permute-start(bf16[2,2,2,1,64,256]{5,4,3,2,1,0:T(8,128)(2,1)S(1)} %get-tuple-element.44), channel_id=1, source_target_pairs={{0,2},{1,3},{2,0},{3,1},{4,6},{5,7},{6,4},{7,5},{8,10},{9,11},{10,... | collective-permute-start | bytes 786440 | tf_op jit(solution)/shard_map/ppermute | solution.py:493
  37.8 10.1 %collective-permute-start.2 = (bf16[2,2,2,1,64,256]{5,4,3,2,1,0:T(8,128)(2,1)S(1)}, bf16[2,2,2,1,64,256]{5,4,3,2,1,0:T(8,128)(2,1)S(1)}, u32[]{:S(2)}, u32[]{:S(2)}) collective-permute-start(bf16[2,2,2,1,64,256]{5,4,3,2,1,0:T(8,128)(2,1)S(1)} %get-tuple-element.45), channel_id=1, source_target_pairs={{0,3},{1,2},{2,1},{3,0},{4,7},{5,6},{6,5},{7,4},{8,11},{9,10},{10,... | collective-permute-start | bytes 786440 | tf_op jit(solution)/shard_map/ppermute | solution.py:493
  49.0 9.2 %collective-permute-start.11 = (bf16[4,2,64,256]{3,2,1,0:T(8,128)(2,1)S(1)}, bf16[4,2,64,256]{3,2,1,0:T(8,128)(2,1)S(1)}, u32[]{:S(2)}, u32[]{:S(2)}) collective-permute-start(bf16[4,2,64,256]{3,2,1,0:T(8,128)(2,1)S(1)} %get-tuple-element.63), channel_id=1, source_target_pairs={{0,2},{1,3},{2,0},{3,1},{4,6},{5,7},{6,4},{7,5},{8,10},{9,11},{10,... | collective-permute-start | bytes 786440 | tf_op jit(solution)/shard_map/ppermute | solution.py:493
  50.4 13.1 %collective-permute-start.12 = (bf16[4,2,64,256]{3,2,1,0:T(8,128)(2,1)S(1)}, bf16[4,2,64,256]{3,2,1,0:T(8,128)(2,1)S(1)}, u32[]{:S(2)}, u32[]{:S(2)}) collective-permute-start(bf16[4,2,64,256]{3,2,1,0:T(8,128)(2,1)S(1)} %get-tuple-element.64), channel_id=1, source_target_pairs={{0,3},{1,2},{2,1},{3,0},{4,7},{5,6},{6,5},{7,4},{8,11},{9,10},{10,... | collective-permute-start | bytes 786440 | tf_op jit(solution)/shard_map/ppermute | solution.py:493
  51.2 12.3 %collective-permute-start.13 = (bf16[4,2,64,256]{3,2,1,0:T(8,128)(2,1)S(1)}, bf16[4,2,64,256]{3,2,1,0:T(8,128)(2,1)S(1)}, u32[]{:S(2)}, u32[]{:S(2)}) collective-permute-start(bf16[4,2,64,256]{3,2,1,0:T(8,128)(2,1)S(1)} %get-tuple-element.65), channel_id=1, source_target_pairs={{0,1},{1,0},{2,3},{3,2},{4,5},{5,4},{6,7},{7,6},{8,9},{9,8},{10,11... | collective-permute-start | bytes 786440 | tf_op jit(solution)/shard_map/ppermute | solution.py:493
  51.2 18.3 %collective-permute-start.8 = (bf16[4,2,64,256]{3,2,1,0:T(8,128)(2,1)S(1)}, bf16[4,2,64,256]{3,2,1,0:T(8,128)(2,1)S(1)}, u32[]{:S(2)}, u32[]{:S(2)}) collective-permute-start(bf16[4,2,64,256]{3,2,1,0:T(8,128)(2,1)S(1)} %get-tuple-element.59), channel_id=1, source_target_pairs={{0,2},{1,3},{2,0},{3,1},{4,6},{5,7},{6,4},{7,5},{8,10},{9,11},{10,... | collective-permute-start | bytes 786440 | tf_op jit(solution)/shard_map/ppermute | solution.py:493
  52.8 22.0 %collective-permute-start.9 = (bf16[4,2,64,256]{3,2,1,0:T(8,128)(2,1)S(1)}, bf16[4,2,64,256]{3,2,1,0:T(8,128)(2,1)S(1)}, u32[]{:S(2)}, u32[]{:S(2)}) collective-permute-start(bf16[4,2,64,256]{3,2,1,0:T(8,128)(2,1)S(1)} %get-tuple-element.60), channel_id=1, source_target_pairs={{0,3},{1,2},{2,1},{3,0},{4,7},{5,6},{6,5},{7,4},{8,11},{9,10},{10,... | collective-permute-start | bytes 786440 | tf_op jit(solution)/shard_map/ppermute | solution.py:493
  58.3 16.5 %collective-permute-start.10 = (bf16[4,2,64,256]{3,2,1,0:T(8,128)(2,1)S(1)}, bf16[4,2,64,256]{3,2,1,0:T(8,128)(2,1)S(1)}, u32[]{:S(2)}, u32[]{:S(2)}) collective-permute-start(bf16[4,2,64,256]{3,2,1,0:T(8,128)(2,1)S(1)} %get-tuple-element.61), channel_id=1, source_target_pairs={{0,1},{1,0},{2,3},{3,2},{4,5},{5,4},{6,7},{7,6},{8,9},{9,8},{10,11... | collective-permute-start | bytes 786440 | tf_op jit(solution)/shard_map/ppermute | solution.py:493
  67.9 12.8 %collective-permute-start.15 = (bf16[256,512]{1,0:T(8,128)(2,1)S(1)}, bf16[256,512]{1,0:T(8,128)(2,1)S(1)}, u32[]{:S(2)}, u32[]{:S(2)}) collective-permute-start(bf16[256,512]{1,0:T(8,128)(2,1)S(1)} %get-tuple-element.68.refs_6_.refs_1_), channel_id=1, source_target_pairs={{0,4},{4,0},{8,12},{12,8},{16,20},{20,16},{24,28},{28,24},{1,5},{5... | collective-permute-start | bytes 786440 | tf_op jit(solution)/shard_map/ppermute | solution.py:497
  79.1 9.5 %copy-start.3 = (f32[4,256,512]{2,1,0:T(8,128)}, f32[4,256,512]{2,1,0:T(8,128)S(1)}, u32[]{:S(2)}) copy-start(f32[4,256,512]{2,1,0:T(8,128)S(1)} %get-tuple-element.70.refs_2_.sum_ref) | copy-start | bytes 6291460
  79.1 8.6 %collective-permute-start.14 = (bf16[256,512]{1,0:T(8,128)(2,1)S(1)}, bf16[256,512]{1,0:T(8,128)(2,1)S(1)}, u32[]{:S(2)}, u32[]{:S(2)}) collective-permute-start(bf16[256,512]{1,0:T(8,128)(2,1)S(1)} %get-tuple-element.69.refs_4_.refs_1_), channel_id=1, source_target_pairs={{0,4},{4,0},{8,12},{12,8},{16,20},{20,16},{24,28},{28,24},{1,5},{5... | collective-permute-start | bytes 786440 | tf_op jit(solution)/shard_map/ppermute | solution.py:497
  81.6 7.7 %collective-permute-start.17 = (bf16[256,512]{1,0:T(8,128)(2,1)S(1)}, bf16[256,512]{1,0:T(8,128)(2,1)S(1)}, u32[]{:S(2)}, u32[]{:S(2)}) collective-permute-start(bf16[256,512]{1,0:T(8,128)(2,1)S(1)} %get-tuple-element.73.refs_4_), channel_id=1, source_target_pairs={{0,8},{4,12},{1,9},{5,13},{2,10},{6,14},{3,11},{7,15}} | collective-permute-start | bytes 786440 | tf_op jit(solution)/shard_map/ppermute | solution.py:501
  88.6 2.3 %collective-permute-start.16 = (bf16[256,512]{1,0:T(8,128)(2,1)S(1)}, bf16[256,512]{1,0:T(8,128)(2,1)S(1)}, u32[]{:S(2)}, u32[]{:S(2)}) collective-permute-start(bf16[256,512]{1,0:T(8,128)(2,1)S(1)} %get-tuple-element.74.refs_3_), channel_id=1, source_target_pairs={{0,8},{4,12},{1,9},{5,13},{2,10},{6,14},{3,11},{7,15}} | collective-permute-start | bytes 786440 | tf_op jit(solution)/shard_map/ppermute | solution.py:501
  89.3 3.3 %copy-start.4 = (f32[4,256,512]{2,1,0:T(8,128)S(1)}, f32[4,256,512]{2,1,0:T(8,128)}, u32[]{:S(2)}) copy-start(f32[4,256,512]{2,1,0:T(8,128)} %copy-done.3) | copy-start | bytes 6291460
  90.3 5.2 %collective-permute-start.19 = (bf16[256,512]{1,0:T(8,128)(2,1)S(1)}, bf16[256,512]{1,0:T(8,128)(2,1)S(1)}, u32[]{:S(2)}, u32[]{:S(2)}) collective-permute-start(bf16[256,512]{1,0:T(8,128)(2,1)S(1)} %combine.4.refs_3_), channel_id=1, source_target_pairs={{8,16},{12,20},{9,17},{13,21},{10,18},{14,22},{11,19},{15,23}} | collective-permute-start | bytes 786440 | tf_op jit(solution)/shard_map/ppermute | solution.py:501
  91.9 5.9 %collective-permute-start.18 = (bf16[256,512]{1,0:T(8,128)(2,1)S(1)}, bf16[256,512]{1,0:T(8,128)(2,1)S(1)}, u32[]{:S(2)}, u32[]{:S(2)}) collective-permute-start(bf16[256,512]{1,0:T(8,128)(2,1)S(1)} %combine.5._), channel_id=1, source_target_pairs={{8,16},{12,20},{9,17},{13,21},{10,18},{14,22},{11,19},{15,23}} | collective-permute-start | bytes 786440 | tf_op jit(solution)/shard_map/ppermute | solution.py:501
  96.5 11.5 %collective-permute-start.21 = (bf16[256,512]{1,0:T(8,128)(2,1)S(1)}, bf16[256,512]{1,0:T(8,128)(2,1)S(1)}, u32[]{:S(2)}, u32[]{:S(2)}) collective-permute-start(bf16[256,512]{1,0:T(8,128)(2,1)S(1)} %combine.6.refs_4_), channel_id=1, source_target_pairs={{16,24},{20,28},{17,25},{21,29},{18,26},{22,30},{19,27},{23,31}} | collective-permute-start | bytes 786440 | tf_op jit(solution)/shard_map/ppermute | solution.py:501
  98.7 14.6 %collective-permute-start.20 = (bf16[256,512]{1,0:T(8,128)(2,1)S(1)}, bf16[256,512]{1,0:T(8,128)(2,1)S(1)}, u32[]{:S(2)}, u32[]{:S(2)}) collective-permute-start(bf16[256,512]{1,0:T(8,128)(2,1)S(1)} %combine.7.refs_7_.refs_5_), channel_id=1, source_target_pairs={{16,24},{20,28},{17,25},{21,29},{18,26},{22,30},{19,27},{23,31}} | collective-permute-start | bytes 786440 | tf_op jit(solution)/shard_map/ppermute | solution.py:501

commit v8 on v7

--- a/solution.py
+++ b/solution.py
@@ -199,6 +199,7 @@
     me = lax.axis_index("energy")
     points = count * energies
     middle = points // 2
+    share = 1.0 / points
     rows, columns = green.shape[2:]
     for k in range(count):
         base = (me ^ k) * energies
@@ -226,8 +227,8 @@
                         b = gr[m] * wi[lag] + gi[m] * wr[lag]
                         re = a if re is None else re + a
                         im = b if im is None else im + b
-                total[(n, 0) + at] = -im / points
-                total[(n, 1) + at] = re / points
+                total[(n, 0) + at] = im * -share
+                total[(n, 1) + at] = re * share
         return 0
 
     lax.fori_loop(0, rows // 8, tile, 0)

time: 117 us -> 117 us (level)
  no operation moved by 1% of the time
where the time goes in v8:
time: 117 us
  waiting for transfers between devices  51.2 us (44%)
  Pallas kernels  41.2 us (35%)
  starting transfers between devices  20.5 us (18%)
  local copies, waits for them, and re-layouts  3.74 us (3%)
    ppermute x12, waiting for transfers between devices, swap(): return lax.ppermute(x, 'energy', [(i, i ^ k) for i in range(count)])  37.3 us
    ppermute x12, starting transfers between devices, swap(): return lax.ppermute(x, 'energy', [(i, i ^ k) for i in range(count)])  9.78 us
    ppermute x6, waiting for transfers between devices, forward(): lax.ppermute(x, 'slab', [(2 * pair + i, 2 * pair + 2 + i) for i in range(...  8.71 us
    pallas_call x2, Pallas kernels, build_sources(): pl.pallas_call(ordered(functools.partial(source_body, energy, owners), le...  8.63 us
    pallas_call x2, Pallas kernels, finish(): pl.pallas_call(body, in_specs=in_specs, out_specs=ANYWHERE, out_shape=jax...  8.32 us
    pallas_call x1, Pallas kernels, build_maps(): pl.pallas_call(lambda *refs: maps_body(*refs[:2], *refs[2 + len(after):])...  7.11 us
    ppermute x6, starting transfers between devices, forward(): lax.ppermute(x, 'slab', [(2 * pair + i, 2 * pair + 2 + i) for i in range(...  5.47 us
    ppermute x4, waiting for transfers between devices, other_of_pair(): lax.ppermute(x, 'slab', [(i, i ^ 1) for i in range(lax.axis_size('slab'))])  5.23 us
  transfers between devices with their start and end apart: 22, of which 10 were waited for; matrix products, arithmetic and copies ran while one was open for 0% of the time, Pallas kernels for 31%

profile of v8, /device:TPU:24, one launch (start us, length us, event | category | flops | bytes accessed | tf_op | source)
XLA Modules:
  0.0 117.2 jit_solution(7063427253604740637)
XLA Ops:
  0.0 1.3 %dynamic-slice_bitcast_fusion = (bf16[1,2,2,3,64,256]{5,4,3,2,1,0:T(8,128)(2,1)S(1)}, bf16[1,2,2,3,64,256]{5,4,3,2,1,0:T(8,128)(2,1)S(1)}) fusion(bf16[2,2,4,256,256]{4,3,2,1,0:T(8,128)(2,1)} %refs_1_.4, s32[]{:T(128)S(6)} %select_n.4, bf16[2,2,4,256,256]{4,3,2,1,0:T(8,128)(2,1)} %refs_0_.4), kind=kLoop, calls=%fused_computation.3 | loop fusion | bytes 1572868 | tf_op jit(solution)/shard_map/stack | solution.py:528
  1.3 0.1 pad_maximum_fusion.refs_2_
  1.4 1.6 %collective-permute-start.6 = (bf16[2,2,2,3,64,256]{5,4,3,2,1,0:T(8,128)(2,1)S(1)}, bf16[2,2,2,3,64,256]{5,4,3,2,1,0:T(8,128)(2,1)S(1)}, u32[]{:S(2)}, u32[]{:S(2)}) collective-permute-start(bf16[2,2,2,3,64,256]{5,4,3,2,1,0:T(8,128)(2,1)S(1)} %pad_maximum_fusion.refs_2_), channel_id=1, source_target_pairs={{0,2},{1,3},{2,0},{3,1},{4,6},{5,7},{6,4},{7,5},{8,10},{9,11},{10,... | collective-permute-start | bytes 2359304 | tf_op jit(solution)/shard_map/ppermute | solution.py:494
  3.0 1.6 %copy-done.2 = bf16[2,2,4,256,256]{4,3,2,1,0:T(8,128)(2,1)S(1)} copy-done((bf16[2,2,4,256,256]{4,3,2,1,0:T(8,128)(2,1)S(1)}, bf16[2,2,4,256,256]{4,3,2,1,0:T(8,128)(2,1)}, u32[]{:S(2)}) %copy-start.2) | copy-done | bytes 2097176
  4.6 0.1 pack.2
  4.8 0.1 collective-permute-start.5
  4.8 0.0 copy-start
  4.9 0.0 copy-start.5
  4.9 0.6 collective-permute-start.7
  5.5 0.5 pack.3
  6.0 0.5 copy-done
  6.4 0.3 copy-done.5
  6.7 7.1 %maps.1 = (bf16[2,4,2,256,512]{4,3,2,1,0:T(8,128)(2,1)S(1)}, bf16[2,4,2,256,512]{4,3,2,1,0:T(8,128)(2,1)S(1)}) custom-call(bf16[2,2,4,256,256]{4,3,2,1,0:T(8,128)(2,1)S(1)} %copy-done, bf16[2,4,256,256]{3,2,1,0:T(8,128)(2,1)S(1)} %copy-done.5, bf16[2,2,2,3,64,256]{5,4,3,2,1,0:T(8,128)(2,1)S(1)} %get-tuple-element.46.refs_2_.refs_0_), custom_call_target="tpu_custom_call" | custom-call | tf_op jit(solution)/shard_map/maps/pallas_call | solution.py:138
  13.8 0.1 slice_bitcast_fusion
  13.9 1.6 %collective-permute-start.4 = (bf16[2,256,512]{2,1,0:T(8,128)(2,1)S(1)}, bf16[2,256,512]{2,1,0:T(8,128)(2,1)S(1)}, u32[]{:S(2)}, u32[]{:S(2)}) collective-permute-start(bf16[2,256,512]{2,1,0:T(8,128)(2,1)S(1)} %get-tuple-element.77.refs_2_), channel_id=1, source_target_pairs={{0,4},{4,0},{8,12},{12,8},{16,20},{20,16},{24,28},{28,24},{1,5},{5... | collective-permute-start | bytes 1572872 | tf_op jit(solution)/shard_map/ppermute | solution.py:498
  15.5 0.5 collective-permute-start.3
  16.0 5.9 %collective-permute-done.6.refs_2_ = bf16[2,2,2,3,64,256]{5,4,3,2,1,0:T(8,128)(2,1)S(1)} collective-permute-done((bf16[2,2,2,3,64,256]{5,4,3,2,1,0:T(8,128)(2,1)S(1)}, bf16[2,2,2,3,64,256]{5,4,3,2,1,0:T(8,128)(2,1)S(1)}, u32[]{:S(2)}, u32[]{:S(2)}) %collective-permute-start.6) | collective-permute-done | bytes 786464 | tf_op jit(solution)/shard_map/ppermute | solution.py:494
  21.9 1.5 %collective-permute-start.1 = (bf16[2,2,2,1,64,256]{5,4,3,2,1,0:T(8,128)(2,1)S(1)}, bf16[2,2,2,1,64,256]{5,4,3,2,1,0:T(8,128)(2,1)S(1)}, u32[]{:S(2)}, u32[]{:S(2)}) collective-permute-start(bf16[2,2,2,1,64,256]{5,4,3,2,1,0:T(8,128)(2,1)S(1)} %get-tuple-element.44), channel_id=1, source_target_pairs={{0,2},{1,3},{2,0},{3,1},{4,6},{5,7},{6,4},{7,5},{8,10},{9,11},{10,... | collective-permute-start | bytes 786440 | tf_op jit(solution)/shard_map/ppermute | solution.py:494
  23.4 14.4 %collective-permute-done.7.refs_3_ = bf16[2,2,2,3,64,256]{5,4,3,2,1,0:T(8,128)(2,1)S(1)} collective-permute-done((bf16[2,2,2,3,64,256]{5,4,3,2,1,0:T(8,128)(2,1)S(1)}, bf16[2,2,2,3,64,256]{5,4,3,2,1,0:T(8,128)(2,1)S(1)}, u32[]{:S(2)}, u32[]{:S(2)}) %collective-permute-start.7) | collective-permute-done | bytes 786464 | tf_op jit(solution)/shard_map/ppermute | solution.py:494
  37.8 1.9 %collective-permute-start.2 = (bf16[2,2,2,1,64,256]{5,4,3,2,1,0:T(8,128)(2,1)S(1)}, bf16[2,2,2,1,64,256]{5,4,3,2,1,0:T(8,128)(2,1)S(1)}, u32[]{:S(2)}, u32[]{:S(2)}) collective-permute-start(bf16[2,2,2,1,64,256]{5,4,3,2,1,0:T(8,128)(2,1)S(1)} %get-tuple-element.45), channel_id=1, source_target_pairs={{0,3},{1,2},{2,1},{3,0},{4,7},{5,6},{6,5},{7,4},{8,11},{9,10},{10,... | collective-permute-start | bytes 786440 | tf_op jit(solution)/shard_map/ppermute | solution.py:494
  39.7 3.6 %convolve.2 = (bf16[4,2,64,256]{3,2,1,0:T(8,128)(2,1)S(1)}, bf16[4,2,64,256]{3,2,1,0:T(8,128)(2,1)S(1)}, bf16[4,2,64,256]{3,2,1,0:T(8,128)(2,1)S(1)}, bf16[4,2,6...) custom-call(bf16[2,2,2,3,64,256]{5,4,3,2,1,0:T(8,128)(2,1)S(1)} %get, ...), custom_call_target="tpu_custom_call" | custom-call | tf_op jit(solution)/shard_map/convolve/pallas_call | solution.py:258
  43.4 0.0 collective-permute-done.3.refs_1_
  43.4 1.5 %pair_maps.1 = (bf16[2,2,256,512]{3,2,1,0:T(8,128)(2,1)S(1)}, bf16[2,2,256,512]{3,2,1,0:T(8,128)(2,1)S(1)}, bf16[2,2,256,512]{3,2,1,0:T(8,128)(2,1)S(1)}) custom-call(bf16[2,256,512]{2,1,0:T(8,128)(2,1)S(1)} %get-tuple-element.78.refs_0_, bf16[2,256,512]{2,1,0:T(8,128)(2,1)S(1)} %collective-permute-done.3.refs_1_, ...), custom_call_target="tpu_custom_call" | custom-call | tf_op jit(solution)/shard_map/pair_maps/pallas_call | solution.py:182
  44.9 0.0 collective-permute-done.refs_1_
  44.9 0.0 collective-permute-done.1.refs_2_
  44.9 3.0 %collective-permute-done.2.refs_3_ = bf16[2,2,2,1,64,256]{5,4,3,2,1,0:T(8,128)(2,1)S(1)} collective-permute-done((bf16[2,2,2,1,64,256]{5,4,3,2,1,0:T(8,128)(2,1)S(1)}, bf16[2,2,2,1,64,256]{5,4,3,2,1,0:T(8,128)(2,1)S(1)}, u32[]{:S(2)}, u32[]{:S(2)}) %collective-permute-start.2) | collective-permute-done | bytes 262176 | tf_op jit(solution)/shard_map/ppermute | solution.py:494
  47.9 1.1 convolve.3
  49.0 1.4 %collective-permute-start.11 = (bf16[4,2,64,256]{3,2,1,0:T(8,128)(2,1)S(1)}, bf16[4,2,64,256]{3,2,1,0:T(8,128)(2,1)S(1)}, u32[]{:S(2)}, u32[]{:S(2)}) collective-permute-start(bf16[4,2,64,256]{3,2,1,0:T(8,128)(2,1)S(1)} %get-tuple-element.63), channel_id=1, source_target_pairs={{0,2},{1,3},{2,0},{3,1},{4,6},{5,7},{6,4},{7,5},{8,10},{9,11},{10,... | collective-permute-start | bytes 786440 | tf_op jit(solution)/shard_map/ppermute | solution.py:494
  50.4 0.8 collective-permute-start.12
  51.2 0.0 collective-permute-start.13
  51.2 1.5 %collective-permute-start.8 = (bf16[4,2,64,256]{3,2,1,0:T(8,128)(2,1)S(1)}, bf16[4,2,64,256]{3,2,1,0:T(8,128)(2,1)S(1)}, u32[]{:S(2)}, u32[]{:S(2)}) collective-permute-start(bf16[4,2,64,256]{3,2,1,0:T(8,128)(2,1)S(1)} %get-tuple-element.59), channel_id=1, source_target_pairs={{0,2},{1,3},{2,0},{3,1},{4,6},{5,7},{6,4},{7,5},{8,10},{9,11},{10,... | collective-permute-start | bytes 786440 | tf_op jit(solution)/shard_map/ppermute | solution.py:494
  52.7 0.3 collective-permute-start.9
  53.1 5.2 %collective-permute-done.11.refs_0_ = bf16[4,2,64,256]{3,2,1,0:T(8,128)(2,1)S(1)} collective-permute-done((bf16[4,2,64,256]{3,2,1,0:T(8,128)(2,1)S(1)}, bf16[4,2,64,256]{3,2,1,0:T(8,128)(2,1)S(1)}, u32[]{:S(2)}, u32[]{:S(2)}) %collective-permute-start.11) | collective-permute-done | bytes 262176 | tf_op jit(solution)/shard_map/ppermute | solution.py:494
  58.3 0.0 collective-permute-start.10
  58.3 1.8 %entry_maps.1.refs_6_.refs_3_ = bf16[1,4,2,256,512]{4,3,2,1,0:T(8,128)(2,1)S(1)} custom-call(bf16[2,4,2,256,512]{4,3,2,1,0:T(8,128)(2,1)S(1)} %get-tuple-element.47.p_ref.refs_5_, bf16[2,2,256,512]{3,2,1,0:T(8,128)(2,1)S(1)} %get-tuple-element.67.i_ref.refs_4_, bf16[4,2,64,256]{3,2,1,0:T(8,128)(2,1)S(1)} %get-tuple-element.66._.refs_3_), custom_call_target="tpu_custom_call" | custom-call | tf_op jit(solution)/shard_map/entry_maps/pallas_call | solution.py:406
  60.1 3.4 %collective-permute-done.12.refs_1_ = bf16[4,2,64,256]{3,2,1,0:T(8,128)(2,1)S(1)} collective-permute-done((bf16[4,2,64,256]{3,2,1,0:T(8,128)(2,1)S(1)}, bf16[4,2,64,256]{3,2,1,0:T(8,128)(2,1)S(1)}, u32[]{:S(2)}, u32[]{:S(2)}) %collective-permute-start.12) | collective-permute-done | bytes 262176 | tf_op jit(solution)/shard_map/ppermute | solution.py:494
  63.5 4.3 %sources.2 = (f32[4,256,512]{2,1,0:T(8,128)S(1)}, bf16[256,512]{1,0:T(8,128)(2,1)S(1)}) custom-call(bf16[4,2,64,256]{3,2,1,0:T(8,128)(2,1)S(1)} %collective-permute-done.11.refs_0_, bf16[4,2,64,256]{3,2,1,0:T(8,128)(2,1)S(1)} %collective-permute-done.12.refs_1_, bf16[4,2,64,256]{3,2,1,0:T(8,128)(2,1)S(1)} %collective-permute-done.13.refs_2_, ...), custom_call_target="tpu_custom_call" | custom-call | tf_op jit(solution)/shard_map/sources/pallas_call | solution.py:306
  67.8 1.5 %collective-permute-start.15 = (bf16[256,512]{1,0:T(8,128)(2,1)S(1)}, bf16[256,512]{1,0:T(8,128)(2,1)S(1)}, u32[]{:S(2)}, u32[]{:S(2)}) collective-permute-start(bf16[256,512]{1,0:T(8,128)(2,1)S(1)} %get-tuple-element.68.refs_6_.refs_1_), channel_id=1, source_target_pairs={{0,4},{4,0},{8,12},{12,8},{16,20},{20,16},{24,28},{28,24},{1,5},{5... | collective-permute-start | bytes 786440 | tf_op jit(solution)/shard_map/ppermute | solution.py:498
  69.4 0.1 collective-permute-done.8.refs_0_
  69.5 5.2 %collective-permute-done.9.refs_1_ = bf16[4,2,64,256]{3,2,1,0:T(8,128)(2,1)S(1)} collective-permute-done((bf16[4,2,64,256]{3,2,1,0:T(8,128)(2,1)S(1)}, bf16[4,2,64,256]{3,2,1,0:T(8,128)(2,1)S(1)}, u32[]{:S(2)}, u32[]{:S(2)}) %collective-permute-start.9) | collective-permute-done | bytes 262176 | tf_op jit(solution)/shard_map/ppermute | solution.py:494
  74.7 0.0 collective-permute-done.10.refs_2_
  74.7 4.3 %sources.3 = (f32[4,256,512]{2,1,0:T(8,128)S(1)}, bf16[256,512]{1,0:T(8,128)(2,1)S(1)}) custom-call(bf16[4,2,64,256]{3,2,1,0:T(8,128)(2,1)S(1)} %collective-permute-done.8.refs_0_, bf16[4,2,64,256]{3,2,1,0:T(8,128)(2,1)S(1)} %collective-permute-done.9.refs_1_, bf16[4,2,64,256]{3,2,1,0:T(8,128)(2,1)S(1)} %collective-permute-done.10.refs_2_, ...), custom_call_target="tpu_custom_call" | custom-call | tf_op jit(solution)/shard_map/sources/pallas_call | solution.py:306
  79.1 0.0 copy-start.3
  79.1 1.6 %collective-permute-start.14 = (bf16[256,512]{1,0:T(8,128)(2,1)S(1)}, bf16[256,512]{1,0:T(8,128)(2,1)S(1)}, u32[]{:S(2)}, u32[]{:S(2)}) collective-permute-start(bf16[256,512]{1,0:T(8,128)(2,1)S(1)} %get-tuple-element.69.refs_4_.refs_1_), channel_id=1, source_target_pairs={{0,4},{4,0},{8,12},{12,8},{16,20},{20,16},{24,28},{28,24},{1,5},{5... | collective-permute-start | bytes 786440 | tf_op jit(solution)/shard_map/ppermute | solution.py:498
  80.6 0.0 collective-permute-done.15.refs_0_.refs_3_
  80.6 0.9 pair_sum.2
  81.6 0.9 collective-permute-start.17
  82.4 5.2 %collective-permute-done.14.refs_0_.before_ref = bf16[256,512]{1,0:T(8,128)(2,1)S(1)} collective-permute-done((bf16[256,512]{1,0:T(8,128)(2,1)S(1)}, bf16[256,512]{1,0:T(8,128)(2,1)S(1)}, u32[]{:S(2)}, u32[]{:S(2)}) %collective-permute-start.14) | collective-permute-done | bytes 262176 | tf_op jit(solution)/shard_map/ppermute | solution.py:498
  87.7 0.9 pair_sum.3
  88.6 0.7 collective-permute-start.16
  89.3 0.0 copy-start.4
  89.3 0.9 combine.4.refs_3_
  90.2 0.7 collective-permute-start.19
  90.9 0.9 combine.5._
  91.9 0.7 collective-permute-start.18
  92.6 2.9 %part_known.1.refs_4_ = f32[4,256,512]{2,1,0:T(8,128)S(1)} custom-call(bf16[256,512]{1,0:T(8,128)(2,1)S(1)} %collective-permute-done.14.refs_0_.before_ref, bf16[2,4,2,256,512]{4,3,2,1,0:T(8,128)(2,1)S(1)} %get-tuple-element.47.p_ref.refs_5_, f32[4,256,512]{2,1,0:T(8,128)S(1)} %copy-done.4, bf16[256,512]{1,0:T(8,128)(2,1)S(1)} %combine.5._), custom_call_target="tpu_custom_call" | custom-call | tf_op jit(solution)/shard_map/part_known/pallas_call | solution.py:424
  95.5 0.9 combine.6.refs_4_
  96.4 1.3 %collective-permute-start.21 = (bf16[256,512]{1,0:T(8,128)(2,1)S(1)}, bf16[256,512]{1,0:T(8,128)(2,1)S(1)}, u32[]{:S(2)}, u32[]{:S(2)}) collective-permute-start(bf16[256,512]{1,0:T(8,128)(2,1)S(1)} %combine.6.refs_4_), channel_id=1, source_target_pairs={{16,24},{20,28},{17,25},{21,29},{18,26},{22,30},{19,27},{23,31}} | collective-permute-start | bytes 786440 | tf_op jit(solution)/shard_map/ppermute | solution.py:502
  97.7 0.9 combine.7.refs_7_.refs_5_
  98.7 1.3 %collective-permute-start.20 = (bf16[256,512]{1,0:T(8,128)(2,1)S(1)}, bf16[256,512]{1,0:T(8,128)(2,1)S(1)}, u32[]{:S(2)}, u32[]{:S(2)}) collective-permute-start(bf16[256,512]{1,0:T(8,128)(2,1)S(1)} %combine.7.refs_7_.refs_5_), channel_id=1, source_target_pairs={{16,24},{20,28},{17,25},{21,29},{18,26},{22,30},{19,27},{23,31}} | collective-permute-start | bytes 786440 | tf_op jit(solution)/shard_map/ppermute | solution.py:502
  100.0 8.0 %collective-permute-done.21.refs_2_ = bf16[256,512]{1,0:T(8,128)(2,1)S(1)} collective-permute-done((bf16[256,512]{1,0:T(8,128)(2,1)S(1)}, bf16[256,512]{1,0:T(8,128)(2,1)S(1)}, u32[]{:S(2)}, u32[]{:S(2)}) %collective-permute-start.21) | collective-permute-done | bytes 262176 | tf_op jit(solution)/shard_map/ppermute | solution.py:502
  108.0 4.6 %finish.2.refs_6_ = f32[2,2,4,256,256]{4,3,2,1,0:T(8,128)} custom-call(bf16[256,512]{1,0:T(8,128)(2,1)S(1)} %collective-permute-done.17.refs_0_, bf16[256,512]{1,0:T(8,128)(2,1)S(1)} %collective-permute-done.19.refs_1_, bf16[256,512]{1,0:T(8,128)(2,1)S(1)} %collective-permute-done.21.refs_2_, bf16[256,512]{1,0:T(8,128)(2,1)S(1)} %collective-permute-done.15.refs_0_.refs_3_, ...), custom_call_target="tpu_custom_call" | custom-call | tf_op jit(solution)/shard_map/finish/pallas_call | solution.py:479
  112.6 0.7 collective-permute-done.20.refs_2_
  113.3 3.7 %finish.3 = f32[2,2,4,256,256]{4,3,2,1,0:T(8,128)} custom-call(bf16[256,512]{1,0:T(8,128)(2,1)S(1)} %collective-permute-done.16.refs_0_, bf16[256,512]{1,0:T(8,128)(2,1)S(1)} %collective-permute-done.18.refs_1_, bf16[256,512]{1,0:T(8,128)(2,1)S(1)} %collective-permute-done.20.refs_2_, ...), custom_call_target="tpu_custom_call", output_to_operand_aliasing={{}: (6, {})} | custom-call | tf_op jit(solution)/shard_map/finish/pallas_call | solution.py:479
  (13 shorter events, 0.0 us)
Async XLA Ops:
  0.0 3.0 %copy-start.1 = (bf16[2,2,4,256,256]{4,3,2,1,0:T(8,128)(2,1)S(1)}, bf16[2,2,4,256,256]{4,3,2,1,0:T(8,128)(2,1)}, u32[]{:S(2)}) copy-start(bf16[2,2,4,256,256]{4,3,2,1,0:T(8,128)(2,1)} %refs_0_.4) | copy-start | bytes 6291460
  1.4 20.5 %collective-permute-start.6 = (bf16[2,2,2,3,64,256]{5,4,3,2,1,0:T(8,128)(2,1)S(1)}, bf16[2,2,2,3,64,256]{5,4,3,2,1,0:T(8,128)(2,1)S(1)}, u32[]{:S(2)}, u32[]{:S(2)}) collective-permute-start(bf16[2,2,2,3,64,256]{5,4,3,2,1,0:T(8,128)(2,1)S(1)} %pad_maximum_fusion.refs_2_), channel_id=1, source_target_pairs={{0,2},{1,3},{2,0},{3,1},{4,6},{5,7},{6,4},{7,5},{8,10},{9,11},{10,... | collective-permute-start | bytes 2359304 | tf_op jit(solution)/shard_map/ppermute | solution.py:494
  3.0 1.6 %copy-start.2 = (bf16[2,2,4,256,256]{4,3,2,1,0:T(8,128)(2,1)S(1)}, bf16[2,2,4,256,256]{4,3,2,1,0:T(8,128)(2,1)}, u32[]{:S(2)}) copy-start(bf16[2,2,4,256,256]{4,3,2,1,0:T(8,128)(2,1)} %refs_1_.4) | copy-start | bytes 6291460
  4.8 17.2 %collective-permute-start.5 = (bf16[2,2,2,3,64,256]{5,4,3,2,1,0:T(8,128)(2,1)S(1)}, bf16[2,2,2,3,64,256]{5,4,3,2,1,0:T(8,128)(2,1)S(1)}, u32[]{:S(2)}, u32[]{:S(2)}) collective-permute-start(bf16[2,2,2,3,64,256]{5,4,3,2,1,0:T(8,128)(2,1)S(1)} %get-tuple-element.48), channel_id=1, source_target_pairs={{0,1},{1,0},{2,3},{3,2},{4,5},{5,4},{6,7},{7,6},{8,9},{9,8},{10,11... | collective-permute-start | bytes 2359304 | tf_op jit(solution)/shard_map/ppermute | solution.py:494
  4.8 1.6 %copy-start = (bf16[2,2,4,256,256]{4,3,2,1,0:T(8,128)(2,1)S(1)}, bf16[2,2,4,256,256]{4,3,2,1,0:T(8,128)(2,1)}, u32[]{:S(2)}) copy-start(bf16[2,2,4,256,256]{4,3,2,1,0:T(8,128)(2,1)} %refs_4_.3) | copy-start | bytes 6291460
  4.9 1.8 %copy-start.5 = (bf16[2,4,256,256]{3,2,1,0:T(8,128)(2,1)S(1)}, bf16[2,4,256,256]{3,2,1,0:T(8,128)(2,1)}, u32[]{:S(2)}) copy-start(bf16[2,4,256,256]{3,2,1,0:T(8,128)(2,1)} %refs_1_.5) | copy-start | bytes 3145732
  4.9 32.9 %collective-permute-start.7 = (bf16[2,2,2,3,64,256]{5,4,3,2,1,0:T(8,128)(2,1)S(1)}, bf16[2,2,2,3,64,256]{5,4,3,2,1,0:T(8,128)(2,1)S(1)}, u32[]{:S(2)}, u32[]{:S(2)}) collective-permute-start(bf16[2,2,2,3,64,256]{5,4,3,2,1,0:T(8,128)(2,1)S(1)} %get-tuple-element.41.refs_2_), channel_id=1, source_target_pairs={{0,3},{1,2},{2,1},{3,0},{4,7},{5,6},{6,5},{7,4},{8,11},{9,10},{10,... | collective-permute-start | bytes 2359304 | tf_op jit(solution)/shard_map/ppermute | solution.py:494
  13.9 29.5 %collective-permute-start.4 = (bf16[2,256,512]{2,1,0:T(8,128)(2,1)S(1)}, bf16[2,256,512]{2,1,0:T(8,128)(2,1)S(1)}, u32[]{:S(2)}, u32[]{:S(2)}) collective-permute-start(bf16[2,256,512]{2,1,0:T(8,128)(2,1)S(1)} %get-tuple-element.77.refs_2_), channel_id=1, source_target_pairs={{0,4},{4,0},{8,12},{12,8},{16,20},{20,16},{24,28},{28,24},{1,5},{5... | collective-permute-start | bytes 1572872 | tf_op jit(solution)/shard_map/ppermute | solution.py:498
  15.5 28.0 %collective-permute-start.3 = (bf16[2,256,512]{2,1,0:T(8,128)(2,1)S(1)}, bf16[2,256,512]{2,1,0:T(8,128)(2,1)S(1)}, u32[]{:S(2)}, u32[]{:S(2)}) collective-permute-start(bf16[2,256,512]{2,1,0:T(8,128)(2,1)S(1)} %get-tuple-element.78.refs_0_), channel_id=1, source_target_pairs={{0,4},{4,0},{8,12},{12,8},{16,20},{20,16},{24,28},{28,24},{1,5},{5... | collective-permute-start | bytes 1572872 | tf_op jit(solution)/shard_map/ppermute | solution.py:498
  21.9 23.0 %collective-permute-start = (bf16[2,2,2,1,64,256]{5,4,3,2,1,0:T(8,128)(2,1)S(1)}, bf16[2,2,2,1,64,256]{5,4,3,2,1,0:T(8,128)(2,1)S(1)}, u32[]{:S(2)}, u32[]{:S(2)}) collective-permute-start(bf16[2,2,2,1,64,256]{5,4,3,2,1,0:T(8,128)(2,1)S(1)} %get-tuple-element.43), channel_id=1, source_target_pairs={{0,1},{1,0},{2,3},{3,2},{4,5},{5,4},{6,7},{7,6},{8,9},{9,8},{10,11... | collective-permute-start | bytes 786440 | tf_op jit(solution)/shard_map/ppermute | solution.py:494
  21.9 23.0 %collective-permute-start.1 = (bf16[2,2,2,1,64,256]{5,4,3,2,1,0:T(8,128)(2,1)S(1)}, bf16[2,2,2,1,64,256]{5,4,3,2,1,0:T(8,128)(2,1)S(1)}, u32[]{:S(2)}, u32[]{:S(2)}) collective-permute-start(bf16[2,2,2,1,64,256]{5,4,3,2,1,0:T(8,128)(2,1)S(1)} %get-tuple-element.44), channel_id=1, source_target_pairs={{0,2},{1,3},{2,0},{3,1},{4,6},{5,7},{6,4},{7,5},{8,10},{9,11},{10,... | collective-permute-start | bytes 786440 | tf_op jit(solution)/shard_map/ppermute | solution.py:494
  37.8 10.1 %collective-permute-start.2 = (bf16[2,2,2,1,64,256]{5,4,3,2,1,0:T(8,128)(2,1)S(1)}, bf16[2,2,2,1,64,256]{5,4,3,2,1,0:T(8,128)(2,1)S(1)}, u32[]{:S(2)}, u32[]{:S(2)}) collective-permute-start(bf16[2,2,2,1,64,256]{5,4,3,2,1,0:T(8,128)(2,1)S(1)} %get-tuple-element.45), channel_id=1, source_target_pairs={{0,3},{1,2},{2,1},{3,0},{4,7},{5,6},{6,5},{7,4},{8,11},{9,10},{10,... | collective-permute-start | bytes 786440 | tf_op jit(solution)/shard_map/ppermute | solution.py:494
  49.0 9.2 %collective-permute-start.11 = (bf16[4,2,64,256]{3,2,1,0:T(8,128)(2,1)S(1)}, bf16[4,2,64,256]{3,2,1,0:T(8,128)(2,1)S(1)}, u32[]{:S(2)}, u32[]{:S(2)}) collective-permute-start(bf16[4,2,64,256]{3,2,1,0:T(8,128)(2,1)S(1)} %get-tuple-element.63), channel_id=1, source_target_pairs={{0,2},{1,3},{2,0},{3,1},{4,6},{5,7},{6,4},{7,5},{8,10},{9,11},{10,... | collective-permute-start | bytes 786440 | tf_op jit(solution)/shard_map/ppermute | solution.py:494
  50.4 13.1 %collective-permute-start.12 = (bf16[4,2,64,256]{3,2,1,0:T(8,128)(2,1)S(1)}, bf16[4,2,64,256]{3,2,1,0:T(8,128)(2,1)S(1)}, u32[]{:S(2)}, u32[]{:S(2)}) collective-permute-start(bf16[4,2,64,256]{3,2,1,0:T(8,128)(2,1)S(1)} %get-tuple-element.64), channel_id=1, source_target_pairs={{0,3},{1,2},{2,1},{3,0},{4,7},{5,6},{6,5},{7,4},{8,11},{9,10},{10,... | collective-permute-start | bytes 786440 | tf_op jit(solution)/shard_map/ppermute | solution.py:494
  51.2 12.3 %collective-permute-start.13 = (bf16[4,2,64,256]{3,2,1,0:T(8,128)(2,1)S(1)}, bf16[4,2,64,256]{3,2,1,0:T(8,128)(2,1)S(1)}, u32[]{:S(2)}, u32[]{:S(2)}) collective-permute-start(bf16[4,2,64,256]{3,2,1,0:T(8,128)(2,1)S(1)} %get-tuple-element.65), channel_id=1, source_target_pairs={{0,1},{1,0},{2,3},{3,2},{4,5},{5,4},{6,7},{7,6},{8,9},{9,8},{10,11... | collective-permute-start | bytes 786440 | tf_op jit(solution)/shard_map/ppermute | solution.py:494
  51.2 18.3 %collective-permute-start.8 = (bf16[4,2,64,256]{3,2,1,0:T(8,128)(2,1)S(1)}, bf16[4,2,64,256]{3,2,1,0:T(8,128)(2,1)S(1)}, u32[]{:S(2)}, u32[]{:S(2)}) collective-permute-start(bf16[4,2,64,256]{3,2,1,0:T(8,128)(2,1)S(1)} %get-tuple-element.59), channel_id=1, source_target_pairs={{0,2},{1,3},{2,0},{3,1},{4,6},{5,7},{6,4},{7,5},{8,10},{9,11},{10,... | collective-permute-start | bytes 786440 | tf_op jit(solution)/shard_map/ppermute | solution.py:494
  52.7 22.0 %collective-permute-start.9 = (bf16[4,2,64,256]{3,2,1,0:T(8,128)(2,1)S(1)}, bf16[4,2,64,256]{3,2,1,0:T(8,128)(2,1)S(1)}, u32[]{:S(2)}, u32[]{:S(2)}) collective-permute-start(bf16[4,2,64,256]{3,2,1,0:T(8,128)(2,1)S(1)} %get-tuple-element.60), channel_id=1, source_target_pairs={{0,3},{1,2},{2,1},{3,0},{4,7},{5,6},{6,5},{7,4},{8,11},{9,10},{10,... | collective-permute-start | bytes 786440 | tf_op jit(solution)/shard_map/ppermute | solution.py:494
  58.3 16.5 %collective-permute-start.10 = (bf16[4,2,64,256]{3,2,1,0:T(8,128)(2,1)S(1)}, bf16[4,2,64,256]{3,2,1,0:T(8,128)(2,1)S(1)}, u32[]{:S(2)}, u32[]{:S(2)}) collective-permute-start(bf16[4,2,64,256]{3,2,1,0:T(8,128)(2,1)S(1)} %get-tuple-element.61), channel_id=1, source_target_pairs={{0,1},{1,0},{2,3},{3,2},{4,5},{5,4},{6,7},{7,6},{8,9},{9,8},{10,11... | collective-permute-start | bytes 786440 | tf_op jit(solution)/shard_map/ppermute | solution.py:494
  67.8 12.8 %collective-permute-start.15 = (bf16[256,512]{1,0:T(8,128)(2,1)S(1)}, bf16[256,512]{1,0:T(8,128)(2,1)S(1)}, u32[]{:S(2)}, u32[]{:S(2)}) collective-permute-start(bf16[256,512]{1,0:T(8,128)(2,1)S(1)} %get-tuple-element.68.refs_6_.refs_1_), channel_id=1, source_target_pairs={{0,4},{4,0},{8,12},{12,8},{16,20},{20,16},{24,28},{28,24},{1,5},{5... | collective-permute-start | bytes 786440 | tf_op jit(solution)/shard_map/ppermute | solution.py:498
  79.1 9.5 %copy-start.3 = (f32[4,256,512]{2,1,0:T(8,128)}, f32[4,256,512]{2,1,0:T(8,128)S(1)}, u32[]{:S(2)}) copy-start(f32[4,256,512]{2,1,0:T(8,128)S(1)} %get-tuple-element.70.refs_2_.sum_ref) | copy-start | bytes 6291460
  79.1 8.6 %collective-permute-start.14 = (bf16[256,512]{1,0:T(8,128)(2,1)S(1)}, bf16[256,512]{1,0:T(8,128)(2,1)S(1)}, u32[]{:S(2)}, u32[]{:S(2)}) collective-permute-start(bf16[256,512]{1,0:T(8,128)(2,1)S(1)} %get-tuple-element.69.refs_4_.refs_1_), channel_id=1, source_target_pairs={{0,4},{4,0},{8,12},{12,8},{16,20},{20,16},{24,28},{28,24},{1,5},{5... | collective-permute-start | bytes 786440 | tf_op jit(solution)/shard_map/ppermute | solution.py:498
  81.6 7.7 %collective-permute-start.17 = (bf16[256,512]{1,0:T(8,128)(2,1)S(1)}, bf16[256,512]{1,0:T(8,128)(2,1)S(1)}, u32[]{:S(2)}, u32[]{:S(2)}) collective-permute-start(bf16[256,512]{1,0:T(8,128)(2,1)S(1)} %get-tuple-element.73.refs_4_), channel_id=1, source_target_pairs={{0,8},{4,12},{1,9},{5,13},{2,10},{6,14},{3,11},{7,15}} | collective-permute-start | bytes 786440 | tf_op jit(solution)/shard_map/ppermute | solution.py:502
  88.6 2.3 %collective-permute-start.16 = (bf16[256,512]{1,0:T(8,128)(2,1)S(1)}, bf16[256,512]{1,0:T(8,128)(2,1)S(1)}, u32[]{:S(2)}, u32[]{:S(2)}) collective-permute-start(bf16[256,512]{1,0:T(8,128)(2,1)S(1)} %get-tuple-element.74.refs_3_), channel_id=1, source_target_pairs={{0,8},{4,12},{1,9},{5,13},{2,10},{6,14},{3,11},{7,15}} | collective-permute-start | bytes 786440 | tf_op jit(solution)/shard_map/ppermute | solution.py:502
  89.3 3.3 %copy-start.4 = (f32[4,256,512]{2,1,0:T(8,128)S(1)}, f32[4,256,512]{2,1,0:T(8,128)}, u32[]{:S(2)}) copy-start(f32[4,256,512]{2,1,0:T(8,128)} %copy-done.3) | copy-start | bytes 6291460
  90.2 5.2 %collective-permute-start.19 = (bf16[256,512]{1,0:T(8,128)(2,1)S(1)}, bf16[256,512]{1,0:T(8,128)(2,1)S(1)}, u32[]{:S(2)}, u32[]{:S(2)}) collective-permute-start(bf16[256,512]{1,0:T(8,128)(2,1)S(1)} %combine.4.refs_3_), channel_id=1, source_target_pairs={{8,16},{12,20},{9,17},{13,21},{10,18},{14,22},{11,19},{15,23}} | collective-permute-start | bytes 786440 | tf_op jit(solution)/shard_map/ppermute | solution.py:502
  91.9 5.9 %collective-permute-start.18 = (bf16[256,512]{1,0:T(8,128)(2,1)S(1)}, bf16[256,512]{1,0:T(8,128)(2,1)S(1)}, u32[]{:S(2)}, u32[]{:S(2)}) collective-permute-start(bf16[256,512]{1,0:T(8,128)(2,1)S(1)} %combine.5._), channel_id=1, source_target_pairs={{8,16},{12,20},{9,17},{13,21},{10,18},{14,22},{11,19},{15,23}} | collective-permute-start | bytes 786440 | tf_op jit(solution)/shard_map/ppermute | solution.py:502
  96.4 11.5 %collective-permute-start.21 = (bf16[256,512]{1,0:T(8,128)(2,1)S(1)}, bf16[256,512]{1,0:T(8,128)(2,1)S(1)}, u32[]{:S(2)}, u32[]{:S(2)}) collective-permute-start(bf16[256,512]{1,0:T(8,128)(2,1)S(1)} %combine.6.refs_4_), channel_id=1, source_target_pairs={{16,24},{20,28},{17,25},{21,29},{18,26},{22,30},{19,27},{23,31}} | collective-permute-start | bytes 786440 | tf_op jit(solution)/shard_map/ppermute | solution.py:502
  98.7 14.6 %collective-permute-start.20 = (bf16[256,512]{1,0:T(8,128)(2,1)S(1)}, bf16[256,512]{1,0:T(8,128)(2,1)S(1)}, u32[]{:S(2)}, u32[]{:S(2)}) collective-permute-start(bf16[256,512]{1,0:T(8,128)(2,1)S(1)} %combine.7.refs_7_.refs_5_), channel_id=1, source_target_pairs={{16,24},{20,28},{17,25},{21,29},{18,26},{22,30},{19,27},{23,31}} | collective-permute-start | bytes 786440 | tf_op jit(solution)/shard_map/ppermute | solution.py:502
